TPU v7x, 32 devices: a whole 2x2x4 slice. The times are simulated.
32 devices in a mesh: dp: 16 (over z, y, x), tensor: 2 (over core).
Axes of the slice: x: 2, y: 2, z: 4, core: 2. Of those that a mesh axis runs over, the one named last changes fastest.
Arguments:
- tokens: bfloat16 [1024, 4096], P(('dp', 'tensor')), may hold values from -6 to 6
- out_grad: bfloat16 [1024, 4096], P(('dp', 'tensor')), may hold values from -6 to 6
- weight_tiles: bfloat16 [128, 3, 112, 3, 128], P('dp', None, 'tensor'), may hold values from -0.3125 to 0.3125
- tile_counts: int32 [3, 112], P(None, 'tensor'), may hold values from 1 to 3, as said below
- tile_rows: int32 [3, 112, 3], P(None, 'tensor'), may hold values from 0 to 31, as said below
Outputs:
- ffn_out: bfloat16 [1024, 4096], P(('dp', 'tensor'))
- input_grad: bfloat16 [1024, 4096], P(('dp', 'tensor'))
- tile_grad: bfloat16 [128, 3, 112, 3, 128], P('dp', None, 'tensor')
Inputs may be any that keep to these rules, and one draw needn't show every extreme that they name: `tile_counts`: for each matrix and each q, the live slots of hidden blocks q * 56 to (q + 1) * 56 - 1 number at most 112 together, and for each matrix some q reaches 112. `tile_rows`: within one hidden block of one matrix the 3 feature blocks are distinct.
All inputs are finite; a program needn't handle non-finite values.
Results may differ from a plain program's by a relative error of at most 0.018.
Values may be sent and summed in bfloat16 or wider, within the bound.
No kernel may reach another device: no remote copies, remote signals or barrier semaphores. Data moves between devices by JAX's collectives and lax.ppermute only.
A program may use at most 128 MiB of HBM per device.

v0:
```python
import math

import jax
import jax.numpy as jnp
from jax import lax
from jax.sharding import PartitionSpec as P


def shards(tokens, out_grad, weight_tiles, tile_counts, tile_rows):
    highest = lax.Precision.HIGHEST
    row_share = weight_tiles.shape[0]
    blocks_dev = weight_tiles.shape[2]
    slot_count = weight_tiles.shape[3]
    tile_size = weight_tiles.shape[4]
    feature_count = tokens.shape[1]
    row_blocks = feature_count // tile_size
    slot_total = blocks_dev * slot_count
    own_rows = tokens.shape[0]
    grad_scale = 1.0 / math.sqrt(own_rows * lax.axis_size("tensor") * lax.axis_size("dp"))
    inputs, grads_in = (
        lax.all_gather(tokens, "tensor", axis=0, tiled=True),
        lax.all_gather(out_grad, "tensor", axis=0, tiled=True),
    )
    group_rows = inputs.shape[0]
    live_all = (
        jnp.arange(slot_count, dtype=jnp.int32)[None, None, :] < tile_counts[:, :, None]
    ).reshape(3, slot_total)
    rows_all = tile_rows.reshape(3, slot_total)
    cols_all = jnp.broadcast_to(
        jnp.repeat(jnp.arange(blocks_dev, dtype=jnp.int32), slot_count)[None, :], (3, slot_total)
    )
    own_tiles = weight_tiles.reshape(row_share, 3, slot_total, tile_size)
    capacity = blocks_dev * (slot_count - 1)
    keep_order = jnp.argsort(jnp.where(live_all, 0, 1).astype(jnp.int32), axis=1, stable=True)[
        :, :capacity
    ]
    picked = jnp.stack(
        [jnp.take(own_tiles[:, matrix], keep_order[matrix], axis=1) for matrix in range(3)], axis=1
    )
    weights = lax.all_gather(picked, "dp", axis=0, tiled=True)
    live_flags = jnp.take_along_axis(live_all, keep_order, axis=1)
    row_ids = jnp.take_along_axis(rows_all, keep_order, axis=1)
    col_ids = jnp.take_along_axis(cols_all, keep_order, axis=1)
    live_mask = live_flags.astype(jnp.float32)
    col_onehot = (
        col_ids[:, :, None] == jnp.arange(blocks_dev, dtype=jnp.int32)[None, None, :]
    ).astype(jnp.float32) * live_mask[:, :, None]
    row_onehot = (
        row_ids[:, :, None] == jnp.arange(row_blocks, dtype=jnp.int32)[None, None, :]
    ).astype(jnp.float32) * live_mask[:, :, None]
    input_blocks = inputs.reshape(group_rows, row_blocks, tile_size)
    grad_blocks = grads_in.reshape(group_rows, row_blocks, tile_size)
    gate_sel = jnp.take(input_blocks, row_ids[0], axis=1)
    up_sel = jnp.take(input_blocks, row_ids[1], axis=1)
    gate_prod = jnp.einsum(
        "tsa,asb->tsb", gate_sel, weights[:, 0], preferred_element_type=jnp.float32
    )
    gate_pre = jnp.einsum("tsb,sj->tjb", gate_prod, col_onehot[0], precision=highest)
    up_prod = jnp.einsum("tsa,asb->tsb", up_sel, weights[:, 1], preferred_element_type=jnp.float32)
    up_pre = jnp.einsum("tsb,sj->tjb", up_prod, col_onehot[1], precision=highest)
    gate_sig = jax.nn.sigmoid(gate_pre)
    gate_act = gate_pre * gate_sig
    hidden = (gate_act * up_pre).astype(jnp.bfloat16)
    hidden_sel = jnp.take(hidden, col_ids[2], axis=1)
    products = jnp.einsum(
        "tsa,asb->tsb", hidden_sel, weights[:, 2], preferred_element_type=jnp.float32
    )
    ffn_rows = lax.psum_scatter(
        jnp.einsum("tsb,sr->trb", products, row_onehot[2], precision=highest)
        .reshape(lax.axis_size("tensor") * own_rows, feature_count)
        .astype(jnp.bfloat16),
        "tensor",
        scatter_dimension=0,
        tiled=True,
    )
    grad_sel = jnp.take(grad_blocks, row_ids[2], axis=1)
    dh_slots = jnp.einsum(
        "tsb,asb->tsa", grad_sel, weights[:, 2], preferred_element_type=jnp.float32
    )
    dh_blocks = jnp.einsum("tsa,sj->tja", dh_slots, col_onehot[2], precision=highest)
    grad_gate = (dh_blocks * up_pre * gate_sig * (1.0 + gate_pre * (1.0 - gate_sig))).astype(
        jnp.bfloat16
    )
    grad_up = (dh_blocks * gate_act).astype(jnp.bfloat16)
    dgate_sel = jnp.take(grad_gate, col_ids[0], axis=1)
    dup_sel = jnp.take(grad_up, col_ids[1], axis=1)
    tile_terms = jnp.stack(
        [
            jnp.einsum("tsa,tsb->asb", gate_sel, dgate_sel, preferred_element_type=jnp.float32),
            jnp.einsum("tsa,tsb->asb", up_sel, dup_sel, preferred_element_type=jnp.float32),
            jnp.einsum("tsa,tsb->asb", hidden_sel, grad_sel, preferred_element_type=jnp.float32),
        ],
        axis=1,
    )
    tile_sums = lax.psum_scatter(
        (tile_terms * (live_mask * grad_scale)[None, :, :, None]).astype(jnp.bfloat16),
        "dp",
        scatter_dimension=0,
        tiled=True,
    ).astype(jnp.float32)
    from_gate = jnp.einsum(
        "tsb,asb->tsa", dgate_sel, weights[:, 0], preferred_element_type=jnp.float32
    )
    from_up = jnp.einsum("tsb,asb->tsa", dup_sel, weights[:, 1], preferred_element_type=jnp.float32)
    summed = jnp.einsum("tsa,sr->tra", from_gate, row_onehot[0], precision=highest)
    summed = summed + jnp.einsum("tsa,sr->tra", from_up, row_onehot[1], precision=highest)
    input_rows = lax.psum_scatter(
        summed.reshape(lax.axis_size("tensor") * own_rows, feature_count).astype(jnp.bfloat16),
        "tensor",
        scatter_dimension=0,
        tiled=True,
    )
    spread = (
        keep_order[:, :, None] == jnp.arange(slot_total, dtype=jnp.int32)[None, None, :]
    ).astype(jnp.float32)
    tile_sums = jnp.einsum("amcb,mcs->amsb", tile_sums, spread, precision=highest)
    tile_grad = tile_sums.reshape(row_share, 3, blocks_dev, slot_count, tile_size).astype(
        jnp.bfloat16
    )
    return (ffn_rows, input_rows, tile_grad)


def solution(mesh):
    return jax.shard_map(
        shards,
        mesh=mesh,
        in_specs=(
            P(("dp", "tensor"), None),
            P(("dp", "tensor"), None),
            P("dp", None, "tensor", None, None),
            P(None, "tensor"),
            P(None, "tensor", None),
        ),
        out_specs=(
            P(("dp", "tensor"), None),
            P(("dp", "tensor"), None),
            P("dp", None, "tensor", None, None),
        ),
        check_vma=False,
    )
```

profile of v0, /device:TPU:0, one launch (start us, length us, event | category | flops | bytes accessed | tf_op | source)
XLA Modules:
  0.0 467.5 jit_solution(14781118430560222980)
XLA Ops:
  9.1 3.3 sort.17
  16.0 5.0 %gather_fusion = pred[336]{0:T(512)(128)(4,1)S(1)} fusion(pred[3,168]{1,0:T(4,128)(4,1)S(1)} %get-tuple-element.42, s32[336]{0:T(512)S(1)} %reshape.194), kind=kCustom, calls=%fused_computation.11 | custom fusion | bytes 3360 | tf_op jit(solution)/shard_map/jit(take_along_axis)/gather | solution.py:41
  21.2 5.1 %gather_fusion.5 = s32[336]{0:T(512)S(1)} fusion(s32[3,168]{1,0:T(4,128)S(1)} %broadcast_in_dim.68, s32[336]{0:T(512)S(1)} %reshape.194), kind=kCustom, calls=%fused_computation.4.clone | custom fusion | bytes 5376 | tf_op jit(solution)/shard_map/jit(take_along_axis)/gather | solution.py:43
  26.7 5.1 %gather_fusion.1 = s32[336]{0:T(512)S(1)} fusion(s32[3,168]{1,0:T(4,128)S(1)} %reshape.73, s32[336]{0:T(512)S(1)} %reshape.194), kind=kCustom, calls=%fused_computation.clone | custom fusion | bytes 5376 | tf_op jit(solution)/shard_map/jit(take_along_axis)/gather | solution.py:42
  32.0 2.3 all_gather.10
  35.4 2.1 gather_fusion.6
  37.5 2.4 all_gather.11
  40.0 2.0 gather_fusion.9
  42.1 152.5 %all-gather.2.cloned.1.call-done = bf16[128,3,112,128]{3,0,2,1:T(8,128)(2,1)} async-done(((bf16[8,3,112,128]{3,0,2,1:T(8,128)(2,1)}), bf16[128,3,112,128]{3,0,2,1:T(8,128)(2,1)}) %all-gather.2.cloned.1.call-update) | async-done | bytes 11010064 | tf_op jit(solution)/shard_map/all_gather | solution.py:40
  194.6 3.3 fusion.21
  197.9 4.1 fusion.9
  203.3 4.1 fusion.11
  207.4 3.0 fusion.20
  210.4 5.1 %fusion.31 = (bf16[64,56,128]{2,1,0:T(8,128)(2,1)S(1)}, bf16[64,56,128]{2,1,0:T(8,128)(2,1)S(1)}, bf16[64,56,128]{2,1,0:T(8,128)(2,1)S(1)}) fusion(f32[56,64,128]{2,0,1:T(8,128)S(1)} %fusion.9, f32[56,64,128]{2,0,1:T(8,128)S(1)} %fusion.11, f32[64,112,128]{2,0,1:T(8,128)S(1)} %fusion.20, f32[3,112,56]{1,2,0:T(8,128)S(1)} %fusion.60), kind=kOutput, calls=%fused_computation.52 | convolution fusion | flops 623443968 | bytes 10121216 | tf_op jit(solution)/shard_map/tsa,sj->tja/dot_general | solution.py:80
  218.1 3.3 gather_fusion.8
  221.4 2.0 gather_fusion.11
  223.4 3.2 gather_fusion.10
  226.6 3.7 convolution_bitcast_fusion
  230.3 1.5 convolution_bitcast_fusion.1
  232.3 1.5 convolution_bitcast_fusion.2
  233.8 5.5 %fusion = bf16[128,3,112,128]{0,3,2,1:T(8,128)(2,1)} fusion(f32[128,1,112,128]{0,3,2,1:T(8,128)S(1)} %convolution_bitcast_fusion, f32[128,1,112,128]{0,3,2,1:T(8,128)S(1)} %convolution_bitcast_fusion.1, f32[128,1,112,128]{0,3,2,1:T(8,128)S(1)} %convolution_bitcast_fusion.2, f32[3,112]{1,0:T(4,128)S(1)} %get-tuple-element.21), kind=kLoop, calls=%fused_computation.13 | loop fusion | flops 22020096 | bytes 33031488 | tf_op jit(solution)/shard_map/convert_element_type | solution.py:96
  239.4 15.0 %copy.52 = bf16[128,3,112,128]{3,2,1,0:T(8,128)(2,1)} copy(bf16[128,3,112,128]{0,3,2,1:T(8,128)(2,1)} %fusion) | data formatting | bytes 22020096 | tf_op jit(solution)/shard_map/convert_element_type | solution.py:96
  255.9 3.2 fusion.19
  259.1 4.0 fusion.53
  264.4 4.6 fusion.22
  269.0 4.0 fusion.1
  273.0 4.7 %fusion.24 = f32[64,112,128]{2,0,1:T(8,128)S(1)} fusion(bf16[128,3,112,128]{3,0,2,1:T(8,128)(2,1)} %all-gather.2.cloned.1.call-done, bf16[112,64,128]{2,1,0:T(8,128)(2,1)S(1)} %copy-done.4, pred[112]{0:T(512)(128)(4,1)S(1)} %get-tuple-element.23), kind=kOutput, calls=%fused_computation.43 | convolution fusion | flops 235798528 | bytes 9175152 | tf_op jit(solution)/shard_map/tsb,asb->tsa/dot_general | solution.py:101
  277.7 4.0 fusion.50
  282.8 155.9 %reduce-scatter.8.cloned.1.call-done = bf16[8,3,112,128]{3,2,1,0:T(8,128)(2,1)} async-done(((bf16[128,3,112,128]{3,2,1,0:T(8,128)(2,1)}), bf16[8,3,112,128]{3,2,1,0:T(8,128)(2,1)}) %reduce-scatter.8.cloned.1.call-update) | async-done | bytes 688144 | tf_op jit(solution)/shard_map/reduce_scatter | solution.py:95
  438.7 1.5 fusion.49
  441.4 7.5 %reduce-scatter.4.cloned.1.call-done = bf16[32,4096]{1,0:T(8,128)(2,1)} async-done(((bf16[64,4096]{1,0:T(8,128)(2,1)}), bf16[32,4096]{1,0:T(8,128)(2,1)}) %reduce-scatter.4.cloned.1.call-update) | async-done | bytes 262160 | tf_op jit(solution)/shard_map/reduce_scatter | solution.py:68
  449.0 11.8 %reduce-scatter.6.cloned.1.call-done = bf16[32,4096]{1,0:T(8,128)(2,1)} async-done(((bf16[64,4096]{1,0:T(8,128)(2,1)}), bf16[32,4096]{1,0:T(8,128)(2,1)}) %reduce-scatter.6.cloned.1.call-update) | async-done | bytes 262160 | tf_op jit(solution)/shard_map/reduce_scatter | solution.py:107
  (86 shorter events, 16.6 us)
Async XLA Ops:
  7.2 1.5 copy-start.12
  7.2 187.4 %all-gather.2.cloned.1.call-start = ((), (), s32[]{:S(2)}) async-start(), calls=%async_computation.3 | async-start | bytes 11698176 | tf_op jit(solution)/shard_map/all_gather | solution.py:40
  15.9 10.6 %copy-start.11 = (s32[3,56,3]{1,2,0:T(4,128)S(1)}, s32[3,56,3]{1,2,0:T(4,128)}, u32[]{:S(2)}) copy-start(s32[3,56,3]{1,2,0:T(4,128)} %param.17) | copy-start | bytes 6052
  15.9 422.8 %reduce-scatter.8.cloned.1.call-start = ((), (), s32[]{:S(2)}) async-start(), calls=%async_computation.6 | async-start | bytes 11698176 | tf_op jit(solution)/shard_map/reduce_scatter | solution.py:95
  21.2 10.8 %copy-start.9 = (bf16[32,4096]{1,0:T(8,128)(2,1)S(1)}, bf16[32,4096]{1,0:T(8,128)(2,1)}, u32[]{:S(2)}) copy-start(bf16[32,4096]{1,0:T(8,128)(2,1)} %param.13) | copy-start | bytes 786436
  35.3 2.1 copy-start.10
  194.6 7.5 %copy-start = (bf16[128,3,112,128]{3,0,2,1:T(8,128)(2,1)S(1)}, bf16[128,3,112,128]{3,0,2,1:T(8,128)(2,1)}, u32[]{:S(2)}) copy-start(bf16[128,3,112,128]{3,0,2,1:T(8,128)(2,1)} %all-gather.2.cloned.1.call-done) | copy-start | bytes 33030148
  197.9 4.2 copy-start.1
  203.3 4.2 copy-start.7
  226.6 3.7 copy-start.5
  230.3 1.5 copy-start.2
  230.3 2.0 copy-start.3
  254.4 1.5 copy-start.8
  254.4 194.5 %reduce-scatter.4.cloned.1.call-start = ((), (), s32[]{:S(2)}) async-start(), calls=%async_computation.4 | async-start | bytes 786432 | tf_op jit(solution)/shard_map/reduce_scatter | solution.py:68
  259.1 5.3 %copy-start.6 = (bf16[112,64,128]{2,1,0:T(8,128)(2,1)S(1)}, bf16[112,64,128]{2,1,0:T(8,128)(2,1)}, u32[]{:S(2)}) copy-start(bf16[112,64,128]{2,1,0:T(8,128)(2,1)} %gather_fusion.11) | copy-start | bytes 5505028
  264.1 196.7 %reduce-scatter.6.cloned.1.call-start = ((), (), s32[]{:S(2)}) async-start(), calls=%async_computation.5 | async-start | bytes 786432 | tf_op jit(solution)/shard_map/reduce_scatter | solution.py:107
  269.0 4.0 copy-start.4
Sparse Core Ops, SparseCore 0:
  16.0 178.5 all-gather.1
  254.6 184.0 reduce-scatter.7
  441.6 7.3 reduce-scatter.3
  451.6 9.1 reduce-scatter.5
where the time goes:
time: 473 us; the launch traced here: 468 us
  waiting for transfers between devices  328 us (69%)
  local copies, waits for them, and re-layouts  56.4 us (12%)
  matrix products  53.5 us (11%)
  between operations  14.4 us (3%)
  other arithmetic  10.4 us (2%)
    reduce_scatter x1, waiting for transfers between devices, shards(): lax.psum_scatter((tile_terms * (live_mask * grad_scale)[None, :, :, None]...  156 us
    all_gather x1, waiting for transfers between devices, shards(): weights = lax.all_gather(picked, 'dp', axis=0, tiled=True)  153 us
    convert_element_type x1, local copies, waits for them, and re-layouts, shards(): (tile_terms * (live_mask * grad_scale)[None, :, :, None]).astype(jnp.bflo...  15 us
    reduce_scatter x1, waiting for transfers between devices, shards(): lax.psum_scatter(summed.reshape(lax.axis_size('tensor') * own_rows, featu...  11.8 us
  transfers between devices with their start and end apart: 4, of which 4 were waited for; matrix products, arithmetic and copies ran while one was open for 11% of the time, Pallas kernels for 0%

commit v1 on v0

v1 whole, which is shorter than its diff:
```python
import functools
import math

import jax
import jax.numpy as jnp
from jax import lax
from jax.experimental import pallas as pl
from jax.experimental.pallas import tpu as pltpu
from jax.sharding import PartitionSpec as P

F32 = jnp.float32
BF16 = jnp.bfloat16


def swap(value, axis, stride):
    size = lax.axis_size(axis)
    return lax.ppermute(value, axis, [(at, at ^ stride) for at in range(size)])


def add(first, *others):
    total = first.astype(F32)
    for other in others:
        total = total + other.astype(F32)
    return total.astype(BF16)


def strides_of(size, unit=1):
    found = []
    step = size // 2
    while step >= 1:
        found.append(step * unit)
        step //= 2
    return found


def gather(items, axis, strides):
    for stride in strides:
        items = {**items, **{at ^ stride: swap(one, axis, stride) for at, one in items.items()}}
    return items


def scatter(items, axis, strides):
    for stride in reversed(strides):
        kept = {}
        for at, one in items.items():
            if not at & stride:
                kept[at] = add(one, swap(items[at ^ stride], axis, stride))
        items = kept
    return items


def layer(
    offsets, counts, rows, *refs, token_parts, weight_parts, slot_count, grad_scale, own_parts
):
    part_count = len(token_parts)
    token_refs, refs = refs[:part_count], refs[part_count:]
    weight_refs, refs = refs[: len(weight_parts)], refs[len(weight_parts) :]
    own_out, other_out, refs = refs[0], refs[1], refs[2:]
    grad_refs, refs = refs[: len(weight_parts)], refs[len(weight_parts) :]
    x_all, g_all, x_turned, ffn_sum, input_sum, tiles, tile_out = refs
    block = pl.program_id(0)
    own_rows = token_refs[0].shape[0] // 2
    tile = tiles.shape[1]
    features = x_all.shape[1]

    @pl.when(block == 0)
    def _():
        for at, ref in enumerate(token_refs):
            x_all[at * own_rows : (at + 1) * own_rows, :] = ref[:own_rows, :]
            g_all[at * own_rows : (at + 1) * own_rows, :] = ref[own_rows:, :]
        ffn_sum[...] = jnp.zeros_like(ffn_sum)
        input_sum[...] = jnp.zeros_like(input_sum)
        for at in range(features // tile):
            x_turned[at * tile : (at + 1) * tile, :] = x_all[:, at * tile : (at + 1) * tile].T

    for ref, (group_at, first, length) in zip(weight_refs, weight_parts):
        for at in range(length):
            offset = pl.multiple_of(offsets[group_at, first + at], ref.shape[3])
            tiles[:, pl.ds(offset, ref.shape[3]), :] = ref[at, 0].astype(F32)

    def columns(matrix, slot):
        return pl.ds(pl.multiple_of(rows[matrix, block, slot] * tile, tile), tile)

    slots = range(slot_count)
    live = [[(slot < counts[matrix, block]).astype(F32) for slot in slots] for matrix in range(3)]

    def tile_of(matrix, slot):
        return (tiles[matrix * slot_count + slot] * live[matrix][slot]).astype(BF16)

    gate_tiles = jnp.concatenate([tile_of(0, slot) for slot in slots], axis=0)
    up_tiles = jnp.concatenate([tile_of(1, slot) for slot in slots], axis=0)
    down_tiles = jnp.concatenate([tile_of(2, slot) for slot in slots], axis=1)
    gate_in = jnp.concatenate([x_all[:, columns(0, slot)] for slot in slots], axis=1)
    up_in = jnp.concatenate([x_all[:, columns(1, slot)] for slot in slots], axis=1)
    grad_in = jnp.concatenate([g_all[:, columns(2, slot)] for slot in slots], axis=1)
    dot = functools.partial(lax.dot_general, preferred_element_type=F32)
    plain = (((1,), (0,)), ((), ()))
    turned = (((1,), (1,)), ((), ()))
    gate_pre = dot(gate_in, gate_tiles, plain)
    up_pre = dot(up_in, up_tiles, plain)
    gate_sig = jax.nn.sigmoid(gate_pre)
    gate_act = gate_pre * gate_sig
    hidden = (gate_act * up_pre).astype(BF16)
    ffn = dot(hidden, down_tiles, plain)
    hidden_grad = dot(grad_in, down_tiles, turned)
    gate_grad = (hidden_grad * up_pre * gate_sig * (1.0 + gate_pre * (1.0 - gate_sig))).astype(BF16)
    up_grad = (hidden_grad * gate_act).astype(BF16)
    from_gate = dot(gate_grad, gate_tiles, turned)
    from_up = dot(up_grad, up_tiles, turned)
    for slot in slots:
        here = slice(slot * tile, (slot + 1) * tile)
        ffn_sum[:, columns(2, slot)] += ffn[:, here]
        input_sum[:, columns(0, slot)] += from_gate[:, here]
        input_sum[:, columns(1, slot)] += from_up[:, here]
    down_terms = dot(hidden.T, grad_in, plain)
    for slot in slots:
        here = slice(slot * tile, (slot + 1) * tile)
        tile_out[slot] = dot(x_turned[columns(0, slot), :], gate_grad, plain) * (
            live[0][slot] * grad_scale
        )
        tile_out[slot_count + slot] = dot(x_turned[columns(1, slot), :], up_grad, plain) * (
            live[1][slot] * grad_scale
        )
        tile_out[2 * slot_count + slot] = down_terms[:, here] * (live[2][slot] * grad_scale)
    for ref, (group_at, first, length) in zip(grad_refs, weight_parts):
        for at in range(length):
            offset = pl.multiple_of(offsets[group_at, first + at], ref.shape[3])
            ref[at, 0] = tile_out[:, pl.ds(offset, ref.shape[3]), :].astype(BF16)

    @pl.when(block == pl.num_programs(0) - 1)
    def _():
        own_at, other_at = 0, 0
        for at in range(part_count):
            source = slice(at * own_rows, (at + 1) * own_rows)
            if at in own_parts:
                ref, place = own_out, own_at
                own_at += 1
            else:
                ref, place = other_out, other_at
                other_at += 1
            ref[place, :own_rows, :] = ffn_sum[source, :].astype(BF16)
            ref[place, own_rows:, :] = input_sum[source, :].astype(BF16)


def shards(tokens, out_grad, weight_tiles, tile_counts, tile_rows):
    row_share, _, blocks_dev, slot_count, tile = weight_tiles.shape
    own_rows, features = tokens.shape
    dp_size, tensor_size = lax.axis_size("dp"), lax.axis_size("tensor")
    far = math.gcd(4, math.gcd(dp_size, blocks_dev))
    near = dp_size // far
    blocks = blocks_dev // far
    terms = 3 * slot_count
    grad_scale = 1.0 / math.sqrt(own_rows * tensor_size * dp_size)
    me = lax.axis_index("dp")
    far_at, near_at = me // near, me % near
    far_strides, near_strides = strides_of(far, near), strides_of(near)
    tensor_strides = strides_of(tensor_size)

    quarters = (
        jnp.transpose(weight_tiles, (2, 1, 3, 0, 4))
        .reshape(far, blocks, terms, row_share, tile)
    )
    held = [lax.dynamic_index_in_dim(quarters, far_at, 0, keepdims=False)]
    for at in range(1, far):
        part = lax.dynamic_index_in_dim(quarters, far_at ^ at, 0, keepdims=False)
        held.append(swap(part, "dp", at * near))
    held = jnp.stack(held)

    both = jnp.concatenate([tokens, out_grad], axis=0)
    token_items = gather({0: both}, "dp", far_strides)
    token_list, token_parts = [], []
    for at in sorted(token_items):
        spread = gather({0: token_items[at]}, "tensor", tensor_strides)
        for other in sorted(spread):
            token_parts.append((at, other))
            token_list.append(spread[other])
    half = far // 2
    split = near == 4 and far % 2 == 0
    if split:
        from_1, from_2 = swap(held, "dp", 1), swap(held, "dp", 2)
        weight_list = [
            held, from_1, from_2, swap(from_1[:half], "dp", 2), swap(from_2[half:], "dp", 1)
        ]
        weight_parts = [(0, 0, far), (1, 0, far), (2, 0, far), (3, 0, half), (3, half, half)]
    else:
        items = gather({0: held}, "dp", near_strides)
        weight_list = [items[at] for at in range(near)]
        weight_parts = [(at, 0, far) for at in range(near)]

    counts = lax.dynamic_slice_in_dim(tile_counts, far_at * blocks, blocks, 1)
    rows = lax.dynamic_slice_in_dim(tile_rows, far_at * blocks, blocks, 1)
    offsets = (
        (jnp.arange(far, dtype=jnp.int32)[None, :] ^ far_at) * near
        + (jnp.arange(near, dtype=jnp.int32)[:, None] ^ near_at)
    ) * row_share

    part_count = len(token_parts)
    group_rows = part_count * own_rows
    own_parts = tuple(at for at, (_, other) in enumerate(token_parts) if other == 0)
    other_count = part_count - len(own_parts)
    whole = lambda shape: pl.BlockSpec(shape, lambda block, *_: (0,) * len(shape))
    weight_specs = [
        pl.BlockSpec(
            (length, 1, terms, row_share, tile), lambda block, *_: (0, block, 0, 0, 0)
        )
        for _, _, length in weight_parts
    ]
    token_specs = [whole((2 * own_rows, features))] * part_count
    flops = 18 * blocks * slot_count * group_rows * tile * tile
    outs = pl.pallas_call(
        functools.partial(
            layer,
            token_parts=token_parts,
            weight_parts=weight_parts,
            slot_count=slot_count,
            grad_scale=grad_scale,
            own_parts=own_parts,
        ),
        grid_spec=pltpu.PrefetchScalarGridSpec(
            num_scalar_prefetch=3,
            grid=(blocks,),
            in_specs=token_specs + weight_specs,
            out_specs=[
                whole((len(own_parts), 2 * own_rows, features)),
                whole((other_count, 2 * own_rows, features)),
            ]
            + weight_specs,
            scratch_shapes=[
                pltpu.VMEM((group_rows, features), BF16),
                pltpu.VMEM((group_rows, features), BF16),
                pltpu.VMEM((features, group_rows), BF16),
                pltpu.VMEM((group_rows, features), F32),
                pltpu.VMEM((group_rows, features), F32),
                pltpu.VMEM((terms, tile, tile), F32),
                pltpu.VMEM((terms, tile, tile), F32),
            ],
        ),
        out_shape=[
            jax.ShapeDtypeStruct((len(own_parts), 2 * own_rows, features), BF16),
            jax.ShapeDtypeStruct((other_count, 2 * own_rows, features), BF16),
        ]
        + [
            jax.ShapeDtypeStruct((length, blocks, terms, row_share, tile), BF16)
            for _, _, length in weight_parts
        ],
        compiler_params=pltpu.CompilerParams(vmem_limit_bytes=56 * 1024 * 1024),
        cost_estimate=pl.CostEstimate(
            flops=flops, bytes_accessed=20_000_000, transcendentals=blocks * group_rows * tile
        ),
    )(offsets, counts, rows, *token_list, *weight_list)
    own_sums, other_sums, tile_terms = outs[0], outs[1], outs[2:]

    other_parts = [part for part in token_parts if part[1] != 0]
    by_part = {part: other_sums[at] for at, part in enumerate(other_parts)}
    if tensor_size == 2:
        own_sums = add(own_sums, swap(other_sums, "tensor", 1))
        sums = {at * near: own_sums[at] for at in range(far)}
    else:
        sums = {}
        for place, at in enumerate(sorted(token_items)):
            items = {0: own_sums[place]}
            items.update({other: by_part[(at, other)] for other in range(1, tensor_size)})
            sums[at] = scatter(items, "tensor", tensor_strides)[0]
    mine = scatter(sums, "dp", far_strides)[0]

    if split:
        own, to_1, to_2, to_3a, to_3b = tile_terms
        got_a, got_b = swap(to_3a, "dp", 1), swap(to_3b, "dp", 2)
        to_2 = jnp.concatenate([add(to_2[:half], got_a), to_2[half:]])
        to_1 = jnp.concatenate([to_1[:half], add(to_1[half:], got_b)])
        summed = add(own, swap(to_1, "dp", 1), swap(to_2, "dp", 2))
    else:
        summed = scatter(dict(enumerate(tile_terms)), "dp", near_strides)[0]
    back = [summed[0]] + [swap(summed[at], "dp", at * near) for at in range(1, far)]
    order = jnp.arange(far, dtype=jnp.int32) ^ far_at
    tile_grad = (
        jnp.take(jnp.stack(back), order, axis=0)
        .reshape(blocks_dev, 3, slot_count, row_share, tile)
        .transpose(3, 1, 0, 2, 4)
    )
    return mine[:own_rows], mine[own_rows:], tile_grad


def solution(mesh):
    return jax.shard_map(
        shards,
        mesh=mesh,
        in_specs=(
            P(("dp", "tensor"), None),
            P(("dp", "tensor"), None),
            P("dp", None, "tensor", None, None),
            P(None, "tensor"),
            P(None, "tensor", None),
        ),
        out_specs=(
            P(("dp", "tensor"), None),
            P(("dp", "tensor"), None),
            P("dp", None, "tensor", None, None),
        ),
        check_vma=False,
    )
```

time: 473 us -> 210 us (0.44); the launches traced: 468 us -> 209 us
  waiting for transfers between devices: 328 us -> 128 us
  matrix products: 53.5 us -> 0 us
  local copies, waits for them, and re-layouts: 56.4 us -> 12.7 us
  starting transfers between devices: 0.34 us -> 32 us
  Pallas kernels: 0 us -> 24.6 us
  between operations: 14.4 us -> 0.9 us
    reduce_scatter x3 -> x0, waiting for transfers between devices: 175 us -> none  [the longest x1 156 us: shards(): lax.psum_scatter((tile_terms * (live_mask * grad_scale)[None, :, :, None]...]
    all_gather x1 -> x0, waiting for transfers between devices: 153 us -> none  [shards(): weights = lax.all_gather(picked, 'dp', axis=0, tiled=True)]
    ppermute x0 -> x25, waiting for transfers between devices: none -> 128 us  [swap(): return lax.ppermute(value, axis, [(at, at ^ stride) for at in range(size)])]
    dot_general x16 -> x0, matrix products: 53.5 us -> none  [the longest x1 5.11 us: shards(): jnp.einsum('tsa,sj->tja', dh_slots, col_onehot[2], precision=highest)]
    ppermute x0 -> x25, starting transfers between devices: none -> 32 us  [swap(): return lax.ppermute(value, axis, [(at, at ^ stride) for at in range(size)])]
    gather x16 -> x1, local copies, waits for them, and re-layouts: 31.1 us -> 1.65 us  [shards(): jnp.take(jnp.stack(back), order, axis=0)]
    pallas_call x0 -> x1, Pallas kernels: none -> 24.6 us  [shards(): pl.pallas_call(functools.partial(layer, token_parts=token_parts, weight_p...]
    convert_element_type x5 -> x0, local copies, waits for them, and re-layouts: 17.7 us -> none  [the longest x1 15 us: shards(): (tile_terms * (live_mask * grad_scale)[None, :, :, None]).astype(jnp.bflo...]
  transfers between devices with their start and end apart: 4 -> 25, of which waited for: 4 -> 14; matrix products, arithmetic and copies ran while one was open for 11% -> 9% of each run, Pallas kernels for 0% -> 0%
where the time goes in v1:
time: 210 us; the launch traced here: 209 us
  waiting for transfers between devices  128 us (61%)
  starting transfers between devices  32 us (15%)
  Pallas kernels  24.6 us (12%)
  local copies, waits for them, and re-layouts  12.7 us (6%)
  other arithmetic  11 us (5%)
    ppermute x25, waiting for transfers between devices, swap(): return lax.ppermute(value, axis, [(at, at ^ stride) for at in range(size)])  128 us
    ppermute x25, starting transfers between devices, swap(): return lax.ppermute(value, axis, [(at, at ^ stride) for at in range(size)])  32 us
    pallas_call x1, Pallas kernels, shards(): pl.pallas_call(functools.partial(layer, token_parts=token_parts, weight_p...  24.6 us
    convert_element_type x6, other arithmetic, add(): return total.astype(BF16)  7.53 us
  transfers between devices with their start and end apart: 25, of which 14 were waited for; matrix products, arithmetic and copies ran while one was open for 9% of the time, Pallas kernels for 0%

profile of v1, /device:TPU:0, one launch (start us, length us, event | category | flops | bytes accessed | tf_op | source)
XLA Modules:
  0.0 209.5 jit_solution(9120690327716276509)
XLA Ops:
  0.7 1.4 copy.9
  2.2 3.1 %collective-permute-start.7 = (bf16[14,9,8,128]{3,2,1,0:T(8,128)(2,1)S(1)}, bf16[14,9,8,128]{3,2,1,0:T(8,128)(2,1)S(1)}, u32[]{:S(2)}, u32[]{:S(2)}) collective-permute-start(bf16[14,9,8,128]{3,2,1,0:T(8,128)(2,1)S(1)} %get-tuple-element.26), channel_id=1, source_target_pairs={{0,8},{2,10},{4,12},{6,14},{8,0},{10,2},{12,4},{14,6},{16,24},{18,... | collective-permute-start | bytes 774152 | tf_op jit(solution)/shard_map/ppermute | solution.py:17
  5.3 2.6 %collective-permute-start.8 = (bf16[14,9,8,128]{3,2,1,0:T(8,128)(2,1)S(1)}, bf16[14,9,8,128]{3,2,1,0:T(8,128)(2,1)S(1)}, u32[]{:S(2)}, u32[]{:S(2)}) collective-permute-start(bf16[14,9,8,128]{3,2,1,0:T(8,128)(2,1)S(1)} %get-tuple-element.25), channel_id=1, source_target_pairs={{0,16},{2,18},{4,20},{6,22},{8,24},{10,26},{12,28},{14,30},{16,0},... | collective-permute-start | bytes 774152 | tf_op jit(solution)/shard_map/ppermute | solution.py:17
  9.3 1.9 collective-permute-start.3
  11.3 5.0 %collective-permute-done.7 = bf16[14,9,8,128]{3,2,1,0:T(8,128)(2,1)S(1)} collective-permute-done((bf16[14,9,8,128]{3,2,1,0:T(8,128)(2,1)S(1)}, bf16[14,9,8,128]{3,2,1,0:T(8,128)(2,1)S(1)}, u32[]{:S(2)}, u32[]{:S(2)}) %collective-permute-start.7) | collective-permute-done | bytes 258080 | tf_op jit(solution)/shard_map/ppermute | solution.py:17
  16.3 21.4 %collective-permute-done.8 = bf16[14,9,8,128]{3,2,1,0:T(8,128)(2,1)S(1)} collective-permute-done((bf16[14,9,8,128]{3,2,1,0:T(8,128)(2,1)S(1)}, bf16[14,9,8,128]{3,2,1,0:T(8,128)(2,1)S(1)}, u32[]{:S(2)}, u32[]{:S(2)}) %collective-permute-start.8) | collective-permute-done | bytes 258080 | tf_op jit(solution)/shard_map/ppermute | solution.py:17
  37.8 1.6 collective-permute-start.10
  39.4 1.5 collective-permute-start.11
  40.9 6.1 %collective-permute-start.1 = (bf16[64,4096]{1,0:T(8,128)(2,1)}, bf16[64,4096]{1,0:T(8,128)(2,1)}, u32[]{:S(2)}, u32[]{:S(2)}) collective-permute-start(bf16[64,4096]{1,0:T(8,128)(2,1)} %constant_dynamic-update-slice_fusion.refs_0_), channel_id=1, source_target_pairs={{0,8},{2,10},{4,12},{6,14},{8,0},{10,2},{12,4},{14,6},{16,24},{18,... | collective-permute-start | bytes 1572872 | tf_op jit(solution)/shard_map/ppermute | solution.py:17
  47.0 6.2 %collective-permute-done.3.refs_4_ = bf16[64,4096]{1,0:T(8,128)(2,1)} collective-permute-done((bf16[64,4096]{1,0:T(8,128)(2,1)}, bf16[64,4096]{1,0:T(8,128)(2,1)}, u32[]{:S(2)}, u32[]{:S(2)}) %collective-permute-start.3) | collective-permute-done | bytes 524320 | tf_op jit(solution)/shard_map/ppermute | solution.py:17
  53.2 11.2 %collective-permute-done.1.refs_2_ = bf16[64,4096]{1,0:T(8,128)(2,1)} collective-permute-done((bf16[64,4096]{1,0:T(8,128)(2,1)}, bf16[64,4096]{1,0:T(8,128)(2,1)}, u32[]{:S(2)}, u32[]{:S(2)}) %collective-permute-start.1) | collective-permute-done | bytes 524320 | tf_op jit(solution)/shard_map/ppermute | solution.py:17
  64.4 11.1 %collective-permute-done.5.refs_6_ = bf16[64,4096]{1,0:T(8,128)(2,1)} collective-permute-done((bf16[64,4096]{1,0:T(8,128)(2,1)}, bf16[64,4096]{1,0:T(8,128)(2,1)}, u32[]{:S(2)}, u32[]{:S(2)}) %collective-permute-start.5) | collective-permute-done | bytes 524320 | tf_op jit(solution)/shard_map/ppermute | solution.py:17
  76.1 1.6 collective-permute-start.12
  78.8 1.3 collective-permute-start.13
  82.3 7.8 %collective-permute-done.12.refs_11_ = bf16[2,14,9,8,128]{4,3,2,1,0:T(8,128)(2,1)} collective-permute-done((bf16[2,14,9,8,128]{4,3,2,1,0:T(8,128)(2,1)S(1)}, bf16[2,14,9,8,128]{4,3,2,1,0:T(8,128)(2,1)}, u32[]{:S(2)}, u32[]{:S(2)}) %collective-permute-start.12) | collective-permute-done | bytes 516128 | tf_op jit(solution)/shard_map/ppermute | solution.py:17
  90.0 2.4 %collective-permute-done.13.refs_12_ = bf16[2,14,9,8,128]{4,3,2,1,0:T(8,128)(2,1)} collective-permute-done((bf16[2,14,9,8,128]{4,3,2,1,0:T(8,128)(2,1)S(1)}, bf16[2,14,9,8,128]{4,3,2,1,0:T(8,128)(2,1)}, u32[]{:S(2)}, u32[]{:S(2)}) %collective-permute-start.13) | collective-permute-done | bytes 516128 | tf_op jit(solution)/shard_map/ppermute | solution.py:17
  92.4 24.6 %shard_map.76 = (bf16[4,64,4096]{2,1,0:T(8,128)(2,1)}, bf16[4,64,4096]{2,1,0:T(8,128)(2,1)}, bf16[4,14,9,8,128]{4,3,2,1,0:T(8,128)(2,1)}, bf16[4,14,9,8,128]{4,3...) custom-call(s32[4,4]{1,0:T(4,128)} %add_multiply_fusion.offsets, ...), custom_call_target="tpu_custom_call" | custom-call | flops 3170893824 | bytes 20000000 | tf_op jit(solution)/shard_map/pallas_call | solution.py:210
  117.7 1.5 collective-permute-start.20
  121.6 10.0 %collective-permute-done.18 = bf16[2,14,9,8,128]{4,3,2,1,0:T(8,128)(2,1)} collective-permute-done((bf16[2,14,9,8,128]{4,3,2,1,0:T(8,128)(2,1)}, bf16[2,14,9,8,128]{4,3,2,1,0:T(8,128)(2,1)}, u32[]{:S(2)}, u32[]{:S(2)}) %collective-permute-start.18) | collective-permute-done | bytes 516128 | tf_op jit(solution)/shard_map/ppermute | solution.py:17
  136.3 1.3 copy-done.2
  137.7 2.4 %add_convert_fusion = bf16[4,64,4096]{2,1,0:T(8,128)(2,1)S(1)} fusion(bf16[4,64,4096]{2,1,0:T(8,128)(2,1)} %copy-done.2, bf16[4,64,4096]{2,1,0:T(8,128)(2,1)S(1)} %copy-done.1), kind=kLoop, calls=%fused_computation.1 | loop fusion | flops 4194304 | bytes 6291456 | tf_op jit(solution)/shard_map/convert_element_type | solution.py:24
  140.9 16.4 %collective-permute-done.19 = bf16[4,14,9,8,128]{4,3,2,1,0:T(8,128)(2,1)S(1)} collective-permute-done((bf16[4,14,9,8,128]{4,3,2,1,0:T(8,128)(2,1)S(1)}, bf16[4,14,9,8,128]{4,3,2,1,0:T(8,128)(2,1)S(1)}, u32[]{:S(2)}, u32[]{:S(2)}) %collective-permute-start.19) | collective-permute-done | bytes 1032224 | tf_op jit(solution)/shard_map/ppermute | solution.py:17
  157.3 2.3 %collective-permute-done.21 = bf16[4,14,9,8,128]{4,3,2,1,0:T(8,128)(2,1)S(1)} collective-permute-done((bf16[4,14,9,8,128]{4,3,2,1,0:T(8,128)(2,1)S(1)}, bf16[4,14,9,8,128]{4,3,2,1,0:T(8,128)(2,1)S(1)}, u32[]{:S(2)}, u32[]{:S(2)}) %collective-permute-start.21) | collective-permute-done | bytes 1032224 | tf_op jit(solution)/shard_map/ppermute | solution.py:17
  160.3 3.1 %collective-permute-start.23 = (bf16[14,9,8,128]{3,2,1,0:T(8,128)(2,1)S(1)}, bf16[14,9,8,128]{3,2,1,0:T(8,128)(2,1)S(1)}, u32[]{:S(2)}, u32[]{:S(2)}) collective-permute-start(bf16[14,9,8,128]{3,2,1,0:T(8,128)(2,1)S(1)} %get-tuple-element.21), channel_id=1, source_target_pairs={{0,16},{2,18},{4,20},{6,22},{8,24},{10,26},{12,28},{14,30},{16,0},... | collective-permute-start | bytes 774152 | tf_op jit(solution)/shard_map/ppermute | solution.py:17
  165.6 3.1 %collective-permute-start.17 = (bf16[64,4096]{1,0:T(8,128)(2,1)}, bf16[64,4096]{1,0:T(8,128)(2,1)}, u32[]{:S(2)}, u32[]{:S(2)}) collective-permute-start(bf16[64,4096]{1,0:T(8,128)(2,1)} %fusion), channel_id=1, source_target_pairs={{0,16},{2,18},{4,20},{6,22},{8,24},{10,26},{12,28},{14,30},{16,0},... | collective-permute-start | bytes 1572872 | tf_op jit(solution)/shard_map/ppermute | solution.py:17
  168.7 4.8 %collective-permute-done.22 = bf16[14,9,8,128]{3,2,1,0:T(8,128)(2,1)S(1)} collective-permute-done((bf16[14,9,8,128]{3,2,1,0:T(8,128)(2,1)S(1)}, bf16[14,9,8,128]{3,2,1,0:T(8,128)(2,1)S(1)}, u32[]{:S(2)}, u32[]{:S(2)}) %collective-permute-start.22) | collective-permute-done | bytes 258080 | tf_op jit(solution)/shard_map/ppermute | solution.py:17
  173.5 8.1 %collective-permute-done.23 = bf16[14,9,8,128]{3,2,1,0:T(8,128)(2,1)S(1)} collective-permute-done((bf16[14,9,8,128]{3,2,1,0:T(8,128)(2,1)S(1)}, bf16[14,9,8,128]{3,2,1,0:T(8,128)(2,1)S(1)}, u32[]{:S(2)}, u32[]{:S(2)}) %collective-permute-start.23) | collective-permute-done | bytes 258080 | tf_op jit(solution)/shard_map/ppermute | solution.py:17
  181.8 1.6 gather_fusion
  183.4 2.4 %fusion.2 = bf16[8,3,56,3,128]{4,2,3,1,0:T(8,128)(2,1)} fusion(bf16[56,3,3,8,128]{4,3,2,1,0:T(8,128)(2,1)} %bitcast.40, pred[56]{0:T(512)(128)(4,1)S(1)} %broadcast_in_dim.17), kind=kLoop, calls=%fused_computation.13 | loop fusion | flops 516096 | bytes 2064440 | tf_op jit(solution)/shard_map/transpose | solution.py:279
  185.8 8.9 %collective-permute-done.15 = bf16[64,4096]{1,0:T(8,128)(2,1)} collective-permute-done((bf16[64,4096]{1,0:T(8,128)(2,1)}, bf16[64,4096]{1,0:T(8,128)(2,1)}, u32[]{:S(2)}, u32[]{:S(2)}) %collective-permute-start.15) | collective-permute-done | bytes 524320 | tf_op jit(solution)/shard_map/ppermute | solution.py:17
  194.7 12.5 %collective-permute-done.17 = bf16[64,4096]{1,0:T(8,128)(2,1)} collective-permute-done((bf16[64,4096]{1,0:T(8,128)(2,1)}, bf16[64,4096]{1,0:T(8,128)(2,1)}, u32[]{:S(2)}, u32[]{:S(2)}) %collective-permute-start.17) | collective-permute-done | bytes 524320 | tf_op jit(solution)/shard_map/ppermute | solution.py:17
  207.2 1.4 add_convert_fusion.2
  (74 shorter events, 17.8 us)
Async XLA Ops:
  0.6 79.5 %copy-start = (s32[3,56,3]{1,2,0:T(4,128)S(1)}, s32[3,56,3]{1,2,0:T(4,128)}, u32[]{:S(2)}) copy-start(s32[3,56,3]{1,2,0:T(4,128)} %param.9) | copy-start | bytes 6052
  2.2 14.1 %collective-permute-start.7 = (bf16[14,9,8,128]{3,2,1,0:T(8,128)(2,1)S(1)}, bf16[14,9,8,128]{3,2,1,0:T(8,128)(2,1)S(1)}, u32[]{:S(2)}, u32[]{:S(2)}) collective-permute-start(bf16[14,9,8,128]{3,2,1,0:T(8,128)(2,1)S(1)} %get-tuple-element.26), channel_id=1, source_target_pairs={{0,8},{2,10},{4,12},{6,14},{8,0},{10,2},{12,4},{14,6},{16,24},{18,... | collective-permute-start | bytes 774152 | tf_op jit(solution)/shard_map/ppermute | solution.py:17
  5.3 32.3 %collective-permute-start.8 = (bf16[14,9,8,128]{3,2,1,0:T(8,128)(2,1)S(1)}, bf16[14,9,8,128]{3,2,1,0:T(8,128)(2,1)S(1)}, u32[]{:S(2)}, u32[]{:S(2)}) collective-permute-start(bf16[14,9,8,128]{3,2,1,0:T(8,128)(2,1)S(1)} %get-tuple-element.25), channel_id=1, source_target_pairs={{0,16},{2,18},{4,20},{6,22},{8,24},{10,26},{12,28},{14,30},{16,0},... | collective-permute-start | bytes 774152 | tf_op jit(solution)/shard_map/ppermute | solution.py:17
  7.9 29.8 %collective-permute-start.9 = (bf16[14,9,8,128]{3,2,1,0:T(8,128)(2,1)S(1)}, bf16[14,9,8,128]{3,2,1,0:T(8,128)(2,1)S(1)}, u32[]{:S(2)}, u32[]{:S(2)}) collective-permute-start(bf16[14,9,8,128]{3,2,1,0:T(8,128)(2,1)S(1)} %get-tuple-element.24), channel_id=1, source_target_pairs={{0,24},{2,26},{4,28},{6,30},{8,16},{10,18},{12,20},{14,22},{16,8},... | collective-permute-start | bytes 774152 | tf_op jit(solution)/shard_map/ppermute | solution.py:17
  9.3 43.9 %collective-permute-start.3 = (bf16[64,4096]{1,0:T(8,128)(2,1)}, bf16[64,4096]{1,0:T(8,128)(2,1)}, u32[]{:S(2)}, u32[]{:S(2)}) collective-permute-start(bf16[64,4096]{1,0:T(8,128)(2,1)} %constant_dynamic-update-slice_fusion.refs_0_), channel_id=1, source_target_pairs={{0,16},{2,18},{4,20},{6,22},{8,24},{10,26},{12,28},{14,30},{16,0},... | collective-permute-start | bytes 1572872 | tf_op jit(solution)/shard_map/ppermute | solution.py:17
  37.7 43.3 %copy-start.10 = (s32[3,56]{1,0:T(4,128)S(1)}, s32[3,56]{1,0:T(4,128)}, u32[]{:S(2)}) copy-start(s32[3,56]{1,0:T(4,128)} %param.8) | copy-start | bytes 2020
  37.8 54.6 %copy-start.5 = (bf16[4,14,9,8,128]{4,3,2,1,0:T(8,128)(2,1)}, bf16[4,14,9,8,128]{4,3,2,1,0:T(8,128)(2,1)S(1)}, u32[]{:S(2)}) copy-start(bf16[4,14,9,8,128]{4,3,2,1,0:T(8,128)(2,1)S(1)} %pad_maximum_fusion.refs_8_) | copy-start | bytes 3096580
  37.8 37.8 %collective-permute-start.10 = (bf16[4,14,9,8,128]{4,3,2,1,0:T(8,128)(2,1)S(1)}, bf16[4,14,9,8,128]{4,3,2,1,0:T(8,128)(2,1)S(1)}, u32[]{:S(2)}, u32[]{:S(2)}) collective-permute-start(bf16[4,14,9,8,128]{4,3,2,1,0:T(8,128)(2,1)S(1)} %pad_maximum_fusion.refs_8_), channel_id=1, source_target_pairs={{0,2},{2,0},{4,6},{6,4},{8,10},{10,8},{12,14},{14,12},{16,18},{18,... | collective-permute-start | bytes 3096584 | tf_op jit(solution)/shard_map/ppermute | solution.py:17
  39.4 36.8 %collective-permute-start.11 = (bf16[4,14,9,8,128]{4,3,2,1,0:T(8,128)(2,1)S(1)}, bf16[4,14,9,8,128]{4,3,2,1,0:T(8,128)(2,1)}, u32[]{:S(2)}, u32[]{:S(2)}) collective-permute-start(bf16[4,14,9,8,128]{4,3,2,1,0:T(8,128)(2,1)S(1)} %pad_maximum_fusion.refs_8_), channel_id=1, source_target_pairs={{0,4},{2,6},{4,0},{6,2},{8,12},{10,14},{12,8},{14,10},{16,20},{18,... | collective-permute-start | bytes 3096584 | tf_op jit(solution)/shard_map/ppermute | solution.py:17
  40.9 23.6 %collective-permute-start.1 = (bf16[64,4096]{1,0:T(8,128)(2,1)}, bf16[64,4096]{1,0:T(8,128)(2,1)}, u32[]{:S(2)}, u32[]{:S(2)}) collective-permute-start(bf16[64,4096]{1,0:T(8,128)(2,1)} %constant_dynamic-update-slice_fusion.refs_0_), channel_id=1, source_target_pairs={{0,8},{2,10},{4,12},{6,14},{8,0},{10,2},{12,4},{14,6},{16,24},{18,... | collective-permute-start | bytes 1572872 | tf_op jit(solution)/shard_map/ppermute | solution.py:17
  53.2 22.4 %collective-permute-start.5 = (bf16[64,4096]{1,0:T(8,128)(2,1)}, bf16[64,4096]{1,0:T(8,128)(2,1)}, u32[]{:S(2)}, u32[]{:S(2)}) collective-permute-start(bf16[64,4096]{1,0:T(8,128)(2,1)} %collective-permute-done.3.refs_4_), channel_id=1, source_target_pairs={{0,8},{2,10},{4,12},{6,14},{8,0},{10,2},{12,4},{14,6},{16,24},{18,... | collective-permute-start | bytes 1572872 | tf_op jit(solution)/shard_map/ppermute | solution.py:17
  53.2 25.6 %collective-permute-start = (bf16[64,4096]{1,0:T(8,128)(2,1)}, bf16[64,4096]{1,0:T(8,128)(2,1)}, u32[]{:S(2)}, u32[]{:S(2)}) collective-permute-start(bf16[64,4096]{1,0:T(8,128)(2,1)} %constant_dynamic-update-slice_fusion.refs_0_), channel_id=1, source_target_pairs={{0,1},{1,0},{2,3},{3,2},{4,5},{5,4},{6,7},{7,6},{8,9},{9,8},{10,11... | collective-permute-start | bytes 1572872 | tf_op jit(solution)/shard_map/ppermute | solution.py:17
  64.4 17.8 %collective-permute-start.4 = (bf16[64,4096]{1,0:T(8,128)(2,1)}, bf16[64,4096]{1,0:T(8,128)(2,1)}, u32[]{:S(2)}, u32[]{:S(2)}) collective-permute-start(bf16[64,4096]{1,0:T(8,128)(2,1)} %collective-permute-done.3.refs_4_), channel_id=1, source_target_pairs={{0,1},{1,0},{2,3},{3,2},{4,5},{5,4},{6,7},{7,6},{8,9},{9,8},{10,11... | collective-permute-start | bytes 1572872 | tf_op jit(solution)/shard_map/ppermute | solution.py:17
  75.6 6.7 %collective-permute-start.2 = (bf16[64,4096]{1,0:T(8,128)(2,1)}, bf16[64,4096]{1,0:T(8,128)(2,1)}, u32[]{:S(2)}, u32[]{:S(2)}) collective-permute-start(bf16[64,4096]{1,0:T(8,128)(2,1)} %collective-permute-done.1.refs_2_), channel_id=1, source_target_pairs={{0,1},{1,0},{2,3},{3,2},{4,5},{5,4},{6,7},{7,6},{8,9},{9,8},{10,11... | collective-permute-start | bytes 1572872 | tf_op jit(solution)/shard_map/ppermute | solution.py:17
  75.6 16.8 %copy-start.9 = (bf16[4,14,9,8,128]{4,3,2,1,0:T(8,128)(2,1)}, bf16[4,14,9,8,128]{4,3,2,1,0:T(8,128)(2,1)S(1)}, u32[]{:S(2)}) copy-start(bf16[4,14,9,8,128]{4,3,2,1,0:T(8,128)(2,1)S(1)} %collective-permute-done.10.refs_9_) | copy-start | bytes 3096580
  75.6 6.7 %collective-permute-start.6 = (bf16[64,4096]{1,0:T(8,128)(2,1)}, bf16[64,4096]{1,0:T(8,128)(2,1)}, u32[]{:S(2)}, u32[]{:S(2)}) collective-permute-start(bf16[64,4096]{1,0:T(8,128)(2,1)} %collective-permute-done.5.refs_6_), channel_id=1, source_target_pairs={{0,1},{1,0},{2,3},{3,2},{4,5},{5,4},{6,7},{7,6},{8,9},{9,8},{10,11... | collective-permute-start | bytes 1572872 | tf_op jit(solution)/shard_map/ppermute | solution.py:17
  76.1 13.9 %collective-permute-start.12 = (bf16[2,14,9,8,128]{4,3,2,1,0:T(8,128)(2,1)S(1)}, bf16[2,14,9,8,128]{4,3,2,1,0:T(8,128)(2,1)}, u32[]{:S(2)}, u32[]{:S(2)}) collective-permute-start(bf16[2,14,9,8,128]{4,3,2,1,0:T(8,128)(2,1)S(1)} %slice.66), channel_id=1, source_target_pairs={{0,4},{2,6},{4,0},{6,2},{8,12},{10,14},{12,8},{14,10},{16,20},{18,... | collective-permute-start | bytes 1548296 | tf_op jit(solution)/shard_map/ppermute | solution.py:17
  78.8 13.6 %collective-permute-start.13 = (bf16[2,14,9,8,128]{4,3,2,1,0:T(8,128)(2,1)S(1)}, bf16[2,14,9,8,128]{4,3,2,1,0:T(8,128)(2,1)}, u32[]{:S(2)}, u32[]{:S(2)}) collective-permute-start(bf16[2,14,9,8,128]{4,3,2,1,0:T(8,128)(2,1)S(1)} %slice.67), channel_id=1, source_target_pairs={{0,2},{2,0},{4,6},{6,4},{8,10},{10,8},{12,14},{14,12},{16,18},{18,... | collective-permute-start | bytes 1548296 | tf_op jit(solution)/shard_map/ppermute | solution.py:17
  117.0 14.6 %copy-start.4 = (bf16[4,14,9,8,128]{4,3,2,1,0:T(8,128)(2,1)S(1)}, bf16[4,14,9,8,128]{4,3,2,1,0:T(8,128)(2,1)}, u32[]{:S(2)}) copy-start(bf16[4,14,9,8,128]{4,3,2,1,0:T(8,128)(2,1)} %get-tuple-element.13) | copy-start | bytes 3096580
  117.0 19.3 %collective-permute-start.14 = (bf16[4,64,4096]{2,1,0:T(8,128)(2,1)}, bf16[4,64,4096]{2,1,0:T(8,128)(2,1)S(1)}, u32[]{:S(2)}, u32[]{:S(2)}) collective-permute-start(bf16[4,64,4096]{2,1,0:T(8,128)(2,1)} %get-tuple-element.11), channel_id=1, source_target_pairs={{0,1},{1,0},{2,3},{3,2},{4,5},{5,4},{6,7},{7,6},{8,9},{9,8},{10,11... | collective-permute-start | bytes 6291464 | tf_op jit(solution)/shard_map/ppermute | solution.py:17
  117.1 14.5 %collective-permute-start.18 = (bf16[2,14,9,8,128]{4,3,2,1,0:T(8,128)(2,1)}, bf16[2,14,9,8,128]{4,3,2,1,0:T(8,128)(2,1)}, u32[]{:S(2)}, u32[]{:S(2)}) collective-permute-start(bf16[2,14,9,8,128]{4,3,2,1,0:T(8,128)(2,1)} %get-tuple-element.14), channel_id=1, source_target_pairs={{0,4},{2,6},{4,0},{6,2},{8,12},{10,14},{12,8},{14,10},{16,20},{18,... | collective-permute-start | bytes 1548296 | tf_op jit(solution)/shard_map/ppermute | solution.py:17
  117.7 16.5 %collective-permute-start.20 = (bf16[2,14,9,8,128]{4,3,2,1,0:T(8,128)(2,1)}, bf16[2,14,9,8,128]{4,3,2,1,0:T(8,128)(2,1)}, u32[]{:S(2)}, u32[]{:S(2)}) collective-permute-start(bf16[2,14,9,8,128]{4,3,2,1,0:T(8,128)(2,1)} %get-tuple-element.16), channel_id=1, source_target_pairs={{0,2},{2,0},{4,6},{6,4},{8,10},{10,8},{12,14},{14,12},{16,18},{18,... | collective-permute-start | bytes 1548296 | tf_op jit(solution)/shard_map/ppermute | solution.py:17
  120.4 13.8 %copy-start.3 = (bf16[4,14,9,8,128]{4,3,2,1,0:T(8,128)(2,1)S(1)}, bf16[4,14,9,8,128]{4,3,2,1,0:T(8,128)(2,1)}, u32[]{:S(2)}) copy-start(bf16[4,14,9,8,128]{4,3,2,1,0:T(8,128)(2,1)} %get-tuple-element.15) | copy-start | bytes 3096580
  132.9 24.4 %collective-permute-start.19 = (bf16[4,14,9,8,128]{4,3,2,1,0:T(8,128)(2,1)S(1)}, bf16[4,14,9,8,128]{4,3,2,1,0:T(8,128)(2,1)S(1)}, u32[]{:S(2)}, u32[]{:S(2)}) collective-permute-start(bf16[4,14,9,8,128]{4,3,2,1,0:T(8,128)(2,1)S(1)} %pad_maximum_fusion.1), channel_id=1, source_target_pairs={{0,2},{2,0},{4,6},{6,4},{8,10},{10,8},{12,14},{14,12},{16,18},{18,... | collective-permute-start | bytes 3096584 | tf_op jit(solution)/shard_map/ppermute | solution.py:17
  135.5 24.2 %collective-permute-start.21 = (bf16[4,14,9,8,128]{4,3,2,1,0:T(8,128)(2,1)S(1)}, bf16[4,14,9,8,128]{4,3,2,1,0:T(8,128)(2,1)S(1)}, u32[]{:S(2)}, u32[]{:S(2)}) collective-permute-start(bf16[4,14,9,8,128]{4,3,2,1,0:T(8,128)(2,1)S(1)} %pad_maximum_fusion.2), channel_id=1, source_target_pairs={{0,4},{2,6},{4,0},{6,2},{8,12},{10,14},{12,8},{14,10},{16,20},{18,... | collective-permute-start | bytes 3096584 | tf_op jit(solution)/shard_map/ppermute | solution.py:17
  140.1 19.6 %copy-start.6 = (bf16[4,14,9,8,128]{4,3,2,1,0:T(8,128)(2,1)S(1)}, bf16[4,14,9,8,128]{4,3,2,1,0:T(8,128)(2,1)}, u32[]{:S(2)}) copy-start(bf16[4,14,9,8,128]{4,3,2,1,0:T(8,128)(2,1)} %get-tuple-element.12) | copy-start | bytes 3096580
  140.9 23.7 %collective-permute-start.16 = (bf16[64,4096]{1,0:T(8,128)(2,1)S(1)}, bf16[64,4096]{1,0:T(8,128)(2,1)S(1)}, u32[]{:S(2)}, u32[]{:S(2)}) collective-permute-start(bf16[64,4096]{1,0:T(8,128)(2,1)S(1)} %get-tuple-element.18), channel_id=1, source_target_pairs={{0,8},{2,10},{4,12},{6,14},{8,0},{10,2},{12,4},{14,6},{16,24},{18,... | collective-permute-start | bytes 1572872 | tf_op jit(solution)/shard_map/ppermute | solution.py:17
  160.2 13.3 %collective-permute-start.22 = (bf16[14,9,8,128]{3,2,1,0:T(8,128)(2,1)S(1)}, bf16[14,9,8,128]{3,2,1,0:T(8,128)(2,1)S(1)}, u32[]{:S(2)}, u32[]{:S(2)}) collective-permute-start(bf16[14,9,8,128]{3,2,1,0:T(8,128)(2,1)S(1)} %get-tuple-element.22), channel_id=1, source_target_pairs={{0,8},{2,10},{4,12},{6,14},{8,0},{10,2},{12,4},{14,6},{16,24},{18,... | collective-permute-start | bytes 774152 | tf_op jit(solution)/shard_map/ppermute | solution.py:17
  160.3 21.3 %collective-permute-start.23 = (bf16[14,9,8,128]{3,2,1,0:T(8,128)(2,1)S(1)}, bf16[14,9,8,128]{3,2,1,0:T(8,128)(2,1)S(1)}, u32[]{:S(2)}, u32[]{:S(2)}) collective-permute-start(bf16[14,9,8,128]{3,2,1,0:T(8,128)(2,1)S(1)} %get-tuple-element.21), channel_id=1, source_target_pairs={{0,16},{2,18},{4,20},{6,22},{8,24},{10,26},{12,28},{14,30},{16,0},... | collective-permute-start | bytes 774152 | tf_op jit(solution)/shard_map/ppermute | solution.py:17
  163.4 18.2 %collective-permute-start.24 = (bf16[14,9,8,128]{3,2,1,0:T(8,128)(2,1)S(1)}, bf16[14,9,8,128]{3,2,1,0:T(8,128)(2,1)S(1)}, u32[]{:S(2)}, u32[]{:S(2)}) collective-permute-start(bf16[14,9,8,128]{3,2,1,0:T(8,128)(2,1)S(1)} %get-tuple-element.20), channel_id=1, source_target_pairs={{0,24},{2,26},{4,28},{6,30},{8,16},{10,18},{12,20},{14,22},{16,8},... | collective-permute-start | bytes 774152 | tf_op jit(solution)/shard_map/ppermute | solution.py:17
  164.6 30.1 %collective-permute-start.15 = (bf16[64,4096]{1,0:T(8,128)(2,1)}, bf16[64,4096]{1,0:T(8,128)(2,1)}, u32[]{:S(2)}, u32[]{:S(2)}) collective-permute-start(bf16[64,4096]{1,0:T(8,128)(2,1)} %get-tuple-element.17), channel_id=1, source_target_pairs={{0,8},{2,10},{4,12},{6,14},{8,0},{10,2},{12,4},{14,6},{16,24},{18,... | collective-permute-start | bytes 1572872 | tf_op jit(solution)/shard_map/ppermute | solution.py:17
  165.6 41.6 %collective-permute-start.17 = (bf16[64,4096]{1,0:T(8,128)(2,1)}, bf16[64,4096]{1,0:T(8,128)(2,1)}, u32[]{:S(2)}, u32[]{:S(2)}) collective-permute-start(bf16[64,4096]{1,0:T(8,128)(2,1)} %fusion), channel_id=1, source_target_pairs={{0,16},{2,18},{4,20},{6,22},{8,24},{10,26},{12,28},{14,30},{16,0},... | collective-permute-start | bytes 1572872 | tf_op jit(solution)/shard_map/ppermute | solution.py:17
  (4 other events, 21.3 us)

commit v2 on v1

v2 whole, which is shorter than its diff:
```python
import functools
import math

import jax
import jax.numpy as jnp
from jax import lax
from jax.experimental import pallas as pl
from jax.experimental.pallas import tpu as pltpu
from jax.sharding import PartitionSpec as P

F32 = jnp.float32
BF16 = jnp.bfloat16
PLAIN = (((1,), (0,)), ((), ()))
TURNED = (((1,), (1,)), ((), ()))
PARAMS = pltpu.CompilerParams(vmem_limit_bytes=56 * 1024 * 1024)
dot = functools.partial(lax.dot_general, preferred_element_type=F32)


def swap(value, axis, stride):
    size = lax.axis_size(axis)
    return lax.ppermute(value, axis, [(at, at ^ stride) for at in range(size)])


def after(value, *others):
    return lax.optimization_barrier((value, *others))[0]


def add(first, *others):
    total = first.astype(F32)
    for other in others:
        total = total + other.astype(F32)
    return total.astype(BF16)


def strides_of(size, unit=1):
    found = []
    step = size // 2
    while step >= 1:
        found.append(step * unit)
        step //= 2
    return found


def gather(items, axis, strides):
    for stride in strides:
        items = {**items, **{at ^ stride: swap(one, axis, stride) for at, one in items.items()}}
    return items


def scatter(items, axis, strides):
    for stride in reversed(strides):
        kept = {}
        for at, one in items.items():
            if not at & stride:
                kept[at] = add(one, swap(items[at ^ stride], axis, stride))
        items = kept
    return items


def whole(shape, at=None):
    at = (0,) * len(shape) if at is None else at
    return pl.BlockSpec(shape, lambda *_: at)


def by_block(shape):
    return pl.BlockSpec((1,) + shape, lambda block, *_: (block,) + (0,) * len(shape))


def pack(block_at, firsts, tiles, *outs, blocks, slot_count):
    for at, out in enumerate(outs):
        capacity = out.shape[0] - slot_count

        def one(place, _, at=at, out=out, capacity=capacity):
            block = block_at[at, place]
            for matrix in range(3):
                first = firsts[matrix, block]
                for slot in range(slot_count):
                    out[first + slot] = tiles[(block * 3 + matrix) * slot_count + slot]
            return _

        lax.fori_loop(0, blocks, one, 0)


def unpack(home, firsts, counts, *refs, slot_count):
    out, held = refs[-2:]
    capacity = refs[0].shape[0]
    for at, ref in enumerate(refs[:-2]):
        held[at * capacity : (at + 1) * capacity] = ref[...]

    def one(block, _):
        base = home[0, block] * capacity
        for matrix in range(3):
            first = base + firsts[matrix, block]
            for slot in range(slot_count):
                value = held[first + slot].astype(F32)
                live = slot < counts[matrix, block]
                out[(block * 3 + matrix) * slot_count + slot] = jnp.where(live, value, 0.0).astype(BF16)
        return _

    lax.fori_loop(0, home.shape[1], one, 0)


def ahead(offsets, firsts, counts, rows, *refs, token_count, weight_parts, slot_count):
    token_refs, refs = refs[:token_count], refs[token_count:]
    weight_refs, refs = refs[: len(weight_parts)], refs[len(weight_parts) :]
    x_turned, whole_tiles, gate_slope, gate_act_out, hidden_out, hidden_turned = refs[:6]
    x_all, tiles = refs[6:]
    block = pl.program_id(0)
    own_rows = token_refs[0].shape[0]
    tile = tiles.shape[1]
    features = x_all.shape[1]

    @pl.when(block == 0)
    def _():
        for at, ref in enumerate(token_refs):
            x_all[at * own_rows : (at + 1) * own_rows, :] = ref[...]
        for at in range(features // tile):
            x_turned[at * tile : (at + 1) * tile, :] = x_all[:, at * tile : (at + 1) * tile].T

    for ref, (group_at, first_part, length) in zip(weight_refs, weight_parts):
        share = ref.shape[2]
        for at in range(length):
            offset = pl.multiple_of(offsets[group_at, first_part + at], share)
            for matrix in range(3):
                for slot in range(slot_count):
                    tiles[matrix * slot_count + slot, pl.ds(offset, share), :] = ref[
                        at, firsts[matrix, block] + slot
                    ].astype(F32)
    slots = range(slot_count)
    for matrix in range(3):
        for slot in slots:
            live = slot < counts[matrix, block]
            whole_tiles[0, matrix * slot_count + slot] = jnp.where(
                live, tiles[matrix * slot_count + slot], 0.0
            ).astype(BF16)

    def columns(matrix, slot):
        return pl.ds(pl.multiple_of(rows[matrix * slot_count + slot, block] * tile, tile), tile)

    gate_in = jnp.concatenate([x_all[:, columns(0, slot)] for slot in slots], axis=1)
    up_in = jnp.concatenate([x_all[:, columns(1, slot)] for slot in slots], axis=1)
    gate_tiles = whole_tiles[0, :slot_count].reshape(slot_count * tile, tile)
    up_tiles = whole_tiles[0, slot_count : 2 * slot_count].reshape(slot_count * tile, tile)
    gate_pre = dot(gate_in, gate_tiles, PLAIN)
    up_pre = dot(up_in, up_tiles, PLAIN)
    gate_sig = jax.nn.sigmoid(gate_pre)
    gate_act = gate_pre * gate_sig
    hidden = (gate_act * up_pre).astype(BF16)
    gate_slope[0] = up_pre * gate_sig * (1.0 + gate_pre * (1.0 - gate_sig))
    gate_act_out[0] = gate_act
    hidden_out[0] = hidden
    hidden_turned[0] = hidden.T


def behind(
    offsets, firsts, counts, rows, *refs, token_count, weight_parts, slot_count, grad_scale, own_parts
):
    token_refs, refs = refs[:token_count], refs[token_count:]
    x_turned, whole_tiles, gate_slope, gate_act, hidden, hidden_turned = refs[:6]
    ffn_own, ffn_other, input_own, input_other = refs[6:10]
    grad_refs, refs = refs[10 : 10 + len(weight_parts)], refs[10 + len(weight_parts) :]
    g_all, ffn_sum, input_sum, tile_out = refs
    block = pl.program_id(0)
    own_rows = token_refs[0].shape[0]
    tile = tile_out.shape[1]
    slots = range(slot_count)

    @pl.when(block == 0)
    def _():
        for at, ref in enumerate(token_refs):
            g_all[at * own_rows : (at + 1) * own_rows, :] = ref[...]
        ffn_sum[...] = jnp.zeros_like(ffn_sum)
        input_sum[...] = jnp.zeros_like(input_sum)

    def columns(matrix, slot):
        return pl.ds(pl.multiple_of(rows[matrix * slot_count + slot, block] * tile, tile), tile)

    gate_tiles = whole_tiles[0, :slot_count].reshape(slot_count * tile, tile)
    up_tiles = whole_tiles[0, slot_count : 2 * slot_count].reshape(slot_count * tile, tile)
    down_tiles = jnp.concatenate([whole_tiles[0, 2 * slot_count + slot] for slot in slots], axis=1)
    grad_in = jnp.concatenate([g_all[:, columns(2, slot)] for slot in slots], axis=1)
    hidden_grad = dot(grad_in, down_tiles, TURNED)
    ffn = dot(hidden[0], down_tiles, PLAIN)
    down_terms = dot(hidden_turned[0], grad_in, PLAIN)
    gate_grad = (hidden_grad * gate_slope[0]).astype(BF16)
    up_grad = (hidden_grad * gate_act[0]).astype(BF16)
    from_gate = dot(gate_grad, gate_tiles, TURNED)
    from_up = dot(up_grad, up_tiles, TURNED)
    for slot in slots:
        here = slice(slot * tile, (slot + 1) * tile)
        ffn_sum[:, columns(2, slot)] += ffn[:, here]
        input_sum[:, columns(0, slot)] += from_gate[:, here]
        input_sum[:, columns(1, slot)] += from_up[:, here]
        tile_out[slot] = dot(x_turned[columns(0, slot), :], gate_grad, PLAIN) * grad_scale
        tile_out[slot_count + slot] = dot(x_turned[columns(1, slot), :], up_grad, PLAIN) * grad_scale
        tile_out[2 * slot_count + slot] = down_terms[:, here] * grad_scale
    for matrix in range(3):
        for slot in slots:

            def store(matrix=matrix, slot=slot):
                for ref, (group_at, first_part, length) in zip(grad_refs, weight_parts):
                    share = ref.shape[2]
                    for at in range(length):
                        offset = pl.multiple_of(offsets[group_at, first_part + at], share)
                        ref[at, firsts[matrix, block] + slot] = tile_out[
                            matrix * slot_count + slot, pl.ds(offset, share), :
                        ].astype(BF16)

            pl.when(slot < counts[matrix, block])(store)

    @pl.when(block == pl.num_programs(0) - 1)
    def _():
        own_at, other_at = 0, 0
        for at in range(token_count):
            source = slice(at * own_rows, (at + 1) * own_rows)
            if at in own_parts:
                ffn_own[own_at] = ffn_sum[source, :].astype(BF16)
                input_own[own_at] = input_sum[source, :].astype(BF16)
                own_at += 1
            else:
                ffn_other[other_at] = ffn_sum[source, :].astype(BF16)
                input_other[other_at] = input_sum[source, :].astype(BF16)
                other_at += 1


def shards(tokens, out_grad, weight_tiles, tile_counts, tile_rows):
    row_share, _, blocks_dev, slot_count, tile = weight_tiles.shape
    own_rows, features = tokens.shape
    dp_size, tensor_size = lax.axis_size("dp"), lax.axis_size("tensor")
    far = math.gcd(4, math.gcd(dp_size, blocks_dev))
    near = dp_size // far
    blocks = blocks_dev // far
    terms = 3 * slot_count
    grad_scale = 1.0 / math.sqrt(own_rows * tensor_size * dp_size)
    me = lax.axis_index("dp")
    far_at, near_at = me // near, me % near
    far_strides, near_strides = strides_of(far, near), strides_of(near)
    tensor_strides = strides_of(tensor_size)

    capacity = (terms * blocks_dev - 3 * blocks_dev + 3 * (slot_count - 1) * (far - 1)) // far
    buffer = capacity + slot_count
    block_ids = jnp.arange(blocks_dev, dtype=jnp.int32)
    load = jnp.sum(tile_counts, axis=0)
    earlier = (load[:, None] > load[None, :]) | (
        (load[:, None] == load[None, :]) & (block_ids[:, None] < block_ids[None, :])
    )
    rank = jnp.sum(earlier.astype(jnp.int32), axis=0)
    home = rank % far
    before = (home[:, None] == home[None, :]) & (rank[:, None] < rank[None, :])
    start = jnp.sum(jnp.where(before, load[:, None], 0), axis=0)
    firsts = start[None, :] + jnp.concatenate(
        [jnp.zeros_like(tile_counts[:1]), tile_counts[:1], tile_counts[:1] + tile_counts[1:2]]
    )
    ranks_of = (
        jnp.arange(blocks, dtype=jnp.int32)[None, :] * far
        + (jnp.arange(far, dtype=jnp.int32)[:, None] ^ far_at)
    )
    block_at = jnp.sum(
        jnp.where(ranks_of[:, :, None] == rank[None, None, :], block_ids[None, None, :], 0), axis=2
    )
    table = jnp.concatenate(
        [firsts, tile_counts, jnp.transpose(tile_rows, (0, 2, 1)).reshape(terms, blocks_dev)]
    )
    own = jnp.sum(
        jnp.where(ranks_of[0][None, :, None] == rank[None, None, :], table[:, None, :], 0), axis=2
    )
    own_firsts, own_counts, own_cols = own[:3], own[3:6], own[6:]
    offsets = (
        (jnp.arange(far, dtype=jnp.int32)[None, :] ^ far_at) * near
        + (jnp.arange(near, dtype=jnp.int32)[:, None] ^ near_at)
    ) * row_share

    tile_list = jnp.transpose(weight_tiles, (2, 1, 3, 0, 4)).reshape(
        blocks_dev * terms, row_share, tile
    )
    packed_shape = (buffer, row_share, tile)
    packed = pl.pallas_call(
        functools.partial(pack, blocks=blocks, slot_count=slot_count),
        grid_spec=pltpu.PrefetchScalarGridSpec(
            num_scalar_prefetch=2,
            grid=(1,),
            in_specs=[whole(tile_list.shape)],
            out_specs=[whole(packed_shape)] * far,
        ),
        out_shape=[jax.ShapeDtypeStruct(packed_shape, BF16)] * far,
        compiler_params=PARAMS,
    )(block_at, firsts, tile_list)
    both = jnp.concatenate([tokens, out_grad], axis=0)
    early = {0: both}
    if far > 1:
        early[near] = swap(both, "dp", near)
    received = [swap(packed[at], "dp", at * near) for at in reversed(range(1, far))][::-1]
    held = jnp.stack([packed[0], *received])

    late_x, late_g = {}, {}
    for stride in far_strides[:-1]:
        x_source, g_source = after((tokens, out_grad), held)
        late_x[stride] = swap(x_source, "dp", stride)
        late_x[stride ^ near] = swap(late_x[stride], "dp", near)
        late_g[stride] = swap(after(g_source, late_x[stride]), "dp", stride)
        late_g[stride ^ near] = swap(late_g[stride], "dp", near)

    half = far // 2
    split = near == 4 and far % 2 == 0
    if split:
        from_1, from_2 = swap(held, "dp", 1), swap(held, "dp", 2)
        weight_list = [
            held, from_1, from_2, swap(from_1[:half], "dp", 2), swap(from_2[half:], "dp", 1)
        ]
        weight_parts = [(0, 0, far), (1, 0, far), (2, 0, far), (3, 0, half), (3, half, half)]
    else:
        items = gather({0: held}, "dp", near_strides)
        weight_list = [items[at] for at in range(near)]
        weight_parts = [(at, 0, far) for at in range(near)]

    far_order = [at * near for at in range(0, far, 2)] + [at * near for at in range(1, far, 2)]
    x_list, g_list, x_specs, g_specs, token_parts = [], [], [], [], []
    token_shape = (own_rows, features)
    for at in far_order:
        if at in early:
            for other, part in gather({0: early[at]}, "tensor", tensor_strides).items():
                token_parts.append((at, other))
                x_list.append(part)
                g_list.append(part)
                x_specs.append(whole(token_shape))
                g_specs.append(whole(token_shape, (1, 0)))
        else:
            x_parts = gather({0: late_x[at]}, "tensor", tensor_strides)
            g_parts = gather({0: late_g[at]}, "tensor", tensor_strides)
            for other in x_parts:
                token_parts.append((at, other))
                x_list.append(x_parts[other])
                g_list.append(g_parts[other])
                x_specs.append(whole(token_shape))
                g_specs.append(whole(token_shape))

    token_count = len(token_parts)
    group_rows = token_count * own_rows
    own_parts = tuple(at for at, (_, other) in enumerate(token_parts) if other == 0)
    other_parts = [part for part in token_parts if part[1] != 0]
    weight_specs = [whole((length,) + packed_shape) for _, _, length in weight_parts]
    middle_specs = [
        whole((features, group_rows)),
        by_block((terms, tile, tile)),
        by_block((group_rows, tile)),
        by_block((group_rows, tile)),
        by_block((group_rows, tile)),
        by_block((tile, group_rows)),
    ]
    middle_shapes = [
        jax.ShapeDtypeStruct((features, group_rows), BF16),
        jax.ShapeDtypeStruct((blocks, terms, tile, tile), BF16),
        jax.ShapeDtypeStruct((blocks, group_rows, tile), F32),
        jax.ShapeDtypeStruct((blocks, group_rows, tile), F32),
        jax.ShapeDtypeStruct((blocks, group_rows, tile), BF16),
        jax.ShapeDtypeStruct((blocks, tile, group_rows), BF16),
    ]
    flops = 2 * blocks * slot_count * group_rows * tile * tile
    middle = pl.pallas_call(
        functools.partial(
            ahead, token_count=token_count, weight_parts=weight_parts, slot_count=slot_count
        ),
        grid_spec=pltpu.PrefetchScalarGridSpec(
            num_scalar_prefetch=4,
            grid=(blocks,),
            in_specs=x_specs + weight_specs,
            out_specs=middle_specs,
            scratch_shapes=[
                pltpu.VMEM((group_rows, features), BF16),
                pltpu.VMEM((terms, tile, tile), F32),
            ],
        ),
        out_shape=middle_shapes,
        compiler_params=PARAMS,
        cost_estimate=pl.CostEstimate(
            flops=2 * flops, bytes_accessed=16_000_000, transcendentals=blocks * group_rows * tile
        ),
    )(offsets, own_firsts, own_counts, own_cols, *x_list, *weight_list)
    own_shape = (len(own_parts), own_rows, features)
    other_shape = (len(other_parts), own_rows, features)
    outs = pl.pallas_call(
        functools.partial(
            behind,
            token_count=token_count,
            weight_parts=weight_parts,
            slot_count=slot_count,
            grad_scale=grad_scale,
            own_parts=own_parts,
        ),
        grid_spec=pltpu.PrefetchScalarGridSpec(
            num_scalar_prefetch=4,
            grid=(blocks,),
            in_specs=g_specs + middle_specs,
            out_specs=[whole(own_shape), whole(other_shape)] * 2 + weight_specs,
            scratch_shapes=[
                pltpu.VMEM((group_rows, features), BF16),
                pltpu.VMEM((group_rows, features), F32),
                pltpu.VMEM((group_rows, features), F32),
                pltpu.VMEM((terms, tile, tile), F32),
            ],
        ),
        out_shape=[
            jax.ShapeDtypeStruct(own_shape, BF16),
            jax.ShapeDtypeStruct(other_shape, BF16),
        ]
        * 2
        + [
            jax.ShapeDtypeStruct((length,) + packed_shape, BF16) for _, _, length in weight_parts
        ],
        compiler_params=PARAMS,
        cost_estimate=pl.CostEstimate(
            flops=7 * flops, bytes_accessed=25_000_000, transcendentals=0
        ),
    )(offsets, own_firsts, own_counts, own_cols, *g_list, *middle)
    tile_terms = outs[4:]

    def finish(own_sums, other_sums):
        if tensor_size == 2 and far == 4:
            from_core = swap(other_sums, "tensor", 1)
            got = swap(add(own_sums[2:], from_core[2:]), "dp", near)
            last = swap(add(own_sums[1], from_core[1], got[1]), "dp", 2 * near)
            return add(own_sums[0], from_core[0], got[0], last)
        sums = {}
        for place, at in enumerate(far_order):
            items = {0: own_sums[place]}
            for index, (far_part, other) in enumerate(other_parts):
                if far_part == at:
                    items[other] = other_sums[index]
            sums[at] = scatter(items, "tensor", tensor_strides)[0]
        return scatter(sums, "dp", far_strides)[0]

    ffn_rows = finish(outs[0], outs[1])
    input_rows = finish(outs[2], outs[3])

    if split:
        own, to_1, to_2, to_3a, to_3b = tile_terms
        got_a, got_b = swap(to_3a, "dp", 1), swap(to_3b, "dp", 2)
        to_2 = jnp.concatenate([add(to_2[:half], got_a), to_2[half:]])
        to_1 = jnp.concatenate([to_1[:half], add(to_1[half:], got_b)])
        from_1, from_2 = swap(to_1, "dp", 1), swap(to_2, "dp", 2)
        summed = [add(own[at], from_1[at], from_2[at]) for at in range(far)]
    else:
        summed = scatter(dict(enumerate(tile_terms)), "dp", near_strides)[0]
    back = [summed[0]] + [swap(summed[at], "dp", at * near) for at in range(1, far)]
    grads = pl.pallas_call(
        functools.partial(unpack, slot_count=slot_count),
        grid_spec=pltpu.PrefetchScalarGridSpec(
            num_scalar_prefetch=3,
            grid=(1,),
            in_specs=[whole(packed_shape)] * far,
            out_specs=whole(tile_list.shape),
            scratch_shapes=[pltpu.VMEM((far * buffer, row_share, tile), BF16)],
        ),
        out_shape=jax.ShapeDtypeStruct(tile_list.shape, BF16),
        compiler_params=PARAMS,
    )((home ^ far_at)[None, :], firsts, tile_counts, *back)
    tile_grad = grads.reshape(blocks_dev, 3, slot_count, row_share, tile).transpose(3, 1, 0, 2, 4)
    return ffn_rows, input_rows, tile_grad


def solution(mesh):
    return jax.shard_map(
        shards,
        mesh=mesh,
        in_specs=(
            P(("dp", "tensor"), None),
            P(("dp", "tensor"), None),
            P("dp", None, "tensor", None, None),
            P(None, "tensor"),
            P(None, "tensor", None),
        ),
        out_specs=(
            P(("dp", "tensor"), None),
            P(("dp", "tensor"), None),
            P("dp", None, "tensor", None, None),
        ),
        check_vma=False,
    )
```

time: 210 us -> 203 us (0.967)
  waiting for transfers between devices: 128 us -> 101 us
  Pallas kernels: 24.6 us -> 43.1 us
    ppermute x25 -> x31, waiting for transfers between devices: 128 us -> 101 us  [swap(): return lax.ppermute(value, axis, [(at, at ^ stride) for at in range(size)])]
    pallas_call x1 -> x4, Pallas kernels: 24.6 us -> 43.1 us  [the longest x1 21.4 us: shards(): pl.pallas_call(functools.partial(behind, token_count=token_count, weight_...]
    convert_element_type x6 -> x9, other arithmetic: 7.53 us -> 4.33 us  [add(): return total.astype(BF16)]
    transpose x1 -> x0, other arithmetic: 2.39 us -> none  [shards(): tile_grad = jnp.take(jnp.stack(back), order, axis=0).reshape(blocks_dev,...]
    reshape x0 -> x2, local copies, waits for them, and re-layouts: none -> 2.32 us  [the longest x1 2.31 us: shards(): grads.reshape(blocks_dev, 3, slot_count, row_share, tile)]
    ppermute x25 -> x31, starting transfers between devices: 32 us -> 31.8 us  [swap(): return lax.ppermute(value, axis, [(at, at ^ stride) for at in range(size)])]
  transfers between devices with their start and end apart: 25 -> 31, of which waited for: 14 -> 16; matrix products, arithmetic and copies ran while one was open for 9% -> 8% of each run, Pallas kernels for 0% -> 9%
where the time goes in v2:
time: 203 us; the launch traced here: 202 us
  waiting for transfers between devices  101 us (50%)
  Pallas kernels  43.1 us (21%)
  starting transfers between devices  31.8 us (16%)
  local copies, waits for them, and re-layouts  14.7 us (7%)
  other arithmetic  9.87 us (5%)
    ppermute x31, waiting for transfers between devices, swap(): return lax.ppermute(value, axis, [(at, at ^ stride) for at in range(size)])  101 us
    ppermute x31, starting transfers between devices, swap(): return lax.ppermute(value, axis, [(at, at ^ stride) for at in range(size)])  31.8 us
    pallas_call x1, Pallas kernels, shards(): pl.pallas_call(functools.partial(behind, token_count=token_count, weight_...  21.4 us
    pallas_call x1, Pallas kernels, shards(): pl.pallas_call(functools.partial(ahead, token_count=token_count, weight_p...  13.9 us
    convert_element_type x9, other arithmetic, add(): return total.astype(BF16)  4.33 us
    pallas_call x1, Pallas kernels, shards(): pl.pallas_call(functools.partial(unpack, slot_count=slot_count), grid_spe...  4.11 us
  transfers between devices with their start and end apart: 31, of which 16 were waited for; matrix products, arithmetic and copies ran while one was open for 8% of the time, Pallas kernels for 9%

profile of v2, /device:TPU:0, one launch (start us, length us, event | category | flops | bytes accessed | tf_op | source)
XLA Modules:
  0.0 201.7 jit_solution(8862486059821741180)
XLA Ops:
  3.6 2.3 %copy.14 = bf16[56,3,3,8,128]{4,3,2,1,0:T(8,128)(2,1)} copy(bf16[56,3,3,8,128]{4,0,2,1,3:T(8,128)(2,1)} %bitcast.37) | data formatting | bytes 2064384 | tf_op jit(solution)/shard_map/transpose | solution.py:273
  6.5 3.6 %shard_map.76 = (bf16[91,8,128]{2,1,0:T(8,128)(2,1)}, bf16[91,8,128]{2,1,0:T(8,128)(2,1)}, bf16[91,8,128]{2,1,0:T(8,128)(2,1)}, bf16[91,8,128]{2,1,0:T(8,128)(2,1)}) custom-call(s32[4,14]{1,0:T(4,128)} %copy.15.block_at, s32[3,56]{1,0:T(4,128)} %add_add_fusion.firsts, bf16[504,8,128]{2,1,0:T(8,128)(2,1)} %bitcast.35), custom_call_target="tpu_custom_call" | custom-call | tf_op jit(solution)/shard_map/pallas_call | solution.py:277
  10.1 3.0 %collective-permute-start.1 = (bf16[91,8,128]{2,1,0:T(8,128)(2,1)}, bf16[91,8,128]{2,1,0:T(8,128)(2,1)S(1)}, u32[]{:S(2)}, u32[]{:S(2)}) collective-permute-start(bf16[91,8,128]{2,1,0:T(8,128)(2,1)} %get-tuple-element.26), channel_id=1, source_target_pairs={{0,8},{2,10},{4,12},{6,14},{8,0},{10,2},{12,4},{14,6},{16,24},{18,... | collective-permute-start | bytes 559112 | tf_op jit(solution)/shard_map/ppermute | solution.py:21
  13.2 2.6 %collective-permute-start.2 = (bf16[91,8,128]{2,1,0:T(8,128)(2,1)}, bf16[91,8,128]{2,1,0:T(8,128)(2,1)S(1)}, u32[]{:S(2)}, u32[]{:S(2)}) collective-permute-start(bf16[91,8,128]{2,1,0:T(8,128)(2,1)} %get-tuple-element.27), channel_id=1, source_target_pairs={{0,16},{2,18},{4,20},{6,22},{8,24},{10,26},{12,28},{14,30},{16,0},... | collective-permute-start | bytes 559112 | tf_op jit(solution)/shard_map/ppermute | solution.py:21
  15.8 5.4 %collective-permute-done.1 = bf16[91,8,128]{2,1,0:T(8,128)(2,1)S(1)} collective-permute-done((bf16[91,8,128]{2,1,0:T(8,128)(2,1)}, bf16[91,8,128]{2,1,0:T(8,128)(2,1)S(1)}, u32[]{:S(2)}, u32[]{:S(2)}) %collective-permute-start.1) | collective-permute-done | bytes 186400 | tf_op jit(solution)/shard_map/ppermute | solution.py:21
  21.2 8.7 %collective-permute-done.2 = bf16[91,8,128]{2,1,0:T(8,128)(2,1)S(1)} collective-permute-done((bf16[91,8,128]{2,1,0:T(8,128)(2,1)}, bf16[91,8,128]{2,1,0:T(8,128)(2,1)S(1)}, u32[]{:S(2)}, u32[]{:S(2)}) %collective-permute-start.2) | collective-permute-done | bytes 186400 | tf_op jit(solution)/shard_map/ppermute | solution.py:21
  30.9 1.6 collective-permute-start.15
  33.5 3.2 %collective-permute-start.7 = (bf16[64,4096]{1,0:T(8,128)(2,1)S(1)}, bf16[64,4096]{1,0:T(8,128)(2,1)S(1)}, u32[]{:S(2)}, u32[]{:S(2)}) collective-permute-start(bf16[64,4096]{1,0:T(8,128)(2,1)S(1)} %constant_dynamic-update-slice_fusion.refs_0_), channel_id=1, source_target_pairs={{0,8},{2,10},{4,12},{6,14},{8,0},{10,2},{12,4},{14,6},{16,24},{18,... | collective-permute-start | bytes 1572872 | tf_op jit(solution)/shard_map/ppermute | solution.py:21
  36.7 1.5 collective-permute-start.14
  39.3 12.8 %collective-permute-done.4.refs_2_ = bf16[32,4096]{1,0:T(8,128)(2,1)} collective-permute-done((bf16[32,4096]{1,0:T(8,128)(2,1)S(1)}, bf16[32,4096]{1,0:T(8,128)(2,1)}, u32[]{:S(2)}, u32[]{:S(2)}) %collective-permute-start.4) | collective-permute-done | bytes 262176 | tf_op jit(solution)/shard_map/ppermute | solution.py:21
  52.1 3.5 %collective-permute-start.5 = (bf16[32,4096]{1,0:T(8,128)(2,1)}, bf16[32,4096]{1,0:T(8,128)(2,1)S(1)}, u32[]{:S(2)}, u32[]{:S(2)}) collective-permute-start(bf16[32,4096]{1,0:T(8,128)(2,1)} %param.6), channel_id=1, source_target_pairs={{0,16},{2,18},{4,20},{6,22},{8,24},{10,26},{12,28},{14,30},{16,0},... | collective-permute-start | bytes 786440 | tf_op jit(solution)/shard_map/ppermute | solution.py:21
  57.1 9.2 %collective-permute-done.5.refs_2_ = bf16[32,4096]{1,0:T(8,128)(2,1)S(1)} collective-permute-done((bf16[32,4096]{1,0:T(8,128)(2,1)}, bf16[32,4096]{1,0:T(8,128)(2,1)S(1)}, u32[]{:S(2)}, u32[]{:S(2)}) %collective-permute-start.5) | collective-permute-done | bytes 262176 | tf_op jit(solution)/shard_map/ppermute | solution.py:21
  67.2 1.8 slice.164
  69.0 1.5 collective-permute-start.17
  73.1 1.9 collective-permute-done.9.refs_6_
  76.2 4.1 %collective-permute-done.17.refs_12_ = bf16[2,91,8,128]{3,2,1,0:T(8,128)(2,1)S(1)} collective-permute-done((bf16[2,91,8,128]{3,2,1,0:T(8,128)(2,1)}, bf16[2,91,8,128]{3,2,1,0:T(8,128)(2,1)S(1)}, u32[]{:S(2)}, u32[]{:S(2)}) %collective-permute-start.17) | collective-permute-done | bytes 372768 | tf_op jit(solution)/shard_map/ppermute | solution.py:21
  80.3 1.3 collective-permute-done.16.refs_11_
  81.6 13.9 %shard_map.77 = (bf16[4096,256]{1,0:T(8,128)(2,1)}, bf16[14,9,128,128]{3,2,1,0:T(8,128)(2,1)}, f32[14,256,128]{2,1,0:T(8,128)}, f32[14,256,128]{2,1,0:T(8,128)},...) custom-call(s32[4,4]{1,0:T(4,128)} %add_multiply_fusion.offsets, s32[3,14]{1,0:T(4,128)} %copy.17.firsts, ...), custom_call_target="tpu_custom_call" | custom-call | flops 704643072 | bytes 16000000 | tf_op jit(solution)/shard_map/pallas_call | solution.py:359
  96.4 21.4 %shard_map.78 = (bf16[4,32,4096]{2,1,0:T(8,128)(2,1)}, bf16[4,32,4096]{2,1,0:T(8,128)(2,1)}, bf16[4,32,4096]{2,1,0:T(8,128)(2,1)}, bf16[4,32,4096]{2,1,0:T(8,128...) custom-call(s32[4,4]{1,0:T(4,128)} %add_multiply_fusion.offsets, ...), custom_call_target="tpu_custom_call" | custom-call | flops 2466250752 | bytes 25000000 | tf_op jit(solution)/shard_map/pallas_call | solution.py:381
  122.2 5.8 %collective-permute-done.26 = bf16[2,91,8,128]{3,2,1,0:T(8,128)(2,1)S(1)} collective-permute-done((bf16[2,91,8,128]{3,2,1,0:T(8,128)(2,1)}, bf16[2,91,8,128]{3,2,1,0:T(8,128)(2,1)S(1)}, u32[]{:S(2)}, u32[]{:S(2)}) %collective-permute-start.26) | collective-permute-done | bytes 372768 | tf_op jit(solution)/shard_map/ppermute | solution.py:21
  129.8 3.4 %collective-permute-done.24 = bf16[2,91,8,128]{3,2,1,0:T(8,128)(2,1)S(1)} collective-permute-done((bf16[2,91,8,128]{3,2,1,0:T(8,128)(2,1)}, bf16[2,91,8,128]{3,2,1,0:T(8,128)(2,1)S(1)}, u32[]{:S(2)}, u32[]{:S(2)}) %collective-permute-start.24) | collective-permute-done | bytes 372768 | tf_op jit(solution)/shard_map/ppermute | solution.py:21
  135.8 12.9 %collective-permute-done.27 = bf16[4,91,8,128]{3,2,1,0:T(8,128)(2,1)S(1)} collective-permute-done((bf16[4,91,8,128]{3,2,1,0:T(8,128)(2,1)S(1)}, bf16[4,91,8,128]{3,2,1,0:T(8,128)(2,1)S(1)}, u32[]{:S(2)}, u32[]{:S(2)}) %collective-permute-start.27) | collective-permute-done | bytes 745504 | tf_op jit(solution)/shard_map/ppermute | solution.py:21
  148.7 2.6 %collective-permute-done.25 = bf16[4,91,8,128]{3,2,1,0:T(8,128)(2,1)S(1)} collective-permute-done((bf16[4,91,8,128]{3,2,1,0:T(8,128)(2,1)S(1)}, bf16[4,91,8,128]{3,2,1,0:T(8,128)(2,1)S(1)}, u32[]{:S(2)}, u32[]{:S(2)}) %collective-permute-start.25) | collective-permute-done | bytes 745504 | tf_op jit(solution)/shard_map/ppermute | solution.py:21
  152.3 2.4 %collective-permute-start.30 = (bf16[91,8,128]{2,1,0:T(8,128)(2,1)S(1)}, bf16[91,8,128]{2,1,0:T(8,128)(2,1)S(1)}, u32[]{:S(2)}, u32[]{:S(2)}) collective-permute-start(bf16[91,8,128]{2,1,0:T(8,128)(2,1)S(1)} %get-tuple-element.47), channel_id=1, source_target_pairs={{0,24},{2,26},{4,28},{6,30},{8,16},{10,18},{12,20},{14,22},{16,8},... | collective-permute-start | bytes 559112 | tf_op jit(solution)/shard_map/ppermute | solution.py:21
  154.9 1.8 collective-permute-start.28
  157.1 4.7 %collective-permute-done.30.refs_3_ = bf16[91,8,128]{2,1,0:T(8,128)(2,1)S(1)} collective-permute-done((bf16[91,8,128]{2,1,0:T(8,128)(2,1)S(1)}, bf16[91,8,128]{2,1,0:T(8,128)(2,1)S(1)}, u32[]{:S(2)}, u32[]{:S(2)}) %collective-permute-start.30) | collective-permute-done | bytes 186400 | tf_op jit(solution)/shard_map/ppermute | solution.py:21
  161.8 8.2 %collective-permute-done.29.refs_2_ = bf16[91,8,128]{2,1,0:T(8,128)(2,1)S(1)} collective-permute-done((bf16[91,8,128]{2,1,0:T(8,128)(2,1)S(1)}, bf16[91,8,128]{2,1,0:T(8,128)(2,1)S(1)}, u32[]{:S(2)}, u32[]{:S(2)}) %collective-permute-start.29) | collective-permute-done | bytes 186400 | tf_op jit(solution)/shard_map/ppermute | solution.py:21
  170.7 4.1 %shard_map.79 = bf16[504,8,128]{2,1,0:T(8,128)(2,1)} custom-call(s32[1,56]{1,0:T(1,128)} %fusion.10.home, s32[3,56]{1,0:T(4,128)} %add_add_fusion.firsts, s32[3,56]{1,0:T(4,128)} %counts.1, bf16[91,8,128]{2,1,0:T(8,128)(2,1)} %get-tuple-element.50.refs_0_, bf16[91,8,128]{2,1,0:T(8,128)(2,1)} %copy-done.17, bf16[91,8,128]{2,1,0:T(8,128)(2,1)} %copy-done.16, ...), custom_call_target="tpu_custom_call" | custom-call | tf_op jit(solution)/shard_map/pallas_call | solution.py:445
  174.8 2.3 %copy.21 = bf16[56,3,3,8,128]{4,0,2,1,3:T(8,128)(2,1)} copy(bf16[56,3,3,8,128]{4,3,2,1,0:T(8,128)(2,1)} %bitcast.36) | data formatting | bytes 2064384 | tf_op jit(solution)/shard_map/reshape | solution.py:457
  178.5 1.8 collective-permute-start.23
  180.3 15.0 %collective-permute-done.20 = bf16[32,4096]{1,0:T(8,128)(2,1)S(1)} collective-permute-done((bf16[32,4096]{1,0:T(8,128)(2,1)S(1)}, bf16[32,4096]{1,0:T(8,128)(2,1)S(1)}, u32[]{:S(2)}, u32[]{:S(2)}) %collective-permute-start.20) | collective-permute-done | bytes 262176 | tf_op jit(solution)/shard_map/ppermute | solution.py:21
  196.2 4.7 %collective-permute-done.23 = bf16[32,4096]{1,0:T(8,128)(2,1)S(1)} collective-permute-done((bf16[32,4096]{1,0:T(8,128)(2,1)S(1)}, bf16[32,4096]{1,0:T(8,128)(2,1)S(1)}, u32[]{:S(2)}, u32[]{:S(2)}) %collective-permute-start.23) | collective-permute-done | bytes 262176 | tf_op jit(solution)/shard_map/ppermute | solution.py:21
  (122 shorter events, 27.8 us)
Async XLA Ops:
  10.1 11.0 %collective-permute-start.1 = (bf16[91,8,128]{2,1,0:T(8,128)(2,1)}, bf16[91,8,128]{2,1,0:T(8,128)(2,1)S(1)}, u32[]{:S(2)}, u32[]{:S(2)}) collective-permute-start(bf16[91,8,128]{2,1,0:T(8,128)(2,1)} %get-tuple-element.26), channel_id=1, source_target_pairs={{0,8},{2,10},{4,12},{6,14},{8,0},{10,2},{12,4},{14,6},{16,24},{18,... | collective-permute-start | bytes 559112 | tf_op jit(solution)/shard_map/ppermute | solution.py:21
  13.2 16.7 %collective-permute-start.2 = (bf16[91,8,128]{2,1,0:T(8,128)(2,1)}, bf16[91,8,128]{2,1,0:T(8,128)(2,1)S(1)}, u32[]{:S(2)}, u32[]{:S(2)}) collective-permute-start(bf16[91,8,128]{2,1,0:T(8,128)(2,1)} %get-tuple-element.27), channel_id=1, source_target_pairs={{0,16},{2,18},{4,20},{6,22},{8,24},{10,26},{12,28},{14,30},{16,0},... | collective-permute-start | bytes 559112 | tf_op jit(solution)/shard_map/ppermute | solution.py:21
  15.8 14.1 %collective-permute-start.3 = (bf16[91,8,128]{2,1,0:T(8,128)(2,1)}, bf16[91,8,128]{2,1,0:T(8,128)(2,1)S(1)}, u32[]{:S(2)}, u32[]{:S(2)}) collective-permute-start(bf16[91,8,128]{2,1,0:T(8,128)(2,1)} %get-tuple-element.28), channel_id=1, source_target_pairs={{0,24},{2,26},{4,28},{6,30},{8,16},{10,18},{12,20},{14,22},{16,8},... | collective-permute-start | bytes 559112 | tf_op jit(solution)/shard_map/ppermute | solution.py:21
  30.9 50.7 %copy-start.1 = (bf16[4,91,8,128]{3,2,1,0:T(8,128)(2,1)}, bf16[4,91,8,128]{3,2,1,0:T(8,128)(2,1)S(1)}, u32[]{:S(2)}) copy-start(bf16[4,91,8,128]{3,2,1,0:T(8,128)(2,1)S(1)} %pad_maximum_fusion.refs_8_) | copy-start | bytes 2236420
  30.9 24.9 %collective-permute-start.15 = (bf16[4,91,8,128]{3,2,1,0:T(8,128)(2,1)S(1)}, bf16[4,91,8,128]{3,2,1,0:T(8,128)(2,1)S(1)}, u32[]{:S(2)}, u32[]{:S(2)}) collective-permute-start(bf16[4,91,8,128]{3,2,1,0:T(8,128)(2,1)S(1)} %pad_maximum_fusion.refs_8_), channel_id=1, source_target_pairs={{0,4},{2,6},{4,0},{6,2},{8,12},{10,14},{12,8},{14,10},{16,20},{18,... | collective-permute-start | bytes 2236424 | tf_op jit(solution)/shard_map/ppermute | solution.py:21
  33.5 22.1 %collective-permute-start.7 = (bf16[64,4096]{1,0:T(8,128)(2,1)S(1)}, bf16[64,4096]{1,0:T(8,128)(2,1)S(1)}, u32[]{:S(2)}, u32[]{:S(2)}) collective-permute-start(bf16[64,4096]{1,0:T(8,128)(2,1)S(1)} %constant_dynamic-update-slice_fusion.refs_0_), channel_id=1, source_target_pairs={{0,8},{2,10},{4,12},{6,14},{8,0},{10,2},{12,4},{14,6},{16,24},{18,... | collective-permute-start | bytes 1572872 | tf_op jit(solution)/shard_map/ppermute | solution.py:21
  36.7 30.5 %collective-permute-start.14 = (bf16[4,91,8,128]{3,2,1,0:T(8,128)(2,1)S(1)}, bf16[4,91,8,128]{3,2,1,0:T(8,128)(2,1)}, u32[]{:S(2)}, u32[]{:S(2)}) collective-permute-start(bf16[4,91,8,128]{3,2,1,0:T(8,128)(2,1)S(1)} %pad_maximum_fusion.refs_8_), channel_id=1, source_target_pairs={{0,2},{2,0},{4,6},{6,4},{8,10},{10,8},{12,14},{14,12},{16,18},{18,... | collective-permute-start | bytes 2236424 | tf_op jit(solution)/shard_map/ppermute | solution.py:21
  38.2 13.9 %collective-permute-start.4 = (bf16[32,4096]{1,0:T(8,128)(2,1)S(1)}, bf16[32,4096]{1,0:T(8,128)(2,1)}, u32[]{:S(2)}, u32[]{:S(2)}) collective-permute-start(bf16[32,4096]{1,0:T(8,128)(2,1)S(1)} %copy-done.14), channel_id=1, source_target_pairs={{0,16},{2,18},{4,20},{6,22},{8,24},{10,26},{12,28},{14,30},{16,0},... | collective-permute-start | bytes 786440 | tf_op jit(solution)/shard_map/ppermute | solution.py:21
  39.3 29.7 %collective-permute-start = (bf16[64,4096]{1,0:T(8,128)(2,1)S(1)}, bf16[64,4096]{1,0:T(8,128)(2,1)S(1)}, u32[]{:S(2)}, u32[]{:S(2)}) collective-permute-start(bf16[64,4096]{1,0:T(8,128)(2,1)S(1)} %constant_dynamic-update-slice_fusion.refs_0_), channel_id=1, source_target_pairs={{0,1},{1,0},{2,3},{3,2},{4,5},{5,4},{6,7},{7,6},{8,9},{9,8},{10,11... | collective-permute-start | bytes 1572872 | tf_op jit(solution)/shard_map/ppermute | solution.py:21
  52.1 14.2 %collective-permute-start.5 = (bf16[32,4096]{1,0:T(8,128)(2,1)}, bf16[32,4096]{1,0:T(8,128)(2,1)S(1)}, u32[]{:S(2)}, u32[]{:S(2)}) collective-permute-start(bf16[32,4096]{1,0:T(8,128)(2,1)} %param.6), channel_id=1, source_target_pairs={{0,16},{2,18},{4,20},{6,22},{8,24},{10,26},{12,28},{14,30},{16,0},... | collective-permute-start | bytes 786440 | tf_op jit(solution)/shard_map/ppermute | solution.py:21
  55.5 10.7 %collective-permute-start.12 = (bf16[32,4096]{1,0:T(8,128)(2,1)}, bf16[32,4096]{1,0:T(8,128)(2,1)}, u32[]{:S(2)}, u32[]{:S(2)}) collective-permute-start(bf16[32,4096]{1,0:T(8,128)(2,1)} %collective-permute-done.4.refs_2_), channel_id=1, source_target_pairs={{0,8},{2,10},{4,12},{6,14},{8,0},{10,2},{12,4},{14,6},{16,24},{18,... | collective-permute-start | bytes 786440 | tf_op jit(solution)/shard_map/ppermute | solution.py:21
  55.8 14.7 %collective-permute-start.11 = (bf16[32,4096]{1,0:T(8,128)(2,1)}, bf16[32,4096]{1,0:T(8,128)(2,1)}, u32[]{:S(2)}, u32[]{:S(2)}) collective-permute-start(bf16[32,4096]{1,0:T(8,128)(2,1)} %collective-permute-done.4.refs_2_), channel_id=1, source_target_pairs={{0,1},{1,0},{2,3},{3,2},{4,5},{5,4},{6,7},{7,6},{8,9},{9,8},{10,11... | collective-permute-start | bytes 786440 | tf_op jit(solution)/shard_map/ppermute | solution.py:21
  66.2 10.0 %collective-permute-start.8 = (bf16[64,4096]{1,0:T(8,128)(2,1)S(1)}, bf16[64,4096]{1,0:T(8,128)(2,1)S(1)}, u32[]{:S(2)}, u32[]{:S(2)}) collective-permute-start(bf16[64,4096]{1,0:T(8,128)(2,1)S(1)} %collective-permute-done.7.refs_4_), channel_id=1, source_target_pairs={{0,1},{1,0},{2,3},{3,2},{4,5},{5,4},{6,7},{7,6},{8,9},{9,8},{10,11... | collective-permute-start | bytes 1572872 | tf_op jit(solution)/shard_map/ppermute | solution.py:21
  66.2 8.8 %collective-permute-start.9 = (bf16[32,4096]{1,0:T(8,128)(2,1)S(1)}, bf16[32,4096]{1,0:T(8,128)(2,1)}, u32[]{:S(2)}, u32[]{:S(2)}) collective-permute-start(bf16[32,4096]{1,0:T(8,128)(2,1)S(1)} %collective-permute-done.5.refs_2_), channel_id=1, source_target_pairs={{0,8},{2,10},{4,12},{6,14},{8,0},{10,2},{12,4},{14,6},{16,24},{18,... | collective-permute-start | bytes 786440 | tf_op jit(solution)/shard_map/ppermute | solution.py:21
  67.2 7.8 %collective-permute-start.13 = (bf16[32,4096]{1,0:T(8,128)(2,1)}, bf16[32,4096]{1,0:T(8,128)(2,1)}, u32[]{:S(2)}, u32[]{:S(2)}) collective-permute-start(bf16[32,4096]{1,0:T(8,128)(2,1)} %collective-permute-done.12.refs_6_), channel_id=1, source_target_pairs={{0,1},{1,0},{2,3},{3,2},{4,5},{5,4},{6,7},{7,6},{8,9},{9,8},{10,11... | collective-permute-start | bytes 786440 | tf_op jit(solution)/shard_map/ppermute | solution.py:21
  69.0 11.3 %collective-permute-start.17 = (bf16[2,91,8,128]{3,2,1,0:T(8,128)(2,1)}, bf16[2,91,8,128]{3,2,1,0:T(8,128)(2,1)S(1)}, u32[]{:S(2)}, u32[]{:S(2)}) collective-permute-start(bf16[2,91,8,128]{3,2,1,0:T(8,128)(2,1)} %slice.165), channel_id=1, source_target_pairs={{0,2},{2,0},{4,6},{6,4},{8,10},{10,8},{12,14},{14,12},{16,18},{18,... | collective-permute-start | bytes 1118216 | tf_op jit(solution)/shard_map/ppermute | solution.py:21
  70.5 11.1 %collective-permute-start.16 = (bf16[2,91,8,128]{3,2,1,0:T(8,128)(2,1)}, bf16[2,91,8,128]{3,2,1,0:T(8,128)(2,1)}, u32[]{:S(2)}, u32[]{:S(2)}) collective-permute-start(bf16[2,91,8,128]{3,2,1,0:T(8,128)(2,1)} %slice.164), channel_id=1, source_target_pairs={{0,4},{2,6},{4,0},{6,2},{8,12},{10,14},{12,8},{14,10},{16,20},{18,... | collective-permute-start | bytes 1118216 | tf_op jit(solution)/shard_map/ppermute | solution.py:21
  75.0 20.5 %collective-permute-start.6 = (bf16[32,4096]{1,0:T(8,128)(2,1)S(1)}, bf16[32,4096]{1,0:T(8,128)(2,1)S(1)}, u32[]{:S(2)}, u32[]{:S(2)}) collective-permute-start(bf16[32,4096]{1,0:T(8,128)(2,1)S(1)} %collective-permute-done.5.refs_2_), channel_id=1, source_target_pairs={{0,1},{1,0},{2,3},{3,2},{4,5},{5,4},{6,7},{7,6},{8,9},{9,8},{10,11... | collective-permute-start | bytes 786440 | tf_op jit(solution)/shard_map/ppermute | solution.py:21
  75.1 20.5 %collective-permute-start.10 = (bf16[32,4096]{1,0:T(8,128)(2,1)}, bf16[32,4096]{1,0:T(8,128)(2,1)S(1)}, u32[]{:S(2)}, u32[]{:S(2)}) collective-permute-start(bf16[32,4096]{1,0:T(8,128)(2,1)} %collective-permute-done.9.refs_6_), channel_id=1, source_target_pairs={{0,1},{1,0},{2,3},{3,2},{4,5},{5,4},{6,7},{7,6},{8,9},{9,8},{10,11... | collective-permute-start | bytes 786440 | tf_op jit(solution)/shard_map/ppermute | solution.py:21
  117.8 10.2 %collective-permute-start.26 = (bf16[2,91,8,128]{3,2,1,0:T(8,128)(2,1)}, bf16[2,91,8,128]{3,2,1,0:T(8,128)(2,1)S(1)}, u32[]{:S(2)}, u32[]{:S(2)}) collective-permute-start(bf16[2,91,8,128]{3,2,1,0:T(8,128)(2,1)} %get-tuple-element.46), channel_id=1, source_target_pairs={{0,2},{2,0},{4,6},{6,4},{8,10},{10,8},{12,14},{14,12},{16,18},{18,... | collective-permute-start | bytes 1118216 | tf_op jit(solution)/shard_map/ppermute | solution.py:21
  118.8 15.8 %collective-permute-start.18 = (bf16[4,32,4096]{2,1,0:T(8,128)(2,1)}, bf16[4,32,4096]{2,1,0:T(8,128)(2,1)S(1)}, u32[]{:S(2)}, u32[]{:S(2)}) collective-permute-start(bf16[4,32,4096]{2,1,0:T(8,128)(2,1)} %get-tuple-element.39), channel_id=1, source_target_pairs={{0,1},{1,0},{2,3},{3,2},{4,5},{5,4},{6,7},{7,6},{8,9},{9,8},{10,11... | collective-permute-start | bytes 3145736 | tf_op jit(solution)/shard_map/ppermute | solution.py:21
  121.4 11.7 %collective-permute-start.24 = (bf16[2,91,8,128]{3,2,1,0:T(8,128)(2,1)}, bf16[2,91,8,128]{3,2,1,0:T(8,128)(2,1)S(1)}, u32[]{:S(2)}, u32[]{:S(2)}) collective-permute-start(bf16[2,91,8,128]{3,2,1,0:T(8,128)(2,1)} %get-tuple-element.44), channel_id=1, source_target_pairs={{0,4},{2,6},{4,0},{6,2},{8,12},{10,14},{12,8},{14,10},{16,20},{18,... | collective-permute-start | bytes 1118216 | tf_op jit(solution)/shard_map/ppermute | solution.py:21
  122.0 34.7 %collective-permute-start.21 = (bf16[4,32,4096]{2,1,0:T(8,128)(2,1)}, bf16[4,32,4096]{2,1,0:T(8,128)(2,1)S(1)}, u32[]{:S(2)}, u32[]{:S(2)}) collective-permute-start(bf16[4,32,4096]{2,1,0:T(8,128)(2,1)} %get-tuple-element.41), channel_id=1, source_target_pairs={{0,1},{1,0},{2,3},{3,2},{4,5},{5,4},{6,7},{7,6},{8,9},{9,8},{10,11... | collective-permute-start | bytes 3145736 | tf_op jit(solution)/shard_map/ppermute | solution.py:21
  129.2 19.5 %collective-permute-start.27 = (bf16[4,91,8,128]{3,2,1,0:T(8,128)(2,1)S(1)}, bf16[4,91,8,128]{3,2,1,0:T(8,128)(2,1)S(1)}, u32[]{:S(2)}, u32[]{:S(2)}) collective-permute-start(bf16[4,91,8,128]{3,2,1,0:T(8,128)(2,1)S(1)} %pad_maximum_fusion.2), channel_id=1, source_target_pairs={{0,4},{2,6},{4,0},{6,2},{8,12},{10,14},{12,8},{14,10},{16,20},{18,... | collective-permute-start | bytes 2236424 | tf_op jit(solution)/shard_map/ppermute | solution.py:21
  133.3 18.0 %collective-permute-start.25 = (bf16[4,91,8,128]{3,2,1,0:T(8,128)(2,1)S(1)}, bf16[4,91,8,128]{3,2,1,0:T(8,128)(2,1)S(1)}, u32[]{:S(2)}, u32[]{:S(2)}) collective-permute-start(bf16[4,91,8,128]{3,2,1,0:T(8,128)(2,1)S(1)} %pad_maximum_fusion.1), channel_id=1, source_target_pairs={{0,2},{2,0},{4,6},{6,4},{8,10},{10,8},{12,14},{14,12},{16,18},{18,... | collective-permute-start | bytes 2236424 | tf_op jit(solution)/shard_map/ppermute | solution.py:21
  134.7 42.4 %collective-permute-start.19 = (bf16[2,32,4096]{2,1,0:T(8,128)(2,1)S(1)}, bf16[2,32,4096]{2,1,0:T(8,128)(2,1)S(1)}, u32[]{:S(2)}, u32[]{:S(2)}) collective-permute-start(bf16[2,32,4096]{2,1,0:T(8,128)(2,1)S(1)} %add_convert_fusion.1), channel_id=1, source_target_pairs={{0,8},{2,10},{4,12},{6,14},{8,0},{10,2},{12,4},{14,6},{16,24},{18,... | collective-permute-start | bytes 1572872 | tf_op jit(solution)/shard_map/ppermute | solution.py:21
  152.3 9.4 %collective-permute-start.30 = (bf16[91,8,128]{2,1,0:T(8,128)(2,1)S(1)}, bf16[91,8,128]{2,1,0:T(8,128)(2,1)S(1)}, u32[]{:S(2)}, u32[]{:S(2)}) collective-permute-start(bf16[91,8,128]{2,1,0:T(8,128)(2,1)S(1)} %get-tuple-element.47), channel_id=1, source_target_pairs={{0,24},{2,26},{4,28},{6,30},{8,16},{10,18},{12,20},{14,22},{16,8},... | collective-permute-start | bytes 559112 | tf_op jit(solution)/shard_map/ppermute | solution.py:21
  154.8 15.2 %collective-permute-start.29 = (bf16[91,8,128]{2,1,0:T(8,128)(2,1)S(1)}, bf16[91,8,128]{2,1,0:T(8,128)(2,1)S(1)}, u32[]{:S(2)}, u32[]{:S(2)}) collective-permute-start(bf16[91,8,128]{2,1,0:T(8,128)(2,1)S(1)} %get-tuple-element.48), channel_id=1, source_target_pairs={{0,16},{2,18},{4,20},{6,22},{8,24},{10,26},{12,28},{14,30},{16,0},... | collective-permute-start | bytes 559112 | tf_op jit(solution)/shard_map/ppermute | solution.py:21
  154.9 15.1 %collective-permute-start.28 = (bf16[91,8,128]{2,1,0:T(8,128)(2,1)S(1)}, bf16[91,8,128]{2,1,0:T(8,128)(2,1)S(1)}, u32[]{:S(2)}, u32[]{:S(2)}) collective-permute-start(bf16[91,8,128]{2,1,0:T(8,128)(2,1)S(1)} %get-tuple-element.49), channel_id=1, source_target_pairs={{0,8},{2,10},{4,12},{6,14},{8,0},{10,2},{12,4},{14,6},{16,24},{18,... | collective-permute-start | bytes 559112 | tf_op jit(solution)/shard_map/ppermute | solution.py:21
  156.8 21.6 %collective-permute-start.22 = (bf16[2,32,4096]{2,1,0:T(8,128)(2,1)S(1)}, bf16[2,32,4096]{2,1,0:T(8,128)(2,1)S(1)}, u32[]{:S(2)}, u32[]{:S(2)}) collective-permute-start(bf16[2,32,4096]{2,1,0:T(8,128)(2,1)S(1)} %add_convert_fusion), channel_id=1, source_target_pairs={{0,8},{2,10},{4,12},{6,14},{8,0},{10,2},{12,4},{14,6},{16,24},{18,... | collective-permute-start | bytes 1572872 | tf_op jit(solution)/shard_map/ppermute | solution.py:21
  177.2 18.2 %collective-permute-start.20 = (bf16[32,4096]{1,0:T(8,128)(2,1)S(1)}, bf16[32,4096]{1,0:T(8,128)(2,1)S(1)}, u32[]{:S(2)}, u32[]{:S(2)}) collective-permute-start(bf16[32,4096]{1,0:T(8,128)(2,1)S(1)} %fusion.2), channel_id=1, source_target_pairs={{0,16},{2,18},{4,20},{6,22},{8,24},{10,26},{12,28},{14,30},{16,0},... | collective-permute-start | bytes 786440 | tf_op jit(solution)/shard_map/ppermute | solution.py:21
  178.5 22.3 %collective-permute-start.23 = (bf16[32,4096]{1,0:T(8,128)(2,1)S(1)}, bf16[32,4096]{1,0:T(8,128)(2,1)S(1)}, u32[]{:S(2)}, u32[]{:S(2)}) collective-permute-start(bf16[32,4096]{1,0:T(8,128)(2,1)S(1)} %fusion.3), channel_id=1, source_target_pairs={{0,16},{2,18},{4,20},{6,22},{8,24},{10,26},{12,28},{14,30},{16,0},... | collective-permute-start | bytes 786440 | tf_op jit(solution)/shard_map/ppermute | solution.py:21
  (20 other events, 364.7 us)

commit v3 on v0

v3 whole, which is shorter than its diff:
```python
import functools
import math

import jax
import jax.numpy as jnp
from jax import lax
from jax.experimental import pallas as pl
from jax.experimental.pallas import tpu as pltpu
from jax.sharding import PartitionSpec as P

F32 = jnp.float32
BF16 = jnp.bfloat16
PLAIN = (((1,), (0,)), ((), ()))
TURNED = (((1,), (1,)), ((), ()))
PARAMS = pltpu.CompilerParams(vmem_limit_bytes=56 * 1024 * 1024)
dot = functools.partial(lax.dot_general, preferred_element_type=F32)


def swap(value, axis, stride):
    size = lax.axis_size(axis)
    return lax.ppermute(value, axis, [(at, at ^ stride) for at in range(size)])


def after(value, *others):
    return lax.optimization_barrier((value, *others))[0]


def add(first, *others):
    total = first.astype(F32)
    for other in others:
        total = total + other.astype(F32)
    return total.astype(BF16)


def strides_of(size, unit=1):
    found = []
    step = size // 2
    while step >= 1:
        found.append(step * unit)
        step //= 2
    return found


def gather(items, axis, strides):
    for stride in strides:
        items = {**items, **{at ^ stride: swap(one, axis, stride) for at, one in items.items()}}
    return items


def scatter(items, axis, strides):
    for stride in reversed(strides):
        kept = {}
        for at, one in items.items():
            if not at & stride:
                kept[at] = add(one, swap(items[at ^ stride], axis, stride))
        items = kept
    return items


def whole(shape, at=None):
    at = (0,) * len(shape) if at is None else at
    return pl.BlockSpec(shape, lambda *_: at)


def by_block(shape):
    return pl.BlockSpec((1,) + shape, lambda block, *_: (block,) + (0,) * len(shape))


def pack(table, tiles, *outs, blocks, slot_count):
    spare = outs[0].shape[0] - 1
    for at, out in enumerate(outs):

        def one(place, _, at=at, out=out):
            column = at * blocks + place
            block = table[0, column]
            for matrix in range(3):
                first, count = table[1 + matrix, column], table[4 + matrix, column]
                for slot in range(slot_count):
                    to = jnp.where(slot < count, first + slot, spare)
                    out[to] = tiles[(block * 3 + matrix) * slot_count + slot]
            return _

        lax.fori_loop(0, blocks, one, 0)


def unpack(table, *refs, chunks, chunk_rows, blocks, slot_count):
    out, sources = refs[-1], refs[:-1]
    far = len(sources) // chunks
    chunk_blocks = blocks // chunks
    for chunk in range(chunks):
        for at in range(far):
            ref = sources[chunk * far + at]

            def one(place, _, at=at, ref=ref, chunk=chunk):
                column = at * blocks + chunk * chunk_blocks + place
                block = table[0, column]
                for matrix in range(3):
                    first = table[1 + matrix, column] - chunk * chunk_rows
                    count = table[4 + matrix, column]
                    for slot in range(slot_count):
                        live = slot < count
                        value = ref[jnp.where(live, first + slot, 0)].astype(F32)
                        out[(block * 3 + matrix) * slot_count + slot] = jnp.where(
                            live, value, 0.0
                        ).astype(BF16)
                return _

            lax.fori_loop(0, chunk_blocks, one, 0)


def offset_of(table, part, at, near, share):
    far_part = (part[1] + at) ^ table[16, 0]
    near_part = part[0] ^ table[16, 1]
    return pl.multiple_of((far_part * near + near_part) * share, share)


def assemble(table, *refs, weight_parts, slot_count, near):
    weight_refs, whole_tiles, tiles = refs[: len(weight_parts)], refs[-2], refs[-1]
    block = pl.program_id(0)
    spare = weight_refs[0].shape[1] - 1
    places = []
    for matrix in range(3):
        first, count = table[1 + matrix, block], table[4 + matrix, block]
        places += [jnp.where(slot < count, first + slot, spare) for slot in range(slot_count)]
    for ref, part in zip(weight_refs, weight_parts):
        share = ref.shape[2]
        for at in range(part[2]):
            offset = offset_of(table, part, at, near, share)
            for index, place in enumerate(places):
                tiles[index, pl.ds(offset, share), :] = ref[at, place].astype(F32)
    for index, place in enumerate(places):
        whole_tiles[0, index] = jnp.where(place != spare, tiles[index], 0.0).astype(BF16)


def store_parts(total, own, other, token_count, own_parts):
    own_rows = own.shape[1]
    own_at, other_at = 0, 0
    for at in range(token_count):
        value = total[at * own_rows : (at + 1) * own_rows, :].astype(BF16)
        if at in own_parts:
            own[own_at] = value
            own_at += 1
        else:
            other[other_at] = value
            other_at += 1


def tokens_at(refs, columns):
    return jnp.concatenate([ref[:, columns] for ref in refs], axis=0)


def ahead(table, *refs, token_count, slot_count, own_parts):
    token_refs, refs = refs[:token_count], refs[token_count:]
    whole_tiles, x_turned, gate_slope, gate_act_out, hidden_turned, ffn_own, ffn_other = refs[:7]
    ffn_sum = refs[7]
    block = pl.program_id(0)
    tile = whole_tiles.shape[3]
    slots = range(slot_count)

    @pl.when(block == 0)
    def _():
        for at in range(x_turned.shape[0] // tile):
            here = slice(at * tile, (at + 1) * tile)
            x_turned[here, :] = tokens_at(token_refs, here).T
        ffn_sum[...] = jnp.zeros_like(ffn_sum)

    def columns(matrix, slot):
        return pl.ds(pl.multiple_of(table[7 + matrix * slot_count + slot, block] * tile, tile), tile)

    gate_in = jnp.concatenate([tokens_at(token_refs, columns(0, slot)) for slot in slots], axis=1)
    up_in = jnp.concatenate([tokens_at(token_refs, columns(1, slot)) for slot in slots], axis=1)
    gate_tiles = whole_tiles[0, :slot_count].reshape(slot_count * tile, tile)
    up_tiles = whole_tiles[0, slot_count : 2 * slot_count].reshape(slot_count * tile, tile)
    down_tiles = jnp.concatenate([whole_tiles[0, 2 * slot_count + slot] for slot in slots], axis=1)
    gate_pre = dot(gate_in, gate_tiles, PLAIN)
    up_pre = dot(up_in, up_tiles, PLAIN)
    gate_sig = jax.nn.sigmoid(gate_pre)
    gate_act = gate_pre * gate_sig
    hidden = (gate_act * up_pre).astype(BF16)
    gate_slope[0] = up_pre * gate_sig * (1.0 + gate_pre * (1.0 - gate_sig))
    gate_act_out[0] = gate_act
    hidden_turned[0] = hidden.T
    ffn = dot(hidden, down_tiles, PLAIN)
    for slot in slots:
        ffn_sum[:, columns(2, slot)] += ffn[:, slot * tile : (slot + 1) * tile]

    @pl.when(block == pl.num_programs(0) - 1)
    def _():
        store_parts(ffn_sum, ffn_own, ffn_other, token_count, own_parts)


def behind(
    table, *refs, token_count, weight_parts, slot_count, grad_scale, own_parts, near, chunk, chunks,
    chunk_rows,
):
    token_refs, refs = refs[:token_count], refs[token_count:]
    whole_tiles, x_turned, gate_slope, gate_act, hidden_turned = refs[:5]
    refs = refs[5:]
    if chunk > 0:
        carried, refs = refs[0], refs[1:]
    if chunk < chunks - 1:
        carry, refs = refs[0], refs[1:]
    else:
        input_own, input_other, refs = refs[0], refs[1], refs[2:]
    grad_refs, refs = refs[: len(weight_parts)], refs[len(weight_parts) :]
    input_sum, tile_out = refs
    step = pl.program_id(0)
    block = step + chunk * pl.num_programs(0)
    tile = tile_out.shape[1]
    slots = range(slot_count)

    @pl.when(step == 0)
    def _():
        input_sum[...] = carried[...] if chunk > 0 else jnp.zeros_like(input_sum)

    def columns(matrix, slot):
        return pl.ds(pl.multiple_of(table[7 + matrix * slot_count + slot, block] * tile, tile), tile)

    gate_tiles = whole_tiles[0, :slot_count].reshape(slot_count * tile, tile)
    up_tiles = whole_tiles[0, slot_count : 2 * slot_count].reshape(slot_count * tile, tile)
    down_tiles = jnp.concatenate([whole_tiles[0, 2 * slot_count + slot] for slot in slots], axis=1)
    grad_in = jnp.concatenate([tokens_at(token_refs, columns(2, slot)) for slot in slots], axis=1)
    hidden_grad = dot(grad_in, down_tiles, TURNED)
    down_terms = dot(hidden_turned[0], grad_in, PLAIN)
    gate_grad = (hidden_grad * gate_slope[0]).astype(BF16)
    up_grad = (hidden_grad * gate_act[0]).astype(BF16)
    from_gate = dot(gate_grad, gate_tiles, TURNED)
    from_up = dot(up_grad, up_tiles, TURNED)
    for slot in slots:
        here = slice(slot * tile, (slot + 1) * tile)
        input_sum[:, columns(0, slot)] += from_gate[:, here]
        input_sum[:, columns(1, slot)] += from_up[:, here]
        tile_out[slot] = dot(x_turned[columns(0, slot), :], gate_grad, PLAIN) * grad_scale
        tile_out[slot_count + slot] = dot(x_turned[columns(1, slot), :], up_grad, PLAIN) * grad_scale
        tile_out[2 * slot_count + slot] = down_terms[:, here] * grad_scale
    spare = grad_refs[0].shape[1] - 1
    places = []
    for matrix in range(3):
        first, count = table[1 + matrix, block] - chunk * chunk_rows, table[4 + matrix, block]
        places += [jnp.where(slot < count, first + slot, spare) for slot in slots]
    for ref, part in zip(grad_refs, weight_parts):
        share = ref.shape[2]
        for at in range(part[2]):
            offset = offset_of(table, part, at, near, share)
            for index, place in enumerate(places):
                ref[at, place] = tile_out[index, pl.ds(offset, share), :].astype(BF16)

    @pl.when(step == pl.num_programs(0) - 1)
    def _():
        if chunk < chunks - 1:
            carry[...] = input_sum[...]
        else:
            store_parts(input_sum, input_own, input_other, token_count, own_parts)


def call(kernel, table, args, in_specs, out_specs, out_shape, grid=1, scratch=(), cost=0):
    return pl.pallas_call(
        kernel,
        grid_spec=pltpu.PrefetchScalarGridSpec(
            num_scalar_prefetch=1,
            grid=(grid,),
            in_specs=in_specs,
            out_specs=out_specs,
            scratch_shapes=scratch,
        ),
        out_shape=out_shape,
        compiler_params=PARAMS,
        cost_estimate=pl.CostEstimate(flops=0, bytes_accessed=cost, transcendentals=0),
    )(table, *args)


def shards(tokens, out_grad, weight_tiles, tile_counts, tile_rows):
    row_share, _, blocks_dev, slot_count, tile = weight_tiles.shape
    own_rows, features = tokens.shape
    dp_size, tensor_size = lax.axis_size("dp"), lax.axis_size("tensor")
    far = math.gcd(4, math.gcd(dp_size, blocks_dev))
    near = dp_size // far
    blocks = blocks_dev // far
    chunks = math.gcd(2, blocks)
    chunk_blocks = blocks // chunks
    groups = far * chunks
    terms = 3 * slot_count
    grad_scale = 1.0 / math.sqrt(own_rows * tensor_size * dp_size)
    me = lax.axis_index("dp")
    far_at, near_at = me // near, me % near
    far_strides, near_strides = strides_of(far, near), strides_of(near)
    tensor_strides = strides_of(tensor_size)
    shape = jax.ShapeDtypeStruct

    both = jnp.concatenate([tokens, out_grad], axis=0)
    early = {0: both}
    if far > 1:
        early[near] = swap(both, "dp", near)

    capacity = (terms * blocks_dev - 3 * blocks_dev + 3 * (slot_count - 1) * (groups - 1)) // groups
    chunk_rows = capacity + 1
    block_ids = jnp.arange(blocks_dev, dtype=jnp.int32)
    load = tile_counts[0] + tile_counts[1] + tile_counts[2]
    earlier = (load[:, None] > load[None, :]) | (
        (load[:, None] == load[None, :]) & (block_ids[:, None] < block_ids[None, :])
    )
    rank = jnp.sum(earlier.astype(jnp.int32), axis=0)
    group = rank % groups
    before = (group[:, None] == group[None, :]) & (rank[:, None] < rank[None, :])
    start = jnp.sum(jnp.where(before, load[:, None], 0), axis=0) + (group // far) * chunk_rows
    ranks_of = (
        jnp.arange(chunk_blocks, dtype=jnp.int32)[None, None, :] * groups
        + jnp.arange(chunks, dtype=jnp.int32)[None, :, None] * far
        + (jnp.arange(far, dtype=jnp.int32)[:, None, None] ^ far_at)
    ).reshape(blocks_dev)
    columns = jnp.concatenate(
        [
            block_ids[None, :],
            start[None, :],
            (start + tile_counts[0])[None, :],
            (start + tile_counts[0] + tile_counts[1])[None, :],
            tile_counts,
            jnp.transpose(tile_rows, (0, 2, 1)).reshape(terms, blocks_dev),
        ]
    )
    table = jnp.sum(
        jnp.where(ranks_of[None, :, None] == rank[None, None, :], columns[:, None, :], 0), axis=2
    )
    place = jnp.where(block_ids == 0, far_at, near_at).astype(jnp.int32)
    table = jnp.concatenate([table, place[None, :]])

    tile_list = jnp.transpose(weight_tiles, (2, 1, 3, 0, 4)).reshape(
        blocks_dev * terms, row_share, tile
    )
    packed_shape = (chunks * chunk_rows, row_share, tile)
    chunk_shape = (chunk_rows, row_share, tile)
    packed = call(
        functools.partial(pack, blocks=blocks, slot_count=slot_count),
        table,
        [tile_list],
        [whole(tile_list.shape)],
        [whole(packed_shape)] * far,
        [shape(packed_shape, BF16)] * far,
        cost=100_000_000,
    )
    received = [swap(packed[at], "dp", at * near) for at in reversed(range(1, far))][::-1]
    held = jnp.stack([packed[0], *received])

    half = far // 2
    split = near == 4 and far % 2 == 0
    if split:
        from_1, from_2 = swap(held, "dp", 1), swap(held, "dp", 2)
        pass_1, pass_2 = from_1[:half], from_2[half:]
        weight_list = [held, from_1, from_2, swap(pass_1, "dp", 2), swap(pass_2, "dp", 1)]
        weight_parts = [(0, 0, far), (1, 0, far), (2, 0, far), (3, 0, half), (3, half, half)]
    else:
        items = gather({0: held}, "dp", near_strides)
        pass_1 = pass_2 = held
        weight_list = [items[at] for at in range(near)]
        weight_parts = [(at, 0, far) for at in range(near)]

    late_x, late_g = {}, {}
    for stride in far_strides[:-1]:
        x_source, g_source = after((tokens, out_grad), held)
        late_x[stride] = swap(x_source, "dp", stride)
        x_back, g_source = after((late_x[stride], g_source), pass_1, pass_2, late_x[stride])
        late_x[stride ^ near] = swap(x_back, "dp", near)
        late_g[stride] = swap(g_source, "dp", stride)
        late_g[stride ^ near] = swap(late_g[stride], "dp", near)

    far_order = [at * near for at in range(0, far, 2)] + [at * near for at in range(1, far, 2)]
    x_list, g_list, x_specs, g_specs, token_parts = [], [], [], [], []
    token_shape = (own_rows, features)
    for at in far_order:
        if at in early:
            for other, part in gather({0: early[at]}, "tensor", tensor_strides).items():
                token_parts.append((at, other))
                x_list.append(part)
                g_list.append(part)
                x_specs.append(whole(token_shape))
                g_specs.append(whole(token_shape, (1, 0)))
        else:
            x_parts = gather({0: late_x[at]}, "tensor", tensor_strides)
            g_parts = gather({0: late_g[at]}, "tensor", tensor_strides)
            for other in x_parts:
                token_parts.append((at, other))
                x_list.append(x_parts[other])
                g_list.append(g_parts[other])
                x_specs.append(whole(token_shape))
                g_specs.append(whole(token_shape))

    token_count = len(token_parts)
    group_rows = token_count * own_rows
    own_parts = tuple(at for at, (_, other) in enumerate(token_parts) if other == 0)
    other_parts = [part for part in token_parts if part[1] != 0]
    own_shape = (len(own_parts), own_rows, features)
    other_shape = (len(other_parts), own_rows, features)

    if far == 4:
        weight_list = list(after(tuple(weight_list), *late_x.values()))
    whole_tiles = call(
        functools.partial(assemble, weight_parts=weight_parts, slot_count=slot_count, near=near),
        table,
        weight_list,
        [whole((length,) + packed_shape) for _, _, length in weight_parts],
        by_block((terms, tile, tile)),
        shape((blocks, terms, tile, tile), BF16),
        grid=blocks,
        scratch=[pltpu.VMEM((terms, tile, tile), F32)],
        cost=20_000_000,
    )
    if far == 4:
        x_list = list(after(tuple(x_list), late_g[far_strides[0]]))
    x_turned, gate_slope, gate_act, hidden_turned, ffn_own, ffn_other = call(
        functools.partial(
            ahead, token_count=token_count, slot_count=slot_count, own_parts=own_parts
        ),
        table,
        [*x_list, whole_tiles],
        x_specs + [by_block((terms, tile, tile))],
        [
            whole((features, group_rows)),
            by_block((group_rows, tile)),
            by_block((group_rows, tile)),
            by_block((tile, group_rows)),
            whole(own_shape),
            whole(other_shape),
        ],
        [
            shape((features, group_rows), BF16),
            shape((blocks, group_rows, tile), F32),
            shape((blocks, group_rows, tile), F32),
            shape((blocks, tile, group_rows), BF16),
            shape(own_shape, BF16),
            shape(other_shape, BF16),
        ],
        grid=blocks,
        scratch=[pltpu.VMEM((group_rows, features), F32)],
        cost=40_000_000,
    )

    def to_near(own_sums, other_sums):
        from_core = swap(other_sums, "tensor", 1)
        return from_core, add(own_sums[half:], from_core[half:])

    def to_far(own_sums, from_core, got):
        return add(own_sums[1], from_core[1], got[1])

    def generic(own_sums, other_sums):
        sums = {}
        for index, at in enumerate(far_order):
            items = {0: own_sums[index]}
            for other_index, (far_part, other) in enumerate(other_parts):
                if far_part == at:
                    items[other] = other_sums[other_index]
            sums[at] = scatter(items, "tensor", tensor_strides)[0]
        return scatter(sums, "dp", far_strides)[0]

    staged = tensor_size == 2 and far == 4 and split and chunks == 2
    if staged:
        ffn_core, ffn_near = to_near(ffn_own, ffn_other)

    def gradients(chunk, carried):
        def block_at(block_shape):
            return pl.BlockSpec(
                (1,) + block_shape,
                lambda block, *_: (block + chunk * chunk_blocks,) + (0,) * len(block_shape),
            )

        last = chunk == chunks - 1
        sum_shape = (group_rows, features)
        return call(
            functools.partial(
                behind,
                token_count=token_count,
                weight_parts=weight_parts,
                slot_count=slot_count,
                grad_scale=grad_scale,
                own_parts=own_parts,
                near=near,
                chunk=chunk,
                chunks=chunks,
                chunk_rows=chunk_rows,
            ),
            table,
            [*g_list, whole_tiles, x_turned, gate_slope, gate_act, hidden_turned, *carried],
            g_specs
            + [
                block_at((terms, tile, tile)),
                whole((features, group_rows)),
                block_at((group_rows, tile)),
                block_at((group_rows, tile)),
                block_at((tile, group_rows)),
            ]
            + [whole(sum_shape)] * len(carried),
            ([whole(own_shape), whole(other_shape)] if last else [whole(sum_shape)])
            + [whole((length,) + chunk_shape) for _, _, length in weight_parts],
            ([shape(own_shape, BF16), shape(other_shape, BF16)] if last else [shape(sum_shape, F32)])
            + [shape((length,) + chunk_shape, BF16) for _, _, length in weight_parts],
            grid=chunk_blocks,
            scratch=[
                pltpu.VMEM((group_rows, features), F32),
                pltpu.VMEM((terms, tile, tile), F32),
            ],
            cost=40_000_000,
        )

    def halves(parts):
        return swap(parts[3], "dp", 1), swap(parts[4], "dp", 2)

    def folded(parts, got_1, got_2):
        to_2 = jnp.concatenate([add(parts[2][:half], got_1), parts[2][half:]])
        to_1 = jnp.concatenate([parts[1][:half], add(parts[1][half:], got_2)])
        return to_1, to_2

    def summed(parts, to_1, to_2):
        from_1, from_2 = swap(to_1, "dp", 1), swap(to_2, "dp", 2)
        return [add(parts[0][at], from_1[at], from_2[at]) for at in range(far)]

    def sent_back(sums):
        return [sums[0]] + [swap(sums[at], "dp", at * near) for at in range(1, far)]

    if staged:
        carry, *first_parts = gradients(0, [])
        first_got = halves(first_parts)
        carry = after(carry, ffn_near)
        input_own, input_other, *second_parts = gradients(1, [carry])
        ffn_got = swap(ffn_near, "dp", near)
        first_folded = folded(first_parts, *first_got)
        second_got = halves(second_parts)
        ffn_last = to_far(ffn_own, ffn_core, ffn_got)
        input_core, input_near = to_near(input_own, input_other)
        ffn_far = swap(ffn_last, "dp", 2 * near)
        input_got = swap(input_near, "dp", near)
        first_sums = summed(first_parts, *first_folded)
        second_folded = after(folded(second_parts, *second_got), input_near, ffn_last)
        first_sums = after(first_sums, *second_folded)
        first_back = sent_back(first_sums)
        input_last = to_far(input_own, input_core, input_got)
        second_sums = after(summed(second_parts, *second_folded), input_last)
        input_far = swap(input_last, "dp", 2 * near)
        back = first_back + sent_back(second_sums)
        ffn_rows = add(ffn_own[0], ffn_core[0], ffn_got[0], ffn_far)
        input_rows = add(input_own[0], input_core[0], input_got[0], input_far)
    else:
        carried, back = [], []
        for chunk in range(chunks):
            outs = gradients(chunk, carried)
            carried, parts = outs[:-len(weight_parts)], outs[-len(weight_parts):]
            if split:
                sums = summed(parts, *folded(parts, *halves(parts)))
            else:
                sums = scatter(dict(enumerate(parts)), "dp", near_strides)[0]
            back += sent_back(sums)
        ffn_rows = generic(ffn_own, ffn_other)
        input_rows = generic(*carried)

    grads = call(
        functools.partial(
            unpack, chunks=chunks, chunk_rows=chunk_rows, blocks=blocks, slot_count=slot_count
        ),
        table,
        back,
        [whole(chunk_shape)] * len(back),
        whole(tile_list.shape),
        shape(tile_list.shape, BF16),
        cost=2_000_000,
    )
    tile_grad = grads.reshape(blocks_dev, 3, slot_count, row_share, tile).transpose(3, 1, 0, 2, 4)
    return ffn_rows, input_rows, tile_grad


def solution(mesh):
    return jax.shard_map(
        shards,
        mesh=mesh,
        in_specs=(
            P(("dp", "tensor"), None),
            P(("dp", "tensor"), None),
            P("dp", None, "tensor", None, None),
            P(None, "tensor"),
            P(None, "tensor", None),
        ),
        out_specs=(
            P(("dp", "tensor"), None),
            P(("dp", "tensor"), None),
            P("dp", None, "tensor", None, None),
        ),
        check_vma=False,
    )
```

time: 473 us -> 211 us (0.45)
  waiting for transfers between devices: 328 us -> 86.2 us
  Pallas kernels: 0 us -> 59.7 us
  matrix products: 53.5 us -> 0 us
  local copies, waits for them, and re-layouts: 56.4 us -> 13.2 us
  starting transfers between devices: 0.34 us -> 40.6 us
  between operations: 14.4 us -> 1.19 us
    reduce_scatter x3 -> x0, waiting for transfers between devices: 175 us -> none  [the longest x1 156 us: shards(): lax.psum_scatter((tile_terms * (live_mask * grad_scale)[None, :, :, None]...]
    all_gather x1 -> x0, waiting for transfers between devices: 153 us -> none  [shards(): weights = lax.all_gather(picked, 'dp', axis=0, tiled=True)]
    ppermute x0 -> x38, waiting for transfers between devices: none -> 86.2 us  [swap(): return lax.ppermute(value, axis, [(at, at ^ stride) for at in range(size)])]
    pallas_call x0 -> x6, Pallas kernels: none -> 59.7 us  [call(): pl.pallas_call(kernel, grid_spec=pltpu.PrefetchScalarGridSpec(num_scalar_...]
    dot_general x16 -> x0, matrix products: 53.5 us -> none  [the longest x1 5.11 us: shards(): jnp.einsum('tsa,sj->tja', dh_slots, col_onehot[2], precision=highest)]
    ppermute x0 -> x38, starting transfers between devices: none -> 40.6 us  [swap(): return lax.ppermute(value, axis, [(at, at ^ stride) for at in range(size)])]
    gather x16 -> x0, local copies, waits for them, and re-layouts: 31.1 us -> none  [the longest x3 5.3 us: shards(): row_ids = jnp.take_along_axis(rows_all, keep_order, axis=1)]
    convert_element_type x5 -> x0, local copies, waits for them, and re-layouts: 17.7 us -> none  [the longest x1 15 us: shards(): (tile_terms * (live_mask * grad_scale)[None, :, :, None]).astype(jnp.bflo...]
  transfers between devices with their start and end apart: 4 -> 38, of which waited for: 4 -> 17; matrix products, arithmetic and copies ran while one was open for 11% -> 5% of each run, Pallas kernels for 0% -> 26%
where the time goes in v3:
time: 211 us; the launch traced here: 210 us
  waiting for transfers between devices  86.2 us (41%)
  Pallas kernels  59.7 us (28%)
  starting transfers between devices  40.6 us (19%)
  local copies, waits for them, and re-layouts  13.2 us (6%)
  other arithmetic  9.01 us (4%)
    ppermute x38, waiting for transfers between devices, swap(): return lax.ppermute(value, axis, [(at, at ^ stride) for at in range(size)])  86.2 us
    pallas_call x6, Pallas kernels, call(): pl.pallas_call(kernel, grid_spec=pltpu.PrefetchScalarGridSpec(num_scalar_...  59.7 us
    ppermute x38, starting transfers between devices, swap(): return lax.ppermute(value, axis, [(at, at ^ stride) for at in range(size)])  40.6 us
    convert_element_type x12, other arithmetic, add(): return total.astype(BF16)  4.85 us
  transfers between devices with their start and end apart: 38, of which 17 were waited for; matrix products, arithmetic and copies ran while one was open for 5% of the time, Pallas kernels for 26%

profile of v3, /device:TPU:0, one launch (start us, length us, event | category | flops | bytes accessed | tf_op | source)
XLA Modules:
  0.0 210.0 jit_solution(14087175128937153719)
XLA Ops:
  3.5 2.3 %copy.10 = bf16[56,3,3,8,128]{4,3,2,1,0:T(8,128)(2,1)} copy(bf16[56,3,3,8,128]{4,0,2,1,3:T(8,128)(2,1)} %bitcast.51) | data formatting | bytes 2064384 | tf_op jit(solution)/shard_map/transpose | solution.py:327
  7.0 4.3 %shard_map.76 = (bf16[96,8,128]{2,1,0:T(8,128)(2,1)}, bf16[96,8,128]{2,1,0:T(8,128)(2,1)}, bf16[96,8,128]{2,1,0:T(8,128)(2,1)}, bf16[96,8,128]{2,1,0:T(8,128)(2,1)}) custom-call(s32[17,56]{1,0:T(8,128)} %pad_add_fusion.table, bf16[504,8,128]{2,1,0:T(8,128)(2,1)} %bitcast.50), custom_call_target="tpu_custom_call" | custom-call | bytes 100000000 | tf_op jit(solution)/shard_map/pallas_call | solution.py:257
  11.3 3.0 %collective-permute-start.1 = (bf16[96,8,128]{2,1,0:T(8,128)(2,1)}, bf16[96,8,128]{2,1,0:T(8,128)(2,1)S(1)}, u32[]{:S(2)}, u32[]{:S(2)}) collective-permute-start(bf16[96,8,128]{2,1,0:T(8,128)(2,1)} %get-tuple-element.55), channel_id=1, source_target_pairs={{0,8},{2,10},{4,12},{6,14},{8,0},{10,2},{12,4},{14,6},{16,24},{18,... | collective-permute-start | bytes 589832 | tf_op jit(solution)/shard_map/ppermute | solution.py:21
  14.3 2.6 %collective-permute-start.2 = (bf16[96,8,128]{2,1,0:T(8,128)(2,1)}, bf16[96,8,128]{2,1,0:T(8,128)(2,1)S(1)}, u32[]{:S(2)}, u32[]{:S(2)}) collective-permute-start(bf16[96,8,128]{2,1,0:T(8,128)(2,1)} %get-tuple-element.56), channel_id=1, source_target_pairs={{0,16},{2,18},{4,20},{6,22},{8,24},{10,26},{12,28},{14,30},{16,0},... | collective-permute-start | bytes 589832 | tf_op jit(solution)/shard_map/ppermute | solution.py:21
  16.9 5.9 %collective-permute-done.1 = bf16[96,8,128]{2,1,0:T(8,128)(2,1)S(1)} collective-permute-done((bf16[96,8,128]{2,1,0:T(8,128)(2,1)}, bf16[96,8,128]{2,1,0:T(8,128)(2,1)S(1)}, u32[]{:S(2)}, u32[]{:S(2)}) %collective-permute-start.1) | collective-permute-done | bytes 196640 | tf_op jit(solution)/shard_map/ppermute | solution.py:21
  22.8 8.8 %collective-permute-done.2 = bf16[96,8,128]{2,1,0:T(8,128)(2,1)S(1)} collective-permute-done((bf16[96,8,128]{2,1,0:T(8,128)(2,1)}, bf16[96,8,128]{2,1,0:T(8,128)(2,1)S(1)}, u32[]{:S(2)}, u32[]{:S(2)}) %collective-permute-start.2) | collective-permute-done | bytes 196640 | tf_op jit(solution)/shard_map/ppermute | solution.py:21
  32.7 1.6 collective-permute-start.9
  34.3 1.5 collective-permute-start.8
  35.8 3.4 %collective-permute-start.6 = (bf16[64,4096]{1,0:T(8,128)(2,1)S(1)}, bf16[64,4096]{1,0:T(8,128)(2,1)S(1)}, u32[]{:S(2)}, u32[]{:S(2)}) collective-permute-start(bf16[64,4096]{1,0:T(8,128)(2,1)S(1)} %constant_dynamic-update-slice_fusion.refs_0_), channel_id=1, source_target_pairs={{0,8},{2,10},{4,12},{6,14},{8,0},{10,2},{12,4},{14,6},{16,24},{18,... | collective-permute-start | bytes 1572872 | tf_op jit(solution)/shard_map/ppermute | solution.py:21
  40.3 9.3 %collective-permute-done.9.refs_2_ = bf16[4,96,8,128]{3,2,1,0:T(8,128)(2,1)S(1)} collective-permute-done((bf16[4,96,8,128]{3,2,1,0:T(8,128)(2,1)S(1)}, bf16[4,96,8,128]{3,2,1,0:T(8,128)(2,1)S(1)}, u32[]{:S(2)}, u32[]{:S(2)}) %collective-permute-start.9) | collective-permute-done | bytes 786464 | tf_op jit(solution)/shard_map/ppermute | solution.py:21
  50.9 3.5 %collective-permute-done.4.refs_2_ = bf16[32,4096]{1,0:T(8,128)(2,1)S(1)} collective-permute-done((bf16[32,4096]{1,0:T(8,128)(2,1)S(1)}, bf16[32,4096]{1,0:T(8,128)(2,1)S(1)}, u32[]{:S(2)}, u32[]{:S(2)}) %collective-permute-start.4) | collective-permute-done | bytes 262176 | tf_op jit(solution)/shard_map/ppermute | solution.py:21
  54.3 4.0 %collective-permute-start.10 = (bf16[32,4096]{1,0:T(8,128)(2,1)S(1)}, bf16[32,4096]{1,0:T(8,128)(2,1)S(1)}, u32[]{:S(2)}, u32[]{:S(2)}) collective-permute-start(bf16[32,4096]{1,0:T(8,128)(2,1)S(1)} %collective-permute-done.4.refs_2_), channel_id=1, source_target_pairs={{0,8},{2,10},{4,12},{6,14},{8,0},{10,2},{12,4},{14,6},{16,24},{18,... | collective-permute-start | bytes 786440 | tf_op jit(solution)/shard_map/ppermute | solution.py:21
  59.0 5.9 %collective-permute-done.10.refs_6_ = bf16[32,4096]{1,0:T(8,128)(2,1)S(1)} collective-permute-done((bf16[32,4096]{1,0:T(8,128)(2,1)S(1)}, bf16[32,4096]{1,0:T(8,128)(2,1)S(1)}, u32[]{:S(2)}, u32[]{:S(2)}) %collective-permute-start.10) | collective-permute-done | bytes 262176 | tf_op jit(solution)/shard_map/ppermute | solution.py:21
  65.4 8.0 %collective-permute-done.12.refs_2_ = bf16[32,4096]{1,0:T(8,128)(2,1)S(1)} collective-permute-done((bf16[32,4096]{1,0:T(8,128)(2,1)S(1)}, bf16[32,4096]{1,0:T(8,128)(2,1)S(1)}, u32[]{:S(2)}, u32[]{:S(2)}) %collective-permute-start.12) | collective-permute-done | bytes 262176 | tf_op jit(solution)/shard_map/ppermute | solution.py:21
  75.3 8.8 %shard_map.77.refs_8_ = bf16[14,9,128,128]{3,2,1,0:T(8,128)(2,1)} custom-call(s32[17,56]{1,0:T(8,128)} %pad_add_fusion.table, bf16[4,96,8,128]{3,2,1,0:T(8,128)(2,1)} %copy-done.4, bf16[4,96,8,128]{3,2,1,0:T(8,128)(2,1)} %copy-done.6, bf16[4,96,8,128]{3,2,1,0:T(8,128)(2,1)} %copy-done.5, bf16[2,96,8,128]{3,2,1,0:T(8,128)(2,1)} %copy-done.19, ...), custom_call_target="tpu_custom_call" | custom-call | bytes 20000000 | tf_op jit(solution)/shard_map/pallas_call | solution.py:257
  85.8 16.2 %shard_map.78 = (bf16[4096,256]{1,0:T(8,128)(2,1)}, f32[14,256,128]{2,1,0:T(8,128)}, f32[14,256,128]{2,1,0:T(8,128)}, bf16[14,128,256]{2,1,0:T(8,128)(2,1)}, bf1...) custom-call(s32[17,56]{1,0:T(8,128)} %pad_add_fusion.table, bf16[64,4096]{1,0:T(8,128)(2,1)} %copy-done, ...), custom_call_target="tpu_custom_call" | custom-call | bytes 40000000 | tf_op jit(solution)/shard_map/pallas_call | solution.py:257
  102.7 2.2 %collective-permute-done.18.refs_3_ = bf16[32,4096]{1,0:T(8,128)(2,1)S(1)} collective-permute-done((bf16[32,4096]{1,0:T(8,128)(2,1)S(1)}, bf16[32,4096]{1,0:T(8,128)(2,1)S(1)}, u32[]{:S(2)}, u32[]{:S(2)}) %collective-permute-start.18) | collective-permute-done | bytes 262176 | tf_op jit(solution)/shard_map/ppermute | solution.py:21
  106.2 12.5 %shard_map.79 = (f32[256,4096]{1,0:T(8,128)}, bf16[4,48,8,128]{3,2,1,0:T(8,128)(2,1)}, bf16[4,48,8,128]{3,2,1,0:T(8,128)(2,1)}, bf16[4,48,8,128]{3,2,1,0:T(8,128...) custom-call(s32[17,56]{1,0:T(8,128)} %pad_add_fusion.table, bf16[64,4096]{1,0:T(8,128)(2,1)} %copy-done, ...), custom_call_target="tpu_custom_call" | custom-call | bytes 40000000 | tf_op jit(solution)/shard_map/pallas_call | solution.py:257
  122.6 3.4 %collective-permute-done.26 = bf16[2,48,8,128]{3,2,1,0:T(8,128)(2,1)S(1)} collective-permute-done((bf16[2,48,8,128]{3,2,1,0:T(8,128)(2,1)}, bf16[2,48,8,128]{3,2,1,0:T(8,128)(2,1)S(1)}, u32[]{:S(2)}, u32[]{:S(2)}) %collective-permute-start.26) | collective-permute-done | bytes 196640 | tf_op jit(solution)/shard_map/ppermute | solution.py:21
  127.7 13.1 %shard_map.80 = (bf16[4,32,4096]{2,1,0:T(8,128)(2,1)}, bf16[4,32,4096]{2,1,0:T(8,128)(2,1)}, bf16[4,48,8,128]{3,2,1,0:T(8,128)(2,1)}, bf16[4,48,8,128]{3,2,1,0:T...) custom-call(s32[17,56]{1,0:T(8,128)} %pad_add_fusion.table, ...), custom_call_target="tpu_custom_call" | custom-call | bytes 40000000 | tf_op jit(solution)/shard_map/pallas_call | solution.py:257
  140.8 1.6 collective-permute-start.28
  142.6 1.4 collective-permute-start.25
  147.7 8.9 %collective-permute-done.29 = bf16[2,48,8,128]{3,2,1,0:T(8,128)(2,1)S(1)} collective-permute-done((bf16[2,48,8,128]{3,2,1,0:T(8,128)(2,1)S(1)}, bf16[2,48,8,128]{3,2,1,0:T(8,128)(2,1)S(1)}, u32[]{:S(2)}, u32[]{:S(2)}) %collective-permute-start.29) | collective-permute-done | bytes 196640 | tf_op jit(solution)/shard_map/ppermute | solution.py:21
  162.8 3.1 %collective-permute-done.33 = bf16[4,48,8,128]{3,2,1,0:T(8,128)(2,1)S(1)} collective-permute-done((bf16[4,48,8,128]{3,2,1,0:T(8,128)(2,1)S(1)}, bf16[4,48,8,128]{3,2,1,0:T(8,128)(2,1)S(1)}, u32[]{:S(2)}, u32[]{:S(2)}) %collective-permute-start.33) | collective-permute-done | bytes 393248 | tf_op jit(solution)/shard_map/ppermute | solution.py:21
  166.9 2.6 %collective-permute-start.32 = (bf16[48,8,128]{2,1,0:T(8,128)(2,1)S(1)}, bf16[48,8,128]{2,1,0:T(8,128)(2,1)S(1)}, u32[]{:S(2)}, u32[]{:S(2)}) collective-permute-start(bf16[48,8,128]{2,1,0:T(8,128)(2,1)S(1)} %get-tuple-element.99), channel_id=1, source_target_pairs={{0,24},{2,26},{4,28},{6,30},{8,16},{10,18},{12,20},{14,22},{16,8},... | collective-permute-start | bytes 294920 | tf_op jit(solution)/shard_map/ppermute | solution.py:21
  170.3 10.7 %collective-permute-done.22 = bf16[2,32,4096]{2,1,0:T(8,128)(2,1)S(1)} collective-permute-done((bf16[2,32,4096]{2,1,0:T(8,128)(2,1)S(1)}, bf16[2,32,4096]{2,1,0:T(8,128)(2,1)S(1)}, u32[]{:S(2)}, u32[]{:S(2)}) %collective-permute-start.22) | collective-permute-done | bytes 524320 | tf_op jit(solution)/shard_map/ppermute | solution.py:21
  182.4 1.9 collective-permute-start.36
  184.3 1.5 collective-permute-start.37
  186.6 4.1 %collective-permute-done.35.refs_5_ = bf16[48,8,128]{2,1,0:T(8,128)(2,1)S(1)} collective-permute-done((bf16[48,8,128]{2,1,0:T(8,128)(2,1)S(1)}, bf16[48,8,128]{2,1,0:T(8,128)(2,1)S(1)}, u32[]{:S(2)}, u32[]{:S(2)}) %collective-permute-start.35) | collective-permute-done | bytes 98336 | tf_op jit(solution)/shard_map/ppermute | solution.py:21
  190.7 10.2 %collective-permute-done.36.refs_6_ = bf16[48,8,128]{2,1,0:T(8,128)(2,1)S(1)} collective-permute-done((bf16[48,8,128]{2,1,0:T(8,128)(2,1)S(1)}, bf16[48,8,128]{2,1,0:T(8,128)(2,1)S(1)}, u32[]{:S(2)}, u32[]{:S(2)}) %collective-permute-start.36) | collective-permute-done | bytes 98336 | tf_op jit(solution)/shard_map/ppermute | solution.py:21
  202.1 4.7 %shard_map.81 = bf16[504,8,128]{2,1,0:T(8,128)(2,1)} custom-call(s32[17,56]{1,0:T(8,128)} %pad_add_fusion.table, bf16[48,8,128]{2,1,0:T(8,128)(2,1)} %get-tuple-element.96.refs_0_, bf16[48,8,128]{2,1,0:T(8,128)(2,1)} %copy-done.26, bf16[48,8,128]{2,1,0:T(8,128)(2,1)} %copy-done.27, bf16[48,8,128]{2,1,0:T(8,128)(2,1)} %copy-done.28, ...), custom_call_target="tpu_custom_call" | custom-call | bytes 2000000 | tf_op jit(solution)/shard_map/pallas_call | solution.py:257
  206.9 2.3 %copy.13 = bf16[56,3,3,8,128]{4,0,2,1,3:T(8,128)(2,1)} copy(bf16[56,3,3,8,128]{4,3,2,1,0:T(8,128)(2,1)} %bitcast.49) | data formatting | bytes 2064384 | tf_op jit(solution)/shard_map/reshape | solution.py:564
  (165 shorter events, 35.3 us)
Async XLA Ops:
  11.3 11.6 %collective-permute-start.1 = (bf16[96,8,128]{2,1,0:T(8,128)(2,1)}, bf16[96,8,128]{2,1,0:T(8,128)(2,1)S(1)}, u32[]{:S(2)}, u32[]{:S(2)}) collective-permute-start(bf16[96,8,128]{2,1,0:T(8,128)(2,1)} %get-tuple-element.55), channel_id=1, source_target_pairs={{0,8},{2,10},{4,12},{6,14},{8,0},{10,2},{12,4},{14,6},{16,24},{18,... | collective-permute-start | bytes 589832 | tf_op jit(solution)/shard_map/ppermute | solution.py:21
  14.3 17.4 %collective-permute-start.2 = (bf16[96,8,128]{2,1,0:T(8,128)(2,1)}, bf16[96,8,128]{2,1,0:T(8,128)(2,1)S(1)}, u32[]{:S(2)}, u32[]{:S(2)}) collective-permute-start(bf16[96,8,128]{2,1,0:T(8,128)(2,1)} %get-tuple-element.56), channel_id=1, source_target_pairs={{0,16},{2,18},{4,20},{6,22},{8,24},{10,26},{12,28},{14,30},{16,0},... | collective-permute-start | bytes 589832 | tf_op jit(solution)/shard_map/ppermute | solution.py:21
  16.9 14.8 %collective-permute-start.3 = (bf16[96,8,128]{2,1,0:T(8,128)(2,1)}, bf16[96,8,128]{2,1,0:T(8,128)(2,1)S(1)}, u32[]{:S(2)}, u32[]{:S(2)}) collective-permute-start(bf16[96,8,128]{2,1,0:T(8,128)(2,1)} %get-tuple-element.57), channel_id=1, source_target_pairs={{0,24},{2,26},{4,28},{6,30},{8,16},{10,18},{12,20},{14,22},{16,8},... | collective-permute-start | bytes 589832 | tf_op jit(solution)/shard_map/ppermute | solution.py:21
  32.7 16.9 %collective-permute-start.9 = (bf16[4,96,8,128]{3,2,1,0:T(8,128)(2,1)S(1)}, bf16[4,96,8,128]{3,2,1,0:T(8,128)(2,1)S(1)}, u32[]{:S(2)}, u32[]{:S(2)}) collective-permute-start(bf16[4,96,8,128]{3,2,1,0:T(8,128)(2,1)S(1)} %pad_maximum_fusion.refs_0_), channel_id=1, source_target_pairs={{0,4},{2,6},{4,0},{6,2},{8,12},{10,14},{12,8},{14,10},{16,20},{18,... | collective-permute-start | bytes 2359304 | tf_op jit(solution)/shard_map/ppermute | solution.py:21
  34.3 16.5 %collective-permute-start.8 = (bf16[4,96,8,128]{3,2,1,0:T(8,128)(2,1)S(1)}, bf16[4,96,8,128]{3,2,1,0:T(8,128)(2,1)S(1)}, u32[]{:S(2)}, u32[]{:S(2)}) collective-permute-start(bf16[4,96,8,128]{3,2,1,0:T(8,128)(2,1)S(1)} %pad_maximum_fusion.refs_0_), channel_id=1, source_target_pairs={{0,2},{2,0},{4,6},{6,4},{8,10},{10,8},{12,14},{14,12},{16,18},{18,... | collective-permute-start | bytes 2359304 | tf_op jit(solution)/shard_map/ppermute | solution.py:21
  35.8 22.6 %collective-permute-start.6 = (bf16[64,4096]{1,0:T(8,128)(2,1)S(1)}, bf16[64,4096]{1,0:T(8,128)(2,1)S(1)}, u32[]{:S(2)}, u32[]{:S(2)}) collective-permute-start(bf16[64,4096]{1,0:T(8,128)(2,1)S(1)} %constant_dynamic-update-slice_fusion.refs_0_), channel_id=1, source_target_pairs={{0,8},{2,10},{4,12},{6,14},{8,0},{10,2},{12,4},{14,6},{16,24},{18,... | collective-permute-start | bytes 1572872 | tf_op jit(solution)/shard_map/ppermute | solution.py:21
  39.2 15.1 %collective-permute-start.4 = (bf16[32,4096]{1,0:T(8,128)(2,1)S(1)}, bf16[32,4096]{1,0:T(8,128)(2,1)S(1)}, u32[]{:S(2)}, u32[]{:S(2)}) collective-permute-start(bf16[32,4096]{1,0:T(8,128)(2,1)S(1)} %copy-done.24), channel_id=1, source_target_pairs={{0,16},{2,18},{4,20},{6,22},{8,24},{10,26},{12,28},{14,30},{16,0},... | collective-permute-start | bytes 786440 | tf_op jit(solution)/shard_map/ppermute | solution.py:21
  54.3 10.6 %collective-permute-start.10 = (bf16[32,4096]{1,0:T(8,128)(2,1)S(1)}, bf16[32,4096]{1,0:T(8,128)(2,1)S(1)}, u32[]{:S(2)}, u32[]{:S(2)}) collective-permute-start(bf16[32,4096]{1,0:T(8,128)(2,1)S(1)} %collective-permute-done.4.refs_2_), channel_id=1, source_target_pairs={{0,8},{2,10},{4,12},{6,14},{8,0},{10,2},{12,4},{14,6},{16,24},{18,... | collective-permute-start | bytes 786440 | tf_op jit(solution)/shard_map/ppermute | solution.py:21
  58.4 15.1 %collective-permute-start.14 = (bf16[2,96,8,128]{3,2,1,0:T(8,128)(2,1)S(1)}, bf16[2,96,8,128]{3,2,1,0:T(8,128)(2,1)S(1)}, u32[]{:S(2)}, u32[]{:S(2)}) collective-permute-start(bf16[2,96,8,128]{3,2,1,0:T(8,128)(2,1)S(1)} %slice.216), channel_id=1, source_target_pairs={{0,2},{2,0},{4,6},{6,4},{8,10},{10,8},{12,14},{14,12},{16,18},{18,... | collective-permute-start | bytes 1179656 | tf_op jit(solution)/shard_map/ppermute | solution.py:21
  58.4 25.6 %collective-permute-start = (bf16[64,4096]{1,0:T(8,128)(2,1)S(1)}, bf16[64,4096]{1,0:T(8,128)(2,1)S(1)}, u32[]{:S(2)}, u32[]{:S(2)}) collective-permute-start(bf16[64,4096]{1,0:T(8,128)(2,1)S(1)} %constant_dynamic-update-slice_fusion.refs_0_), channel_id=1, source_target_pairs={{0,1},{1,0},{2,3},{3,2},{4,5},{5,4},{6,7},{7,6},{8,9},{9,8},{10,11... | collective-permute-start | bytes 1572872 | tf_op jit(solution)/shard_map/ppermute | solution.py:21
  58.4 15.0 %collective-permute-start.12 = (bf16[32,4096]{1,0:T(8,128)(2,1)S(1)}, bf16[32,4096]{1,0:T(8,128)(2,1)S(1)}, u32[]{:S(2)}, u32[]{:S(2)}) collective-permute-start(bf16[32,4096]{1,0:T(8,128)(2,1)S(1)} %copy-done.25), channel_id=1, source_target_pairs={{0,16},{2,18},{4,20},{6,22},{8,24},{10,26},{12,28},{14,30},{16,0},... | collective-permute-start | bytes 786440 | tf_op jit(solution)/shard_map/ppermute | solution.py:21
  58.5 25.6 %collective-permute-start.7 = (bf16[64,4096]{1,0:T(8,128)(2,1)S(1)}, bf16[64,4096]{1,0:T(8,128)(2,1)S(1)}, u32[]{:S(2)}, u32[]{:S(2)}) collective-permute-start(bf16[64,4096]{1,0:T(8,128)(2,1)S(1)} %collective-permute-done.6.refs_4_), channel_id=1, source_target_pairs={{0,1},{1,0},{2,3},{3,2},{4,5},{5,4},{6,7},{7,6},{8,9},{9,8},{10,11... | collective-permute-start | bytes 1572872 | tf_op jit(solution)/shard_map/ppermute | solution.py:21
  65.0 9.0 %collective-permute-start.13 = (bf16[2,96,8,128]{3,2,1,0:T(8,128)(2,1)S(1)}, bf16[2,96,8,128]{3,2,1,0:T(8,128)(2,1)S(1)}, u32[]{:S(2)}, u32[]{:S(2)}) collective-permute-start(bf16[2,96,8,128]{3,2,1,0:T(8,128)(2,1)S(1)} %slice.215), channel_id=1, source_target_pairs={{0,4},{2,6},{4,0},{6,2},{8,12},{10,14},{12,8},{14,10},{16,20},{18,... | collective-permute-start | bytes 1179656 | tf_op jit(solution)/shard_map/ppermute | solution.py:21
  73.4 10.7 %collective-permute-start.5 = (bf16[32,4096]{1,0:T(8,128)(2,1)S(1)}, bf16[32,4096]{1,0:T(8,128)(2,1)S(1)}, u32[]{:S(2)}, u32[]{:S(2)}) collective-permute-start(bf16[32,4096]{1,0:T(8,128)(2,1)S(1)} %collective-permute-done.4.refs_2_), channel_id=1, source_target_pairs={{0,1},{1,0},{2,3},{3,2},{4,5},{5,4},{6,7},{7,6},{8,9},{9,8},{10,11... | collective-permute-start | bytes 786440 | tf_op jit(solution)/shard_map/ppermute | solution.py:21
  73.4 10.7 %collective-permute-start.11 = (bf16[32,4096]{1,0:T(8,128)(2,1)S(1)}, bf16[32,4096]{1,0:T(8,128)(2,1)S(1)}, u32[]{:S(2)}, u32[]{:S(2)}) collective-permute-start(bf16[32,4096]{1,0:T(8,128)(2,1)S(1)} %collective-permute-done.10.refs_6_), channel_id=1, source_target_pairs={{0,1},{1,0},{2,3},{3,2},{4,5},{5,4},{6,7},{7,6},{8,9},{9,8},{10,11... | collective-permute-start | bytes 786440 | tf_op jit(solution)/shard_map/ppermute | solution.py:21
  73.9 28.7 %collective-permute-start.19 = (bf16[32,4096]{1,0:T(8,128)(2,1)S(1)}, bf16[32,4096]{1,0:T(8,128)(2,1)S(1)}, u32[]{:S(2)}, u32[]{:S(2)}) collective-permute-start(bf16[32,4096]{1,0:T(8,128)(2,1)S(1)} %collective-permute-done.12.refs_2_), channel_id=1, source_target_pairs={{0,8},{2,10},{4,12},{6,14},{8,0},{10,2},{12,4},{14,6},{16,24},{18,... | collective-permute-start | bytes 786440 | tf_op jit(solution)/shard_map/ppermute | solution.py:21
  102.1 25.5 %collective-permute-start.15 = (bf16[4,32,4096]{2,1,0:T(8,128)(2,1)}, bf16[4,32,4096]{2,1,0:T(8,128)(2,1)S(1)}, u32[]{:S(2)}, u32[]{:S(2)}) collective-permute-start(bf16[4,32,4096]{2,1,0:T(8,128)(2,1)} %get-tuple-element.76), channel_id=1, source_target_pairs={{0,1},{1,0},{2,3},{3,2},{4,5},{5,4},{6,7},{7,6},{8,9},{9,8},{10,11... | collective-permute-start | bytes 3145736 | tf_op jit(solution)/shard_map/ppermute | solution.py:21
  122.1 20.4 %collective-permute-start.24 = (bf16[2,48,8,128]{3,2,1,0:T(8,128)(2,1)}, bf16[2,48,8,128]{3,2,1,0:T(8,128)(2,1)S(1)}, u32[]{:S(2)}, u32[]{:S(2)}) collective-permute-start(bf16[2,48,8,128]{3,2,1,0:T(8,128)(2,1)} %get-tuple-element.87), channel_id=1, source_target_pairs={{0,4},{2,6},{4,0},{6,2},{8,12},{10,14},{12,8},{14,10},{16,20},{18,... | collective-permute-start | bytes 589832 | tf_op jit(solution)/shard_map/ppermute | solution.py:21
  127.0 33.2 %collective-permute-start.27 = (bf16[4,48,8,128]{3,2,1,0:T(8,128)(2,1)S(1)}, bf16[4,48,8,128]{3,2,1,0:T(8,128)(2,1)S(1)}, u32[]{:S(2)}, u32[]{:S(2)}) collective-permute-start(bf16[4,48,8,128]{3,2,1,0:T(8,128)(2,1)S(1)} %pad_maximum_fusion.2), channel_id=1, source_target_pairs={{0,4},{2,6},{4,0},{6,2},{8,12},{10,14},{12,8},{14,10},{16,20},{18,... | collective-permute-start | bytes 1179656 | tf_op jit(solution)/shard_map/ppermute | solution.py:21
  142.6 17.7 %collective-permute-start.25 = (bf16[4,48,8,128]{3,2,1,0:T(8,128)(2,1)S(1)}, bf16[4,48,8,128]{3,2,1,0:T(8,128)(2,1)S(1)}, u32[]{:S(2)}, u32[]{:S(2)}) collective-permute-start(bf16[4,48,8,128]{3,2,1,0:T(8,128)(2,1)S(1)} %pad_maximum_fusion.1), channel_id=1, source_target_pairs={{0,2},{2,0},{4,6},{6,4},{8,10},{10,8},{12,14},{14,12},{16,18},{18,... | collective-permute-start | bytes 1179656 | tf_op jit(solution)/shard_map/ppermute | solution.py:21
  144.0 12.8 %collective-permute-start.16 = (bf16[2,32,4096]{2,1,0:T(8,128)(2,1)S(1)}, bf16[2,32,4096]{2,1,0:T(8,128)(2,1)S(1)}, u32[]{:S(2)}, u32[]{:S(2)}) collective-permute-start(bf16[2,32,4096]{2,1,0:T(8,128)(2,1)S(1)} %add_convert_fusion.1), channel_id=1, source_target_pairs={{0,8},{2,10},{4,12},{6,14},{8,0},{10,2},{12,4},{14,6},{16,24},{18,... | collective-permute-start | bytes 1572872 | tf_op jit(solution)/shard_map/ppermute | solution.py:21
  147.3 9.3 %collective-permute-start.29 = (bf16[2,48,8,128]{3,2,1,0:T(8,128)(2,1)S(1)}, bf16[2,48,8,128]{3,2,1,0:T(8,128)(2,1)S(1)}, u32[]{:S(2)}, u32[]{:S(2)}) collective-permute-start(bf16[2,48,8,128]{3,2,1,0:T(8,128)(2,1)S(1)} %copy-done.34), channel_id=1, source_target_pairs={{0,2},{2,0},{4,6},{6,4},{8,10},{10,8},{12,14},{14,12},{16,18},{18,... | collective-permute-start | bytes 589832 | tf_op jit(solution)/shard_map/ppermute | solution.py:21
  147.6 9.3 %collective-permute-start.21 = (bf16[4,32,4096]{2,1,0:T(8,128)(2,1)S(1)}, bf16[4,32,4096]{2,1,0:T(8,128)(2,1)S(1)}, u32[]{:S(2)}, u32[]{:S(2)}) collective-permute-start(bf16[4,32,4096]{2,1,0:T(8,128)(2,1)S(1)} %copy-done.33), channel_id=1, source_target_pairs={{0,1},{1,0},{2,3},{3,2},{4,5},{5,4},{6,7},{7,6},{8,9},{9,8},{10,11... | collective-permute-start | bytes 3145736 | tf_op jit(solution)/shard_map/ppermute | solution.py:21
  158.9 22.2 %collective-permute-start.22 = (bf16[2,32,4096]{2,1,0:T(8,128)(2,1)S(1)}, bf16[2,32,4096]{2,1,0:T(8,128)(2,1)S(1)}, u32[]{:S(2)}, u32[]{:S(2)}) collective-permute-start(bf16[2,32,4096]{2,1,0:T(8,128)(2,1)S(1)} %add_convert_fusion), channel_id=1, source_target_pairs={{0,8},{2,10},{4,12},{6,14},{8,0},{10,2},{12,4},{14,6},{16,24},{18,... | collective-permute-start | bytes 1572872 | tf_op jit(solution)/shard_map/ppermute | solution.py:21
  161.1 20.2 %collective-permute-start.17 = (bf16[32,4096]{1,0:T(8,128)(2,1)S(1)}, bf16[32,4096]{1,0:T(8,128)(2,1)S(1)}, u32[]{:S(2)}, u32[]{:S(2)}) collective-permute-start(bf16[32,4096]{1,0:T(8,128)(2,1)S(1)} %fusion.2), channel_id=1, source_target_pairs={{0,16},{2,18},{4,20},{6,22},{8,24},{10,26},{12,28},{14,30},{16,0},... | collective-permute-start | bytes 786440 | tf_op jit(solution)/shard_map/ppermute | solution.py:21
  161.5 20.9 %collective-permute-start.30 = (bf16[48,8,128]{2,1,0:T(8,128)(2,1)S(1)}, bf16[48,8,128]{2,1,0:T(8,128)(2,1)S(1)}, u32[]{:S(2)}, u32[]{:S(2)}) collective-permute-start(bf16[48,8,128]{2,1,0:T(8,128)(2,1)S(1)} %get-tuple-element.97), channel_id=1, source_target_pairs={{0,8},{2,10},{4,12},{6,14},{8,0},{10,2},{12,4},{14,6},{16,24},{18,... | collective-permute-start | bytes 294920 | tf_op jit(solution)/shard_map/ppermute | solution.py:21
  165.9 18.3 %collective-permute-start.31 = (bf16[48,8,128]{2,1,0:T(8,128)(2,1)S(1)}, bf16[48,8,128]{2,1,0:T(8,128)(2,1)S(1)}, u32[]{:S(2)}, u32[]{:S(2)}) collective-permute-start(bf16[48,8,128]{2,1,0:T(8,128)(2,1)S(1)} %get-tuple-element.98), channel_id=1, source_target_pairs={{0,16},{2,18},{4,20},{6,22},{8,24},{10,26},{12,28},{14,30},{16,0},... | collective-permute-start | bytes 294920 | tf_op jit(solution)/shard_map/ppermute | solution.py:21
  166.9 19.6 %collective-permute-start.32 = (bf16[48,8,128]{2,1,0:T(8,128)(2,1)S(1)}, bf16[48,8,128]{2,1,0:T(8,128)(2,1)S(1)}, u32[]{:S(2)}, u32[]{:S(2)}) collective-permute-start(bf16[48,8,128]{2,1,0:T(8,128)(2,1)S(1)} %get-tuple-element.99), channel_id=1, source_target_pairs={{0,24},{2,26},{4,28},{6,30},{8,16},{10,18},{12,20},{14,22},{16,8},... | collective-permute-start | bytes 294920 | tf_op jit(solution)/shard_map/ppermute | solution.py:21
  181.2 28.0 %collective-permute-start.23 = (bf16[32,4096]{1,0:T(8,128)(2,1)S(1)}, bf16[32,4096]{1,0:T(8,128)(2,1)S(1)}, u32[]{:S(2)}, u32[]{:S(2)}) collective-permute-start(bf16[32,4096]{1,0:T(8,128)(2,1)S(1)} %fusion.3), channel_id=1, source_target_pairs={{0,16},{2,18},{4,20},{6,22},{8,24},{10,26},{12,28},{14,30},{16,0},... | collective-permute-start | bytes 786440 | tf_op jit(solution)/shard_map/ppermute | solution.py:21
  181.3 9.4 %collective-permute-start.35 = (bf16[48,8,128]{2,1,0:T(8,128)(2,1)S(1)}, bf16[48,8,128]{2,1,0:T(8,128)(2,1)S(1)}, u32[]{:S(2)}, u32[]{:S(2)}) collective-permute-start(bf16[48,8,128]{2,1,0:T(8,128)(2,1)S(1)} %get-tuple-element.102), channel_id=1, source_target_pairs={{0,8},{2,10},{4,12},{6,14},{8,0},{10,2},{12,4},{14,6},{16,24},{18,... | collective-permute-start | bytes 294920 | tf_op jit(solution)/shard_map/ppermute | solution.py:21
  182.4 18.5 %collective-permute-start.36 = (bf16[48,8,128]{2,1,0:T(8,128)(2,1)S(1)}, bf16[48,8,128]{2,1,0:T(8,128)(2,1)S(1)}, u32[]{:S(2)}, u32[]{:S(2)}) collective-permute-start(bf16[48,8,128]{2,1,0:T(8,128)(2,1)S(1)} %get-tuple-element.103), channel_id=1, source_target_pairs={{0,16},{2,18},{4,20},{6,22},{8,24},{10,26},{12,28},{14,30},{16,0},... | collective-permute-start | bytes 294920 | tf_op jit(solution)/shard_map/ppermute | solution.py:21
  184.3 16.6 %collective-permute-start.37 = (bf16[48,8,128]{2,1,0:T(8,128)(2,1)S(1)}, bf16[48,8,128]{2,1,0:T(8,128)(2,1)S(1)}, u32[]{:S(2)}, u32[]{:S(2)}) collective-permute-start(bf16[48,8,128]{2,1,0:T(8,128)(2,1)S(1)} %get-tuple-element.104), channel_id=1, source_target_pairs={{0,24},{2,26},{4,28},{6,30},{8,16},{10,18},{12,20},{14,22},{16,8},... | collective-permute-start | bytes 294920 | tf_op jit(solution)/shard_map/ppermute | solution.py:21
  (41 other events, 490.8 us)

commit v4 on v3

v4 whole, which is shorter than its diff:
```python
import functools
import math

import jax
import jax.numpy as jnp
from jax import lax
from jax.experimental import pallas as pl
from jax.experimental.pallas import tpu as pltpu
from jax.sharding import PartitionSpec as P

F32 = jnp.float32
BF16 = jnp.bfloat16
PLAIN = (((1,), (0,)), ((), ()))
TURNED = (((1,), (1,)), ((), ()))
PARAMS = pltpu.CompilerParams(vmem_limit_bytes=56 * 1024 * 1024)
dot = functools.partial(lax.dot_general, preferred_element_type=F32)


def swap(value, axis, stride):
    size = lax.axis_size(axis)
    return lax.ppermute(value, axis, [(at, at ^ stride) for at in range(size)])


def after(value, *others):
    return lax.optimization_barrier((value, *others))[0]


def add(first, *others):
    total = first.astype(F32)
    for other in others:
        total = total + other.astype(F32)
    return total.astype(BF16)


def strides_of(size, unit=1):
    found = []
    step = size // 2
    while step >= 1:
        found.append(step * unit)
        step //= 2
    return found


def gather(items, axis, strides):
    for stride in strides:
        items = {**items, **{at ^ stride: swap(one, axis, stride) for at, one in items.items()}}
    return items


def scatter(items, axis, strides):
    for stride in reversed(strides):
        kept = {}
        for at, one in items.items():
            if not at & stride:
                kept[at] = add(one, swap(items[at ^ stride], axis, stride))
        items = kept
    return items


def whole(shape, at=None):
    at = (0,) * len(shape) if at is None else at
    return pl.BlockSpec(shape, lambda *_: at)


def by_block(shape):
    return pl.BlockSpec((1,) + shape, lambda block, *_: (block,) + (0,) * len(shape))


def pack(table, tiles, *refs, blocks, slot_count):
    outs, lines = refs[:-1], refs[-1]
    spare = outs[0].shape[0] - 1
    share, terms, blocks_dev, _ = tiles.shape
    for row in range(share):
        for term in range(terms):
            at = (row * terms + term) * blocks_dev
            lines[at : at + blocks_dev, :] = tiles[row, term].astype(F32)
    for at, out in enumerate(outs):

        def one(place, _, at=at, out=out):
            column = at * blocks + place
            block = table[0, column]
            for matrix in range(3):
                first, count = table[1 + matrix, column], table[4 + matrix, column]
                for slot in range(slot_count):
                    to = jnp.where(slot < count, first + slot, spare)
                    source = (matrix * slot_count + slot) * blocks_dev + block
                    out[to] = lines[pl.ds(source, share, stride=terms * blocks_dev), :].astype(BF16)
            return _

        lax.fori_loop(0, blocks, one, 0)


def unpack(table, *refs, chunks, chunk_rows, blocks, slot_count):
    out, sources = refs[-1], refs[:-1]
    far = len(sources) // chunks
    chunk_blocks = blocks // chunks
    for chunk in range(chunks):
        for at in range(far):
            ref = sources[chunk * far + at]

            def one(place, _, at=at, ref=ref, chunk=chunk):
                column = at * blocks + chunk * chunk_blocks + place
                block = table[0, column]
                for matrix in range(3):
                    first = table[1 + matrix, column] - chunk * chunk_rows
                    count = table[4 + matrix, column]
                    for slot in range(slot_count):
                        live = slot < count
                        value = ref[jnp.where(live, first + slot, 0)].astype(F32)
                        out[(block * 3 + matrix) * slot_count + slot] = jnp.where(
                            live, value, 0.0
                        ).astype(BF16)
                return _

            lax.fori_loop(0, chunk_blocks, one, 0)


def offset_of(table, part, at, near, share):
    far_part = (part[1] + at) ^ table[16, 0]
    near_part = part[0] ^ table[16, 1]
    return pl.multiple_of((far_part * near + near_part) * share, share)


def assemble(table, *refs, weight_parts, near):
    weight_refs, out, tiles = refs[: len(weight_parts)], refs[-2], refs[-1]
    for ref, part in zip(weight_refs, weight_parts):
        share = ref.shape[2]
        for at in range(part[2]):
            offset = offset_of(table, part, at, near, share)
            tiles[:, pl.ds(offset, share), :] = ref[at].astype(F32)
    out[...] = tiles[...].astype(BF16)

    @pl.when(pl.program_id(0) == pl.num_programs(0) - 1)
    def _():
        out[out.shape[0] - 1] = jnp.zeros(out.shape[1:], BF16)


def places_of(table, block, slot_count, spare, base=0):
    places = []
    for matrix in range(3):
        first, count = table[1 + matrix, block] - base, table[4 + matrix, block]
        places += [jnp.where(slot < count, first + slot, spare) for slot in range(slot_count)]
    return places


def store_parts(total, own, other, token_count, own_parts):
    own_rows = own.shape[1]
    own_at, other_at = 0, 0
    for at in range(token_count):
        value = total[at * own_rows : (at + 1) * own_rows, :].astype(BF16)
        if at in own_parts:
            own[own_at] = value
            own_at += 1
        else:
            other[other_at] = value
            other_at += 1


def tokens_at(refs, columns):
    return jnp.concatenate([ref[:, columns] for ref in refs], axis=0)


def columns_of(table, block, index, tile):
    return pl.ds(pl.multiple_of(table[7 + index, block] * tile, tile), tile)


def ahead(table, *refs, token_count, slot_count, own_parts):
    token_refs, refs = refs[:token_count], refs[token_count:]
    tiles, x_turned, gate_slope, gate_act_out, hidden_turned, ffn_own, ffn_other, ffn_sum = refs
    block = pl.program_id(0)
    tile = tiles.shape[1]
    gate, up, down = (range(at * slot_count, (at + 1) * slot_count) for at in range(3))
    places = places_of(table, block, slot_count, tiles.shape[0] - 1)

    @pl.when(block == 0)
    def _():
        for at in range(x_turned.shape[0] // tile):
            here = slice(at * tile, (at + 1) * tile)
            x_turned[here, :] = tokens_at(token_refs, here).T
        ffn_sum[...] = jnp.zeros_like(ffn_sum)

    def tokens_of(indices):
        return jnp.concatenate(
            [tokens_at(token_refs, columns_of(table, block, index, tile)) for index in indices], axis=1
        )

    gate_tiles = jnp.concatenate([tiles[places[index]] for index in gate], axis=0)
    up_tiles = jnp.concatenate([tiles[places[index]] for index in up], axis=0)
    down_tiles = jnp.concatenate([tiles[places[index]] for index in down], axis=1)
    gate_pre = dot(tokens_of(gate), gate_tiles, PLAIN)
    up_pre = dot(tokens_of(up), up_tiles, PLAIN)
    gate_sig = jax.nn.sigmoid(gate_pre)
    gate_act = gate_pre * gate_sig
    hidden = (gate_act * up_pre).astype(BF16)
    gate_slope[0] = up_pre * gate_sig * (1.0 + gate_pre * (1.0 - gate_sig))
    gate_act_out[0] = gate_act
    hidden_turned[0] = hidden.T
    ffn = dot(hidden, down_tiles, PLAIN)
    for at, index in enumerate(down):
        ffn_sum[:, columns_of(table, block, index, tile)] += ffn[:, at * tile : (at + 1) * tile]

    @pl.when(block == pl.num_programs(0) - 1)
    def _():
        store_parts(ffn_sum, ffn_own, ffn_other, token_count, own_parts)


def behind(
    table, *refs, token_count, weight_parts, slot_count, grad_scale, near, chunk, chunk_rows
):
    token_refs, refs = refs[:token_count], refs[token_count:]
    tiles, x_turned, gate_slope, gate_act, hidden_turned, gate_out, up_out = refs[:7]
    grad_refs, sums = refs[7:-1], refs[-1]
    step = pl.program_id(0)
    block = step + chunk * pl.num_programs(0)
    tile = tiles.shape[1]
    gate, up, down = (range(at * slot_count, (at + 1) * slot_count) for at in range(3))
    places = places_of(table, block, slot_count, tiles.shape[0] - 1)
    down_tiles = jnp.concatenate([tiles[places[index]] for index in down], axis=1)
    grad_in = jnp.concatenate(
        [tokens_at(token_refs, columns_of(table, block, index, tile)) for index in down], axis=1
    )
    hidden_grad = dot(grad_in, down_tiles, TURNED)
    gate_grad = (hidden_grad * gate_slope[0]).astype(BF16)
    up_grad = (hidden_grad * gate_act[0]).astype(BF16)
    gate_out[0] = gate_grad
    up_out[0] = up_grad
    to = places_of(table, block, slot_count, sums.shape[0] - 1, chunk * chunk_rows)
    down_terms = dot(hidden_turned[0], grad_in, PLAIN) * grad_scale
    for at, index in enumerate(down):
        sums[to[index]] = down_terms[:, at * tile : (at + 1) * tile]
    for indices, grad in ((gate, gate_grad), (up, up_grad)):
        turned = jnp.concatenate(
            [x_turned[columns_of(table, block, index, tile), :] for index in indices], axis=0
        )
        tile_terms = dot(turned, grad, PLAIN) * grad_scale
        for at, index in enumerate(indices):
            sums[to[index]] = tile_terms[at * tile : (at + 1) * tile]

    @pl.when(step == pl.num_programs(0) - 1)
    def _():
        for ref, part in zip(grad_refs, weight_parts):
            share = ref.shape[2]
            for at in range(part[2]):
                offset = offset_of(table, part, at, near, share)
                ref[at] = sums[:, pl.ds(offset, share), :].astype(BF16)


def inward(table, *refs, chunks, slot_count, token_count, own_parts):
    grads, tiles, input_own, input_other, input_sum = refs[: 2 * chunks], *refs[2 * chunks :]
    step = pl.program_id(0)
    tile = tiles.shape[1]

    @pl.when(step == 0)
    def _():
        input_sum[...] = jnp.zeros_like(input_sum)

    for chunk in range(chunks):
        block = step + chunk * pl.num_programs(0)
        places = places_of(table, block, slot_count, tiles.shape[0] - 1)
        for matrix in range(2):
            indices = range(matrix * slot_count, (matrix + 1) * slot_count)
            whole_tiles = jnp.concatenate([tiles[places[index]] for index in indices], axis=0)
            terms = dot(grads[2 * chunk + matrix][0], whole_tiles, TURNED)
            for at, index in enumerate(indices):
                input_sum[:, columns_of(table, block, index, tile)] += terms[
                    :, at * tile : (at + 1) * tile
                ]

    @pl.when(step == pl.num_programs(0) - 1)
    def _():
        store_parts(input_sum, input_own, input_other, token_count, own_parts)


def call(kernel, table, args, in_specs, out_specs, out_shape, grid=1, scratch=(), cost=0):
    return pl.pallas_call(
        kernel,
        grid_spec=pltpu.PrefetchScalarGridSpec(
            num_scalar_prefetch=1,
            grid=(grid,),
            in_specs=in_specs,
            out_specs=out_specs,
            scratch_shapes=scratch,
        ),
        out_shape=out_shape,
        compiler_params=PARAMS,
        cost_estimate=pl.CostEstimate(flops=0, bytes_accessed=cost, transcendentals=0),
    )(table, *args)


def shards(tokens, out_grad, weight_tiles, tile_counts, tile_rows):
    row_share, _, blocks_dev, slot_count, tile = weight_tiles.shape
    own_rows, features = tokens.shape
    dp_size, tensor_size = lax.axis_size("dp"), lax.axis_size("tensor")
    far = math.gcd(4, math.gcd(dp_size, blocks_dev))
    near = dp_size // far
    blocks = blocks_dev // far
    chunks = math.gcd(2, blocks)
    chunk_blocks = blocks // chunks
    groups = far * chunks
    terms = 3 * slot_count
    grad_scale = 1.0 / math.sqrt(own_rows * tensor_size * dp_size)
    me = lax.axis_index("dp")
    far_at, near_at = me // near, me % near
    far_strides, near_strides = strides_of(far, near), strides_of(near)
    tensor_strides = strides_of(tensor_size)
    shape = jax.ShapeDtypeStruct

    x_items, g_items = {0: tokens}, {0: out_grad}
    if far > 1:
        x_items[near] = swap(tokens, "dp", near)

    capacity = (terms * blocks_dev - 3 * blocks_dev + 3 * (slot_count - 1) * (groups - 1)) // groups
    chunk_rows = capacity + 1
    block_ids = jnp.arange(blocks_dev, dtype=jnp.int32)
    load = tile_counts[0] + tile_counts[1] + tile_counts[2]
    earlier = (load[:, None] > load[None, :]) | (
        (load[:, None] == load[None, :]) & (block_ids[:, None] < block_ids[None, :])
    )
    rank = jnp.sum(earlier.astype(jnp.int32), axis=0)
    group = rank % groups
    before = (group[:, None] == group[None, :]) & (rank[:, None] < rank[None, :])
    start = jnp.sum(jnp.where(before, load[:, None], 0), axis=0) + (group // far) * chunk_rows
    ranks_of = (
        jnp.arange(chunk_blocks, dtype=jnp.int32)[None, None, :] * groups
        + jnp.arange(chunks, dtype=jnp.int32)[None, :, None] * far
        + (jnp.arange(far, dtype=jnp.int32)[:, None, None] ^ far_at)
    ).reshape(blocks_dev)
    columns = jnp.concatenate(
        [
            block_ids[None, :],
            start[None, :],
            (start + tile_counts[0])[None, :],
            (start + tile_counts[0] + tile_counts[1])[None, :],
            tile_counts,
            jnp.transpose(tile_rows, (0, 2, 1)).reshape(terms, blocks_dev),
        ]
    )
    table = jnp.sum(
        jnp.where(ranks_of[None, :, None] == rank[None, None, :], columns[:, None, :], 0), axis=2
    )
    place = jnp.where(block_ids == 0, far_at, near_at).astype(jnp.int32)
    table = jnp.concatenate([table, place[None, :]])

    tile_lines = jnp.transpose(weight_tiles, (0, 1, 3, 2, 4)).reshape(
        row_share, terms, blocks_dev, tile
    )
    slots = chunks * chunk_rows
    packed_shape = (slots, row_share, tile)
    chunk_shape = (chunk_rows, row_share, tile)
    packed = call(
        functools.partial(pack, blocks=blocks, slot_count=slot_count),
        table,
        [tile_lines],
        [whole(tile_lines.shape)],
        [whole(packed_shape)] * far,
        [shape(packed_shape, BF16)] * far,
        scratch=[pltpu.VMEM((row_share * terms * blocks_dev, tile), F32)],
        cost=1_000_000,
    )
    if far > 1:
        packed = after(tuple(packed), x_items[near])
    received = [swap(packed[at], "dp", at * near) for at in reversed(range(1, far))][::-1]
    held = jnp.stack([packed[0], *received])

    half = far // 2
    split = near == 4 and far % 2 == 0
    if split:
        from_1, from_2 = swap(held, "dp", 1), swap(held, "dp", 2)
        pass_1, pass_2 = from_1[:half], from_2[half:]
        weight_list = [held, from_1, from_2, swap(pass_1, "dp", 2), swap(pass_2, "dp", 1)]
        weight_parts = [(0, 0, far), (1, 0, far), (2, 0, far), (3, 0, half), (3, half, half)]
    else:
        items = gather({0: held}, "dp", near_strides)
        pass_1 = pass_2 = held
        weight_list = [items[at] for at in range(near)]
        weight_parts = [(at, 0, far) for at in range(near)]

    if far == 4:
        x_source, g_source = after((tokens, out_grad), held)
        x_items[2 * near] = swap(x_source, "dp", 2 * near)
        g_items[near] = swap(g_source, "dp", near)
        x_back, g_source = after((x_items[2 * near], g_source), pass_1, pass_2, x_items[2 * near])
        x_items[3 * near] = swap(x_back, "dp", near)
        g_items[2 * near] = swap(g_source, "dp", 2 * near)
        g_items[3 * near] = swap(g_items[2 * near], "dp", near)
        weight_list = list(after(tuple(weight_list), x_items[2 * near]))
    elif far == 2:
        g_items[near] = swap(out_grad, "dp", near)

    far_order = [at * near for at in range(0, far, 2)] + [at * near for at in range(1, far, 2)]
    x_list, g_list, token_parts = [], [], []
    token_shape = (own_rows, features)
    for at in far_order:
        x_parts = gather({0: x_items[at]}, "tensor", tensor_strides)
        g_parts = gather({0: g_items[at]}, "tensor", tensor_strides)
        for other in x_parts:
            token_parts.append((at, other))
            x_list.append(x_parts[other])
            g_list.append(g_parts[other])

    token_count = len(token_parts)
    group_rows = token_count * own_rows
    own_parts = tuple(at for at, (_, other) in enumerate(token_parts) if other == 0)
    other_parts = [part for part in token_parts if part[1] != 0]
    own_shape = (len(own_parts), own_rows, features)
    other_shape = (len(other_parts), own_rows, features)

    token_specs = [whole(token_shape)] * token_count
    steps = max(at for at in range(1, 9) if slots % at == 0)
    tiles_shape = (slots, tile, tile)
    tiles = call(
        functools.partial(assemble, weight_parts=weight_parts, near=near),
        table,
        weight_list,
        [
            pl.BlockSpec((length, slots // steps, row_share, tile), lambda step, *_: (0, step, 0, 0))
            for _, _, length in weight_parts
        ],
        pl.BlockSpec((slots // steps, tile, tile), lambda step, *_: (step, 0, 0)),
        shape(tiles_shape, BF16),
        grid=steps,
        scratch=[pltpu.VMEM((slots // steps, tile, tile), F32)],
        cost=10_000_000,
    )
    if far == 4:
        x_list = list(after(tuple(x_list), g_items[2 * near]))
    x_turned, gate_slope, gate_act, hidden_turned, ffn_own, ffn_other = call(
        functools.partial(
            ahead, token_count=token_count, slot_count=slot_count, own_parts=own_parts
        ),
        table,
        [*x_list, tiles],
        token_specs + [whole(tiles_shape)],
        [
            whole((features, group_rows)),
            by_block((group_rows, tile)),
            by_block((group_rows, tile)),
            by_block((tile, group_rows)),
            whole(own_shape),
            whole(other_shape),
        ],
        [
            shape((features, group_rows), BF16),
            shape((blocks, group_rows, tile), F32),
            shape((blocks, group_rows, tile), F32),
            shape((blocks, tile, group_rows), BF16),
            shape(own_shape, BF16),
            shape(other_shape, BF16),
        ],
        grid=blocks,
        scratch=[pltpu.VMEM((group_rows, features), F32)],
        cost=40_000_000,
    )

    def to_near(own_sums, other_sums):
        from_core = swap(other_sums, "tensor", 1)
        return from_core, add(own_sums[half:], from_core[half:])

    def to_far(own_sums, from_core, got):
        return add(own_sums[1], from_core[1], got[1])

    def generic(own_sums, other_sums):
        sums = {}
        for index, at in enumerate(far_order):
            items = {0: own_sums[index]}
            for other_index, (far_part, other) in enumerate(other_parts):
                if far_part == at:
                    items[other] = other_sums[other_index]
            sums[at] = scatter(items, "tensor", tensor_strides)[0]
        return scatter(sums, "dp", far_strides)[0]

    staged = tensor_size == 2 and far == 4 and split and chunks == 2
    if staged:
        ffn_core, ffn_near = to_near(ffn_own, ffn_other)

    def gradients(chunk):
        def block_at(block_shape):
            return pl.BlockSpec(
                (1,) + block_shape,
                lambda block, *_: (block + chunk * chunk_blocks,) + (0,) * len(block_shape),
            )

        outs = call(
            functools.partial(
                behind,
                token_count=token_count,
                weight_parts=weight_parts,
                slot_count=slot_count,
                grad_scale=grad_scale,
                near=near,
                chunk=chunk,
                chunk_rows=chunk_rows,
            ),
            table,
            [*g_list, tiles, x_turned, gate_slope, gate_act, hidden_turned],
            token_specs
            + [
                whole(tiles_shape),
                whole((features, group_rows)),
                block_at((group_rows, tile)),
                block_at((group_rows, tile)),
                block_at((tile, group_rows)),
            ],
            [by_block((group_rows, tile))] * 2
            + [whole((length,) + chunk_shape) for _, _, length in weight_parts],
            [shape((chunk_blocks, group_rows, tile), BF16)] * 2
            + [shape((length,) + chunk_shape, BF16) for _, _, length in weight_parts],
            grid=chunk_blocks,
            scratch=[pltpu.VMEM((chunk_rows, tile, tile), F32)],
            cost=25_000_000,
        )
        return outs[:2], outs[2:]

    def input_gradients(grads):
        return call(
            functools.partial(
                inward,
                chunks=chunks,
                slot_count=slot_count,
                token_count=token_count,
                own_parts=own_parts,
            ),
            table,
            [*grads, tiles],
            [by_block((group_rows, tile))] * len(grads) + [whole(tiles_shape)],
            [whole(own_shape), whole(other_shape)],
            [shape(own_shape, BF16), shape(other_shape, BF16)],
            grid=chunk_blocks,
            scratch=[pltpu.VMEM((group_rows, features), F32)],
            cost=25_000_000,
        )

    def halves(parts):
        return swap(parts[3], "dp", 1), swap(parts[4], "dp", 2)

    def folded(parts, got_1, got_2):
        to_2 = jnp.concatenate([add(parts[2][:half], got_1), parts[2][half:]])
        to_1 = jnp.concatenate([parts[1][:half], add(parts[1][half:], got_2)])
        return to_1, to_2

    def summed(parts, to_1, to_2):
        from_1, from_2 = swap(to_1, "dp", 1), swap(to_2, "dp", 2)
        return [add(parts[0][at], from_1[at], from_2[at]) for at in range(far)]

    def sent_back(sums):
        return [sums[0]] + [swap(sums[at], "dp", at * near) for at in range(1, far)]

    if staged:
        first_grads, first_parts = gradients(0)
        first_got = halves(first_parts)
        hidden_turned = after(hidden_turned, ffn_near, *first_grads)
        second_grads, second_parts = gradients(1)
        ffn_got = swap(ffn_near, "dp", near)
        first_folded = folded(first_parts, *first_got)
        second_got = halves(second_parts)
        second_grads = after(tuple(second_grads), *first_folded)
        input_own, input_other = input_gradients([*first_grads, *second_grads])
        ffn_last = to_far(ffn_own, ffn_core, ffn_got)
        ffn_far = swap(ffn_last, "dp", 2 * near)
        input_core, input_near = to_near(input_own, input_other)
        input_got = swap(input_near, "dp", near)
        first_sums = summed(first_parts, *first_folded)
        second_folded = after(folded(second_parts, *second_got), *second_grads)
        first_back = sent_back(after(first_sums, input_near))
        input_last = to_far(input_own, input_core, input_got)
        second_sums = summed(second_parts, *second_folded)
        input_far = swap(input_last, "dp", 2 * near)
        back = first_back + sent_back(second_sums)
        ffn_rows = add(ffn_own[0], ffn_core[0], ffn_got[0], ffn_far)
        input_rows = add(input_own[0], input_core[0], input_got[0], input_far)
    else:
        grads, back = [], []
        for chunk in range(chunks):
            chunk_grads, parts = gradients(chunk)
            grads += chunk_grads
            if split:
                sums = summed(parts, *folded(parts, *halves(parts)))
            else:
                sums = scatter(dict(enumerate(parts)), "dp", near_strides)[0]
            back += sent_back(sums)
        ffn_rows = generic(ffn_own, ffn_other)
        input_rows = generic(*input_gradients(grads))

    grads = call(
        functools.partial(
            unpack, chunks=chunks, chunk_rows=chunk_rows, blocks=blocks, slot_count=slot_count
        ),
        table,
        back,
        [whole(chunk_shape)] * len(back),
        whole((blocks_dev * terms, row_share, tile)),
        shape((blocks_dev * terms, row_share, tile), BF16),
        cost=2_000_000,
    )
    tile_grad = grads.reshape(blocks_dev, 3, slot_count, row_share, tile).transpose(3, 1, 0, 2, 4)
    return ffn_rows, input_rows, tile_grad


def solution(mesh):
    return jax.shard_map(
        shards,
        mesh=mesh,
        in_specs=(
            P(("dp", "tensor"), None),
            P(("dp", "tensor"), None),
            P("dp", None, "tensor", None, None),
            P(None, "tensor"),
            P(None, "tensor", None),
        ),
        out_specs=(
            P(("dp", "tensor"), None),
            P(("dp", "tensor"), None),
            P("dp", None, "tensor", None, None),
        ),
        check_vma=False,
    )
```

time: 211 us -> 209 us (level)
  waiting for transfers between devices: 86.2 us -> 66.4 us
  starting transfers between devices: 40.6 us -> 59 us
  local copies, waits for them, and re-layouts: 13.2 us -> 8.26 us
  Pallas kernels: 59.7 us -> 63.5 us
    ppermute x38 -> x41, waiting for transfers between devices: 86.2 us -> 66.4 us  [swap(): return lax.ppermute(value, axis, [(at, at ^ stride) for at in range(size)])]
    ppermute x38 -> x41, starting transfers between devices: 40.6 us -> 59 us  [swap(): return lax.ppermute(value, axis, [(at, at ^ stride) for at in range(size)])]
    pallas_call x6 -> x7, Pallas kernels: 59.7 us -> 63.5 us  [call(): pl.pallas_call(kernel, grid_spec=pltpu.PrefetchScalarGridSpec(num_scalar_...]
    transpose x1 -> x0, local copies, waits for them, and re-layouts: 2.31 us -> none  [shards(): jnp.transpose(weight_tiles, (2, 1, 3, 0, 4))]
  transfers between devices with their start and end apart: 38 -> 41, of which waited for: 17 -> 17; matrix products, arithmetic and copies ran while one was open for 5% -> 6% of each run, Pallas kernels for 26% -> 31%
where the time goes in v4:
time: 209 us; the launch traced here: 207 us
  waiting for transfers between devices  66.4 us (32%)
  Pallas kernels  63.5 us (30%)
  starting transfers between devices  59 us (28%)
  other arithmetic  9 us (4%)
  local copies, waits for them, and re-layouts  8.26 us (4%)
    ppermute x41, waiting for transfers between devices, swap(): return lax.ppermute(value, axis, [(at, at ^ stride) for at in range(size)])  66.4 us
    pallas_call x7, Pallas kernels, call(): pl.pallas_call(kernel, grid_spec=pltpu.PrefetchScalarGridSpec(num_scalar_...  63.5 us
    ppermute x41, starting transfers between devices, swap(): return lax.ppermute(value, axis, [(at, at ^ stride) for at in range(size)])  59 us
    convert_element_type x12, other arithmetic, add(): return total.astype(BF16)  4.84 us
  transfers between devices with their start and end apart: 41, of which 17 were waited for; matrix products, arithmetic and copies ran while one was open for 6% of the time, Pallas kernels for 31%

profile of v4, /device:TPU:0, one launch (start us, length us, event | category | flops | bytes accessed | tf_op | source)
XLA Modules:
  0.0 207.3 jit_solution(15381434734071686770)
XLA Ops:
  0.7 3.1 %collective-permute-start.1 = (bf16[32,4096]{1,0:T(8,128)(2,1)}, bf16[32,4096]{1,0:T(8,128)(2,1)S(1)}, u32[]{:S(2)}, u32[]{:S(2)}) collective-permute-start(bf16[32,4096]{1,0:T(8,128)(2,1)} %refs_0_.2), channel_id=1, source_target_pairs={{0,8},{2,10},{4,12},{6,14},{8,0},{10,2},{12,4},{14,6},{16,24},{18,... | collective-permute-start | bytes 786440 | tf_op jit(solution)/shard_map/ppermute | solution.py:21
  8.4 4.4 %shard_map.76 = (bf16[96,8,128]{2,1,0:T(8,128)(2,1)}, bf16[96,8,128]{2,1,0:T(8,128)(2,1)}, bf16[96,8,128]{2,1,0:T(8,128)(2,1)}, bf16[96,8,128]{2,1,0:T(8,128)(2,1)}) custom-call(s32[17,56]{1,0:T(8,128)} %pad_add_fusion.table, bf16[8,9,56,128]{3,2,1,0:T(8,128)(2,1)} %bitcast.51), custom_call_target="tpu_custom_call" | custom-call | bytes 1000000 | tf_op jit(solution)/shard_map/pallas_call | solution.py:275
  12.8 3.0 %collective-permute-start.3 = (bf16[96,8,128]{2,1,0:T(8,128)(2,1)}, bf16[96,8,128]{2,1,0:T(8,128)(2,1)S(1)}, u32[]{:S(2)}, u32[]{:S(2)}) collective-permute-start(bf16[96,8,128]{2,1,0:T(8,128)(2,1)} %get-tuple-element.65), channel_id=1, source_target_pairs={{0,16},{2,18},{4,20},{6,22},{8,24},{10,26},{12,28},{14,30},{16,0},... | collective-permute-start | bytes 589832 | tf_op jit(solution)/shard_map/ppermute | solution.py:21
  17.1 6.2 %collective-permute-done.2 = bf16[96,8,128]{2,1,0:T(8,128)(2,1)S(1)} collective-permute-done((bf16[96,8,128]{2,1,0:T(8,128)(2,1)}, bf16[96,8,128]{2,1,0:T(8,128)(2,1)S(1)}, u32[]{:S(2)}, u32[]{:S(2)}) %collective-permute-start.2) | collective-permute-done | bytes 196640 | tf_op jit(solution)/shard_map/ppermute | solution.py:21
  23.4 6.9 %collective-permute-done.3 = bf16[96,8,128]{2,1,0:T(8,128)(2,1)S(1)} collective-permute-done((bf16[96,8,128]{2,1,0:T(8,128)(2,1)}, bf16[96,8,128]{2,1,0:T(8,128)(2,1)S(1)}, u32[]{:S(2)}, u32[]{:S(2)}) %collective-permute-start.3) | collective-permute-done | bytes 196640 | tf_op jit(solution)/shard_map/ppermute | solution.py:21
  31.3 1.9 collective-permute-start.9
  34.7 5.2 %collective-permute-start.5 = (bf16[32,4096]{1,0:T(8,128)(2,1)S(1)}, bf16[32,4096]{1,0:T(8,128)(2,1)S(1)}, u32[]{:S(2)}, u32[]{:S(2)}) collective-permute-start(bf16[32,4096]{1,0:T(8,128)(2,1)S(1)} %copy-done.20), channel_id=1, source_target_pairs={{0,16},{2,18},{4,20},{6,22},{8,24},{10,26},{12,28},{14,30},{16,0},... | collective-permute-start | bytes 786440 | tf_op jit(solution)/shard_map/ppermute | solution.py:21
  40.4 8.7 %collective-permute-done.9.refs_2_ = bf16[4,96,8,128]{3,2,1,0:T(8,128)(2,1)S(1)} collective-permute-done((bf16[4,96,8,128]{3,2,1,0:T(8,128)(2,1)S(1)}, bf16[4,96,8,128]{3,2,1,0:T(8,128)(2,1)S(1)}, u32[]{:S(2)}, u32[]{:S(2)}) %collective-permute-start.9) | collective-permute-done | bytes 786464 | tf_op jit(solution)/shard_map/ppermute | solution.py:21
  49.0 4.4 %collective-permute-start.20 = (bf16[32,4096]{1,0:T(8,128)(2,1)S(1)}, bf16[32,4096]{1,0:T(8,128)(2,1)S(1)}, u32[]{:S(2)}, u32[]{:S(2)}) collective-permute-start(bf16[32,4096]{1,0:T(8,128)(2,1)S(1)} %copy-done.3), channel_id=1, source_target_pairs={{0,8},{2,10},{4,12},{6,14},{8,0},{10,2},{12,4},{14,6},{16,24},{18,... | collective-permute-start | bytes 786440 | tf_op jit(solution)/shard_map/ppermute | solution.py:21
  53.5 3.2 %collective-permute-start.12 = (bf16[32,4096]{1,0:T(8,128)(2,1)S(1)}, bf16[32,4096]{1,0:T(8,128)(2,1)S(1)}, u32[]{:S(2)}, u32[]{:S(2)}) collective-permute-start(bf16[32,4096]{1,0:T(8,128)(2,1)S(1)} %copy-done.3), channel_id=1, source_target_pairs={{0,16},{2,18},{4,20},{6,22},{8,24},{10,26},{12,28},{14,30},{16,0},... | collective-permute-start | bytes 786440 | tf_op jit(solution)/shard_map/ppermute | solution.py:21
  58.7 1.9 collective-permute-start.10
  60.6 5.1 %collective-permute-done.20.refs_4_ = bf16[32,4096]{1,0:T(8,128)(2,1)S(1)} collective-permute-done((bf16[32,4096]{1,0:T(8,128)(2,1)S(1)}, bf16[32,4096]{1,0:T(8,128)(2,1)S(1)}, u32[]{:S(2)}, u32[]{:S(2)}) %collective-permute-start.20) | collective-permute-done | bytes 262176 | tf_op jit(solution)/shard_map/ppermute | solution.py:21
  65.7 4.2 %collective-permute-start.22 = (bf16[32,4096]{1,0:T(8,128)(2,1)S(1)}, bf16[32,4096]{1,0:T(8,128)(2,1)S(1)}, u32[]{:S(2)}, u32[]{:S(2)}) collective-permute-start(bf16[32,4096]{1,0:T(8,128)(2,1)S(1)} %collective-permute-done.12.refs_2_), channel_id=1, source_target_pairs={{0,8},{2,10},{4,12},{6,14},{8,0},{10,2},{12,4},{14,6},{16,24},{18,... | collective-permute-start | bytes 786440 | tf_op jit(solution)/shard_map/ppermute | solution.py:21
  71.5 3.3 %collective-permute-done.22.refs_6_ = bf16[32,4096]{1,0:T(8,128)(2,1)S(1)} collective-permute-done((bf16[32,4096]{1,0:T(8,128)(2,1)S(1)}, bf16[32,4096]{1,0:T(8,128)(2,1)S(1)}, u32[]{:S(2)}, u32[]{:S(2)}) %collective-permute-start.22) | collective-permute-done | bytes 262176 | tf_op jit(solution)/shard_map/ppermute | solution.py:21
  74.8 7.5 %shard_map.77.refs_8_.refs_4_ = bf16[96,128,128]{2,1,0:T(8,128)(2,1)} custom-call(s32[17,56]{1,0:T(8,128)} %pad_add_fusion.table, bf16[4,96,8,128]{3,2,1,0:T(8,128)(2,1)} %copy-done, bf16[4,96,8,128]{3,2,1,0:T(8,128)(2,1)} %copy-done.2, bf16[4,96,8,128]{3,2,1,0:T(8,128)(2,1)} %copy-done.1, bf16[2,96,8,128]{3,2,1,0:T(8,128)(2,1)} %copy-done.19, ...), custom_call_target="tpu_custom_call" | custom-call | bytes 10000000 | tf_op jit(solution)/shard_map/pallas_call | solution.py:275
  83.1 14.8 %shard_map.78 = (bf16[4096,256]{1,0:T(8,128)(2,1)}, f32[14,256,128]{2,1,0:T(8,128)}, f32[14,256,128]{2,1,0:T(8,128)}, bf16[14,128,256]{2,1,0:T(8,128)(2,1)}, bf1...) custom-call(s32[17,56]{1,0:T(8,128)} %pad_add_fusion.table, bf16[32,4096]{1,0:T(8,128)(2,1)} %refs_0_.2, ...), custom_call_target="tpu_custom_call" | custom-call | bytes 40000000 | tf_op jit(solution)/shard_map/pallas_call | solution.py:275
  99.4 11.1 %shard_map.79 = (bf16[7,256,128]{2,1,0:T(8,128)(2,1)}, bf16[7,256,128]{2,1,0:T(8,128)(2,1)}, bf16[4,48,8,128]{3,2,1,0:T(8,128)(2,1)}, bf16[4,48,8,128]{3,2,1,0:T...) custom-call(s32[17,56]{1,0:T(8,128)} %pad_add_fusion.table, ...), custom_call_target="tpu_custom_call" | custom-call | bytes 25000000 | tf_op jit(solution)/shard_map/pallas_call | solution.py:275
  110.5 1.9 collective-permute-start.25
  115.8 1.8 collective-permute-done.25
  118.7 1.8 collective-permute-start.30
  122.3 11.1 %shard_map.80 = (bf16[7,256,128]{2,1,0:T(8,128)(2,1)}, bf16[7,256,128]{2,1,0:T(8,128)(2,1)}, bf16[4,48,8,128]{3,2,1,0:T(8,128)(2,1)}, bf16[4,48,8,128]{3,2,1,0:T...) custom-call(s32[17,56]{1,0:T(8,128)} %pad_add_fusion.table, ...), custom_call_target="tpu_custom_call" | custom-call | bytes 25000000 | tf_op jit(solution)/shard_map/pallas_call | solution.py:275
  133.4 10.0 %shard_map.81 = (bf16[4,32,4096]{2,1,0:T(8,128)(2,1)}, bf16[4,32,4096]{2,1,0:T(8,128)(2,1)}) custom-call(s32[17,56]{1,0:T(8,128)} %pad_add_fusion.table, bf16[7,256,128]{2,1,0:T(8,128)(2,1)} %get-tuple-element.90.refs_0_, bf16[7,256,128]{2,1,0:T(8,128)(2,1)} %get-tuple-element.91.refs_1_, bf16[7,256,128]{2,1,0:T(8,128)(2,1)} %get-tuple-element.99.refs_2_, ...), custom_call_target="tpu_custom_call" | custom-call | bytes 25000000 | tf_op jit(solution)/shard_map/pallas_call | solution.py:275
  151.0 3.1 %collective-permute-done.35 = bf16[2,48,8,128]{3,2,1,0:T(8,128)(2,1)S(1)} collective-permute-done((bf16[2,48,8,128]{3,2,1,0:T(8,128)(2,1)S(1)}, bf16[2,48,8,128]{3,2,1,0:T(8,128)(2,1)S(1)}, u32[]{:S(2)}, u32[]{:S(2)}) %collective-permute-start.35) | collective-permute-done | bytes 196640 | tf_op jit(solution)/shard_map/ppermute | solution.py:21
  157.1 3.3 %collective-permute-done.16 = bf16[2,32,4096]{2,1,0:T(8,128)(2,1)S(1)} collective-permute-done((bf16[2,32,4096]{2,1,0:T(8,128)(2,1)S(1)}, bf16[2,32,4096]{2,1,0:T(8,128)(2,1)S(1)}, u32[]{:S(2)}, u32[]{:S(2)}) %collective-permute-start.16) | collective-permute-done | bytes 524320 | tf_op jit(solution)/shard_map/ppermute | solution.py:21
  160.5 3.5 %collective-permute-start.17 = (bf16[32,4096]{1,0:T(8,128)(2,1)S(1)}, bf16[32,4096]{1,0:T(8,128)(2,1)S(1)}, u32[]{:S(2)}, u32[]{:S(2)}) collective-permute-start(bf16[32,4096]{1,0:T(8,128)(2,1)S(1)} %fusion.2), channel_id=1, source_target_pairs={{0,16},{2,18},{4,20},{6,22},{8,24},{10,26},{12,28},{14,30},{16,0},... | collective-permute-start | bytes 786440 | tf_op jit(solution)/shard_map/ppermute | solution.py:21
  166.5 3.2 %collective-permute-start.40 = (bf16[48,8,128]{2,1,0:T(8,128)(2,1)S(1)}, bf16[48,8,128]{2,1,0:T(8,128)(2,1)S(1)}, u32[]{:S(2)}, u32[]{:S(2)}) collective-permute-start(bf16[48,8,128]{2,1,0:T(8,128)(2,1)S(1)} %get-tuple-element.118), channel_id=1, source_target_pairs={{0,24},{2,26},{4,28},{6,30},{8,16},{10,18},{12,20},{14,22},{16,8},... | collective-permute-start | bytes 294920 | tf_op jit(solution)/shard_map/ppermute | solution.py:21
  170.8 7.8 %collective-permute-done.27 = bf16[2,32,4096]{2,1,0:T(8,128)(2,1)S(1)} collective-permute-done((bf16[2,32,4096]{2,1,0:T(8,128)(2,1)S(1)}, bf16[2,32,4096]{2,1,0:T(8,128)(2,1)S(1)}, u32[]{:S(2)}, u32[]{:S(2)}) %collective-permute-start.27) | collective-permute-done | bytes 524320 | tf_op jit(solution)/shard_map/ppermute | solution.py:21
  178.7 3.6 %collective-permute-done.40.refs_7_ = bf16[48,8,128]{2,1,0:T(8,128)(2,1)S(1)} collective-permute-done((bf16[48,8,128]{2,1,0:T(8,128)(2,1)S(1)}, bf16[48,8,128]{2,1,0:T(8,128)(2,1)S(1)}, u32[]{:S(2)}, u32[]{:S(2)}) %collective-permute-start.40) | collective-permute-done | bytes 98336 | tf_op jit(solution)/shard_map/ppermute | solution.py:21
  182.4 2.1 %collective-permute-start.32 = (bf16[48,8,128]{2,1,0:T(8,128)(2,1)S(1)}, bf16[48,8,128]{2,1,0:T(8,128)(2,1)S(1)}, u32[]{:S(2)}, u32[]{:S(2)}) collective-permute-start(bf16[48,8,128]{2,1,0:T(8,128)(2,1)S(1)} %get-tuple-element.106), channel_id=1, source_target_pairs={{0,16},{2,18},{4,20},{6,22},{8,24},{10,26},{12,28},{14,30},{16,0},... | collective-permute-start | bytes 294920 | tf_op jit(solution)/shard_map/ppermute | solution.py:21
  187.3 11.5 %collective-permute-done.32.refs_2_ = bf16[48,8,128]{2,1,0:T(8,128)(2,1)S(1)} collective-permute-done((bf16[48,8,128]{2,1,0:T(8,128)(2,1)S(1)}, bf16[48,8,128]{2,1,0:T(8,128)(2,1)S(1)}, u32[]{:S(2)}, u32[]{:S(2)}) %collective-permute-start.32) | collective-permute-done | bytes 98336 | tf_op jit(solution)/shard_map/ppermute | solution.py:21
  199.5 4.7 %shard_map.82 = bf16[504,8,128]{2,1,0:T(8,128)(2,1)} custom-call(s32[17,56]{1,0:T(8,128)} %pad_add_fusion.table, bf16[48,8,128]{2,1,0:T(8,128)(2,1)} %get-tuple-element.104.refs_0_, bf16[48,8,128]{2,1,0:T(8,128)(2,1)} %copy-done.31, bf16[48,8,128]{2,1,0:T(8,128)(2,1)} %copy-done.32, bf16[48,8,128]{2,1,0:T(8,128)(2,1)} %copy-done.33, ...), custom_call_target="tpu_custom_call" | custom-call | bytes 2000000 | tf_op jit(solution)/shard_map/pallas_call | solution.py:275
  204.2 2.3 %copy.11 = bf16[56,3,3,8,128]{4,0,2,1,3:T(8,128)(2,1)} copy(bf16[56,3,3,8,128]{4,3,2,1,0:T(8,128)(2,1)} %bitcast.50) | data formatting | bytes 2064384 | tf_op jit(solution)/shard_map/reshape | solution.py:595
  (171 shorter events, 39.7 us)
Async XLA Ops:
  0.7 12.1 %collective-permute-start.1 = (bf16[32,4096]{1,0:T(8,128)(2,1)}, bf16[32,4096]{1,0:T(8,128)(2,1)S(1)}, u32[]{:S(2)}, u32[]{:S(2)}) collective-permute-start(bf16[32,4096]{1,0:T(8,128)(2,1)} %refs_0_.2), channel_id=1, source_target_pairs={{0,8},{2,10},{4,12},{6,14},{8,0},{10,2},{12,4},{14,6},{16,24},{18,... | collective-permute-start | bytes 786440 | tf_op jit(solution)/shard_map/ppermute | solution.py:21
  12.7 10.6 %collective-permute-start.2 = (bf16[96,8,128]{2,1,0:T(8,128)(2,1)}, bf16[96,8,128]{2,1,0:T(8,128)(2,1)S(1)}, u32[]{:S(2)}, u32[]{:S(2)}) collective-permute-start(bf16[96,8,128]{2,1,0:T(8,128)(2,1)} %get-tuple-element.64), channel_id=1, source_target_pairs={{0,8},{2,10},{4,12},{6,14},{8,0},{10,2},{12,4},{14,6},{16,24},{18,... | collective-permute-start | bytes 589832 | tf_op jit(solution)/shard_map/ppermute | solution.py:21
  12.8 17.4 %collective-permute-start.3 = (bf16[96,8,128]{2,1,0:T(8,128)(2,1)}, bf16[96,8,128]{2,1,0:T(8,128)(2,1)S(1)}, u32[]{:S(2)}, u32[]{:S(2)}) collective-permute-start(bf16[96,8,128]{2,1,0:T(8,128)(2,1)} %get-tuple-element.65), channel_id=1, source_target_pairs={{0,16},{2,18},{4,20},{6,22},{8,24},{10,26},{12,28},{14,30},{16,0},... | collective-permute-start | bytes 589832 | tf_op jit(solution)/shard_map/ppermute | solution.py:21
  15.8 14.4 %collective-permute-start.4 = (bf16[96,8,128]{2,1,0:T(8,128)(2,1)}, bf16[96,8,128]{2,1,0:T(8,128)(2,1)S(1)}, u32[]{:S(2)}, u32[]{:S(2)}) collective-permute-start(bf16[96,8,128]{2,1,0:T(8,128)(2,1)} %get-tuple-element.66), channel_id=1, source_target_pairs={{0,24},{2,26},{4,28},{6,30},{8,16},{10,18},{12,20},{14,22},{16,8},... | collective-permute-start | bytes 589832 | tf_op jit(solution)/shard_map/ppermute | solution.py:21
  31.3 17.7 %collective-permute-start.9 = (bf16[4,96,8,128]{3,2,1,0:T(8,128)(2,1)S(1)}, bf16[4,96,8,128]{3,2,1,0:T(8,128)(2,1)S(1)}, u32[]{:S(2)}, u32[]{:S(2)}) collective-permute-start(bf16[4,96,8,128]{3,2,1,0:T(8,128)(2,1)S(1)} %pad_maximum_fusion.refs_0_), channel_id=1, source_target_pairs={{0,4},{2,6},{4,0},{6,2},{8,12},{10,14},{12,8},{14,10},{16,20},{18,... | collective-permute-start | bytes 2359304 | tf_op jit(solution)/shard_map/ppermute | solution.py:21
  33.2 20.2 %collective-permute-start.8 = (bf16[4,96,8,128]{3,2,1,0:T(8,128)(2,1)S(1)}, bf16[4,96,8,128]{3,2,1,0:T(8,128)(2,1)S(1)}, u32[]{:S(2)}, u32[]{:S(2)}) collective-permute-start(bf16[4,96,8,128]{3,2,1,0:T(8,128)(2,1)S(1)} %pad_maximum_fusion.refs_0_), channel_id=1, source_target_pairs={{0,2},{2,0},{4,6},{6,4},{8,10},{10,8},{12,14},{14,12},{16,18},{18,... | collective-permute-start | bytes 2359304 | tf_op jit(solution)/shard_map/ppermute | solution.py:21
  34.7 18.8 %collective-permute-start.5 = (bf16[32,4096]{1,0:T(8,128)(2,1)S(1)}, bf16[32,4096]{1,0:T(8,128)(2,1)S(1)}, u32[]{:S(2)}, u32[]{:S(2)}) collective-permute-start(bf16[32,4096]{1,0:T(8,128)(2,1)S(1)} %copy-done.20), channel_id=1, source_target_pairs={{0,16},{2,18},{4,20},{6,22},{8,24},{10,26},{12,28},{14,30},{16,0},... | collective-permute-start | bytes 786440 | tf_op jit(solution)/shard_map/ppermute | solution.py:21
  39.9 18.3 %collective-permute-start = (bf16[32,4096]{1,0:T(8,128)(2,1)S(1)}, bf16[32,4096]{1,0:T(8,128)(2,1)S(1)}, u32[]{:S(2)}, u32[]{:S(2)}) collective-permute-start(bf16[32,4096]{1,0:T(8,128)(2,1)S(1)} %copy-done.20), channel_id=1, source_target_pairs={{0,1},{1,0},{2,3},{3,2},{4,5},{5,4},{6,7},{7,6},{8,9},{9,8},{10,11... | collective-permute-start | bytes 786440 | tf_op jit(solution)/shard_map/ppermute | solution.py:21
  39.9 18.8 %collective-permute-start.7 = (bf16[32,4096]{1,0:T(8,128)(2,1)S(1)}, bf16[32,4096]{1,0:T(8,128)(2,1)S(1)}, u32[]{:S(2)}, u32[]{:S(2)}) collective-permute-start(bf16[32,4096]{1,0:T(8,128)(2,1)S(1)} %collective-permute-done.1.refs_4_), channel_id=1, source_target_pairs={{0,1},{1,0},{2,3},{3,2},{4,5},{5,4},{6,7},{7,6},{8,9},{9,8},{10,11... | collective-permute-start | bytes 786440 | tf_op jit(solution)/shard_map/ppermute | solution.py:21
  49.0 16.7 %collective-permute-start.20 = (bf16[32,4096]{1,0:T(8,128)(2,1)S(1)}, bf16[32,4096]{1,0:T(8,128)(2,1)S(1)}, u32[]{:S(2)}, u32[]{:S(2)}) collective-permute-start(bf16[32,4096]{1,0:T(8,128)(2,1)S(1)} %copy-done.3), channel_id=1, source_target_pairs={{0,8},{2,10},{4,12},{6,14},{8,0},{10,2},{12,4},{14,6},{16,24},{18,... | collective-permute-start | bytes 786440 | tf_op jit(solution)/shard_map/ppermute | solution.py:21
  53.5 12.2 %collective-permute-start.12 = (bf16[32,4096]{1,0:T(8,128)(2,1)S(1)}, bf16[32,4096]{1,0:T(8,128)(2,1)S(1)}, u32[]{:S(2)}, u32[]{:S(2)}) collective-permute-start(bf16[32,4096]{1,0:T(8,128)(2,1)S(1)} %copy-done.3), channel_id=1, source_target_pairs={{0,16},{2,18},{4,20},{6,22},{8,24},{10,26},{12,28},{14,30},{16,0},... | collective-permute-start | bytes 786440 | tf_op jit(solution)/shard_map/ppermute | solution.py:21
  56.7 14.2 %collective-permute-start.14 = (bf16[2,96,8,128]{3,2,1,0:T(8,128)(2,1)S(1)}, bf16[2,96,8,128]{3,2,1,0:T(8,128)(2,1)S(1)}, u32[]{:S(2)}, u32[]{:S(2)}) collective-permute-start(bf16[2,96,8,128]{3,2,1,0:T(8,128)(2,1)S(1)} %slice.216), channel_id=1, source_target_pairs={{0,2},{2,0},{4,6},{6,4},{8,10},{10,8},{12,14},{14,12},{16,18},{18,... | collective-permute-start | bytes 1179656 | tf_op jit(solution)/shard_map/ppermute | solution.py:21
  58.2 12.8 %collective-permute-start.13 = (bf16[2,96,8,128]{3,2,1,0:T(8,128)(2,1)S(1)}, bf16[2,96,8,128]{3,2,1,0:T(8,128)(2,1)S(1)}, u32[]{:S(2)}, u32[]{:S(2)}) collective-permute-start(bf16[2,96,8,128]{3,2,1,0:T(8,128)(2,1)S(1)} %slice.215), channel_id=1, source_target_pairs={{0,4},{2,6},{4,0},{6,2},{8,12},{10,14},{12,8},{14,10},{16,20},{18,... | collective-permute-start | bytes 1179656 | tf_op jit(solution)/shard_map/ppermute | solution.py:21
  58.7 11.7 %collective-permute-start.10 = (bf16[32,4096]{1,0:T(8,128)(2,1)S(1)}, bf16[32,4096]{1,0:T(8,128)(2,1)S(1)}, u32[]{:S(2)}, u32[]{:S(2)}) collective-permute-start(bf16[32,4096]{1,0:T(8,128)(2,1)S(1)} %collective-permute-done.5.refs_2_), channel_id=1, source_target_pairs={{0,8},{2,10},{4,12},{6,14},{8,0},{10,2},{12,4},{14,6},{16,24},{18,... | collective-permute-start | bytes 786440 | tf_op jit(solution)/shard_map/ppermute | solution.py:21
  70.4 11.9 %collective-permute-start.11 = (bf16[32,4096]{1,0:T(8,128)(2,1)S(1)}, bf16[32,4096]{1,0:T(8,128)(2,1)S(1)}, u32[]{:S(2)}, u32[]{:S(2)}) collective-permute-start(bf16[32,4096]{1,0:T(8,128)(2,1)S(1)} %collective-permute-done.10.refs_6_), channel_id=1, source_target_pairs={{0,1},{1,0},{2,3},{3,2},{4,5},{5,4},{6,7},{7,6},{8,9},{9,8},{10,11... | collective-permute-start | bytes 786440 | tf_op jit(solution)/shard_map/ppermute | solution.py:21
  70.4 28.0 %collective-permute-start.18 = (bf16[32,4096]{1,0:T(8,128)(2,1)S(1)}, bf16[32,4096]{1,0:T(8,128)(2,1)S(1)}, u32[]{:S(2)}, u32[]{:S(2)}) collective-permute-start(bf16[32,4096]{1,0:T(8,128)(2,1)S(1)} %copy-done.3), channel_id=1, source_target_pairs={{0,1},{1,0},{2,3},{3,2},{4,5},{5,4},{6,7},{7,6},{8,9},{9,8},{10,11... | collective-permute-start | bytes 786440 | tf_op jit(solution)/shard_map/ppermute | solution.py:21
  70.9 27.5 %collective-permute-start.21 = (bf16[32,4096]{1,0:T(8,128)(2,1)S(1)}, bf16[32,4096]{1,0:T(8,128)(2,1)S(1)}, u32[]{:S(2)}, u32[]{:S(2)}) collective-permute-start(bf16[32,4096]{1,0:T(8,128)(2,1)S(1)} %collective-permute-done.20.refs_4_), channel_id=1, source_target_pairs={{0,1},{1,0},{2,3},{3,2},{4,5},{5,4},{6,7},{7,6},{8,9},{9,8},{10,11... | collective-permute-start | bytes 786440 | tf_op jit(solution)/shard_map/ppermute | solution.py:21
  71.0 27.4 %collective-permute-start.19 = (bf16[32,4096]{1,0:T(8,128)(2,1)S(1)}, bf16[32,4096]{1,0:T(8,128)(2,1)S(1)}, u32[]{:S(2)}, u32[]{:S(2)}) collective-permute-start(bf16[32,4096]{1,0:T(8,128)(2,1)S(1)} %collective-permute-done.12.refs_2_), channel_id=1, source_target_pairs={{0,1},{1,0},{2,3},{3,2},{4,5},{5,4},{6,7},{7,6},{8,9},{9,8},{10,11... | collective-permute-start | bytes 786440 | tf_op jit(solution)/shard_map/ppermute | solution.py:21
  74.8 23.7 %collective-permute-start.23 = (bf16[32,4096]{1,0:T(8,128)(2,1)S(1)}, bf16[32,4096]{1,0:T(8,128)(2,1)S(1)}, u32[]{:S(2)}, u32[]{:S(2)}) collective-permute-start(bf16[32,4096]{1,0:T(8,128)(2,1)S(1)} %collective-permute-done.22.refs_6_), channel_id=1, source_target_pairs={{0,1},{1,0},{2,3},{3,2},{4,5},{5,4},{6,7},{7,6},{8,9},{9,8},{10,11... | collective-permute-start | bytes 786440 | tf_op jit(solution)/shard_map/ppermute | solution.py:21
  97.9 24.3 %collective-permute-start.15 = (bf16[4,32,4096]{2,1,0:T(8,128)(2,1)}, bf16[4,32,4096]{2,1,0:T(8,128)(2,1)S(1)}, u32[]{:S(2)}, u32[]{:S(2)}) collective-permute-start(bf16[4,32,4096]{2,1,0:T(8,128)(2,1)} %get-tuple-element.85), channel_id=1, source_target_pairs={{0,1},{1,0},{2,3},{3,2},{4,5},{5,4},{6,7},{7,6},{8,9},{9,8},{10,11... | collective-permute-start | bytes 3145736 | tf_op jit(solution)/shard_map/ppermute | solution.py:21
  118.7 26.1 %collective-permute-start.30 = (bf16[4,48,8,128]{3,2,1,0:T(8,128)(2,1)S(1)}, bf16[4,48,8,128]{3,2,1,0:T(8,128)(2,1)S(1)}, u32[]{:S(2)}, u32[]{:S(2)}) collective-permute-start(bf16[4,48,8,128]{3,2,1,0:T(8,128)(2,1)S(1)} %pad_maximum_fusion.2), channel_id=1, source_target_pairs={{0,4},{2,6},{4,0},{6,2},{8,12},{10,14},{12,8},{14,10},{16,20},{18,... | collective-permute-start | bytes 1179656 | tf_op jit(solution)/shard_map/ppermute | solution.py:21
  121.6 23.3 %collective-permute-start.29 = (bf16[4,48,8,128]{3,2,1,0:T(8,128)(2,1)S(1)}, bf16[4,48,8,128]{3,2,1,0:T(8,128)(2,1)S(1)}, u32[]{:S(2)}, u32[]{:S(2)}) collective-permute-start(bf16[4,48,8,128]{3,2,1,0:T(8,128)(2,1)S(1)} %pad_maximum_fusion.1), channel_id=1, source_target_pairs={{0,2},{2,0},{4,6},{6,4},{8,10},{10,8},{12,14},{14,12},{16,18},{18,... | collective-permute-start | bytes 1179656 | tf_op jit(solution)/shard_map/ppermute | solution.py:21
  143.5 13.1 %collective-permute-start.26 = (bf16[4,32,4096]{2,1,0:T(8,128)(2,1)}, bf16[4,32,4096]{2,1,0:T(8,128)(2,1)S(1)}, u32[]{:S(2)}, u32[]{:S(2)}) collective-permute-start(bf16[4,32,4096]{2,1,0:T(8,128)(2,1)} %get-tuple-element.102), channel_id=1, source_target_pairs={{0,1},{1,0},{2,3},{3,2},{4,5},{5,4},{6,7},{7,6},{8,9},{9,8},{10,11... | collective-permute-start | bytes 3145736 | tf_op jit(solution)/shard_map/ppermute | solution.py:21
  145.7 14.8 %collective-permute-start.16 = (bf16[2,32,4096]{2,1,0:T(8,128)(2,1)S(1)}, bf16[2,32,4096]{2,1,0:T(8,128)(2,1)S(1)}, u32[]{:S(2)}, u32[]{:S(2)}) collective-permute-start(bf16[2,32,4096]{2,1,0:T(8,128)(2,1)S(1)} %add_convert_fusion.1), channel_id=1, source_target_pairs={{0,8},{2,10},{4,12},{6,14},{8,0},{10,2},{12,4},{14,6},{16,24},{18,... | collective-permute-start | bytes 1572872 | tf_op jit(solution)/shard_map/ppermute | solution.py:21
  156.7 21.9 %collective-permute-start.27 = (bf16[2,32,4096]{2,1,0:T(8,128)(2,1)S(1)}, bf16[2,32,4096]{2,1,0:T(8,128)(2,1)S(1)}, u32[]{:S(2)}, u32[]{:S(2)}) collective-permute-start(bf16[2,32,4096]{2,1,0:T(8,128)(2,1)S(1)} %add_convert_fusion), channel_id=1, source_target_pairs={{0,8},{2,10},{4,12},{6,14},{8,0},{10,2},{12,4},{14,6},{16,24},{18,... | collective-permute-start | bytes 1572872 | tf_op jit(solution)/shard_map/ppermute | solution.py:21
  160.5 25.8 %collective-permute-start.17 = (bf16[32,4096]{1,0:T(8,128)(2,1)S(1)}, bf16[32,4096]{1,0:T(8,128)(2,1)S(1)}, u32[]{:S(2)}, u32[]{:S(2)}) collective-permute-start(bf16[32,4096]{1,0:T(8,128)(2,1)S(1)} %fusion.2), channel_id=1, source_target_pairs={{0,16},{2,18},{4,20},{6,22},{8,24},{10,26},{12,28},{14,30},{16,0},... | collective-permute-start | bytes 786440 | tf_op jit(solution)/shard_map/ppermute | solution.py:21
  166.5 15.9 %collective-permute-start.40 = (bf16[48,8,128]{2,1,0:T(8,128)(2,1)S(1)}, bf16[48,8,128]{2,1,0:T(8,128)(2,1)S(1)}, u32[]{:S(2)}, u32[]{:S(2)}) collective-permute-start(bf16[48,8,128]{2,1,0:T(8,128)(2,1)S(1)} %get-tuple-element.118), channel_id=1, source_target_pairs={{0,24},{2,26},{4,28},{6,30},{8,16},{10,18},{12,20},{14,22},{16,8},... | collective-permute-start | bytes 294920 | tf_op jit(solution)/shard_map/ppermute | solution.py:21
  169.7 14.9 %collective-permute-start.39 = (bf16[48,8,128]{2,1,0:T(8,128)(2,1)S(1)}, bf16[48,8,128]{2,1,0:T(8,128)(2,1)S(1)}, u32[]{:S(2)}, u32[]{:S(2)}) collective-permute-start(bf16[48,8,128]{2,1,0:T(8,128)(2,1)S(1)} %get-tuple-element.119), channel_id=1, source_target_pairs={{0,16},{2,18},{4,20},{6,22},{8,24},{10,26},{12,28},{14,30},{16,0},... | collective-permute-start | bytes 294920 | tf_op jit(solution)/shard_map/ppermute | solution.py:21
  169.7 17.6 %collective-permute-start.38 = (bf16[48,8,128]{2,1,0:T(8,128)(2,1)S(1)}, bf16[48,8,128]{2,1,0:T(8,128)(2,1)S(1)}, u32[]{:S(2)}, u32[]{:S(2)}) collective-permute-start(bf16[48,8,128]{2,1,0:T(8,128)(2,1)S(1)} %get-tuple-element.120), channel_id=1, source_target_pairs={{0,8},{2,10},{4,12},{6,14},{8,0},{10,2},{12,4},{14,6},{16,24},{18,... | collective-permute-start | bytes 294920 | tf_op jit(solution)/shard_map/ppermute | solution.py:21
  182.4 16.5 %collective-permute-start.32 = (bf16[48,8,128]{2,1,0:T(8,128)(2,1)S(1)}, bf16[48,8,128]{2,1,0:T(8,128)(2,1)S(1)}, u32[]{:S(2)}, u32[]{:S(2)}) collective-permute-start(bf16[48,8,128]{2,1,0:T(8,128)(2,1)S(1)} %get-tuple-element.106), channel_id=1, source_target_pairs={{0,16},{2,18},{4,20},{6,22},{8,24},{10,26},{12,28},{14,30},{16,0},... | collective-permute-start | bytes 294920 | tf_op jit(solution)/shard_map/ppermute | solution.py:21
  184.6 14.3 %collective-permute-start.33 = (bf16[48,8,128]{2,1,0:T(8,128)(2,1)S(1)}, bf16[48,8,128]{2,1,0:T(8,128)(2,1)S(1)}, u32[]{:S(2)}, u32[]{:S(2)}) collective-permute-start(bf16[48,8,128]{2,1,0:T(8,128)(2,1)S(1)} %get-tuple-element.107), channel_id=1, source_target_pairs={{0,24},{2,26},{4,28},{6,30},{8,16},{10,18},{12,20},{14,22},{16,8},... | collective-permute-start | bytes 294920 | tf_op jit(solution)/shard_map/ppermute | solution.py:21
  186.4 20.1 %collective-permute-start.28 = (bf16[32,4096]{1,0:T(8,128)(2,1)S(1)}, bf16[32,4096]{1,0:T(8,128)(2,1)S(1)}, u32[]{:S(2)}, u32[]{:S(2)}) collective-permute-start(bf16[32,4096]{1,0:T(8,128)(2,1)S(1)} %fusion.3), channel_id=1, source_target_pairs={{0,16},{2,18},{4,20},{6,22},{8,24},{10,26},{12,28},{14,30},{16,0},... | collective-permute-start | bytes 786440 | tf_op jit(solution)/shard_map/ppermute | solution.py:21
  (45 other events, 612.6 us)

commit v5 on v4

v5 whole, which is shorter than its diff:
```python
import functools
import math

import jax
import jax.numpy as jnp
from jax import lax
from jax.experimental import pallas as pl
from jax.experimental.pallas import tpu as pltpu
from jax.sharding import PartitionSpec as P

F32 = jnp.float32
BF16 = jnp.bfloat16
PLAIN = (((1,), (0,)), ((), ()))
TURNED = (((1,), (1,)), ((), ()))
MIB = 1024 * 1024
UNROLL = 2
dot = functools.partial(lax.dot_general, preferred_element_type=F32)


def swap(value, axis, stride):
    size = lax.axis_size(axis)
    return lax.ppermute(value, axis, [(at, at ^ stride) for at in range(size)])


def after(value, *others):
    return lax.optimization_barrier((value, *others))[0]


def add(first, *others):
    total = first.astype(F32)
    for other in others:
        total = total + other.astype(F32)
    return total.astype(BF16)


def strides_of(size, unit=1):
    found = []
    step = size // 2
    while step >= 1:
        found.append(step * unit)
        step //= 2
    return found


def gather(items, axis, strides):
    for stride in strides:
        items = {**items, **{at ^ stride: swap(one, axis, stride) for at, one in items.items()}}
    return items


def scatter(items, axis, strides):
    for stride in reversed(strides):
        kept = {}
        for at, one in items.items():
            if not at & stride:
                kept[at] = add(one, swap(items[at ^ stride], axis, stride))
        items = kept
    return items


def whole(shape):
    return pl.BlockSpec(shape, lambda *_: (0,) * len(shape), pipeline_mode=pl.Buffered(1))


def pack(table, tiles, *refs, blocks, slot_count):
    outs, lines = refs[:-1], refs[-1]
    spare = outs[0].shape[0] - 1
    share, terms, blocks_dev, _ = tiles.shape
    for row in range(share):
        for term in range(terms):
            at = (row * terms + term) * blocks_dev
            lines[at : at + blocks_dev, :] = tiles[row, term].astype(F32)
    for at, out in enumerate(outs):

        def one(place, _, at=at, out=out):
            column = at * blocks + place
            block = table[0, column]
            for matrix in range(3):
                first, count = table[1 + matrix, column], table[4 + matrix, column]
                for slot in range(slot_count):
                    to = jnp.where(slot < count, first + slot, spare)
                    source = (matrix * slot_count + slot) * blocks_dev + block
                    out[to] = lines[pl.ds(source, share, stride=terms * blocks_dev), :].astype(BF16)
            return _

        lax.fori_loop(0, blocks, one, 0, unroll=True)


def unpack(table, *refs, chunks, chunk_rows, blocks, slot_count):
    out, lines, sources = refs[-2], refs[-1], refs[:-2]
    share, terms, blocks_dev, _ = out.shape
    far = len(sources) // chunks
    chunk_blocks = blocks // chunks
    for chunk in range(chunks):
        for at in range(far):
            ref = sources[chunk * far + at]

            def one(place, _, at=at, ref=ref, chunk=chunk):
                column = at * blocks + chunk * chunk_blocks + place
                block = table[0, column]
                for matrix in range(3):
                    first = table[1 + matrix, column] - chunk * chunk_rows
                    count = table[4 + matrix, column]
                    for slot in range(slot_count):
                        live = slot < count
                        value = ref[jnp.where(live, first + slot, 0)].astype(F32)
                        target = (matrix * slot_count + slot) * blocks_dev + block
                        lines[pl.ds(target, share, stride=terms * blocks_dev), :] = jnp.where(
                            live, value, 0.0
                        )
                return _

            lax.fori_loop(0, chunk_blocks, one, 0, unroll=True)
    for row in range(share):
        for term in range(terms):
            at = (row * terms + term) * blocks_dev
            out[row, term] = lines[at : at + blocks_dev, :].astype(BF16)


def offset_of(table, part, at, near, share):
    far_part = (part[1] + at) ^ table[16, 0]
    near_part = part[0] ^ table[16, 1]
    return pl.multiple_of((far_part * near + near_part) * share, share)


def assemble(table, *refs, weight_parts, near):
    weight_refs, out, tiles = refs[: len(weight_parts)], refs[-2], refs[-1]
    for ref, part in zip(weight_refs, weight_parts):
        share = ref.shape[2]
        for at in range(part[2]):
            offset = offset_of(table, part, at, near, share)
            tiles[:, pl.ds(offset, share), :] = ref[at].astype(F32)
    out[...] = tiles[...].astype(BF16)

    @pl.when(pl.program_id(0) == pl.num_programs(0) - 1)
    def _():
        out[out.shape[0] - 1] = jnp.zeros(out.shape[1:], BF16)


def places_of(table, block, slot_count, spare, base=0):
    places = []
    for matrix in range(3):
        first, count = table[1 + matrix, block] - base, table[4 + matrix, block]
        places += [jnp.where(slot < count, first + slot, spare) for slot in range(slot_count)]
    return places


def store_parts(total, own, other, parts):
    own_rows = own.shape[1]
    for at, (is_other, place) in enumerate(parts):
        ref = other if is_other else own
        ref[place] = total[at * own_rows : (at + 1) * own_rows, :].astype(BF16)


def tokens_at(refs, columns):
    return jnp.concatenate([ref[:, columns] for ref in refs], axis=0)


def columns_of(table, block, index, tile):
    return pl.ds(pl.multiple_of(table[7 + index, block] * tile, tile), tile)


def triples(slot_count):
    return [range(at * slot_count, (at + 1) * slot_count) for at in range(3)]


def in_turn(first, rest, blocks):
    group = max(size for size in range(1, UNROLL + 1) if blocks % size == 0)

    def some(at, _):
        held = first(at * group)
        for block in range(group):
            following = first(at * group + block + 1) if block + 1 < group else None
            rest(at * group + block, *held)
            held = following
        return _

    lax.fori_loop(0, blocks // group, some, 0)


def ahead(table, *refs, token_count, slot_count, parts):
    token_refs, refs = refs[:token_count], refs[token_count:]
    tiles, x_turned, gate_slope, gate_act_out, hidden_turned, ffn_own, ffn_other, ffn_sum = refs
    tile = tiles.shape[1]
    gate, up, down = triples(slot_count)

    for at in range(x_turned.shape[0] // tile):
        here = slice(at * tile, (at + 1) * tile)
        x_turned[here, :] = tokens_at(token_refs, here).T
    ffn_sum[...] = jnp.zeros_like(ffn_sum)

    def first(block):
        places = places_of(table, block, slot_count, tiles.shape[0] - 1)
        sums = []
        for indices in (gate, up):
            columns = [columns_of(table, block, index, tile) for index in indices]
            values = jnp.concatenate([tokens_at(token_refs, column) for column in columns], axis=1)
            weights = jnp.concatenate([tiles[places[index]] for index in indices], axis=0)
            sums.append(dot(values, weights, PLAIN))
        return places, *sums

    def rest(block, places, gate_pre, up_pre):
        gate_sig = jax.nn.sigmoid(gate_pre)
        gate_act = gate_pre * gate_sig
        hidden = (gate_act * up_pre).astype(BF16)
        gate_slope[block] = up_pre * gate_sig * (1.0 + gate_pre * (1.0 - gate_sig))
        gate_act_out[block] = gate_act
        hidden_turned[block] = hidden.T
        down_tiles = jnp.concatenate([tiles[places[index]] for index in down], axis=1)
        ffn = dot(hidden, down_tiles, PLAIN)
        for at, index in enumerate(down):
            ffn_sum[:, columns_of(table, block, index, tile)] += ffn[:, at * tile : (at + 1) * tile]

    in_turn(first, rest, gate_slope.shape[0])
    store_parts(ffn_sum, ffn_own, ffn_other, parts)


def behind(
    table, *refs, token_count, weight_parts, slot_count, grad_scale, near, chunks, chunk_rows, parts
):
    token_refs, refs = refs[:token_count], refs[token_count:]
    tiles, x_turned, gate_slope, gate_act, hidden_turned, input_own, input_other = refs[:7]
    grad_refs, input_sum, sums = refs[7:-2], refs[-2], refs[-1]
    tile = tiles.shape[1]
    gate, up, down = triples(slot_count)
    input_sum[...] = jnp.zeros_like(input_sum)

    def first(block):
        places = places_of(table, block, slot_count, tiles.shape[0] - 1)
        columns = [columns_of(table, block, index, tile) for index in range(3 * slot_count)]
        down_tiles = jnp.concatenate([tiles[places[index]] for index in down], axis=1)
        grad_in = jnp.concatenate([tokens_at(token_refs, columns[index]) for index in down], axis=1)
        return places, columns, grad_in, dot(grad_in, down_tiles, TURNED)

    def rest(block, places, columns, grad_in, hidden_grad):
        gate_grad = (hidden_grad * gate_slope[block]).astype(BF16)
        up_grad = (hidden_grad * gate_act[block]).astype(BF16)
        down_terms = dot(hidden_turned[block], grad_in, PLAIN) * grad_scale
        for at, index in enumerate(down):
            sums[places[index]] = down_terms[:, at * tile : (at + 1) * tile]
        for indices, grad in ((gate, gate_grad), (up, up_grad)):
            weights = jnp.concatenate([tiles[places[index]] for index in indices], axis=0)
            back = dot(grad, weights, TURNED)
            turned = jnp.concatenate([x_turned[columns[index], :] for index in indices], axis=0)
            terms = dot(turned, grad, PLAIN) * grad_scale
            for at, index in enumerate(indices):
                sums[places[index]] = terms[at * tile : (at + 1) * tile]
                input_sum[:, columns[index]] += back[:, at * tile : (at + 1) * tile]

    in_turn(first, rest, gate_slope.shape[0])
    store_parts(input_sum, input_own, input_other, parts)
    for chunk in range(chunks):
        rows = slice(chunk * chunk_rows, (chunk + 1) * chunk_rows)
        for index, part in enumerate(weight_parts):
            ref = grad_refs[chunk * len(weight_parts) + index]
            share = ref.shape[2]
            for at in range(part[2]):
                offset = offset_of(table, part, at, near, share)
                ref[at] = sums[rows, pl.ds(offset, share), :].astype(BF16)


def call(kernel, table, args, in_specs, out_specs, out_shape, grid=1, scratch=(), cost=0, vmem=40):
    return pl.pallas_call(
        kernel,
        grid_spec=pltpu.PrefetchScalarGridSpec(
            num_scalar_prefetch=1,
            grid=(grid,),
            in_specs=in_specs,
            out_specs=out_specs,
            scratch_shapes=scratch,
        ),
        out_shape=out_shape,
        compiler_params=pltpu.CompilerParams(vmem_limit_bytes=vmem * MIB),
        cost_estimate=pl.CostEstimate(flops=0, bytes_accessed=cost, transcendentals=0),
    )(table, *args)


def shards(tokens, out_grad, weight_tiles, tile_counts, tile_rows):
    row_share, _, blocks_dev, slot_count, tile = weight_tiles.shape
    own_rows, features = tokens.shape
    dp_size, tensor_size = lax.axis_size("dp"), lax.axis_size("tensor")
    far = math.gcd(4, math.gcd(dp_size, blocks_dev))
    near = dp_size // far
    blocks = blocks_dev // far
    chunks = math.gcd(2, blocks)
    chunk_blocks = blocks // chunks
    groups = far * chunks
    terms = 3 * slot_count
    grad_scale = 1.0 / math.sqrt(own_rows * tensor_size * dp_size)
    me = lax.axis_index("dp")
    far_at, near_at = me // near, me % near
    far_strides, near_strides = strides_of(far, near), strides_of(near)
    tensor_strides = strides_of(tensor_size)
    shape = jax.ShapeDtypeStruct

    x_items, g_items = {0: tokens}, {0: out_grad}
    if far > 1:
        x_items[near] = swap(tokens, "dp", near)

    capacity = (terms * blocks_dev - 3 * blocks_dev + 3 * (slot_count - 1) * (groups - 1)) // groups
    chunk_rows = capacity + 1
    block_ids = jnp.arange(blocks_dev, dtype=jnp.int32)
    load = tile_counts[0] + tile_counts[1] + tile_counts[2]
    earlier = (load[:, None] > load[None, :]) | (
        (load[:, None] == load[None, :]) & (block_ids[:, None] < block_ids[None, :])
    )
    rank = jnp.sum(earlier.astype(jnp.int32), axis=0)
    group = rank % groups
    before = (group[:, None] == group[None, :]) & (rank[:, None] < rank[None, :])
    start = jnp.sum(jnp.where(before, load[:, None], 0), axis=0) + (group // far) * chunk_rows
    ranks_of = (
        jnp.arange(chunk_blocks, dtype=jnp.int32)[None, None, :] * groups
        + jnp.arange(chunks, dtype=jnp.int32)[None, :, None] * far
        + (jnp.arange(far, dtype=jnp.int32)[:, None, None] ^ far_at)
    ).reshape(blocks_dev)
    columns = jnp.concatenate(
        [
            block_ids[None, :],
            start[None, :],
            (start + tile_counts[0])[None, :],
            (start + tile_counts[0] + tile_counts[1])[None, :],
            tile_counts,
            jnp.transpose(tile_rows, (0, 2, 1)).reshape(terms, blocks_dev),
        ]
    )
    table = jnp.sum(
        jnp.where(ranks_of[None, :, None] == rank[None, None, :], columns[:, None, :], 0), axis=2
    )
    place = jnp.where(block_ids == 0, far_at, near_at).astype(jnp.int32)
    table = jnp.concatenate([table, place[None, :]])

    tile_lines = jnp.transpose(weight_tiles, (0, 1, 3, 2, 4)).reshape(
        row_share, terms, blocks_dev, tile
    )
    slots = chunks * chunk_rows
    packed_shape = (slots, row_share, tile)
    chunk_shape = (chunk_rows, row_share, tile)
    packed = call(
        functools.partial(pack, blocks=blocks, slot_count=slot_count),
        table,
        [tile_lines],
        [whole(tile_lines.shape)],
        [whole(packed_shape)] * far,
        [shape(packed_shape, BF16)] * far,
        scratch=[pltpu.VMEM((row_share * terms * blocks_dev, tile), F32)],
        cost=1_000_000,
        vmem=24,
    )
    staged = tensor_size == 2 and far == 4 and near == 4 and chunks == 2
    if far > 1:
        packed = after(tuple(packed), x_items[near])
    received = [swap(packed[at], "dp", at * near) for at in reversed(range(1, far))][::-1]
    held = jnp.stack([packed[0], *received])
    x_core, g_core = {}, {}
    if staged:
        x_core = {at: swap(x_items[at], "tensor", 1) for at in (0, near)}
        g_core = {0: swap(out_grad, "tensor", 1)}
        held = after(held, *x_core.values(), *g_core.values())

    half = far // 2
    split = near == 4 and far % 2 == 0
    if split:
        from_1, from_2 = swap(held, "dp", 1), swap(held, "dp", 2)
        pass_1, pass_2 = from_1[:half], from_2[half:]
        weight_list = [held, from_1, from_2, swap(pass_1, "dp", 2), swap(pass_2, "dp", 1)]
        weight_parts = [(0, 0, far), (1, 0, far), (2, 0, far), (3, 0, half), (3, half, half)]
    else:
        items = gather({0: held}, "dp", near_strides)
        pass_1 = pass_2 = held
        weight_list = [items[at] for at in range(near)]
        weight_parts = [(at, 0, far) for at in range(near)]

    if far == 4:
        x_source, g_source = after((tokens, out_grad), held)
        x_items[2 * near] = swap(x_source, "dp", 2 * near)
        g_items[near] = swap(g_source, "dp", near)
        x_back, g_source = after((x_items[2 * near], g_source), pass_1, pass_2, x_items[2 * near])
        x_items[3 * near] = swap(x_back, "dp", near)
        g_items[2 * near] = swap(g_source, "dp", 2 * near)
        g_items[3 * near] = swap(g_items[2 * near], "dp", near)
        weight_list = list(after(tuple(weight_list), x_items[2 * near]))
    elif far == 2:
        g_items[near] = swap(out_grad, "dp", near)

    far_order = [at * near for at in range(0, far, 2)] + [at * near for at in range(1, far, 2)]
    if staged:
        order = [at * near for at in range(far)]
        x_late = swap(jnp.concatenate([x_items[at] for at in order[2:]]), "tensor", 1)
        g_late = swap(jnp.concatenate([g_items[at] for at in order[1:]]), "tensor", 1)
        x_list = [x_items[at] for at in order] + [x_core[at] for at in order[:2]] + [x_late]
        g_list = [g_items[at] for at in order] + [g_core[0], g_late]
        parts = [(other, far_order.index(at)) for other in (False, True) for at in order]
        other_parts = [(at, 1) for at in far_order]
    else:
        x_list, g_list, parts, other_parts = [], [], [], []
        for place, at in enumerate(far_order):
            x_parts = gather({0: x_items[at]}, "tensor", tensor_strides)
            g_parts = gather({0: g_items[at]}, "tensor", tensor_strides)
            for other in x_parts:
                parts.append((other != 0, len(other_parts) if other else place))
                if other:
                    other_parts.append((at, other))
                x_list.append(x_parts[other])
                g_list.append(g_parts[other])

    group_rows = far * tensor_size * own_rows
    own_shape = (far, own_rows, features)
    other_shape = (len(other_parts), own_rows, features)
    steps = 2 if slots % 2 == 0 else 1
    tiles_shape = (slots, tile, tile)
    tiles = call(
        functools.partial(assemble, weight_parts=weight_parts, near=near),
        table,
        weight_list,
        [
            pl.BlockSpec((length, slots // steps, row_share, tile), lambda step, *_: (0, step, 0, 0))
            for _, _, length in weight_parts
        ],
        pl.BlockSpec((slots // steps, tile, tile), lambda step, *_: (step, 0, 0)),
        shape(tiles_shape, BF16),
        grid=steps,
        scratch=[pltpu.VMEM((slots // steps, tile, tile), F32)],
        cost=10_000_000,
        vmem=24,
    )
    if far == 4:
        x_list = list(after(tuple(x_list), g_items[2 * near]))
    def specs_of(*groups):
        return [whole(one.shape) for group in groups for one in group]

    middle_shapes = [
        shape((features, group_rows), BF16),
        shape((blocks, group_rows, tile), F32),
        shape((blocks, group_rows, tile), F32),
        shape((blocks, tile, group_rows), BF16),
    ]
    sum_shapes = [shape(own_shape, BF16), shape(other_shape, BF16)]
    outs = call(
        functools.partial(ahead, token_count=len(x_list), slot_count=slot_count, parts=parts),
        table,
        [*x_list, tiles],
        specs_of(x_list, [tiles]),
        specs_of(middle_shapes, sum_shapes),
        middle_shapes + sum_shapes,
        scratch=[pltpu.VMEM((group_rows, features), F32)],
        cost=30_000_000,
    )
    middle, (ffn_own, ffn_other) = outs[:4], outs[4:]

    def to_near(own_sums, other_sums):
        from_core = swap(other_sums, "tensor", 1)
        return from_core, add(own_sums[half:], from_core[half:])

    def to_far(own_sums, from_core, got):
        return add(own_sums[1], from_core[1], got[1])

    def generic(own_sums, other_sums):
        sums = {}
        for index, at in enumerate(far_order):
            items = {0: own_sums[index]}
            for other_index, (far_part, other) in enumerate(other_parts):
                if far_part == at:
                    items[other] = other_sums[other_index]
            sums[at] = scatter(items, "tensor", tensor_strides)[0]
        return scatter(sums, "dp", far_strides)[0]

    if staged:
        ffn_core, ffn_near = to_near(ffn_own, ffn_other)
        middle = after(tuple(middle), ffn_near)
    part_shapes = [
        shape((length,) + chunk_shape, BF16) for _ in range(chunks) for _, _, length in weight_parts
    ]
    outs = call(
        functools.partial(
            behind,
            token_count=len(g_list),
            weight_parts=weight_parts,
            slot_count=slot_count,
            grad_scale=grad_scale,
            near=near,
            chunks=chunks,
            chunk_rows=chunk_rows,
            parts=parts,
        ),
        table,
        [*g_list, tiles, *middle],
        specs_of(g_list, [tiles], middle),
        specs_of(sum_shapes, part_shapes),
        sum_shapes + part_shapes,
        scratch=[pltpu.VMEM((group_rows, features), F32), pltpu.VMEM(tiles_shape, F32)],
        cost=40_000_000,
    )
    (input_own, input_other), tile_terms = outs[:2], outs[2:]
    tile_terms = [
        tile_terms[chunk * len(weight_parts) : (chunk + 1) * len(weight_parts)]
        for chunk in range(chunks)
    ]

    def halves(parts):
        return swap(parts[3], "dp", 1), swap(parts[4], "dp", 2)

    def folded(parts, got_1, got_2):
        others = ((0, 0),) * 3
        to_2 = add(parts[2], jnp.pad(got_1, ((0, far - half), *others)))
        to_1 = add(parts[1], jnp.pad(got_2, ((half, 0), *others)))
        return to_1, to_2

    def summed(parts, to_1, to_2):
        from_1, from_2 = swap(to_1, "dp", 1), swap(to_2, "dp", 2)
        return [add(parts[0][at], from_1[at], from_2[at]) for at in range(far)]

    def sent_back(sums):
        return [sums[0]] + [swap(sums[at], "dp", at * near) for at in range(1, far)]

    if staged:
        first_parts, second_parts = tile_terms
        first_got, second_got = halves(first_parts), halves(second_parts)
        ffn_got = swap(ffn_near, "dp", near)
        ffn_last = to_far(ffn_own, ffn_core, ffn_got)
        ffn_far = swap(ffn_last, "dp", 2 * near)
        input_core, input_near = to_near(input_own, input_other)
        input_got = swap(input_near, "dp", near)
        first_sums = summed(first_parts, *folded(first_parts, *first_got))
        second_folded = after(folded(second_parts, *second_got), input_near)
        first_back = sent_back(after(tuple(first_sums), *second_folded))
        input_last = to_far(input_own, input_core, input_got)
        input_far = swap(input_last, "dp", 2 * near)
        second_sums = summed(second_parts, *second_folded)
        back = first_back + sent_back(after(tuple(second_sums), input_last))
        ffn_rows = add(ffn_own[0], ffn_core[0], ffn_got[0], ffn_far)
        input_rows = add(input_own[0], input_core[0], input_got[0], input_far)
    else:
        back = []
        for terms_of in tile_terms:
            if split:
                sums = summed(terms_of, *folded(terms_of, *halves(terms_of)))
            else:
                sums = scatter(dict(enumerate(terms_of)), "dp", near_strides)[0]
            back += sent_back(sums)
        ffn_rows = generic(ffn_own, ffn_other)
        input_rows = generic(input_own, input_other)

    grads = call(
        functools.partial(
            unpack, chunks=chunks, chunk_rows=chunk_rows, blocks=blocks, slot_count=slot_count
        ),
        table,
        back,
        specs_of(back),
        whole(tile_lines.shape),
        shape(tile_lines.shape, BF16),
        scratch=[pltpu.VMEM((row_share * terms * blocks_dev, tile), F32)],
        cost=2_000_000,
        vmem=24,
    )
    tile_grad = jnp.transpose(
        grads.reshape(row_share, 3, slot_count, blocks_dev, tile), (0, 1, 3, 2, 4)
    )
    return ffn_rows, input_rows, tile_grad


def solution(mesh):
    return jax.shard_map(
        shards,
        mesh=mesh,
        in_specs=(
            P(("dp", "tensor"), None),
            P(("dp", "tensor"), None),
            P("dp", None, "tensor", None, None),
            P(None, "tensor"),
            P(None, "tensor", None),
        ),
        out_specs=(
            P(("dp", "tensor"), None),
            P(("dp", "tensor"), None),
            P("dp", None, "tensor", None, None),
        ),
        check_vma=False,
    )
```

time: 209 us -> 175 us (0.84)
  Pallas kernels: 63.5 us -> 24.1 us
  waiting for transfers between devices: 66.4 us -> 89.2 us
  starting transfers between devices: 59 us -> 51.9 us
  local copies, waits for them, and re-layouts: 8.26 us -> 2.88 us
  other arithmetic: 9 us -> 5.24 us
    pallas_call x7 -> x5, Pallas kernels: 63.5 us -> 24.1 us  [call(): pl.pallas_call(kernel, grid_spec=pltpu.PrefetchScalarGridSpec(num_scalar_...]
    ppermute x41 -> x38, waiting for transfers between devices: 66.4 us -> 89.2 us  [swap(): return lax.ppermute(value, axis, [(at, at ^ stride) for at in range(size)])]
    ppermute x41 -> x38, starting transfers between devices: 59 us -> 51.9 us  [swap(): return lax.ppermute(value, axis, [(at, at ^ stride) for at in range(size)])]
    reshape x1 -> x0, local copies, waits for them, and re-layouts: 2.31 us -> none  [shards(): grads.reshape(blocks_dev, 3, slot_count, row_share, tile)]
    convert_element_type x12, other arithmetic: 4.84 us -> 2.67 us  [add(): return total.astype(BF16)]
  transfers between devices with their start and end apart: 41 -> 38, of which waited for: 17 -> 19; matrix products, arithmetic and copies ran while one was open for 6% -> 3% of each run, Pallas kernels for 31% -> 4%
where the time goes in v5:
time: 175 us; the launch traced here: 174 us
  waiting for transfers between devices  89.2 us (51%)
  starting transfers between devices  51.9 us (30%)
  Pallas kernels  24.1 us (14%)
  other arithmetic  5.24 us (3%)
  local copies, waits for them, and re-layouts  2.88 us (2%)
    ppermute x38, waiting for transfers between devices, swap(): return lax.ppermute(value, axis, [(at, at ^ stride) for at in range(size)])  89.2 us
    ppermute x38, starting transfers between devices, swap(): return lax.ppermute(value, axis, [(at, at ^ stride) for at in range(size)])  51.9 us
    pallas_call x5, Pallas kernels, call(): pl.pallas_call(kernel, grid_spec=pltpu.PrefetchScalarGridSpec(num_scalar_...  24.1 us
  transfers between devices with their start and end apart: 38, of which 19 were waited for; matrix products, arithmetic and copies ran while one was open for 3% of the time, Pallas kernels for 4%

profile of v5, /device:TPU:0, one launch (start us, length us, event | category | flops | bytes accessed | tf_op | source)
XLA Modules:
  0.0 174.3 jit_solution(17432574004492211418)
XLA Ops:
  0.6 3.1 %collective-permute-start = (bf16[32,4096]{1,0:T(8,128)(2,1)}, bf16[32,4096]{1,0:T(8,128)(2,1)S(1)}, u32[]{:S(2)}, u32[]{:S(2)}) collective-permute-start(bf16[32,4096]{1,0:T(8,128)(2,1)} %refs_0_.1), channel_id=1, source_target_pairs={{0,8},{2,10},{4,12},{6,14},{8,0},{10,2},{12,4},{14,6},{16,24},{18,... | collective-permute-start | bytes 786440 | tf_op jit(solution)/shard_map/ppermute | solution.py:22
  9.0 1.6 shard_map.76
  10.6 3.4 %collective-permute-start.3 = (bf16[96,8,128]{2,1,0:T(8,128)(2,1)S(1)}, bf16[96,8,128]{2,1,0:T(8,128)(2,1)S(1)}, u32[]{:S(2)}, u32[]{:S(2)}) collective-permute-start(bf16[96,8,128]{2,1,0:T(8,128)(2,1)S(1)} %get-tuple-element.67), channel_id=1, source_target_pairs={{0,24},{2,26},{4,28},{6,30},{8,16},{10,18},{12,20},{14,22},{16,8},... | collective-permute-start | bytes 589832 | tf_op jit(solution)/shard_map/ppermute | solution.py:22
  15.6 4.8 %collective-permute-done.3 = bf16[96,8,128]{2,1,0:T(8,128)(2,1)S(1)} collective-permute-done((bf16[96,8,128]{2,1,0:T(8,128)(2,1)S(1)}, bf16[96,8,128]{2,1,0:T(8,128)(2,1)S(1)}, u32[]{:S(2)}, u32[]{:S(2)}) %collective-permute-start.3) | collective-permute-done | bytes 196640 | tf_op jit(solution)/shard_map/ppermute | solution.py:22
  20.4 10.1 %collective-permute-done.2 = bf16[96,8,128]{2,1,0:T(8,128)(2,1)S(1)} collective-permute-done((bf16[96,8,128]{2,1,0:T(8,128)(2,1)S(1)}, bf16[96,8,128]{2,1,0:T(8,128)(2,1)S(1)}, u32[]{:S(2)}, u32[]{:S(2)}) %collective-permute-start.2) | collective-permute-done | bytes 196640 | tf_op jit(solution)/shard_map/ppermute | solution.py:22
  33.8 15.4 %collective-permute-done.8.refs_1_ = bf16[4,96,8,128]{3,2,1,0:T(8,128)(2,1)S(1)} collective-permute-done((bf16[4,96,8,128]{3,2,1,0:T(8,128)(2,1)S(1)}, bf16[4,96,8,128]{3,2,1,0:T(8,128)(2,1)S(1)}, u32[]{:S(2)}, u32[]{:S(2)}) %collective-permute-start.8) | collective-permute-done | bytes 786464 | tf_op jit(solution)/shard_map/ppermute | solution.py:22
  50.6 6.4 %collective-permute-done.10.refs_3_ = bf16[32,4096]{1,0:T(8,128)(2,1)S(1)} collective-permute-done((bf16[32,4096]{1,0:T(8,128)(2,1)S(1)}, bf16[32,4096]{1,0:T(8,128)(2,1)S(1)}, u32[]{:S(2)}, u32[]{:S(2)}) %collective-permute-start.10) | collective-permute-done | bytes 262176 | tf_op jit(solution)/shard_map/ppermute | solution.py:22
  57.0 1.6 collective-permute-start.13
  59.2 2.1 %collective-permute-start.12 = (bf16[32,4096]{1,0:T(8,128)(2,1)S(1)}, bf16[32,4096]{1,0:T(8,128)(2,1)S(1)}, u32[]{:S(2)}, u32[]{:S(2)}) collective-permute-start(bf16[32,4096]{1,0:T(8,128)(2,1)S(1)} %copy-done.3), channel_id=1, source_target_pairs={{0,16},{2,18},{4,20},{6,22},{8,24},{10,26},{12,28},{14,30},{16,0},... | collective-permute-start | bytes 786440 | tf_op jit(solution)/shard_map/ppermute | solution.py:22
  61.2 7.3 %collective-permute-done.13.refs_3_ = bf16[2,96,8,128]{3,2,1,0:T(8,128)(2,1)S(1)} collective-permute-done((bf16[2,96,8,128]{3,2,1,0:T(8,128)(2,1)S(1)}, bf16[2,96,8,128]{3,2,1,0:T(8,128)(2,1)S(1)}, u32[]{:S(2)}, u32[]{:S(2)}) %collective-permute-start.13) | collective-permute-done | bytes 393248 | tf_op jit(solution)/shard_map/ppermute | solution.py:22
  69.8 2.2 %shard_map.77.refs_7_.refs_6_ = bf16[96,128,128]{2,1,0:T(8,128)(2,1)S(1)} custom-call(s32[17,56]{1,0:T(8,128)S(1)} %pad_add_fusion.table, bf16[4,96,8,128]{3,2,1,0:T(8,128)(2,1)S(1)} %pad_maximum_fusion.refs_0_, bf16[4,96,8,128]{3,2,1,0:T(8,128)(2,1)S(1)} %collective-permute-done.8.refs_1_, bf16[4,96,8,128]{3,2,1,0:T(8,128)(2,1)S(1)} %collective-permute-done.9.refs_2_, ...), custom_call_target="tpu_custom_call" | custom-call | bytes 10000000 | tf_op jit(solution)/shard_map/pallas_call | solution.py:263
  72.0 1.7 collective-permute-done.12.refs_2_
  73.7 6.3 %shard_map.78 = (bf16[4096,256]{1,0:T(8,128)(2,1)S(1)}, f32[14,256,128]{2,1,0:T(8,128)S(1)}, f32[14,256,128]{2,1,0:T(8,128)S(1)}, bf16[14,128,256]{2,1,0:T(8,128...) custom-call(s32[17,56]{1,0:T(8,128)S(1)} %pad_add_fusion.table, ...), custom_call_target="tpu_custom_call" | custom-call | bytes 30000000 | tf_op jit(solution)/shard_map/pallas_call | solution.py:263
  80.2 2.0 %collective-permute-start.19 = (bf16[32,4096]{1,0:T(8,128)(2,1)S(1)}, bf16[32,4096]{1,0:T(8,128)(2,1)S(1)}, u32[]{:S(2)}, u32[]{:S(2)}) collective-permute-start(bf16[32,4096]{1,0:T(8,128)(2,1)S(1)} %collective-permute-done.12.refs_2_), channel_id=1, source_target_pairs={{0,8},{2,10},{4,12},{6,14},{8,0},{10,2},{12,4},{14,6},{16,24},{18,... | collective-permute-start | bytes 786440 | tf_op jit(solution)/shard_map/ppermute | solution.py:22
  82.2 7.1 %collective-permute-done.18.refs_1_ = bf16[32,4096]{1,0:T(8,128)(2,1)S(1)} collective-permute-done((bf16[32,4096]{1,0:T(8,128)(2,1)S(1)}, bf16[32,4096]{1,0:T(8,128)(2,1)S(1)}, u32[]{:S(2)}, u32[]{:S(2)}) %collective-permute-start.18) | collective-permute-done | bytes 262176 | tf_op jit(solution)/shard_map/ppermute | solution.py:22
  89.3 5.2 %collective-permute-done.19.refs_3_ = bf16[32,4096]{1,0:T(8,128)(2,1)S(1)} collective-permute-done((bf16[32,4096]{1,0:T(8,128)(2,1)S(1)}, bf16[32,4096]{1,0:T(8,128)(2,1)S(1)}, u32[]{:S(2)}, u32[]{:S(2)}) %collective-permute-start.19) | collective-permute-done | bytes 262176 | tf_op jit(solution)/shard_map/ppermute | solution.py:22
  94.7 2.1 %collective-permute-done.20.refs_5_ = bf16[96,4096]{1,0:T(8,128)(2,1)S(1)} collective-permute-done((bf16[96,4096]{1,0:T(8,128)(2,1)S(1)}, bf16[96,4096]{1,0:T(8,128)(2,1)S(1)}, u32[]{:S(2)}, u32[]{:S(2)}) %collective-permute-start.20) | collective-permute-done | bytes 786464 | tf_op jit(solution)/shard_map/ppermute | solution.py:22
  96.8 11.0 %shard_map.79 = (bf16[4,32,4096]{2,1,0:T(8,128)(2,1)S(1)}, bf16[4,32,4096]{2,1,0:T(8,128)(2,1)S(1)}, bf16[4,48,8,128]{3,2,1,0:T(8,128)(2,1)S(1)}, bf16[4,48,8,12...) custom-call(s32[17,56]{1,0:T(8,128)S(1)} %pad_add_fusion.table, ...), custom_call_target="tpu_custom_call" | custom-call | bytes 40000000 | tf_op jit(solution)/shard_map/pallas_call | solution.py:263
  111.7 3.2 %collective-permute-done.26 = bf16[2,48,8,128]{3,2,1,0:T(8,128)(2,1)S(1)} collective-permute-done((bf16[2,48,8,128]{3,2,1,0:T(8,128)(2,1)S(1)}, bf16[2,48,8,128]{3,2,1,0:T(8,128)(2,1)S(1)}, u32[]{:S(2)}, u32[]{:S(2)}) %collective-permute-start.26) | collective-permute-done | bytes 196640 | tf_op jit(solution)/shard_map/ppermute | solution.py:22
  117.9 3.6 %collective-permute-done.28 = bf16[2,48,8,128]{3,2,1,0:T(8,128)(2,1)S(1)} collective-permute-done((bf16[2,48,8,128]{3,2,1,0:T(8,128)(2,1)S(1)}, bf16[2,48,8,128]{3,2,1,0:T(8,128)(2,1)S(1)}, u32[]{:S(2)}, u32[]{:S(2)}) %collective-permute-start.28) | collective-permute-done | bytes 196640 | tf_op jit(solution)/shard_map/ppermute | solution.py:22
  122.4 1.8 %collective-permute-start.22 = (bf16[2,32,4096]{2,1,0:T(8,128)(2,1)S(1)}, bf16[2,32,4096]{2,1,0:T(8,128)(2,1)S(1)}, u32[]{:S(2)}, u32[]{:S(2)}) collective-permute-start(bf16[2,32,4096]{2,1,0:T(8,128)(2,1)S(1)} %add_convert_fusion), channel_id=1, source_target_pairs={{0,8},{2,10},{4,12},{6,14},{8,0},{10,2},{12,4},{14,6},{16,24},{18,... | collective-permute-start | bytes 1572872 | tf_op jit(solution)/shard_map/ppermute | solution.py:22
  126.3 3.7 %collective-permute-done.27 = bf16[4,48,8,128]{3,2,1,0:T(8,128)(2,1)S(1)} collective-permute-done((bf16[4,48,8,128]{3,2,1,0:T(8,128)(2,1)S(1)}, bf16[4,48,8,128]{3,2,1,0:T(8,128)(2,1)S(1)}, u32[]{:S(2)}, u32[]{:S(2)}) %collective-permute-start.27) | collective-permute-done | bytes 393248 | tf_op jit(solution)/shard_map/ppermute | solution.py:22
  130.0 2.9 %collective-permute-start.17 = (bf16[32,4096]{1,0:T(8,128)(2,1)S(1)}, bf16[32,4096]{1,0:T(8,128)(2,1)S(1)}, u32[]{:S(2)}, u32[]{:S(2)}) collective-permute-start(bf16[32,4096]{1,0:T(8,128)(2,1)S(1)} %fusion.2), channel_id=1, source_target_pairs={{0,16},{2,18},{4,20},{6,22},{8,24},{10,26},{12,28},{14,30},{16,0},... | collective-permute-start | bytes 786440 | tf_op jit(solution)/shard_map/ppermute | solution.py:22
  133.8 1.8 %collective-permute-start.30 = (bf16[48,8,128]{2,1,0:T(8,128)(2,1)S(1)}, bf16[48,8,128]{2,1,0:T(8,128)(2,1)S(1)}, u32[]{:S(2)}, u32[]{:S(2)}) collective-permute-start(bf16[48,8,128]{2,1,0:T(8,128)(2,1)S(1)} %get-tuple-element.109), channel_id=1, source_target_pairs={{0,8},{2,10},{4,12},{6,14},{8,0},{10,2},{12,4},{14,6},{16,24},{18,... | collective-permute-start | bytes 294920 | tf_op jit(solution)/shard_map/ppermute | solution.py:22
  135.6 2.1 %collective-permute-done.34 = bf16[4,48,8,128]{3,2,1,0:T(8,128)(2,1)S(1)} collective-permute-done((bf16[4,48,8,128]{3,2,1,0:T(8,128)(2,1)S(1)}, bf16[4,48,8,128]{3,2,1,0:T(8,128)(2,1)S(1)}, u32[]{:S(2)}, u32[]{:S(2)}) %collective-permute-start.34) | collective-permute-done | bytes 393248 | tf_op jit(solution)/shard_map/ppermute | solution.py:22
  137.8 2.9 %collective-permute-start.31 = (bf16[48,8,128]{2,1,0:T(8,128)(2,1)S(1)}, bf16[48,8,128]{2,1,0:T(8,128)(2,1)S(1)}, u32[]{:S(2)}, u32[]{:S(2)}) collective-permute-start(bf16[48,8,128]{2,1,0:T(8,128)(2,1)S(1)} %get-tuple-element.110), channel_id=1, source_target_pairs={{0,16},{2,18},{4,20},{6,22},{8,24},{10,26},{12,28},{14,30},{16,0},... | collective-permute-start | bytes 294920 | tf_op jit(solution)/shard_map/ppermute | solution.py:22
  140.7 1.8 %collective-permute-start.32 = (bf16[48,8,128]{2,1,0:T(8,128)(2,1)S(1)}, bf16[48,8,128]{2,1,0:T(8,128)(2,1)S(1)}, u32[]{:S(2)}, u32[]{:S(2)}) collective-permute-start(bf16[48,8,128]{2,1,0:T(8,128)(2,1)S(1)} %get-tuple-element.111), channel_id=1, source_target_pairs={{0,24},{2,26},{4,28},{6,30},{8,16},{10,18},{12,20},{14,22},{16,8},... | collective-permute-start | bytes 294920 | tf_op jit(solution)/shard_map/ppermute | solution.py:22
  143.3 3.3 %collective-permute-done.17 = bf16[32,4096]{1,0:T(8,128)(2,1)S(1)} collective-permute-done((bf16[32,4096]{1,0:T(8,128)(2,1)S(1)}, bf16[32,4096]{1,0:T(8,128)(2,1)S(1)}, u32[]{:S(2)}, u32[]{:S(2)}) %collective-permute-start.17) | collective-permute-done | bytes 262176 | tf_op jit(solution)/shard_map/ppermute | solution.py:22
  146.7 8.9 %collective-permute-start.35 = (bf16[48,8,128]{2,1,0:T(8,128)(2,1)S(1)}, bf16[48,8,128]{2,1,0:T(8,128)(2,1)S(1)}, u32[]{:S(2)}, u32[]{:S(2)}) collective-permute-start(bf16[48,8,128]{2,1,0:T(8,128)(2,1)S(1)} %get-tuple-element.114), channel_id=1, source_target_pairs={{0,8},{2,10},{4,12},{6,14},{8,0},{10,2},{12,4},{14,6},{16,24},{18,... | collective-permute-start | bytes 294920 | tf_op jit(solution)/shard_map/ppermute | solution.py:22
  155.5 3.5 %collective-permute-start.36 = (bf16[48,8,128]{2,1,0:T(8,128)(2,1)S(1)}, bf16[48,8,128]{2,1,0:T(8,128)(2,1)S(1)}, u32[]{:S(2)}, u32[]{:S(2)}) collective-permute-start(bf16[48,8,128]{2,1,0:T(8,128)(2,1)S(1)} %get-tuple-element.115), channel_id=1, source_target_pairs={{0,16},{2,18},{4,20},{6,22},{8,24},{10,26},{12,28},{14,30},{16,0},... | collective-permute-start | bytes 294920 | tf_op jit(solution)/shard_map/ppermute | solution.py:22
  161.4 9.0 %collective-permute-done.36.refs_6_ = bf16[48,8,128]{2,1,0:T(8,128)(2,1)S(1)} collective-permute-done((bf16[48,8,128]{2,1,0:T(8,128)(2,1)S(1)}, bf16[48,8,128]{2,1,0:T(8,128)(2,1)S(1)}, u32[]{:S(2)}, u32[]{:S(2)}) %collective-permute-start.36) | collective-permute-done | bytes 98336 | tf_op jit(solution)/shard_map/ppermute | solution.py:22
  170.4 3.0 %shard_map.80 = bf16[8,9,56,128]{3,2,1,0:T(8,128)(2,1)} custom-call(s32[17,56]{1,0:T(8,128)S(1)} %pad_add_fusion.table, bf16[48,8,128]{2,1,0:T(8,128)(2,1)S(1)} %get-tuple-element.108.refs_0_, bf16[48,8,128]{2,1,0:T(8,128)(2,1)S(1)} %collective-permute-done.30.refs_1_, bf16[48,8,128]{2,1,0:T(8,128)(2,1)S(1)} %collective-permute-done.31.refs_2_, ...), custom_call_target="tpu_custom_call" | custom-call | bytes 2000000 | tf_op jit(solution)/shard_map/pallas_call | solution.py:263
  (92 shorter events, 28.3 us)
Async XLA Ops:
  0.6 10.0 %collective-permute-start = (bf16[32,4096]{1,0:T(8,128)(2,1)}, bf16[32,4096]{1,0:T(8,128)(2,1)S(1)}, u32[]{:S(2)}, u32[]{:S(2)}) collective-permute-start(bf16[32,4096]{1,0:T(8,128)(2,1)} %refs_0_.1), channel_id=1, source_target_pairs={{0,8},{2,10},{4,12},{6,14},{8,0},{10,2},{12,4},{14,6},{16,24},{18,... | collective-permute-start | bytes 786440 | tf_op jit(solution)/shard_map/ppermute | solution.py:22
  10.6 9.8 %collective-permute-start.3 = (bf16[96,8,128]{2,1,0:T(8,128)(2,1)S(1)}, bf16[96,8,128]{2,1,0:T(8,128)(2,1)S(1)}, u32[]{:S(2)}, u32[]{:S(2)}) collective-permute-start(bf16[96,8,128]{2,1,0:T(8,128)(2,1)S(1)} %get-tuple-element.67), channel_id=1, source_target_pairs={{0,24},{2,26},{4,28},{6,30},{8,16},{10,18},{12,20},{14,22},{16,8},... | collective-permute-start | bytes 589832 | tf_op jit(solution)/shard_map/ppermute | solution.py:22
  14.0 16.5 %collective-permute-start.2 = (bf16[96,8,128]{2,1,0:T(8,128)(2,1)S(1)}, bf16[96,8,128]{2,1,0:T(8,128)(2,1)S(1)}, u32[]{:S(2)}, u32[]{:S(2)}) collective-permute-start(bf16[96,8,128]{2,1,0:T(8,128)(2,1)S(1)} %get-tuple-element.66), channel_id=1, source_target_pairs={{0,16},{2,18},{4,20},{6,22},{8,24},{10,26},{12,28},{14,30},{16,0},... | collective-permute-start | bytes 589832 | tf_op jit(solution)/shard_map/ppermute | solution.py:22
  14.0 16.5 %collective-permute-start.1 = (bf16[96,8,128]{2,1,0:T(8,128)(2,1)S(1)}, bf16[96,8,128]{2,1,0:T(8,128)(2,1)S(1)}, u32[]{:S(2)}, u32[]{:S(2)}) collective-permute-start(bf16[96,8,128]{2,1,0:T(8,128)(2,1)S(1)} %get-tuple-element.65), channel_id=1, source_target_pairs={{0,8},{2,10},{4,12},{6,14},{8,0},{10,2},{12,4},{14,6},{16,24},{18,... | collective-permute-start | bytes 589832 | tf_op jit(solution)/shard_map/ppermute | solution.py:22
  15.1 15.6 %collective-permute-start.4 = (bf16[32,4096]{1,0:T(8,128)(2,1)}, bf16[32,4096]{1,0:T(8,128)(2,1)S(1)}, u32[]{:S(2)}, u32[]{:S(2)}) collective-permute-start(bf16[32,4096]{1,0:T(8,128)(2,1)} %refs_0_.1), channel_id=1, source_target_pairs={{0,1},{1,0},{2,3},{3,2},{4,5},{5,4},{6,7},{7,6},{8,9},{9,8},{10,11... | collective-permute-start | bytes 786440 | tf_op jit(solution)/shard_map/ppermute | solution.py:22
  15.1 15.6 %collective-permute-start.6 = (bf16[32,4096]{1,0:T(8,128)(2,1)}, bf16[32,4096]{1,0:T(8,128)(2,1)S(1)}, u32[]{:S(2)}, u32[]{:S(2)}) collective-permute-start(bf16[32,4096]{1,0:T(8,128)(2,1)} %refs_0_.2), channel_id=1, source_target_pairs={{0,1},{1,0},{2,3},{3,2},{4,5},{5,4},{6,7},{7,6},{8,9},{9,8},{10,11... | collective-permute-start | bytes 786440 | tf_op jit(solution)/shard_map/ppermute | solution.py:22
  20.4 10.3 %collective-permute-start.5 = (bf16[32,4096]{1,0:T(8,128)(2,1)S(1)}, bf16[32,4096]{1,0:T(8,128)(2,1)S(1)}, u32[]{:S(2)}, u32[]{:S(2)}) collective-permute-start(bf16[32,4096]{1,0:T(8,128)(2,1)S(1)} %collective-permute-done.refs_1_), channel_id=1, source_target_pairs={{0,1},{1,0},{2,3},{3,2},{4,5},{5,4},{6,7},{7,6},{8,9},{9,8},{10,11... | collective-permute-start | bytes 786440 | tf_op jit(solution)/shard_map/ppermute | solution.py:22
  30.7 18.5 %collective-permute-start.8 = (bf16[4,96,8,128]{3,2,1,0:T(8,128)(2,1)S(1)}, bf16[4,96,8,128]{3,2,1,0:T(8,128)(2,1)S(1)}, u32[]{:S(2)}, u32[]{:S(2)}) collective-permute-start(bf16[4,96,8,128]{3,2,1,0:T(8,128)(2,1)S(1)} %pad_maximum_fusion.refs_0_), channel_id=1, source_target_pairs={{0,2},{2,0},{4,6},{6,4},{8,10},{10,8},{12,14},{14,12},{16,18},{18,... | collective-permute-start | bytes 2359304 | tf_op jit(solution)/shard_map/ppermute | solution.py:22
  32.2 18.2 %collective-permute-start.9 = (bf16[4,96,8,128]{3,2,1,0:T(8,128)(2,1)S(1)}, bf16[4,96,8,128]{3,2,1,0:T(8,128)(2,1)S(1)}, u32[]{:S(2)}, u32[]{:S(2)}) collective-permute-start(bf16[4,96,8,128]{3,2,1,0:T(8,128)(2,1)S(1)} %pad_maximum_fusion.refs_0_), channel_id=1, source_target_pairs={{0,4},{2,6},{4,0},{6,2},{8,12},{10,14},{12,8},{14,10},{16,20},{18,... | collective-permute-start | bytes 2359304 | tf_op jit(solution)/shard_map/ppermute | solution.py:22
  33.8 16.7 %collective-permute-start.7 = (bf16[32,4096]{1,0:T(8,128)(2,1)S(1)}, bf16[32,4096]{1,0:T(8,128)(2,1)S(1)}, u32[]{:S(2)}, u32[]{:S(2)}) collective-permute-start(bf16[32,4096]{1,0:T(8,128)(2,1)S(1)} %copy-done.2), channel_id=1, source_target_pairs={{0,16},{2,18},{4,20},{6,22},{8,24},{10,26},{12,28},{14,30},{16,0},... | collective-permute-start | bytes 786440 | tf_op jit(solution)/shard_map/ppermute | solution.py:22
  57.0 16.7 %collective-permute-start.11 = (bf16[64,4096]{1,0:T(8,128)(2,1)S(1)}, bf16[64,4096]{1,0:T(8,128)(2,1)S(1)}, u32[]{:S(2)}, u32[]{:S(2)}) collective-permute-start(bf16[64,4096]{1,0:T(8,128)(2,1)S(1)} %pad_maximum_fusion.2), channel_id=1, source_target_pairs={{0,1},{1,0},{2,3},{3,2},{4,5},{5,4},{6,7},{7,6},{8,9},{9,8},{10,11... | collective-permute-start | bytes 1572872 | tf_op jit(solution)/shard_map/ppermute | solution.py:22
  57.0 11.5 %collective-permute-start.13 = (bf16[2,96,8,128]{3,2,1,0:T(8,128)(2,1)S(1)}, bf16[2,96,8,128]{3,2,1,0:T(8,128)(2,1)S(1)}, u32[]{:S(2)}, u32[]{:S(2)}) collective-permute-start(bf16[2,96,8,128]{3,2,1,0:T(8,128)(2,1)S(1)} %slice.183), channel_id=1, source_target_pairs={{0,4},{2,6},{4,0},{6,2},{8,12},{10,14},{12,8},{14,10},{16,20},{18,... | collective-permute-start | bytes 1179656 | tf_op jit(solution)/shard_map/ppermute | solution.py:22
  58.6 11.2 %collective-permute-start.14 = (bf16[2,96,8,128]{3,2,1,0:T(8,128)(2,1)S(1)}, bf16[2,96,8,128]{3,2,1,0:T(8,128)(2,1)S(1)}, u32[]{:S(2)}, u32[]{:S(2)}) collective-permute-start(bf16[2,96,8,128]{3,2,1,0:T(8,128)(2,1)S(1)} %slice.184), channel_id=1, source_target_pairs={{0,2},{2,0},{4,6},{6,4},{8,10},{10,8},{12,14},{14,12},{16,18},{18,... | collective-permute-start | bytes 1179656 | tf_op jit(solution)/shard_map/ppermute | solution.py:22
  59.2 14.5 %collective-permute-start.12 = (bf16[32,4096]{1,0:T(8,128)(2,1)S(1)}, bf16[32,4096]{1,0:T(8,128)(2,1)S(1)}, u32[]{:S(2)}, u32[]{:S(2)}) collective-permute-start(bf16[32,4096]{1,0:T(8,128)(2,1)S(1)} %copy-done.3), channel_id=1, source_target_pairs={{0,16},{2,18},{4,20},{6,22},{8,24},{10,26},{12,28},{14,30},{16,0},... | collective-permute-start | bytes 786440 | tf_op jit(solution)/shard_map/ppermute | solution.py:22
  80.0 14.6 %collective-permute-start.15 = (bf16[4,32,4096]{2,1,0:T(8,128)(2,1)S(1)}, bf16[4,32,4096]{2,1,0:T(8,128)(2,1)S(1)}, u32[]{:S(2)}, u32[]{:S(2)}) collective-permute-start(bf16[4,32,4096]{2,1,0:T(8,128)(2,1)S(1)} %get-tuple-element.86), channel_id=1, source_target_pairs={{0,1},{1,0},{2,3},{3,2},{4,5},{5,4},{6,7},{7,6},{8,9},{9,8},{10,11... | collective-permute-start | bytes 3145736 | tf_op jit(solution)/shard_map/ppermute | solution.py:22
  80.2 14.3 %collective-permute-start.19 = (bf16[32,4096]{1,0:T(8,128)(2,1)S(1)}, bf16[32,4096]{1,0:T(8,128)(2,1)S(1)}, u32[]{:S(2)}, u32[]{:S(2)}) collective-permute-start(bf16[32,4096]{1,0:T(8,128)(2,1)S(1)} %collective-permute-done.12.refs_2_), channel_id=1, source_target_pairs={{0,8},{2,10},{4,12},{6,14},{8,0},{10,2},{12,4},{14,6},{16,24},{18,... | collective-permute-start | bytes 786440 | tf_op jit(solution)/shard_map/ppermute | solution.py:22
  109.4 12.9 %collective-permute-start.21 = (bf16[4,32,4096]{2,1,0:T(8,128)(2,1)S(1)}, bf16[4,32,4096]{2,1,0:T(8,128)(2,1)S(1)}, u32[]{:S(2)}, u32[]{:S(2)}) collective-permute-start(bf16[4,32,4096]{2,1,0:T(8,128)(2,1)S(1)} %get-tuple-element.96), channel_id=1, source_target_pairs={{0,1},{1,0},{2,3},{3,2},{4,5},{5,4},{6,7},{7,6},{8,9},{9,8},{10,11... | collective-permute-start | bytes 3145736 | tf_op jit(solution)/shard_map/ppermute | solution.py:22
  109.4 15.4 %collective-permute-start.16 = (bf16[2,32,4096]{2,1,0:T(8,128)(2,1)S(1)}, bf16[2,32,4096]{2,1,0:T(8,128)(2,1)S(1)}, u32[]{:S(2)}, u32[]{:S(2)}) collective-permute-start(bf16[2,32,4096]{2,1,0:T(8,128)(2,1)S(1)} %add_convert_fusion.1), channel_id=1, source_target_pairs={{0,8},{2,10},{4,12},{6,14},{8,0},{10,2},{12,4},{14,6},{16,24},{18,... | collective-permute-start | bytes 1572872 | tf_op jit(solution)/shard_map/ppermute | solution.py:22
  110.1 11.4 %collective-permute-start.28 = (bf16[2,48,8,128]{3,2,1,0:T(8,128)(2,1)S(1)}, bf16[2,48,8,128]{3,2,1,0:T(8,128)(2,1)S(1)}, u32[]{:S(2)}, u32[]{:S(2)}) collective-permute-start(bf16[2,48,8,128]{3,2,1,0:T(8,128)(2,1)S(1)} %get-tuple-element.103), channel_id=1, source_target_pairs={{0,4},{2,6},{4,0},{6,2},{8,12},{10,14},{12,8},{14,10},{16,20},{18,... | collective-permute-start | bytes 589832 | tf_op jit(solution)/shard_map/ppermute | solution.py:22
  117.4 12.6 %collective-permute-start.27 = (bf16[4,48,8,128]{3,2,1,0:T(8,128)(2,1)S(1)}, bf16[4,48,8,128]{3,2,1,0:T(8,128)(2,1)S(1)}, u32[]{:S(2)}, u32[]{:S(2)}) collective-permute-start(bf16[4,48,8,128]{3,2,1,0:T(8,128)(2,1)S(1)} %add_convert_fusion.4), channel_id=1, source_target_pairs={{0,4},{2,6},{4,0},{6,2},{8,12},{10,14},{12,8},{14,10},{16,20},{18,... | collective-permute-start | bytes 1179656 | tf_op jit(solution)/shard_map/ppermute | solution.py:22
  121.6 12.1 %collective-permute-start.25 = (bf16[4,48,8,128]{3,2,1,0:T(8,128)(2,1)S(1)}, bf16[4,48,8,128]{3,2,1,0:T(8,128)(2,1)S(1)}, u32[]{:S(2)}, u32[]{:S(2)}) collective-permute-start(bf16[4,48,8,128]{3,2,1,0:T(8,128)(2,1)S(1)} %add_convert_fusion.5), channel_id=1, source_target_pairs={{0,2},{2,0},{4,6},{6,4},{8,10},{10,8},{12,14},{14,12},{16,18},{18,... | collective-permute-start | bytes 1179656 | tf_op jit(solution)/shard_map/ppermute | solution.py:22
  122.4 20.2 %collective-permute-start.22 = (bf16[2,32,4096]{2,1,0:T(8,128)(2,1)S(1)}, bf16[2,32,4096]{2,1,0:T(8,128)(2,1)S(1)}, u32[]{:S(2)}, u32[]{:S(2)}) collective-permute-start(bf16[2,32,4096]{2,1,0:T(8,128)(2,1)S(1)} %add_convert_fusion), channel_id=1, source_target_pairs={{0,8},{2,10},{4,12},{6,14},{8,0},{10,2},{12,4},{14,6},{16,24},{18,... | collective-permute-start | bytes 1572872 | tf_op jit(solution)/shard_map/ppermute | solution.py:22
  124.2 13.5 %collective-permute-start.34 = (bf16[4,48,8,128]{3,2,1,0:T(8,128)(2,1)S(1)}, bf16[4,48,8,128]{3,2,1,0:T(8,128)(2,1)S(1)}, u32[]{:S(2)}, u32[]{:S(2)}) collective-permute-start(bf16[4,48,8,128]{3,2,1,0:T(8,128)(2,1)S(1)} %add_convert_fusion.2), channel_id=1, source_target_pairs={{0,4},{2,6},{4,0},{6,2},{8,12},{10,14},{12,8},{14,10},{16,20},{18,... | collective-permute-start | bytes 1179656 | tf_op jit(solution)/shard_map/ppermute | solution.py:22
  124.8 15.9 %collective-permute-start.33 = (bf16[4,48,8,128]{3,2,1,0:T(8,128)(2,1)S(1)}, bf16[4,48,8,128]{3,2,1,0:T(8,128)(2,1)S(1)}, u32[]{:S(2)}, u32[]{:S(2)}) collective-permute-start(bf16[4,48,8,128]{3,2,1,0:T(8,128)(2,1)S(1)} %add_convert_fusion.3), channel_id=1, source_target_pairs={{0,2},{2,0},{4,6},{6,4},{8,10},{10,8},{12,14},{14,12},{16,18},{18,... | collective-permute-start | bytes 1179656 | tf_op jit(solution)/shard_map/ppermute | solution.py:22
  130.0 16.7 %collective-permute-start.17 = (bf16[32,4096]{1,0:T(8,128)(2,1)S(1)}, bf16[32,4096]{1,0:T(8,128)(2,1)S(1)}, u32[]{:S(2)}, u32[]{:S(2)}) collective-permute-start(bf16[32,4096]{1,0:T(8,128)(2,1)S(1)} %fusion.2), channel_id=1, source_target_pairs={{0,16},{2,18},{4,20},{6,22},{8,24},{10,26},{12,28},{14,30},{16,0},... | collective-permute-start | bytes 786440 | tf_op jit(solution)/shard_map/ppermute | solution.py:22
  133.8 21.7 %collective-permute-start.30 = (bf16[48,8,128]{2,1,0:T(8,128)(2,1)S(1)}, bf16[48,8,128]{2,1,0:T(8,128)(2,1)S(1)}, u32[]{:S(2)}, u32[]{:S(2)}) collective-permute-start(bf16[48,8,128]{2,1,0:T(8,128)(2,1)S(1)} %get-tuple-element.109), channel_id=1, source_target_pairs={{0,8},{2,10},{4,12},{6,14},{8,0},{10,2},{12,4},{14,6},{16,24},{18,... | collective-permute-start | bytes 294920 | tf_op jit(solution)/shard_map/ppermute | solution.py:22
  137.8 21.3 %collective-permute-start.31 = (bf16[48,8,128]{2,1,0:T(8,128)(2,1)S(1)}, bf16[48,8,128]{2,1,0:T(8,128)(2,1)S(1)}, u32[]{:S(2)}, u32[]{:S(2)}) collective-permute-start(bf16[48,8,128]{2,1,0:T(8,128)(2,1)S(1)} %get-tuple-element.110), channel_id=1, source_target_pairs={{0,16},{2,18},{4,20},{6,22},{8,24},{10,26},{12,28},{14,30},{16,0},... | collective-permute-start | bytes 294920 | tf_op jit(solution)/shard_map/ppermute | solution.py:22
  140.7 20.8 %collective-permute-start.32 = (bf16[48,8,128]{2,1,0:T(8,128)(2,1)S(1)}, bf16[48,8,128]{2,1,0:T(8,128)(2,1)S(1)}, u32[]{:S(2)}, u32[]{:S(2)}) collective-permute-start(bf16[48,8,128]{2,1,0:T(8,128)(2,1)S(1)} %get-tuple-element.111), channel_id=1, source_target_pairs={{0,24},{2,26},{4,28},{6,30},{8,16},{10,18},{12,20},{14,22},{16,8},... | collective-permute-start | bytes 294920 | tf_op jit(solution)/shard_map/ppermute | solution.py:22
  142.7 30.7 %collective-permute-start.23 = (bf16[32,4096]{1,0:T(8,128)(2,1)S(1)}, bf16[32,4096]{1,0:T(8,128)(2,1)S(1)}, u32[]{:S(2)}, u32[]{:S(2)}) collective-permute-start(bf16[32,4096]{1,0:T(8,128)(2,1)S(1)} %fusion.3), channel_id=1, source_target_pairs={{0,16},{2,18},{4,20},{6,22},{8,24},{10,26},{12,28},{14,30},{16,0},... | collective-permute-start | bytes 786440 | tf_op jit(solution)/shard_map/ppermute | solution.py:22
  146.7 14.8 %collective-permute-start.35 = (bf16[48,8,128]{2,1,0:T(8,128)(2,1)S(1)}, bf16[48,8,128]{2,1,0:T(8,128)(2,1)S(1)}, u32[]{:S(2)}, u32[]{:S(2)}) collective-permute-start(bf16[48,8,128]{2,1,0:T(8,128)(2,1)S(1)} %get-tuple-element.114), channel_id=1, source_target_pairs={{0,8},{2,10},{4,12},{6,14},{8,0},{10,2},{12,4},{14,6},{16,24},{18,... | collective-permute-start | bytes 294920 | tf_op jit(solution)/shard_map/ppermute | solution.py:22
  155.5 14.9 %collective-permute-start.36 = (bf16[48,8,128]{2,1,0:T(8,128)(2,1)S(1)}, bf16[48,8,128]{2,1,0:T(8,128)(2,1)S(1)}, u32[]{:S(2)}, u32[]{:S(2)}) collective-permute-start(bf16[48,8,128]{2,1,0:T(8,128)(2,1)S(1)} %get-tuple-element.115), channel_id=1, source_target_pairs={{0,16},{2,18},{4,20},{6,22},{8,24},{10,26},{12,28},{14,30},{16,0},... | collective-permute-start | bytes 294920 | tf_op jit(solution)/shard_map/ppermute | solution.py:22
  159.1 11.3 %collective-permute-start.37 = (bf16[48,8,128]{2,1,0:T(8,128)(2,1)S(1)}, bf16[48,8,128]{2,1,0:T(8,128)(2,1)S(1)}, u32[]{:S(2)}, u32[]{:S(2)}) collective-permute-start(bf16[48,8,128]{2,1,0:T(8,128)(2,1)S(1)} %get-tuple-element.116), channel_id=1, source_target_pairs={{0,24},{2,26},{4,28},{6,30},{8,16},{10,18},{12,20},{14,22},{16,8},... | collective-permute-start | bytes 294920 | tf_op jit(solution)/shard_map/ppermute | solution.py:22
  (10 other events, 102.6 us)

commit v6 on v5

--- a/solution.py
+++ b/solution.py
@@ -58,8 +58,9 @@
     return items
 
 
-def whole(shape):
-    return pl.BlockSpec(shape, lambda *_: (0,) * len(shape), pipeline_mode=pl.Buffered(1))
+def whole(shape, at=None):
+    at = (0,) * len(shape) if at is None else at
+    return pl.BlockSpec(shape, lambda *_: at, pipeline_mode=pl.Buffered(1))
 
 
 def pack(table, tiles, *refs, blocks, slot_count):
@@ -370,25 +371,32 @@
         weight_list = [items[at] for at in range(near)]
         weight_parts = [(at, 0, far) for at in range(near)]
 
-    if far == 4:
-        x_source, g_source = after((tokens, out_grad), held)
-        x_items[2 * near] = swap(x_source, "dp", 2 * near)
+    pairs = {}
+    if staged:
+        pair, g_source = after((jnp.concatenate([tokens, out_grad]), out_grad), held)
+        pairs[2 * near] = swap(pair, "dp", 2 * near)
         g_items[near] = swap(g_source, "dp", near)
-        x_back, g_source = after((x_items[2 * near], g_source), pass_1, pass_2, x_items[2 * near])
-        x_items[3 * near] = swap(x_back, "dp", near)
-        g_items[2 * near] = swap(g_source, "dp", 2 * near)
-        g_items[3 * near] = swap(g_items[2 * near], "dp", near)
-        weight_list = list(after(tuple(weight_list), x_items[2 * near]))
-    elif far == 2:
-        g_items[near] = swap(out_grad, "dp", near)
+        source = after(pairs[2 * near], pass_1, pass_2, g_items[near])
+        pairs[3 * near] = swap(source, "dp", near)
+        g_core[near] = swap(g_items[near], "tensor", 1)
+        pairs_core = {2 * near: swap(pairs[2 * near], "tensor", 1)}
+        last = after(pairs[3 * near], *weight_list[3:], g_core[near], pairs_core[2 * near])
+        pairs_core[3 * near] = swap(last, "tensor", 1)
+    else:
+        for items, value in ((x_items, tokens), (g_items, out_grad)):
+            items.update(gather({0: value}, "dp", far_strides))
 
     far_order = [at * near for at in range(0, far, 2)] + [at * near for at in range(1, far, 2)]
     if staged:
         order = [at * near for at in range(far)]
-        x_late = swap(jnp.concatenate([x_items[at] for at in order[2:]]), "tensor", 1)
-        g_late = swap(jnp.concatenate([g_items[at] for at in order[1:]]), "tensor", 1)
-        x_list = [x_items[at] for at in order] + [x_core[at] for at in order[:2]] + [x_late]
-        g_list = [g_items[at] for at in order] + [g_core[0], g_late]
+        token_shape = (own_rows, features)
+        singles = [x_items[0], x_items[near], x_core[0], x_core[near]]
+        doubles = [pairs[at] for at in order[2:]] + [pairs_core[at] for at in order[2:]]
+        x_list = singles[:2] + doubles[:2] + singles[2:] + doubles[2:]
+        singles = [g_items[0], g_items[near], g_core[0], g_core[near]]
+        g_list = singles[:2] + doubles[:2] + singles[2:] + doubles[2:]
+        x_specs = [whole(token_shape)] * len(x_list)
+        g_specs = [whole(token_shape, (1 if at in (2, 3, 6, 7) else 0, 0)) for at in range(len(g_list))]
         parts = [(other, far_order.index(at)) for other in (False, True) for at in order]
         other_parts = [(at, 1) for at in far_order]
     else:
@@ -402,6 +410,7 @@
                     other_parts.append((at, other))
                 x_list.append(x_parts[other])
                 g_list.append(g_parts[other])
+        x_specs = g_specs = [whole((own_rows, features))] * len(x_list)
 
     group_rows = far * tensor_size * own_rows
     own_shape = (far, own_rows, features)
@@ -423,8 +432,6 @@
         cost=10_000_000,
         vmem=24,
     )
-    if far == 4:
-        x_list = list(after(tuple(x_list), g_items[2 * near]))
     def specs_of(*groups):
         return [whole(one.shape) for group in groups for one in group]
 
@@ -439,7 +446,7 @@
         functools.partial(ahead, token_count=len(x_list), slot_count=slot_count, parts=parts),
         table,
         [*x_list, tiles],
-        specs_of(x_list, [tiles]),
+        x_specs + specs_of([tiles]),
         specs_of(middle_shapes, sum_shapes),
         middle_shapes + sum_shapes,
         scratch=[pltpu.VMEM((group_rows, features), F32)],
@@ -484,7 +491,7 @@
         ),
         table,
         [*g_list, tiles, *middle],
-        specs_of(g_list, [tiles], middle),
+        g_specs + specs_of([tiles], middle),
         specs_of(sum_shapes, part_shapes),
         sum_shapes + part_shapes,
         scratch=[pltpu.VMEM((group_rows, features), F32), pltpu.VMEM(tiles_shape, F32)],
@@ -513,20 +520,22 @@
         return [sums[0]] + [swap(sums[at], "dp", at * near) for at in range(1, far)]
 
     if staged:
+        ffn_got = swap(ffn_near, "dp", near)
+        tile_terms, input_other = after((tile_terms, input_other), ffn_got)
         first_parts, second_parts = tile_terms
         first_got, second_got = halves(first_parts), halves(second_parts)
-        ffn_got = swap(ffn_near, "dp", near)
         ffn_last = to_far(ffn_own, ffn_core, ffn_got)
         ffn_far = swap(ffn_last, "dp", 2 * near)
         input_core, input_near = to_near(input_own, input_other)
         input_got = swap(input_near, "dp", near)
         first_sums = summed(first_parts, *folded(first_parts, *first_got))
         second_folded = after(folded(second_parts, *second_got), input_near)
-        first_back = sent_back(after(tuple(first_sums), *second_folded))
-        input_last = to_far(input_own, input_core, input_got)
+        first_back = sent_back(after(tuple(first_sums), *second_folded, input_got))
+        input_last = after(to_far(input_own, input_core, input_got), ffn_far)
         input_far = swap(input_last, "dp", 2 * near)
         second_sums = summed(second_parts, *second_folded)
         back = first_back + sent_back(after(tuple(second_sums), input_last))
+        back = list(after(tuple(back), input_far))
         ffn_rows = add(ffn_own[0], ffn_core[0], ffn_got[0], ffn_far)
         input_rows = add(input_own[0], input_core[0], input_got[0], input_far)
     else:

time: 175 us -> 170 us (0.971)
  starting transfers between devices: 51.9 us -> 36.2 us
  waiting for transfers between devices: 89.2 us -> 94.4 us
  local copies, waits for them, and re-layouts: 2.88 us -> 5.82 us
  Pallas kernels: 24.1 us -> 26.6 us
    ppermute x38 -> x37, starting transfers between devices: 51.9 us -> 36.2 us  [swap(): return lax.ppermute(value, axis, [(at, at ^ stride) for at in range(size)])]
    ppermute x38 -> x37, waiting for transfers between devices: 89.2 us -> 94.4 us  [swap(): return lax.ppermute(value, axis, [(at, at ^ stride) for at in range(size)])]
    unnamed x8 -> x10, local copies, waits for them, and re-layouts: 1.23 us -> 4.17 us
    pallas_call x5, Pallas kernels: 24.1 us -> 26.6 us  [call(): pl.pallas_call(kernel, grid_spec=pltpu.PrefetchScalarGridSpec(num_scalar_...]
  transfers between devices with their start and end apart: 38 -> 37, of which waited for: 19 -> 17; matrix products, arithmetic and copies ran while one was open for 3% -> 3% of each run, Pallas kernels for 4% -> 9%
where the time goes in v6:
time: 170 us; the launch traced here: 169 us
  waiting for transfers between devices  94.4 us (56%)
  starting transfers between devices  36.2 us (21%)
  Pallas kernels  26.6 us (16%)
  local copies, waits for them, and re-layouts  5.82 us (3%)
  other arithmetic  5.18 us (3%)
    ppermute x37, waiting for transfers between devices, swap(): return lax.ppermute(value, axis, [(at, at ^ stride) for at in range(size)])  94.4 us
    ppermute x37, starting transfers between devices, swap(): return lax.ppermute(value, axis, [(at, at ^ stride) for at in range(size)])  36.2 us
    pallas_call x5, Pallas kernels, call(): pl.pallas_call(kernel, grid_spec=pltpu.PrefetchScalarGridSpec(num_scalar_...  26.6 us
    unnamed x10, local copies, waits for them, and re-layouts  4.17 us
  transfers between devices with their start and end apart: 37, of which 17 were waited for; matrix products, arithmetic and copies ran while one was open for 3% of the time, Pallas kernels for 9%

profile of v6, /device:TPU:0, one launch (start us, length us, event | category | flops | bytes accessed | tf_op | source)
XLA Modules:
  0.0 169.2 jit_solution(11311971022278899214)
XLA Ops:
  0.7 3.1 %collective-permute-start = (bf16[32,4096]{1,0:T(8,128)(2,1)}, bf16[32,4096]{1,0:T(8,128)(2,1)S(1)}, u32[]{:S(2)}, u32[]{:S(2)}) collective-permute-start(bf16[32,4096]{1,0:T(8,128)(2,1)} %refs_0_.2), channel_id=1, source_target_pairs={{0,8},{2,10},{4,12},{6,14},{8,0},{10,2},{12,4},{14,6},{16,24},{18,... | collective-permute-start | bytes 786440 | tf_op jit(solution)/shard_map/ppermute | solution.py:22
  9.0 1.6 shard_map.76
  10.6 3.4 %collective-permute-start.3 = (bf16[96,8,128]{2,1,0:T(8,128)(2,1)S(1)}, bf16[96,8,128]{2,1,0:T(8,128)(2,1)S(1)}, u32[]{:S(2)}, u32[]{:S(2)}) collective-permute-start(bf16[96,8,128]{2,1,0:T(8,128)(2,1)S(1)} %get-tuple-element.75), channel_id=1, source_target_pairs={{0,24},{2,26},{4,28},{6,30},{8,16},{10,18},{12,20},{14,22},{16,8},... | collective-permute-start | bytes 589832 | tf_op jit(solution)/shard_map/ppermute | solution.py:22
  15.6 4.8 %collective-permute-done.3 = bf16[96,8,128]{2,1,0:T(8,128)(2,1)S(1)} collective-permute-done((bf16[96,8,128]{2,1,0:T(8,128)(2,1)S(1)}, bf16[96,8,128]{2,1,0:T(8,128)(2,1)S(1)}, u32[]{:S(2)}, u32[]{:S(2)}) %collective-permute-start.3) | collective-permute-done | bytes 196640 | tf_op jit(solution)/shard_map/ppermute | solution.py:22
  20.4 10.1 %collective-permute-done.2 = bf16[96,8,128]{2,1,0:T(8,128)(2,1)S(1)} collective-permute-done((bf16[96,8,128]{2,1,0:T(8,128)(2,1)S(1)}, bf16[96,8,128]{2,1,0:T(8,128)(2,1)S(1)}, u32[]{:S(2)}, u32[]{:S(2)}) %collective-permute-start.2) | collective-permute-done | bytes 196640 | tf_op jit(solution)/shard_map/ppermute | solution.py:22
  30.7 1.6 collective-permute-start.8
  32.3 1.5 collective-permute-start.9
  33.9 3.2 %collective-permute-start.10 = (bf16[32,4096]{1,0:T(8,128)(2,1)S(1)}, bf16[32,4096]{1,0:T(8,128)(2,1)S(1)}, u32[]{:S(2)}, u32[]{:S(2)}) collective-permute-start(bf16[32,4096]{1,0:T(8,128)(2,1)S(1)} %copy-done.3), channel_id=1, source_target_pairs={{0,8},{2,10},{4,12},{6,14},{8,0},{10,2},{12,4},{14,6},{16,24},{18,... | collective-permute-start | bytes 786440 | tf_op jit(solution)/shard_map/ppermute | solution.py:22
  37.1 21.1 %collective-permute-done.7.refs_2_ = bf16[64,4096]{1,0:T(8,128)(2,1)S(1)} collective-permute-done((bf16[64,4096]{1,0:T(8,128)(2,1)S(1)}, bf16[64,4096]{1,0:T(8,128)(2,1)S(1)}, u32[]{:S(2)}, u32[]{:S(2)}) %collective-permute-start.7) | collective-permute-done | bytes 524320 | tf_op jit(solution)/shard_map/ppermute | solution.py:22
  59.5 1.5 collective-permute-done.15.refs_5_
  61.0 8.9 %collective-permute-done.13.refs_3_ = bf16[2,96,8,128]{3,2,1,0:T(8,128)(2,1)S(1)} collective-permute-done((bf16[2,96,8,128]{3,2,1,0:T(8,128)(2,1)S(1)}, bf16[2,96,8,128]{3,2,1,0:T(8,128)(2,1)S(1)}, u32[]{:S(2)}, u32[]{:S(2)}) %collective-permute-start.13) | collective-permute-done | bytes 393248 | tf_op jit(solution)/shard_map/ppermute | solution.py:22
  70.2 2.5 %collective-permute-done.11.refs_3_ = bf16[64,4096]{1,0:T(8,128)(2,1)S(1)} collective-permute-done((bf16[64,4096]{1,0:T(8,128)(2,1)S(1)}, bf16[64,4096]{1,0:T(8,128)(2,1)S(1)}, u32[]{:S(2)}, u32[]{:S(2)}) %collective-permute-start.11) | collective-permute-done | bytes 524320 | tf_op jit(solution)/shard_map/ppermute | solution.py:22
  72.7 2.2 %shard_map.77.refs_8_ = bf16[96,128,128]{2,1,0:T(8,128)(2,1)S(1)} custom-call(s32[17,56]{1,0:T(8,128)S(1)} %pad_add_fusion.table, bf16[4,96,8,128]{3,2,1,0:T(8,128)(2,1)S(1)} %pad_maximum_fusion.refs_0_, bf16[4,96,8,128]{3,2,1,0:T(8,128)(2,1)S(1)} %collective-permute-done.8.refs_1_, bf16[4,96,8,128]{3,2,1,0:T(8,128)(2,1)S(1)} %collective-permute-done.9.refs_2_, ...), custom_call_target="tpu_custom_call" | custom-call | bytes 10000000 | tf_op jit(solution)/shard_map/pallas_call | solution.py:264
  74.9 1.6 copy-done
  76.5 8.2 %shard_map.78 = (bf16[4096,256]{1,0:T(8,128)(2,1)S(1)}, f32[14,256,128]{2,1,0:T(8,128)S(1)}, f32[14,256,128]{2,1,0:T(8,128)S(1)}, bf16[14,128,256]{2,1,0:T(8,128...) custom-call(s32[17,56]{1,0:T(8,128)S(1)} %pad_add_fusion.table, ...), custom_call_target="tpu_custom_call" | custom-call | bytes 30000000 | tf_op jit(solution)/shard_map/pallas_call | solution.py:264
  86.6 2.3 %collective-permute-done.17 = bf16[4,32,4096]{2,1,0:T(8,128)(2,1)S(1)} collective-permute-done((bf16[4,32,4096]{2,1,0:T(8,128)(2,1)S(1)}, bf16[4,32,4096]{2,1,0:T(8,128)(2,1)S(1)}, u32[]{:S(2)}, u32[]{:S(2)}) %collective-permute-start.17) | collective-permute-done | bytes 1048608 | tf_op jit(solution)/shard_map/ppermute | solution.py:22
  89.4 11.6 %shard_map.79 = (bf16[4,32,4096]{2,1,0:T(8,128)(2,1)S(1)}, bf16[4,32,4096]{2,1,0:T(8,128)(2,1)S(1)}, bf16[4,48,8,128]{3,2,1,0:T(8,128)(2,1)S(1)}, bf16[4,48,8,12...) custom-call(s32[17,56]{1,0:T(8,128)S(1)} %pad_add_fusion.table, ...), custom_call_target="tpu_custom_call" | custom-call | bytes 40000000 | tf_op jit(solution)/shard_map/pallas_call | solution.py:264
  100.9 2.3 %collective-permute-done.18 = bf16[2,32,4096]{2,1,0:T(8,128)(2,1)S(1)} collective-permute-done((bf16[2,32,4096]{2,1,0:T(8,128)(2,1)S(1)}, bf16[2,32,4096]{2,1,0:T(8,128)(2,1)S(1)}, u32[]{:S(2)}, u32[]{:S(2)}) %collective-permute-start.18) | collective-permute-done | bytes 524320 | tf_op jit(solution)/shard_map/ppermute | solution.py:22
  104.3 1.5 collective-permute-start.27
  105.8 1.5 collective-permute-start.28
  107.3 3.5 %collective-permute-done.25 = bf16[2,48,8,128]{3,2,1,0:T(8,128)(2,1)S(1)} collective-permute-done((bf16[2,48,8,128]{3,2,1,0:T(8,128)(2,1)S(1)}, bf16[2,48,8,128]{3,2,1,0:T(8,128)(2,1)S(1)}, u32[]{:S(2)}, u32[]{:S(2)}) %collective-permute-start.25) | collective-permute-done | bytes 196640 | tf_op jit(solution)/shard_map/ppermute | solution.py:22
  111.6 1.6 collective-permute-start.24
  113.1 2.6 %collective-permute-done.27 = bf16[2,48,8,128]{3,2,1,0:T(8,128)(2,1)S(1)} collective-permute-done((bf16[2,48,8,128]{3,2,1,0:T(8,128)(2,1)S(1)}, bf16[2,48,8,128]{3,2,1,0:T(8,128)(2,1)S(1)}, u32[]{:S(2)}, u32[]{:S(2)}) %collective-permute-start.27) | collective-permute-done | bytes 196640 | tf_op jit(solution)/shard_map/ppermute | solution.py:22
  116.8 1.5 collective-permute-start.32
  118.4 5.7 %collective-permute-done.26 = bf16[4,48,8,128]{3,2,1,0:T(8,128)(2,1)S(1)} collective-permute-done((bf16[4,48,8,128]{3,2,1,0:T(8,128)(2,1)S(1)}, bf16[4,48,8,128]{3,2,1,0:T(8,128)(2,1)S(1)}, u32[]{:S(2)}, u32[]{:S(2)}) %collective-permute-start.26) | collective-permute-done | bytes 393248 | tf_op jit(solution)/shard_map/ppermute | solution.py:22
  125.3 6.9 %collective-permute-done.33 = bf16[4,48,8,128]{3,2,1,0:T(8,128)(2,1)S(1)} collective-permute-done((bf16[4,48,8,128]{3,2,1,0:T(8,128)(2,1)S(1)}, bf16[4,48,8,128]{3,2,1,0:T(8,128)(2,1)S(1)}, u32[]{:S(2)}, u32[]{:S(2)}) %collective-permute-start.33) | collective-permute-done | bytes 393248 | tf_op jit(solution)/shard_map/ppermute | solution.py:22
  132.7 2.4 %collective-permute-start.30 = (bf16[48,8,128]{2,1,0:T(8,128)(2,1)S(1)}, bf16[48,8,128]{2,1,0:T(8,128)(2,1)S(1)}, u32[]{:S(2)}, u32[]{:S(2)}) collective-permute-start(bf16[48,8,128]{2,1,0:T(8,128)(2,1)S(1)} %get-tuple-element.118), channel_id=1, source_target_pairs={{0,16},{2,18},{4,20},{6,22},{8,24},{10,26},{12,28},{14,30},{16,0},... | collective-permute-start | bytes 294920 | tf_op jit(solution)/shard_map/ppermute | solution.py:22
  135.2 10.3 %collective-permute-done.19 = bf16[32,4096]{1,0:T(8,128)(2,1)S(1)} collective-permute-done((bf16[32,4096]{1,0:T(8,128)(2,1)S(1)}, bf16[32,4096]{1,0:T(8,128)(2,1)S(1)}, u32[]{:S(2)}, u32[]{:S(2)}) %collective-permute-start.19) | collective-permute-done | bytes 262176 | tf_op jit(solution)/shard_map/ppermute | solution.py:22
  145.6 3.0 %collective-permute-start.31 = (bf16[48,8,128]{2,1,0:T(8,128)(2,1)S(1)}, bf16[48,8,128]{2,1,0:T(8,128)(2,1)S(1)}, u32[]{:S(2)}, u32[]{:S(2)}) collective-permute-start(bf16[48,8,128]{2,1,0:T(8,128)(2,1)S(1)} %get-tuple-element.119), channel_id=1, source_target_pairs={{0,24},{2,26},{4,28},{6,30},{8,16},{10,18},{12,20},{14,22},{16,8},... | collective-permute-start | bytes 294920 | tf_op jit(solution)/shard_map/ppermute | solution.py:22
  150.6 2.4 %collective-permute-start.36 = (bf16[48,8,128]{2,1,0:T(8,128)(2,1)S(1)}, bf16[48,8,128]{2,1,0:T(8,128)(2,1)S(1)}, u32[]{:S(2)}, u32[]{:S(2)}) collective-permute-start(bf16[48,8,128]{2,1,0:T(8,128)(2,1)S(1)} %get-tuple-element.124), channel_id=1, source_target_pairs={{0,24},{2,26},{4,28},{6,30},{8,16},{10,18},{12,20},{14,22},{16,8},... | collective-permute-start | bytes 294920 | tf_op jit(solution)/shard_map/ppermute | solution.py:22
  154.4 10.9 %collective-permute-done.35.refs_6_ = bf16[48,8,128]{2,1,0:T(8,128)(2,1)S(1)} collective-permute-done((bf16[48,8,128]{2,1,0:T(8,128)(2,1)S(1)}, bf16[48,8,128]{2,1,0:T(8,128)(2,1)S(1)}, u32[]{:S(2)}, u32[]{:S(2)}) %collective-permute-start.35) | collective-permute-done | bytes 98336 | tf_op jit(solution)/shard_map/ppermute | solution.py:22
  165.3 3.0 %shard_map.80 = bf16[8,9,56,128]{3,2,1,0:T(8,128)(2,1)} custom-call(s32[17,56]{1,0:T(8,128)S(1)} %pad_add_fusion.table, bf16[48,8,128]{2,1,0:T(8,128)(2,1)S(1)} %get-tuple-element.125.refs_0_, bf16[48,8,128]{2,1,0:T(8,128)(2,1)S(1)} %collective-permute-done.29.refs_1_, bf16[48,8,128]{2,1,0:T(8,128)(2,1)S(1)} %collective-permute-done.30.refs_2_, ...), custom_call_target="tpu_custom_call" | custom-call | bytes 2000000 | tf_op jit(solution)/shard_map/pallas_call | solution.py:264
  (91 shorter events, 20.0 us)
Async XLA Ops:
  0.7 10.0 %collective-permute-start = (bf16[32,4096]{1,0:T(8,128)(2,1)}, bf16[32,4096]{1,0:T(8,128)(2,1)S(1)}, u32[]{:S(2)}, u32[]{:S(2)}) collective-permute-start(bf16[32,4096]{1,0:T(8,128)(2,1)} %refs_0_.2), channel_id=1, source_target_pairs={{0,8},{2,10},{4,12},{6,14},{8,0},{10,2},{12,4},{14,6},{16,24},{18,... | collective-permute-start | bytes 786440 | tf_op jit(solution)/shard_map/ppermute | solution.py:22
  10.6 9.8 %collective-permute-start.3 = (bf16[96,8,128]{2,1,0:T(8,128)(2,1)S(1)}, bf16[96,8,128]{2,1,0:T(8,128)(2,1)S(1)}, u32[]{:S(2)}, u32[]{:S(2)}) collective-permute-start(bf16[96,8,128]{2,1,0:T(8,128)(2,1)S(1)} %get-tuple-element.75), channel_id=1, source_target_pairs={{0,24},{2,26},{4,28},{6,30},{8,16},{10,18},{12,20},{14,22},{16,8},... | collective-permute-start | bytes 589832 | tf_op jit(solution)/shard_map/ppermute | solution.py:22
  14.0 16.5 %collective-permute-start.2 = (bf16[96,8,128]{2,1,0:T(8,128)(2,1)S(1)}, bf16[96,8,128]{2,1,0:T(8,128)(2,1)S(1)}, u32[]{:S(2)}, u32[]{:S(2)}) collective-permute-start(bf16[96,8,128]{2,1,0:T(8,128)(2,1)S(1)} %get-tuple-element.74), channel_id=1, source_target_pairs={{0,16},{2,18},{4,20},{6,22},{8,24},{10,26},{12,28},{14,30},{16,0},... | collective-permute-start | bytes 589832 | tf_op jit(solution)/shard_map/ppermute | solution.py:22
  14.0 16.5 %collective-permute-start.1 = (bf16[96,8,128]{2,1,0:T(8,128)(2,1)S(1)}, bf16[96,8,128]{2,1,0:T(8,128)(2,1)S(1)}, u32[]{:S(2)}, u32[]{:S(2)}) collective-permute-start(bf16[96,8,128]{2,1,0:T(8,128)(2,1)S(1)} %get-tuple-element.73), channel_id=1, source_target_pairs={{0,8},{2,10},{4,12},{6,14},{8,0},{10,2},{12,4},{14,6},{16,24},{18,... | collective-permute-start | bytes 589832 | tf_op jit(solution)/shard_map/ppermute | solution.py:22
  15.1 15.6 %collective-permute-start.4 = (bf16[32,4096]{1,0:T(8,128)(2,1)}, bf16[32,4096]{1,0:T(8,128)(2,1)S(1)}, u32[]{:S(2)}, u32[]{:S(2)}) collective-permute-start(bf16[32,4096]{1,0:T(8,128)(2,1)} %refs_0_.2), channel_id=1, source_target_pairs={{0,1},{1,0},{2,3},{3,2},{4,5},{5,4},{6,7},{7,6},{8,9},{9,8},{10,11... | collective-permute-start | bytes 786440 | tf_op jit(solution)/shard_map/ppermute | solution.py:22
  15.1 15.6 %collective-permute-start.6 = (bf16[32,4096]{1,0:T(8,128)(2,1)}, bf16[32,4096]{1,0:T(8,128)(2,1)S(1)}, u32[]{:S(2)}, u32[]{:S(2)}) collective-permute-start(bf16[32,4096]{1,0:T(8,128)(2,1)} %refs_0_.3), channel_id=1, source_target_pairs={{0,1},{1,0},{2,3},{3,2},{4,5},{5,4},{6,7},{7,6},{8,9},{9,8},{10,11... | collective-permute-start | bytes 786440 | tf_op jit(solution)/shard_map/ppermute | solution.py:22
  20.4 10.3 %collective-permute-start.5 = (bf16[32,4096]{1,0:T(8,128)(2,1)S(1)}, bf16[32,4096]{1,0:T(8,128)(2,1)S(1)}, u32[]{:S(2)}, u32[]{:S(2)}) collective-permute-start(bf16[32,4096]{1,0:T(8,128)(2,1)S(1)} %collective-permute-done.refs_1_), channel_id=1, source_target_pairs={{0,1},{1,0},{2,3},{3,2},{4,5},{5,4},{6,7},{7,6},{8,9},{9,8},{10,11... | collective-permute-start | bytes 786440 | tf_op jit(solution)/shard_map/ppermute | solution.py:22
  30.7 27.5 %collective-permute-start.8 = (bf16[4,96,8,128]{3,2,1,0:T(8,128)(2,1)S(1)}, bf16[4,96,8,128]{3,2,1,0:T(8,128)(2,1)S(1)}, u32[]{:S(2)}, u32[]{:S(2)}) collective-permute-start(bf16[4,96,8,128]{3,2,1,0:T(8,128)(2,1)S(1)} %pad_maximum_fusion.refs_0_), channel_id=1, source_target_pairs={{0,2},{2,0},{4,6},{6,4},{8,10},{10,8},{12,14},{14,12},{16,18},{18,... | collective-permute-start | bytes 2359304 | tf_op jit(solution)/shard_map/ppermute | solution.py:22
  32.3 26.0 %collective-permute-start.9 = (bf16[4,96,8,128]{3,2,1,0:T(8,128)(2,1)S(1)}, bf16[4,96,8,128]{3,2,1,0:T(8,128)(2,1)S(1)}, u32[]{:S(2)}, u32[]{:S(2)}) collective-permute-start(bf16[4,96,8,128]{3,2,1,0:T(8,128)(2,1)S(1)} %pad_maximum_fusion.refs_0_), channel_id=1, source_target_pairs={{0,4},{2,6},{4,0},{6,2},{8,12},{10,14},{12,8},{14,10},{16,20},{18,... | collective-permute-start | bytes 2359304 | tf_op jit(solution)/shard_map/ppermute | solution.py:22
  33.8 24.4 %collective-permute-start.7 = (bf16[64,4096]{1,0:T(8,128)(2,1)S(1)}, bf16[64,4096]{1,0:T(8,128)(2,1)S(1)}, u32[]{:S(2)}, u32[]{:S(2)}) collective-permute-start(bf16[64,4096]{1,0:T(8,128)(2,1)S(1)} %pad_maximum_fusion.1), channel_id=1, source_target_pairs={{0,16},{2,18},{4,20},{6,22},{8,24},{10,26},{12,28},{14,30},{16,0},... | collective-permute-start | bytes 1572872 | tf_op jit(solution)/shard_map/ppermute | solution.py:22
  33.9 24.4 %collective-permute-start.10 = (bf16[32,4096]{1,0:T(8,128)(2,1)S(1)}, bf16[32,4096]{1,0:T(8,128)(2,1)S(1)}, u32[]{:S(2)}, u32[]{:S(2)}) collective-permute-start(bf16[32,4096]{1,0:T(8,128)(2,1)S(1)} %copy-done.3), channel_id=1, source_target_pairs={{0,8},{2,10},{4,12},{6,14},{8,0},{10,2},{12,4},{14,6},{16,24},{18,... | collective-permute-start | bytes 786440 | tf_op jit(solution)/shard_map/ppermute | solution.py:22
  58.3 14.4 %collective-permute-start.11 = (bf16[64,4096]{1,0:T(8,128)(2,1)S(1)}, bf16[64,4096]{1,0:T(8,128)(2,1)S(1)}, u32[]{:S(2)}, u32[]{:S(2)}) collective-permute-start(bf16[64,4096]{1,0:T(8,128)(2,1)S(1)} %collective-permute-done.7.refs_2_), channel_id=1, source_target_pairs={{0,8},{2,10},{4,12},{6,14},{8,0},{10,2},{12,4},{14,6},{16,24},{18,... | collective-permute-start | bytes 1572872 | tf_op jit(solution)/shard_map/ppermute | solution.py:22
  58.4 11.6 %collective-permute-start.13 = (bf16[2,96,8,128]{3,2,1,0:T(8,128)(2,1)S(1)}, bf16[2,96,8,128]{3,2,1,0:T(8,128)(2,1)S(1)}, u32[]{:S(2)}, u32[]{:S(2)}) collective-permute-start(bf16[2,96,8,128]{3,2,1,0:T(8,128)(2,1)S(1)} %slice.183), channel_id=1, source_target_pairs={{0,4},{2,6},{4,0},{6,2},{8,12},{10,14},{12,8},{14,10},{16,20},{18,... | collective-permute-start | bytes 1179656 | tf_op jit(solution)/shard_map/ppermute | solution.py:22
  59.0 11.2 %collective-permute-start.14 = (bf16[2,96,8,128]{3,2,1,0:T(8,128)(2,1)S(1)}, bf16[2,96,8,128]{3,2,1,0:T(8,128)(2,1)S(1)}, u32[]{:S(2)}, u32[]{:S(2)}) collective-permute-start(bf16[2,96,8,128]{3,2,1,0:T(8,128)(2,1)S(1)} %slice.184), channel_id=1, source_target_pairs={{0,2},{2,0},{4,6},{6,4},{8,10},{10,8},{12,14},{14,12},{16,18},{18,... | collective-permute-start | bytes 1179656 | tf_op jit(solution)/shard_map/ppermute | solution.py:22
  89.0 14.3 %collective-permute-start.18 = (bf16[2,32,4096]{2,1,0:T(8,128)(2,1)S(1)}, bf16[2,32,4096]{2,1,0:T(8,128)(2,1)S(1)}, u32[]{:S(2)}, u32[]{:S(2)}) collective-permute-start(bf16[2,32,4096]{2,1,0:T(8,128)(2,1)S(1)} %add_convert_fusion.1), channel_id=1, source_target_pairs={{0,8},{2,10},{4,12},{6,14},{8,0},{10,2},{12,4},{14,6},{16,24},{18,... | collective-permute-start | bytes 1572872 | tf_op jit(solution)/shard_map/ppermute | solution.py:22
  103.2 7.5 %collective-permute-start.25 = (bf16[2,48,8,128]{3,2,1,0:T(8,128)(2,1)S(1)}, bf16[2,48,8,128]{3,2,1,0:T(8,128)(2,1)S(1)}, u32[]{:S(2)}, u32[]{:S(2)}) collective-permute-start(bf16[2,48,8,128]{3,2,1,0:T(8,128)(2,1)S(1)} %get-tuple-element.109), channel_id=1, source_target_pairs={{0,2},{2,0},{4,6},{6,4},{8,10},{10,8},{12,14},{14,12},{16,18},{18,... | collective-permute-start | bytes 589832 | tf_op jit(solution)/shard_map/ppermute | solution.py:22
  103.8 12.1 %collective-permute-start.20 = (bf16[4,32,4096]{2,1,0:T(8,128)(2,1)S(1)}, bf16[4,32,4096]{2,1,0:T(8,128)(2,1)S(1)}, u32[]{:S(2)}, u32[]{:S(2)}) collective-permute-start(bf16[4,32,4096]{2,1,0:T(8,128)(2,1)S(1)} %get-tuple-element.103), channel_id=1, source_target_pairs={{0,1},{1,0},{2,3},{3,2},{4,5},{5,4},{6,7},{7,6},{8,9},{9,8},{10,11... | collective-permute-start | bytes 3145736 | tf_op jit(solution)/shard_map/ppermute | solution.py:22
  103.8 7.7 %collective-permute-start.23 = (bf16[2,48,8,128]{3,2,1,0:T(8,128)(2,1)S(1)}, bf16[2,48,8,128]{3,2,1,0:T(8,128)(2,1)S(1)}, u32[]{:S(2)}, u32[]{:S(2)}) collective-permute-start(bf16[2,48,8,128]{3,2,1,0:T(8,128)(2,1)S(1)} %get-tuple-element.107), channel_id=1, source_target_pairs={{0,4},{2,6},{4,0},{6,2},{8,12},{10,14},{12,8},{14,10},{16,20},{18,... | collective-permute-start | bytes 589832 | tf_op jit(solution)/shard_map/ppermute | solution.py:22
  104.3 11.4 %collective-permute-start.27 = (bf16[2,48,8,128]{3,2,1,0:T(8,128)(2,1)S(1)}, bf16[2,48,8,128]{3,2,1,0:T(8,128)(2,1)S(1)}, u32[]{:S(2)}, u32[]{:S(2)}) collective-permute-start(bf16[2,48,8,128]{3,2,1,0:T(8,128)(2,1)S(1)} %get-tuple-element.111), channel_id=1, source_target_pairs={{0,4},{2,6},{4,0},{6,2},{8,12},{10,14},{12,8},{14,10},{16,20},{18,... | collective-permute-start | bytes 589832 | tf_op jit(solution)/shard_map/ppermute | solution.py:22
  105.8 10.0 %collective-permute-start.28 = (bf16[2,48,8,128]{3,2,1,0:T(8,128)(2,1)S(1)}, bf16[2,48,8,128]{3,2,1,0:T(8,128)(2,1)S(1)}, u32[]{:S(2)}, u32[]{:S(2)}) collective-permute-start(bf16[2,48,8,128]{3,2,1,0:T(8,128)(2,1)S(1)} %get-tuple-element.113), channel_id=1, source_target_pairs={{0,2},{2,0},{4,6},{6,4},{8,10},{10,8},{12,14},{14,12},{16,18},{18,... | collective-permute-start | bytes 589832 | tf_op jit(solution)/shard_map/ppermute | solution.py:22
  110.8 13.3 %collective-permute-start.26 = (bf16[4,48,8,128]{3,2,1,0:T(8,128)(2,1)S(1)}, bf16[4,48,8,128]{3,2,1,0:T(8,128)(2,1)S(1)}, u32[]{:S(2)}, u32[]{:S(2)}) collective-permute-start(bf16[4,48,8,128]{3,2,1,0:T(8,128)(2,1)S(1)} %add_convert_fusion.4), channel_id=1, source_target_pairs={{0,4},{2,6},{4,0},{6,2},{8,12},{10,14},{12,8},{14,10},{16,20},{18,... | collective-permute-start | bytes 1179656 | tf_op jit(solution)/shard_map/ppermute | solution.py:22
  111.6 13.6 %collective-permute-start.24 = (bf16[4,48,8,128]{3,2,1,0:T(8,128)(2,1)S(1)}, bf16[4,48,8,128]{3,2,1,0:T(8,128)(2,1)S(1)}, u32[]{:S(2)}, u32[]{:S(2)}) collective-permute-start(bf16[4,48,8,128]{3,2,1,0:T(8,128)(2,1)S(1)} %add_convert_fusion.5), channel_id=1, source_target_pairs={{0,2},{2,0},{4,6},{6,4},{8,10},{10,8},{12,14},{14,12},{16,18},{18,... | collective-permute-start | bytes 1179656 | tf_op jit(solution)/shard_map/ppermute | solution.py:22
  116.0 16.4 %collective-permute-start.21 = (bf16[2,32,4096]{2,1,0:T(8,128)(2,1)S(1)}, bf16[2,32,4096]{2,1,0:T(8,128)(2,1)S(1)}, u32[]{:S(2)}, u32[]{:S(2)}) collective-permute-start(bf16[2,32,4096]{2,1,0:T(8,128)(2,1)S(1)} %add_convert_fusion), channel_id=1, source_target_pairs={{0,8},{2,10},{4,12},{6,14},{8,0},{10,2},{12,4},{14,6},{16,24},{18,... | collective-permute-start | bytes 1572872 | tf_op jit(solution)/shard_map/ppermute | solution.py:22
  116.3 15.8 %collective-permute-start.33 = (bf16[4,48,8,128]{3,2,1,0:T(8,128)(2,1)S(1)}, bf16[4,48,8,128]{3,2,1,0:T(8,128)(2,1)S(1)}, u32[]{:S(2)}, u32[]{:S(2)}) collective-permute-start(bf16[4,48,8,128]{3,2,1,0:T(8,128)(2,1)S(1)} %add_convert_fusion.2), channel_id=1, source_target_pairs={{0,4},{2,6},{4,0},{6,2},{8,12},{10,14},{12,8},{14,10},{16,20},{18,... | collective-permute-start | bytes 1179656 | tf_op jit(solution)/shard_map/ppermute | solution.py:22
  116.8 15.3 %collective-permute-start.32 = (bf16[4,48,8,128]{3,2,1,0:T(8,128)(2,1)S(1)}, bf16[4,48,8,128]{3,2,1,0:T(8,128)(2,1)S(1)}, u32[]{:S(2)}, u32[]{:S(2)}) collective-permute-start(bf16[4,48,8,128]{3,2,1,0:T(8,128)(2,1)S(1)} %add_convert_fusion.3), channel_id=1, source_target_pairs={{0,2},{2,0},{4,6},{6,4},{8,10},{10,8},{12,14},{14,12},{16,18},{18,... | collective-permute-start | bytes 1179656 | tf_op jit(solution)/shard_map/ppermute | solution.py:22
  124.1 21.5 %collective-permute-start.19 = (bf16[32,4096]{1,0:T(8,128)(2,1)S(1)}, bf16[32,4096]{1,0:T(8,128)(2,1)S(1)}, u32[]{:S(2)}, u32[]{:S(2)}) collective-permute-start(bf16[32,4096]{1,0:T(8,128)(2,1)S(1)} %fusion.2), channel_id=1, source_target_pairs={{0,16},{2,18},{4,20},{6,22},{8,24},{10,26},{12,28},{14,30},{16,0},... | collective-permute-start | bytes 786440 | tf_op jit(solution)/shard_map/ppermute | solution.py:22
  132.3 16.8 %collective-permute-start.29 = (bf16[48,8,128]{2,1,0:T(8,128)(2,1)S(1)}, bf16[48,8,128]{2,1,0:T(8,128)(2,1)S(1)}, u32[]{:S(2)}, u32[]{:S(2)}) collective-permute-start(bf16[48,8,128]{2,1,0:T(8,128)(2,1)S(1)} %get-tuple-element.117), channel_id=1, source_target_pairs={{0,8},{2,10},{4,12},{6,14},{8,0},{10,2},{12,4},{14,6},{16,24},{18,... | collective-permute-start | bytes 294920 | tf_op jit(solution)/shard_map/ppermute | solution.py:22
  132.7 17.9 %collective-permute-start.30 = (bf16[48,8,128]{2,1,0:T(8,128)(2,1)S(1)}, bf16[48,8,128]{2,1,0:T(8,128)(2,1)S(1)}, u32[]{:S(2)}, u32[]{:S(2)}) collective-permute-start(bf16[48,8,128]{2,1,0:T(8,128)(2,1)S(1)} %get-tuple-element.118), channel_id=1, source_target_pairs={{0,16},{2,18},{4,20},{6,22},{8,24},{10,26},{12,28},{14,30},{16,0},... | collective-permute-start | bytes 294920 | tf_op jit(solution)/shard_map/ppermute | solution.py:22
  145.6 19.7 %collective-permute-start.22 = (bf16[32,4096]{1,0:T(8,128)(2,1)S(1)}, bf16[32,4096]{1,0:T(8,128)(2,1)S(1)}, u32[]{:S(2)}, u32[]{:S(2)}) collective-permute-start(bf16[32,4096]{1,0:T(8,128)(2,1)S(1)} %fusion.3), channel_id=1, source_target_pairs={{0,16},{2,18},{4,20},{6,22},{8,24},{10,26},{12,28},{14,30},{16,0},... | collective-permute-start | bytes 786440 | tf_op jit(solution)/shard_map/ppermute | solution.py:22
  145.6 8.9 %collective-permute-start.31 = (bf16[48,8,128]{2,1,0:T(8,128)(2,1)S(1)}, bf16[48,8,128]{2,1,0:T(8,128)(2,1)S(1)}, u32[]{:S(2)}, u32[]{:S(2)}) collective-permute-start(bf16[48,8,128]{2,1,0:T(8,128)(2,1)S(1)} %get-tuple-element.119), channel_id=1, source_target_pairs={{0,24},{2,26},{4,28},{6,30},{8,16},{10,18},{12,20},{14,22},{16,8},... | collective-permute-start | bytes 294920 | tf_op jit(solution)/shard_map/ppermute | solution.py:22
  149.2 16.1 %collective-permute-start.35 = (bf16[48,8,128]{2,1,0:T(8,128)(2,1)S(1)}, bf16[48,8,128]{2,1,0:T(8,128)(2,1)S(1)}, u32[]{:S(2)}, u32[]{:S(2)}) collective-permute-start(bf16[48,8,128]{2,1,0:T(8,128)(2,1)S(1)} %get-tuple-element.123), channel_id=1, source_target_pairs={{0,16},{2,18},{4,20},{6,22},{8,24},{10,26},{12,28},{14,30},{16,0},... | collective-permute-start | bytes 294920 | tf_op jit(solution)/shard_map/ppermute | solution.py:22
  150.6 14.7 %collective-permute-start.36 = (bf16[48,8,128]{2,1,0:T(8,128)(2,1)S(1)}, bf16[48,8,128]{2,1,0:T(8,128)(2,1)S(1)}, u32[]{:S(2)}, u32[]{:S(2)}) collective-permute-start(bf16[48,8,128]{2,1,0:T(8,128)(2,1)S(1)} %get-tuple-element.124), channel_id=1, source_target_pairs={{0,24},{2,26},{4,28},{6,30},{8,16},{10,18},{12,20},{14,22},{16,8},... | collective-permute-start | bytes 294920 | tf_op jit(solution)/shard_map/ppermute | solution.py:22
  (10 other events, 87.3 us)

commit v7 on v5

--- a/solution.py
+++ b/solution.py
@@ -282,7 +282,7 @@
     far = math.gcd(4, math.gcd(dp_size, blocks_dev))
     near = dp_size // far
     blocks = blocks_dev // far
-    chunks = math.gcd(2, blocks)
+    chunks = 1
     chunk_blocks = blocks // chunks
     groups = far * chunks
     terms = 3 * slot_count
@@ -346,7 +346,7 @@
         cost=1_000_000,
         vmem=24,
     )
-    staged = tensor_size == 2 and far == 4 and near == 4 and chunks == 2
+    staged = tensor_size == 2 and far == 4 and near == 4
     if far > 1:
         packed = after(tuple(packed), x_items[near])
     received = [swap(packed[at], "dp", at * near) for at in reversed(range(1, far))][::-1]
@@ -370,23 +370,25 @@
         weight_list = [items[at] for at in range(near)]
         weight_parts = [(at, 0, far) for at in range(near)]
 
-    if far == 4:
+    if staged:
         x_source, g_source = after((tokens, out_grad), held)
         x_items[2 * near] = swap(x_source, "dp", 2 * near)
         g_items[near] = swap(g_source, "dp", near)
-        x_back, g_source = after((x_items[2 * near], g_source), pass_1, pass_2, x_items[2 * near])
-        x_items[3 * near] = swap(x_back, "dp", near)
+        x_source, g_source = after((x_items[2 * near], out_grad), x_items[2 * near], g_items[near])
+        x_items[3 * near] = swap(x_source, "dp", near)
         g_items[2 * near] = swap(g_source, "dp", 2 * near)
         g_items[3 * near] = swap(g_items[2 * near], "dp", near)
-        weight_list = list(after(tuple(weight_list), x_items[2 * near]))
-    elif far == 2:
-        g_items[near] = swap(out_grad, "dp", near)
+        x_late = jnp.concatenate([x_items[2 * near], x_items[3 * near]])
+        x_late = swap(after(x_late, *weight_list[3:], g_items[2 * near]), "tensor", 1)
+        g_late = jnp.concatenate([g_items[at * near] for at in range(1, far)])
+        g_late = swap(g_late, "tensor", 1)
+    else:
+        for items, value in ((x_items, tokens), (g_items, out_grad)):
+            items.update(gather({0: value}, "dp", far_strides))
 
     far_order = [at * near for at in range(0, far, 2)] + [at * near for at in range(1, far, 2)]
     if staged:
         order = [at * near for at in range(far)]
-        x_late = swap(jnp.concatenate([x_items[at] for at in order[2:]]), "tensor", 1)
-        g_late = swap(jnp.concatenate([g_items[at] for at in order[1:]]), "tensor", 1)
         x_list = [x_items[at] for at in order] + [x_core[at] for at in order[:2]] + [x_late]
         g_list = [g_items[at] for at in order] + [g_core[0], g_late]
         parts = [(other, far_order.index(at)) for other in (False, True) for at in order]
@@ -423,8 +425,6 @@
         cost=10_000_000,
         vmem=24,
     )
-    if far == 4:
-        x_list = list(after(tuple(x_list), g_items[2 * near]))
     def specs_of(*groups):
         return [whole(one.shape) for group in groups for one in group]
 
@@ -465,7 +465,7 @@
         return scatter(sums, "dp", far_strides)[0]
 
     if staged:
-        ffn_core, ffn_near = to_near(ffn_own, ffn_other)
+        ffn_core, ffn_near = to_near(ffn_own, after(ffn_other, g_items[3 * near]))
         middle = after(tuple(middle), ffn_near)
     part_shapes = [
         shape((length,) + chunk_shape, BF16) for _ in range(chunks) for _, _, length in weight_parts
@@ -513,20 +513,19 @@
         return [sums[0]] + [swap(sums[at], "dp", at * near) for at in range(1, far)]
 
     if staged:
-        first_parts, second_parts = tile_terms
-        first_got, second_got = halves(first_parts), halves(second_parts)
         ffn_got = swap(ffn_near, "dp", near)
+        tile_terms, input_other = after((tile_terms, input_other), ffn_got)
+        (tile_terms,) = tile_terms
+        got = halves(tile_terms)
         ffn_last = to_far(ffn_own, ffn_core, ffn_got)
         ffn_far = swap(ffn_last, "dp", 2 * near)
         input_core, input_near = to_near(input_own, input_other)
         input_got = swap(input_near, "dp", near)
-        first_sums = summed(first_parts, *folded(first_parts, *first_got))
-        second_folded = after(folded(second_parts, *second_got), input_near)
-        first_back = sent_back(after(tuple(first_sums), *second_folded))
+        to_1, to_2 = after(folded(tile_terms, *got), input_near, ffn_far)
         input_last = to_far(input_own, input_core, input_got)
         input_far = swap(input_last, "dp", 2 * near)
-        second_sums = summed(second_parts, *second_folded)
-        back = first_back + sent_back(after(tuple(second_sums), input_last))
+        sums = after(tuple(summed(tile_terms, to_1, to_2)), input_last)
+        back = list(after(tuple(sent_back(sums)), input_far))
         ffn_rows = add(ffn_own[0], ffn_core[0], ffn_got[0], ffn_far)
         input_rows = add(input_own[0], input_core[0], input_got[0], input_far)
     else:

time: 175 us -> 147 us (0.84)
  starting transfers between devices: 51.9 us -> 35.5 us
  waiting for transfers between devices: 89.2 us -> 78.9 us
    ppermute x38 -> x31, starting transfers between devices: 51.9 us -> 35.5 us  [swap(): return lax.ppermute(value, axis, [(at, at ^ stride) for at in range(size)])]
    ppermute x38 -> x31, waiting for transfers between devices: 89.2 us -> 78.9 us  [swap(): return lax.ppermute(value, axis, [(at, at ^ stride) for at in range(size)])]
  transfers between devices with their start and end apart: 38 -> 31, of which waited for: 19 -> 17; matrix products, arithmetic and copies ran while one was open for 3% -> 5% of each run, Pallas kernels for 4% -> 14%
where the time goes in v7:
time: 147 us
  waiting for transfers between devices  78.9 us (54%)
  starting transfers between devices  35.5 us (24%)
  Pallas kernels  23.6 us (16%)
  other arithmetic  5.13 us (3%)
  local copies, waits for them, and re-layouts  2.88 us (2%)
    ppermute x31, waiting for transfers between devices, swap(): return lax.ppermute(value, axis, [(at, at ^ stride) for at in range(size)])  78.9 us
    ppermute x31, starting transfers between devices, swap(): return lax.ppermute(value, axis, [(at, at ^ stride) for at in range(size)])  35.5 us
    pallas_call x5, Pallas kernels, call(): pl.pallas_call(kernel, grid_spec=pltpu.PrefetchScalarGridSpec(num_scalar_...  23.6 us
  transfers between devices with their start and end apart: 31, of which 17 were waited for; matrix products, arithmetic and copies ran while one was open for 5% of the time, Pallas kernels for 14%

profile of v7, /device:TPU:0, one launch (start us, length us, event | category | flops | bytes accessed | tf_op | source)
XLA Modules:
  0.0 146.8 jit_solution(17416374676184575487)
XLA Ops:
  0.6 3.1 %collective-permute-start = (bf16[32,4096]{1,0:T(8,128)(2,1)}, bf16[32,4096]{1,0:T(8,128)(2,1)S(1)}, u32[]{:S(2)}, u32[]{:S(2)}) collective-permute-start(bf16[32,4096]{1,0:T(8,128)(2,1)} %refs_0_.2), channel_id=1, source_target_pairs={{0,8},{2,10},{4,12},{6,14},{8,0},{10,2},{12,4},{14,6},{16,24},{18,... | collective-permute-start | bytes 786440 | tf_op jit(solution)/shard_map/ppermute | solution.py:22
  7.7 1.2 copy-done.1
  8.9 1.6 %shard_map.76 = (bf16[89,8,128]{2,1,0:T(8,128)(2,1)S(1)}, bf16[89,8,128]{2,1,0:T(8,128)(2,1)S(1)}, bf16[89,8,128]{2,1,0:T(8,128)(2,1)S(1)}, bf16[89,8,128]{2,1,0:T(8,128)(2,1)S(1)}) custom-call(s32[17,56]{1,0:T(8,128)S(1)} %pad_add_fusion.table, bf16[8,9,56,128]{3,2,1,0:T(8,128)(2,1)S(1)} %bitcast.43), custom_call_target="tpu_custom_call" | custom-call | bytes 1000000 | tf_op jit(solution)/shard_map/pallas_call | solution.py:263
  10.5 3.5 %collective-permute-start.3 = (bf16[89,8,128]{2,1,0:T(8,128)(2,1)S(1)}, bf16[89,8,128]{2,1,0:T(8,128)(2,1)S(1)}, u32[]{:S(2)}, u32[]{:S(2)}) collective-permute-start(bf16[89,8,128]{2,1,0:T(8,128)(2,1)S(1)} %get-tuple-element.58), channel_id=1, source_target_pairs={{0,24},{2,26},{4,28},{6,30},{8,16},{10,18},{12,20},{14,22},{16,8},... | collective-permute-start | bytes 546824 | tf_op jit(solution)/shard_map/ppermute | solution.py:22
  14.0 1.0 collective-permute-start.1
  15.5 4.5 %collective-permute-done.3 = bf16[89,8,128]{2,1,0:T(8,128)(2,1)S(1)} collective-permute-done((bf16[89,8,128]{2,1,0:T(8,128)(2,1)S(1)}, bf16[89,8,128]{2,1,0:T(8,128)(2,1)S(1)}, u32[]{:S(2)}, u32[]{:S(2)}) %collective-permute-start.3) | collective-permute-done | bytes 182304 | tf_op jit(solution)/shard_map/ppermute | solution.py:22
  20.0 9.2 %collective-permute-done.2 = bf16[89,8,128]{2,1,0:T(8,128)(2,1)S(1)} collective-permute-done((bf16[89,8,128]{2,1,0:T(8,128)(2,1)S(1)}, bf16[89,8,128]{2,1,0:T(8,128)(2,1)S(1)}, u32[]{:S(2)}, u32[]{:S(2)}) %collective-permute-start.2) | collective-permute-done | bytes 182304 | tf_op jit(solution)/shard_map/ppermute | solution.py:22
  29.4 1.6 %collective-permute-start.10 = (bf16[4,89,8,128]{3,2,1,0:T(8,128)(2,1)S(1)}, bf16[4,89,8,128]{3,2,1,0:T(8,128)(2,1)S(1)}, u32[]{:S(2)}, u32[]{:S(2)}) collective-permute-start(bf16[4,89,8,128]{3,2,1,0:T(8,128)(2,1)S(1)} %pad_maximum_fusion.1.refs_0_), channel_id=1, source_target_pairs={{0,2},{2,0},{4,6},{6,4},{8,10},{10,8},{12,14},{14,12},{16,18},{18,... | collective-permute-start | bytes 2187272 | tf_op jit(solution)/shard_map/ppermute | solution.py:22
  30.9 1.5 %collective-permute-start.12 = (bf16[4,89,8,128]{3,2,1,0:T(8,128)(2,1)S(1)}, bf16[4,89,8,128]{3,2,1,0:T(8,128)(2,1)S(1)}, u32[]{:S(2)}, u32[]{:S(2)}) collective-permute-start(bf16[4,89,8,128]{3,2,1,0:T(8,128)(2,1)S(1)} %pad_maximum_fusion.1.refs_0_), channel_id=1, source_target_pairs={{0,4},{2,6},{4,0},{6,2},{8,12},{10,14},{12,8},{14,10},{16,20},{18,... | collective-permute-start | bytes 2187272 | tf_op jit(solution)/shard_map/ppermute | solution.py:22
  32.9 2.8 %collective-permute-start.8 = (bf16[32,4096]{1,0:T(8,128)(2,1)S(1)}, bf16[32,4096]{1,0:T(8,128)(2,1)S(1)}, u32[]{:S(2)}, u32[]{:S(2)}) collective-permute-start(bf16[32,4096]{1,0:T(8,128)(2,1)S(1)} %copy-done.3), channel_id=1, source_target_pairs={{0,8},{2,10},{4,12},{6,14},{8,0},{10,2},{12,4},{14,6},{16,24},{18,... | collective-permute-start | bytes 786440 | tf_op jit(solution)/shard_map/ppermute | solution.py:22
  35.6 9.9 %collective-permute-done.7.refs_2_ = bf16[32,4096]{1,0:T(8,128)(2,1)S(1)} collective-permute-done((bf16[32,4096]{1,0:T(8,128)(2,1)S(1)}, bf16[32,4096]{1,0:T(8,128)(2,1)S(1)}, u32[]{:S(2)}, u32[]{:S(2)}) %collective-permute-start.7) | collective-permute-done | bytes 262176 | tf_op jit(solution)/shard_map/ppermute | solution.py:22
  46.3 2.3 %collective-permute-start.14 = (bf16[32,4096]{1,0:T(8,128)(2,1)S(1)}, bf16[32,4096]{1,0:T(8,128)(2,1)S(1)}, u32[]{:S(2)}, u32[]{:S(2)}) collective-permute-start(bf16[32,4096]{1,0:T(8,128)(2,1)S(1)} %copy-done.3), channel_id=1, source_target_pairs={{0,16},{2,18},{4,20},{6,22},{8,24},{10,26},{12,28},{14,30},{16,0},... | collective-permute-start | bytes 786440 | tf_op jit(solution)/shard_map/ppermute | solution.py:22
  49.9 9.2 %collective-permute-done.9.refs_3_ = bf16[32,4096]{1,0:T(8,128)(2,1)S(1)} collective-permute-done((bf16[32,4096]{1,0:T(8,128)(2,1)S(1)}, bf16[32,4096]{1,0:T(8,128)(2,1)S(1)}, u32[]{:S(2)}, u32[]{:S(2)}) %collective-permute-start.9) | collective-permute-done | bytes 262176 | tf_op jit(solution)/shard_map/ppermute | solution.py:22
  59.1 1.4 collective-permute-done.14.refs_2_
  60.9 1.8 %shard_map.77.refs_7_.refs_6_ = bf16[89,128,128]{2,1,0:T(8,128)(2,1)S(1)} custom-call(s32[17,56]{1,0:T(8,128)S(1)} %pad_add_fusion.table, bf16[4,89,8,128]{3,2,1,0:T(8,128)(2,1)S(1)} %pad_maximum_fusion.1.refs_0_, bf16[4,89,8,128]{3,2,1,0:T(8,128)(2,1)S(1)} %collective-permute-done.10.refs_1_, bf16[4,89,8,128]{3,2,1,0:T(8,128)(2,1)S(1)} %collective-permute-done.12.refs_2_, ...), custom_call_target="tpu_custom_call" | custom-call | bytes 10000000 | tf_op jit(solution)/shard_map/pallas_call | solution.py:263
  62.8 6.3 %shard_map.78 = (bf16[4096,256]{1,0:T(8,128)(2,1)S(1)}, f32[14,256,128]{2,1,0:T(8,128)S(1)}, f32[14,256,128]{2,1,0:T(8,128)S(1)}, bf16[14,128,256]{2,1,0:T(8,128...) custom-call(s32[17,56]{1,0:T(8,128)S(1)} %pad_add_fusion.table, ...), custom_call_target="tpu_custom_call" | custom-call | bytes 30000000 | tf_op jit(solution)/shard_map/pallas_call | solution.py:263
  69.9 2.0 %collective-permute-done.17 = bf16[4,32,4096]{2,1,0:T(8,128)(2,1)S(1)} collective-permute-done((bf16[4,32,4096]{2,1,0:T(8,128)(2,1)S(1)}, bf16[4,32,4096]{2,1,0:T(8,128)(2,1)S(1)}, u32[]{:S(2)}, u32[]{:S(2)}) %collective-permute-start.17) | collective-permute-done | bytes 1048608 | tf_op jit(solution)/shard_map/ppermute | solution.py:22
  72.0 1.7 %collective-permute-start.18 = (bf16[2,32,4096]{2,1,0:T(8,128)(2,1)S(1)}, bf16[2,32,4096]{2,1,0:T(8,128)(2,1)S(1)}, u32[]{:S(2)}, u32[]{:S(2)}) collective-permute-start(bf16[2,32,4096]{2,1,0:T(8,128)(2,1)S(1)} %add_convert_fusion.3), channel_id=1, source_target_pairs={{0,8},{2,10},{4,12},{6,14},{8,0},{10,2},{12,4},{14,6},{16,24},{18,... | collective-permute-start | bytes 1572872 | tf_op jit(solution)/shard_map/ppermute | solution.py:22
  73.8 10.9 %shard_map.79 = (bf16[4,32,4096]{2,1,0:T(8,128)(2,1)S(1)}, bf16[4,32,4096]{2,1,0:T(8,128)(2,1)S(1)}, bf16[4,89,8,128]{3,2,1,0:T(8,128)(2,1)S(1)}, bf16[4,89,8,12...) custom-call(s32[17,56]{1,0:T(8,128)S(1)} %pad_add_fusion.table, ...), custom_call_target="tpu_custom_call" | custom-call | bytes 40000000 | tf_op jit(solution)/shard_map/pallas_call | solution.py:263
  84.6 1.4 collective-permute-done.18
  87.1 1.6 %collective-permute-done.21 = bf16[4,32,4096]{2,1,0:T(8,128)(2,1)S(1)} collective-permute-done((bf16[4,32,4096]{2,1,0:T(8,128)(2,1)S(1)}, bf16[4,32,4096]{2,1,0:T(8,128)(2,1)S(1)}, u32[]{:S(2)}, u32[]{:S(2)}) %collective-permute-start.21) | collective-permute-done | bytes 1048608 | tf_op jit(solution)/shard_map/ppermute | solution.py:22
  88.9 1.7 %collective-permute-start.22 = (bf16[2,32,4096]{2,1,0:T(8,128)(2,1)S(1)}, bf16[2,32,4096]{2,1,0:T(8,128)(2,1)S(1)}, u32[]{:S(2)}, u32[]{:S(2)}) collective-permute-start(bf16[2,32,4096]{2,1,0:T(8,128)(2,1)S(1)} %add_convert_fusion.2), channel_id=1, source_target_pairs={{0,8},{2,10},{4,12},{6,14},{8,0},{10,2},{12,4},{14,6},{16,24},{18,... | collective-permute-start | bytes 1572872 | tf_op jit(solution)/shard_map/ppermute | solution.py:22
  90.7 1.3 collective-permute-start.19
  92.0 5.0 %collective-permute-done.24 = bf16[2,89,8,128]{3,2,1,0:T(8,128)(2,1)S(1)} collective-permute-done((bf16[2,89,8,128]{3,2,1,0:T(8,128)(2,1)S(1)}, bf16[2,89,8,128]{3,2,1,0:T(8,128)(2,1)S(1)}, u32[]{:S(2)}, u32[]{:S(2)}) %collective-permute-start.24) | collective-permute-done | bytes 364576 | tf_op jit(solution)/shard_map/ppermute | solution.py:22
  97.3 10.4 %collective-permute-done.19 = bf16[32,4096]{1,0:T(8,128)(2,1)S(1)} collective-permute-done((bf16[32,4096]{1,0:T(8,128)(2,1)S(1)}, bf16[32,4096]{1,0:T(8,128)(2,1)S(1)}, u32[]{:S(2)}, u32[]{:S(2)}) %collective-permute-start.19) | collective-permute-done | bytes 262176 | tf_op jit(solution)/shard_map/ppermute | solution.py:22
  109.0 3.4 %collective-permute-start.23 = (bf16[32,4096]{1,0:T(8,128)(2,1)S(1)}, bf16[32,4096]{1,0:T(8,128)(2,1)S(1)}, u32[]{:S(2)}, u32[]{:S(2)}) collective-permute-start(bf16[32,4096]{1,0:T(8,128)(2,1)S(1)} %fusion.3), channel_id=1, source_target_pairs={{0,16},{2,18},{4,20},{6,22},{8,24},{10,26},{12,28},{14,30},{16,0},... | collective-permute-start | bytes 786440 | tf_op jit(solution)/shard_map/ppermute | solution.py:22
  113.3 11.9 %collective-permute-done.27 = bf16[4,89,8,128]{3,2,1,0:T(8,128)(2,1)S(1)} collective-permute-done((bf16[4,89,8,128]{3,2,1,0:T(8,128)(2,1)S(1)}, bf16[4,89,8,128]{3,2,1,0:T(8,128)(2,1)S(1)}, u32[]{:S(2)}, u32[]{:S(2)}) %collective-permute-start.27) | collective-permute-done | bytes 729120 | tf_op jit(solution)/shard_map/ppermute | solution.py:22
  125.8 3.4 %collective-permute-start.28 = (bf16[89,8,128]{2,1,0:T(8,128)(2,1)S(1)}, bf16[89,8,128]{2,1,0:T(8,128)(2,1)S(1)}, u32[]{:S(2)}, u32[]{:S(2)}) collective-permute-start(bf16[89,8,128]{2,1,0:T(8,128)(2,1)S(1)} %get-tuple-element.92), channel_id=1, source_target_pairs={{0,8},{2,10},{4,12},{6,14},{8,0},{10,2},{12,4},{14,6},{16,24},{18,... | collective-permute-start | bytes 546824 | tf_op jit(solution)/shard_map/ppermute | solution.py:22
  129.3 2.3 %collective-permute-start.30 = (bf16[89,8,128]{2,1,0:T(8,128)(2,1)S(1)}, bf16[89,8,128]{2,1,0:T(8,128)(2,1)S(1)}, u32[]{:S(2)}, u32[]{:S(2)}) collective-permute-start(bf16[89,8,128]{2,1,0:T(8,128)(2,1)S(1)} %get-tuple-element.94), channel_id=1, source_target_pairs={{0,24},{2,26},{4,28},{6,30},{8,16},{10,18},{12,20},{14,22},{16,8},... | collective-permute-start | bytes 546824 | tf_op jit(solution)/shard_map/ppermute | solution.py:22
  132.5 1.9 %collective-permute-done.28.refs_1_ = bf16[89,8,128]{2,1,0:T(8,128)(2,1)S(1)} collective-permute-done((bf16[89,8,128]{2,1,0:T(8,128)(2,1)S(1)}, bf16[89,8,128]{2,1,0:T(8,128)(2,1)S(1)}, u32[]{:S(2)}, u32[]{:S(2)}) %collective-permute-start.28) | collective-permute-done | bytes 182304 | tf_op jit(solution)/shard_map/ppermute | solution.py:22
  134.3 9.5 %collective-permute-done.29.refs_2_ = bf16[89,8,128]{2,1,0:T(8,128)(2,1)S(1)} collective-permute-done((bf16[89,8,128]{2,1,0:T(8,128)(2,1)S(1)}, bf16[89,8,128]{2,1,0:T(8,128)(2,1)S(1)}, u32[]{:S(2)}, u32[]{:S(2)}) %collective-permute-start.29) | collective-permute-done | bytes 182304 | tf_op jit(solution)/shard_map/ppermute | solution.py:22
  143.8 3.0 %shard_map.80 = bf16[8,9,56,128]{3,2,1,0:T(8,128)(2,1)} custom-call(s32[17,56]{1,0:T(8,128)S(1)} %pad_add_fusion.table, bf16[89,8,128]{2,1,0:T(8,128)(2,1)S(1)} %get-tuple-element.95.refs_0_, bf16[89,8,128]{2,1,0:T(8,128)(2,1)S(1)} %collective-permute-done.28.refs_1_, bf16[89,8,128]{2,1,0:T(8,128)(2,1)S(1)} %collective-permute-done.29.refs_2_, ...), custom_call_target="tpu_custom_call" | custom-call | bytes 2000000 | tf_op jit(solution)/shard_map/pallas_call | solution.py:263
  (73 shorter events, 13.5 us)
Async XLA Ops:
  0.6 9.9 %collective-permute-start = (bf16[32,4096]{1,0:T(8,128)(2,1)}, bf16[32,4096]{1,0:T(8,128)(2,1)S(1)}, u32[]{:S(2)}, u32[]{:S(2)}) collective-permute-start(bf16[32,4096]{1,0:T(8,128)(2,1)} %refs_0_.2), channel_id=1, source_target_pairs={{0,8},{2,10},{4,12},{6,14},{8,0},{10,2},{12,4},{14,6},{16,24},{18,... | collective-permute-start | bytes 786440 | tf_op jit(solution)/shard_map/ppermute | solution.py:22
  8.9 24.0 %copy-start.3 = (bf16[32,4096]{1,0:T(8,128)(2,1)S(1)}, bf16[32,4096]{1,0:T(8,128)(2,1)}, u32[]{:S(2)}) copy-start(bf16[32,4096]{1,0:T(8,128)(2,1)} %refs_0_.3) | copy-start | bytes 786436
  10.5 9.5 %collective-permute-start.3 = (bf16[89,8,128]{2,1,0:T(8,128)(2,1)S(1)}, bf16[89,8,128]{2,1,0:T(8,128)(2,1)S(1)}, u32[]{:S(2)}, u32[]{:S(2)}) collective-permute-start(bf16[89,8,128]{2,1,0:T(8,128)(2,1)S(1)} %get-tuple-element.58), channel_id=1, source_target_pairs={{0,24},{2,26},{4,28},{6,30},{8,16},{10,18},{12,20},{14,22},{16,8},... | collective-permute-start | bytes 546824 | tf_op jit(solution)/shard_map/ppermute | solution.py:22
  14.0 15.2 %collective-permute-start.2 = (bf16[89,8,128]{2,1,0:T(8,128)(2,1)S(1)}, bf16[89,8,128]{2,1,0:T(8,128)(2,1)S(1)}, u32[]{:S(2)}, u32[]{:S(2)}) collective-permute-start(bf16[89,8,128]{2,1,0:T(8,128)(2,1)S(1)} %get-tuple-element.57), channel_id=1, source_target_pairs={{0,16},{2,18},{4,20},{6,22},{8,24},{10,26},{12,28},{14,30},{16,0},... | collective-permute-start | bytes 546824 | tf_op jit(solution)/shard_map/ppermute | solution.py:22
  14.0 15.2 %collective-permute-start.1 = (bf16[89,8,128]{2,1,0:T(8,128)(2,1)S(1)}, bf16[89,8,128]{2,1,0:T(8,128)(2,1)S(1)}, u32[]{:S(2)}, u32[]{:S(2)}) collective-permute-start(bf16[89,8,128]{2,1,0:T(8,128)(2,1)S(1)} %get-tuple-element.56), channel_id=1, source_target_pairs={{0,8},{2,10},{4,12},{6,14},{8,0},{10,2},{12,4},{14,6},{16,24},{18,... | collective-permute-start | bytes 546824 | tf_op jit(solution)/shard_map/ppermute | solution.py:22
  15.0 14.3 %collective-permute-start.4 = (bf16[32,4096]{1,0:T(8,128)(2,1)}, bf16[32,4096]{1,0:T(8,128)(2,1)S(1)}, u32[]{:S(2)}, u32[]{:S(2)}) collective-permute-start(bf16[32,4096]{1,0:T(8,128)(2,1)} %refs_0_.2), channel_id=1, source_target_pairs={{0,1},{1,0},{2,3},{3,2},{4,5},{5,4},{6,7},{7,6},{8,9},{9,8},{10,11... | collective-permute-start | bytes 786440 | tf_op jit(solution)/shard_map/ppermute | solution.py:22
  15.0 14.3 %collective-permute-start.6 = (bf16[32,4096]{1,0:T(8,128)(2,1)}, bf16[32,4096]{1,0:T(8,128)(2,1)S(1)}, u32[]{:S(2)}, u32[]{:S(2)}) collective-permute-start(bf16[32,4096]{1,0:T(8,128)(2,1)} %refs_0_.3), channel_id=1, source_target_pairs={{0,1},{1,0},{2,3},{3,2},{4,5},{5,4},{6,7},{7,6},{8,9},{9,8},{10,11... | collective-permute-start | bytes 786440 | tf_op jit(solution)/shard_map/ppermute | solution.py:22
  20.0 9.3 %collective-permute-start.5 = (bf16[32,4096]{1,0:T(8,128)(2,1)S(1)}, bf16[32,4096]{1,0:T(8,128)(2,1)S(1)}, u32[]{:S(2)}, u32[]{:S(2)}) collective-permute-start(bf16[32,4096]{1,0:T(8,128)(2,1)S(1)} %collective-permute-done.refs_1_), channel_id=1, source_target_pairs={{0,1},{1,0},{2,3},{3,2},{4,5},{5,4},{6,7},{7,6},{8,9},{9,8},{10,11... | collective-permute-start | bytes 786440 | tf_op jit(solution)/shard_map/ppermute | solution.py:22
  29.4 19.3 %collective-permute-start.10 = (bf16[4,89,8,128]{3,2,1,0:T(8,128)(2,1)S(1)}, bf16[4,89,8,128]{3,2,1,0:T(8,128)(2,1)S(1)}, u32[]{:S(2)}, u32[]{:S(2)}) collective-permute-start(bf16[4,89,8,128]{3,2,1,0:T(8,128)(2,1)S(1)} %pad_maximum_fusion.1.refs_0_), channel_id=1, source_target_pairs={{0,2},{2,0},{4,6},{6,4},{8,10},{10,8},{12,14},{14,12},{16,18},{18,... | collective-permute-start | bytes 2187272 | tf_op jit(solution)/shard_map/ppermute | solution.py:22
  30.9 18.3 %collective-permute-start.12 = (bf16[4,89,8,128]{3,2,1,0:T(8,128)(2,1)S(1)}, bf16[4,89,8,128]{3,2,1,0:T(8,128)(2,1)S(1)}, u32[]{:S(2)}, u32[]{:S(2)}) collective-permute-start(bf16[4,89,8,128]{3,2,1,0:T(8,128)(2,1)S(1)} %pad_maximum_fusion.1.refs_0_), channel_id=1, source_target_pairs={{0,4},{2,6},{4,0},{6,2},{8,12},{10,14},{12,8},{14,10},{16,20},{18,... | collective-permute-start | bytes 2187272 | tf_op jit(solution)/shard_map/ppermute | solution.py:22
  32.4 13.1 %collective-permute-start.7 = (bf16[32,4096]{1,0:T(8,128)(2,1)S(1)}, bf16[32,4096]{1,0:T(8,128)(2,1)S(1)}, u32[]{:S(2)}, u32[]{:S(2)}) collective-permute-start(bf16[32,4096]{1,0:T(8,128)(2,1)S(1)} %copy-done.2), channel_id=1, source_target_pairs={{0,16},{2,18},{4,20},{6,22},{8,24},{10,26},{12,28},{14,30},{16,0},... | collective-permute-start | bytes 786440 | tf_op jit(solution)/shard_map/ppermute | solution.py:22
  32.9 13.1 %collective-permute-start.8 = (bf16[32,4096]{1,0:T(8,128)(2,1)S(1)}, bf16[32,4096]{1,0:T(8,128)(2,1)S(1)}, u32[]{:S(2)}, u32[]{:S(2)}) collective-permute-start(bf16[32,4096]{1,0:T(8,128)(2,1)S(1)} %copy-done.3), channel_id=1, source_target_pairs={{0,8},{2,10},{4,12},{6,14},{8,0},{10,2},{12,4},{14,6},{16,24},{18,... | collective-permute-start | bytes 786440 | tf_op jit(solution)/shard_map/ppermute | solution.py:22
  46.0 13.1 %collective-permute-start.9 = (bf16[32,4096]{1,0:T(8,128)(2,1)S(1)}, bf16[32,4096]{1,0:T(8,128)(2,1)S(1)}, u32[]{:S(2)}, u32[]{:S(2)}) collective-permute-start(bf16[32,4096]{1,0:T(8,128)(2,1)S(1)} %collective-permute-done.7.refs_2_), channel_id=1, source_target_pairs={{0,8},{2,10},{4,12},{6,14},{8,0},{10,2},{12,4},{14,6},{16,24},{18,... | collective-permute-start | bytes 786440 | tf_op jit(solution)/shard_map/ppermute | solution.py:22
  46.3 14.2 %collective-permute-start.14 = (bf16[32,4096]{1,0:T(8,128)(2,1)S(1)}, bf16[32,4096]{1,0:T(8,128)(2,1)S(1)}, u32[]{:S(2)}, u32[]{:S(2)}) collective-permute-start(bf16[32,4096]{1,0:T(8,128)(2,1)S(1)} %copy-done.3), channel_id=1, source_target_pairs={{0,16},{2,18},{4,20},{6,22},{8,24},{10,26},{12,28},{14,30},{16,0},... | collective-permute-start | bytes 786440 | tf_op jit(solution)/shard_map/ppermute | solution.py:22
  48.7 11.8 %collective-permute-start.11 = (bf16[2,89,8,128]{3,2,1,0:T(8,128)(2,1)S(1)}, bf16[2,89,8,128]{3,2,1,0:T(8,128)(2,1)S(1)}, u32[]{:S(2)}, u32[]{:S(2)}) collective-permute-start(bf16[2,89,8,128]{3,2,1,0:T(8,128)(2,1)S(1)} %slice.135), channel_id=1, source_target_pairs={{0,4},{2,6},{4,0},{6,2},{8,12},{10,14},{12,8},{14,10},{16,20},{18,... | collective-permute-start | bytes 1093640 | tf_op jit(solution)/shard_map/ppermute | solution.py:22
  49.3 11.2 %collective-permute-start.13 = (bf16[2,89,8,128]{3,2,1,0:T(8,128)(2,1)S(1)}, bf16[2,89,8,128]{3,2,1,0:T(8,128)(2,1)S(1)}, u32[]{:S(2)}, u32[]{:S(2)}) collective-permute-start(bf16[2,89,8,128]{3,2,1,0:T(8,128)(2,1)S(1)} %slice.136), channel_id=1, source_target_pairs={{0,2},{2,0},{4,6},{6,4},{8,10},{10,8},{12,14},{14,12},{16,18},{18,... | collective-permute-start | bytes 1093640 | tf_op jit(solution)/shard_map/ppermute | solution.py:22
  60.5 2.2 %collective-permute-start.15 = (bf16[64,4096]{1,0:T(8,128)(2,1)S(1)}, bf16[64,4096]{1,0:T(8,128)(2,1)S(1)}, u32[]{:S(2)}, u32[]{:S(2)}) collective-permute-start(bf16[64,4096]{1,0:T(8,128)(2,1)S(1)} %pad_maximum_fusion.2), channel_id=1, source_target_pairs={{0,1},{1,0},{2,3},{3,2},{4,5},{5,4},{6,7},{7,6},{8,9},{9,8},{10,11... | collective-permute-start | bytes 1572872 | tf_op jit(solution)/shard_map/ppermute | solution.py:22
  60.5 8.7 %collective-permute-start.16 = (bf16[32,4096]{1,0:T(8,128)(2,1)S(1)}, bf16[32,4096]{1,0:T(8,128)(2,1)S(1)}, u32[]{:S(2)}, u32[]{:S(2)}) collective-permute-start(bf16[32,4096]{1,0:T(8,128)(2,1)S(1)} %collective-permute-done.14.refs_2_), channel_id=1, source_target_pairs={{0,8},{2,10},{4,12},{6,14},{8,0},{10,2},{12,4},{14,6},{16,24},{18,... | collective-permute-start | bytes 786440 | tf_op jit(solution)/shard_map/ppermute | solution.py:22
  69.2 2.7 %collective-permute-start.17 = (bf16[4,32,4096]{2,1,0:T(8,128)(2,1)S(1)}, bf16[4,32,4096]{2,1,0:T(8,128)(2,1)S(1)}, u32[]{:S(2)}, u32[]{:S(2)}) collective-permute-start(bf16[4,32,4096]{2,1,0:T(8,128)(2,1)S(1)} %get-tuple-element.67), channel_id=1, source_target_pairs={{0,1},{1,0},{2,3},{3,2},{4,5},{5,4},{6,7},{7,6},{8,9},{9,8},{10,11... | collective-permute-start | bytes 3145736 | tf_op jit(solution)/shard_map/ppermute | solution.py:22
  69.4 4.4 %collective-permute-start.20 = (bf16[96,4096]{1,0:T(8,128)(2,1)S(1)}, bf16[96,4096]{1,0:T(8,128)(2,1)S(1)}, u32[]{:S(2)}, u32[]{:S(2)}) collective-permute-start(bf16[96,4096]{1,0:T(8,128)(2,1)S(1)} %pad_maximum_fusion), channel_id=1, source_target_pairs={{0,1},{1,0},{2,3},{3,2},{4,5},{5,4},{6,7},{7,6},{8,9},{9,8},{10,11... | collective-permute-start | bytes 2359304 | tf_op jit(solution)/shard_map/ppermute | solution.py:22
  72.0 14.0 %collective-permute-start.18 = (bf16[2,32,4096]{2,1,0:T(8,128)(2,1)S(1)}, bf16[2,32,4096]{2,1,0:T(8,128)(2,1)S(1)}, u32[]{:S(2)}, u32[]{:S(2)}) collective-permute-start(bf16[2,32,4096]{2,1,0:T(8,128)(2,1)S(1)} %add_convert_fusion.3), channel_id=1, source_target_pairs={{0,8},{2,10},{4,12},{6,14},{8,0},{10,2},{12,4},{14,6},{16,24},{18,... | collective-permute-start | bytes 1572872 | tf_op jit(solution)/shard_map/ppermute | solution.py:22
  86.1 2.7 %collective-permute-start.21 = (bf16[4,32,4096]{2,1,0:T(8,128)(2,1)S(1)}, bf16[4,32,4096]{2,1,0:T(8,128)(2,1)S(1)}, u32[]{:S(2)}, u32[]{:S(2)}) collective-permute-start(bf16[4,32,4096]{2,1,0:T(8,128)(2,1)S(1)} %get-tuple-element.83), channel_id=1, source_target_pairs={{0,1},{1,0},{2,3},{3,2},{4,5},{5,4},{6,7},{7,6},{8,9},{9,8},{10,11... | collective-permute-start | bytes 3145736 | tf_op jit(solution)/shard_map/ppermute | solution.py:22
  86.1 10.9 %collective-permute-start.24 = (bf16[2,89,8,128]{3,2,1,0:T(8,128)(2,1)S(1)}, bf16[2,89,8,128]{3,2,1,0:T(8,128)(2,1)S(1)}, u32[]{:S(2)}, u32[]{:S(2)}) collective-permute-start(bf16[2,89,8,128]{3,2,1,0:T(8,128)(2,1)S(1)} %get-tuple-element.86), channel_id=1, source_target_pairs={{0,4},{2,6},{4,0},{6,2},{8,12},{10,14},{12,8},{14,10},{16,20},{18,... | collective-permute-start | bytes 1093640 | tf_op jit(solution)/shard_map/ppermute | solution.py:22
  86.6 10.6 %collective-permute-start.25 = (bf16[2,89,8,128]{3,2,1,0:T(8,128)(2,1)S(1)}, bf16[2,89,8,128]{3,2,1,0:T(8,128)(2,1)S(1)}, u32[]{:S(2)}, u32[]{:S(2)}) collective-permute-start(bf16[2,89,8,128]{3,2,1,0:T(8,128)(2,1)S(1)} %get-tuple-element.88), channel_id=1, source_target_pairs={{0,2},{2,0},{4,6},{6,4},{8,10},{10,8},{12,14},{14,12},{16,18},{18,... | collective-permute-start | bytes 1093640 | tf_op jit(solution)/shard_map/ppermute | solution.py:22
  88.9 20.0 %collective-permute-start.22 = (bf16[2,32,4096]{2,1,0:T(8,128)(2,1)S(1)}, bf16[2,32,4096]{2,1,0:T(8,128)(2,1)S(1)}, u32[]{:S(2)}, u32[]{:S(2)}) collective-permute-start(bf16[2,32,4096]{2,1,0:T(8,128)(2,1)S(1)} %add_convert_fusion.2), channel_id=1, source_target_pairs={{0,8},{2,10},{4,12},{6,14},{8,0},{10,2},{12,4},{14,6},{16,24},{18,... | collective-permute-start | bytes 1572872 | tf_op jit(solution)/shard_map/ppermute | solution.py:22
  90.7 17.0 %collective-permute-start.19 = (bf16[32,4096]{1,0:T(8,128)(2,1)S(1)}, bf16[32,4096]{1,0:T(8,128)(2,1)S(1)}, u32[]{:S(2)}, u32[]{:S(2)}) collective-permute-start(bf16[32,4096]{1,0:T(8,128)(2,1)S(1)} %fusion.2), channel_id=1, source_target_pairs={{0,16},{2,18},{4,20},{6,22},{8,24},{10,26},{12,28},{14,30},{16,0},... | collective-permute-start | bytes 786440 | tf_op jit(solution)/shard_map/ppermute | solution.py:22
  107.7 17.5 %collective-permute-start.27 = (bf16[4,89,8,128]{3,2,1,0:T(8,128)(2,1)S(1)}, bf16[4,89,8,128]{3,2,1,0:T(8,128)(2,1)S(1)}, u32[]{:S(2)}, u32[]{:S(2)}) collective-permute-start(bf16[4,89,8,128]{3,2,1,0:T(8,128)(2,1)S(1)} %add_convert_fusion), channel_id=1, source_target_pairs={{0,4},{2,6},{4,0},{6,2},{8,12},{10,14},{12,8},{14,10},{16,20},{18,... | collective-permute-start | bytes 2187272 | tf_op jit(solution)/shard_map/ppermute | solution.py:22
  108.2 17.2 %collective-permute-start.26 = (bf16[4,89,8,128]{3,2,1,0:T(8,128)(2,1)S(1)}, bf16[4,89,8,128]{3,2,1,0:T(8,128)(2,1)S(1)}, u32[]{:S(2)}, u32[]{:S(2)}) collective-permute-start(bf16[4,89,8,128]{3,2,1,0:T(8,128)(2,1)S(1)} %add_convert_fusion.1), channel_id=1, source_target_pairs={{0,2},{2,0},{4,6},{6,4},{8,10},{10,8},{12,14},{14,12},{16,18},{18,... | collective-permute-start | bytes 2187272 | tf_op jit(solution)/shard_map/ppermute | solution.py:22
  109.0 22.6 %collective-permute-start.23 = (bf16[32,4096]{1,0:T(8,128)(2,1)S(1)}, bf16[32,4096]{1,0:T(8,128)(2,1)S(1)}, u32[]{:S(2)}, u32[]{:S(2)}) collective-permute-start(bf16[32,4096]{1,0:T(8,128)(2,1)S(1)} %fusion.3), channel_id=1, source_target_pairs={{0,16},{2,18},{4,20},{6,22},{8,24},{10,26},{12,28},{14,30},{16,0},... | collective-permute-start | bytes 786440 | tf_op jit(solution)/shard_map/ppermute | solution.py:22
  125.8 8.6 %collective-permute-start.28 = (bf16[89,8,128]{2,1,0:T(8,128)(2,1)S(1)}, bf16[89,8,128]{2,1,0:T(8,128)(2,1)S(1)}, u32[]{:S(2)}, u32[]{:S(2)}) collective-permute-start(bf16[89,8,128]{2,1,0:T(8,128)(2,1)S(1)} %get-tuple-element.92), channel_id=1, source_target_pairs={{0,8},{2,10},{4,12},{6,14},{8,0},{10,2},{12,4},{14,6},{16,24},{18,... | collective-permute-start | bytes 546824 | tf_op jit(solution)/shard_map/ppermute | solution.py:22
  129.2 14.6 %collective-permute-start.29 = (bf16[89,8,128]{2,1,0:T(8,128)(2,1)S(1)}, bf16[89,8,128]{2,1,0:T(8,128)(2,1)S(1)}, u32[]{:S(2)}, u32[]{:S(2)}) collective-permute-start(bf16[89,8,128]{2,1,0:T(8,128)(2,1)S(1)} %get-tuple-element.93), channel_id=1, source_target_pairs={{0,16},{2,18},{4,20},{6,22},{8,24},{10,26},{12,28},{14,30},{16,0},... | collective-permute-start | bytes 546824 | tf_op jit(solution)/shard_map/ppermute | solution.py:22
  129.3 14.5 %collective-permute-start.30 = (bf16[89,8,128]{2,1,0:T(8,128)(2,1)S(1)}, bf16[89,8,128]{2,1,0:T(8,128)(2,1)S(1)}, u32[]{:S(2)}, u32[]{:S(2)}) collective-permute-start(bf16[89,8,128]{2,1,0:T(8,128)(2,1)S(1)} %get-tuple-element.94), channel_id=1, source_target_pairs={{0,24},{2,26},{4,28},{6,30},{8,16},{10,18},{12,20},{14,22},{16,8},... | collective-permute-start | bytes 546824 | tf_op jit(solution)/shard_map/ppermute | solution.py:22
  (3 other events, 31.1 us)

commit v8 on v7

--- a/solution.py
+++ b/solution.py
@@ -13,7 +13,7 @@
 PLAIN = (((1,), (0,)), ((), ()))
 TURNED = (((1,), (1,)), ((), ()))
 MIB = 1024 * 1024
-UNROLL = 2
+UNROLL = 7
 dot = functools.partial(lax.dot_general, preferred_element_type=F32)
 
 
@@ -86,31 +86,26 @@
         lax.fori_loop(0, blocks, one, 0, unroll=True)
 
 
-def unpack(table, *refs, chunks, chunk_rows, blocks, slot_count):
+def unpack(table, *refs, blocks, slot_count):
     out, lines, sources = refs[-2], refs[-1], refs[:-2]
     share, terms, blocks_dev, _ = out.shape
-    far = len(sources) // chunks
-    chunk_blocks = blocks // chunks
-    for chunk in range(chunks):
-        for at in range(far):
-            ref = sources[chunk * far + at]
-
-            def one(place, _, at=at, ref=ref, chunk=chunk):
-                column = at * blocks + chunk * chunk_blocks + place
-                block = table[0, column]
-                for matrix in range(3):
-                    first = table[1 + matrix, column] - chunk * chunk_rows
-                    count = table[4 + matrix, column]
-                    for slot in range(slot_count):
-                        live = slot < count
-                        value = ref[jnp.where(live, first + slot, 0)].astype(F32)
-                        target = (matrix * slot_count + slot) * blocks_dev + block
-                        lines[pl.ds(target, share, stride=terms * blocks_dev), :] = jnp.where(
-                            live, value, 0.0
-                        )
-                return _
-
-            lax.fori_loop(0, chunk_blocks, one, 0, unroll=True)
+    for at, ref in enumerate(sources):
+
+        def one(place, _, at=at, ref=ref):
+            column = at * blocks + place
+            block = table[0, column]
+            for matrix in range(3):
+                first, count = table[1 + matrix, column], table[4 + matrix, column]
+                for slot in range(slot_count):
+                    live = slot < count
+                    value = ref[jnp.where(live, first + slot, 0)].astype(F32)
+                    target = (matrix * slot_count + slot) * blocks_dev + block
+                    lines[pl.ds(target, share, stride=terms * blocks_dev), :] = jnp.where(
+                        live, value, 0.0
+                    )
+            return _
+
+        lax.fori_loop(0, blocks, one, 0, unroll=True)
     for row in range(share):
         for term in range(terms):
             at = (row * terms + term) * blocks_dev
@@ -137,10 +132,10 @@
         out[out.shape[0] - 1] = jnp.zeros(out.shape[1:], BF16)
 
 
-def places_of(table, block, slot_count, spare, base=0):
+def places_of(table, block, slot_count, spare):
     places = []
     for matrix in range(3):
-        first, count = table[1 + matrix, block] - base, table[4 + matrix, block]
+        first, count = table[1 + matrix, block], table[4 + matrix, block]
         places += [jnp.where(slot < count, first + slot, spare) for slot in range(slot_count)]
     return places
 
@@ -215,9 +210,7 @@
     store_parts(ffn_sum, ffn_own, ffn_other, parts)
 
 
-def behind(
-    table, *refs, token_count, weight_parts, slot_count, grad_scale, near, chunks, chunk_rows, parts
-):
+def behind(table, *refs, token_count, weight_parts, slot_count, grad_scale, near, parts):
     token_refs, refs = refs[:token_count], refs[token_count:]
     tiles, x_turned, gate_slope, gate_act, hidden_turned, input_own, input_other = refs[:7]
     grad_refs, input_sum, sums = refs[7:-2], refs[-2], refs[-1]
@@ -249,14 +242,19 @@
 
     in_turn(first, rest, gate_slope.shape[0])
     store_parts(input_sum, input_own, input_other, parts)
-    for chunk in range(chunks):
-        rows = slice(chunk * chunk_rows, (chunk + 1) * chunk_rows)
-        for index, part in enumerate(weight_parts):
-            ref = grad_refs[chunk * len(weight_parts) + index]
-            share = ref.shape[2]
-            for at in range(part[2]):
-                offset = offset_of(table, part, at, near, share)
-                ref[at] = sums[rows, pl.ds(offset, share), :].astype(BF16)
+    for ref, part in zip(grad_refs, weight_parts):
+        share = ref.shape[2]
+        for at in range(part[2]):
+            offset = offset_of(table, part, at, near, share)
+            ref[at] = sums[:, pl.ds(offset, share), :].astype(BF16)
+
+
+def fold(table, part_1, part_2, got_1, got_2, out_1, out_2):
+    half = got_1.shape[0]
+    out_2[:half] = add(part_2[:half], got_1[...])
+    out_2[half:] = part_2[half:]
+    out_1[:half] = part_1[:half]
+    out_1[half:] = add(part_1[half:], got_2[...])
 
 
 def call(kernel, table, args, in_specs, out_specs, out_shape, grid=1, scratch=(), cost=0, vmem=40):
@@ -282,9 +280,6 @@
     far = math.gcd(4, math.gcd(dp_size, blocks_dev))
     near = dp_size // far
     blocks = blocks_dev // far
-    chunks = 1
-    chunk_blocks = blocks // chunks
-    groups = far * chunks
     terms = 3 * slot_count
     grad_scale = 1.0 / math.sqrt(own_rows * tensor_size * dp_size)
     me = lax.axis_index("dp")
@@ -297,21 +292,20 @@
     if far > 1:
         x_items[near] = swap(tokens, "dp", near)
 
-    capacity = (terms * blocks_dev - 3 * blocks_dev + 3 * (slot_count - 1) * (groups - 1)) // groups
-    chunk_rows = capacity + 1
+    capacity = (terms * blocks_dev - 3 * blocks_dev + 3 * (slot_count - 1) * (far - 1)) // far
+    slots = capacity + 1
     block_ids = jnp.arange(blocks_dev, dtype=jnp.int32)
     load = tile_counts[0] + tile_counts[1] + tile_counts[2]
     earlier = (load[:, None] > load[None, :]) | (
         (load[:, None] == load[None, :]) & (block_ids[:, None] < block_ids[None, :])
     )
     rank = jnp.sum(earlier.astype(jnp.int32), axis=0)
-    group = rank % groups
-    before = (group[:, None] == group[None, :]) & (rank[:, None] < rank[None, :])
-    start = jnp.sum(jnp.where(before, load[:, None], 0), axis=0) + (group // far) * chunk_rows
+    home = rank % far
+    before = (home[:, None] == home[None, :]) & (rank[:, None] < rank[None, :])
+    start = jnp.sum(jnp.where(before, load[:, None], 0), axis=0)
     ranks_of = (
-        jnp.arange(chunk_blocks, dtype=jnp.int32)[None, None, :] * groups
-        + jnp.arange(chunks, dtype=jnp.int32)[None, :, None] * far
-        + (jnp.arange(far, dtype=jnp.int32)[:, None, None] ^ far_at)
+        jnp.arange(blocks, dtype=jnp.int32)[None, :] * far
+        + (jnp.arange(far, dtype=jnp.int32)[:, None] ^ far_at)
     ).reshape(blocks_dev)
     columns = jnp.concatenate(
         [
@@ -332,9 +326,7 @@
     tile_lines = jnp.transpose(weight_tiles, (0, 1, 3, 2, 4)).reshape(
         row_share, terms, blocks_dev, tile
     )
-    slots = chunks * chunk_rows
     packed_shape = (slots, row_share, tile)
-    chunk_shape = (chunk_rows, row_share, tile)
     packed = call(
         functools.partial(pack, blocks=blocks, slot_count=slot_count),
         table,
@@ -347,8 +339,6 @@
         vmem=24,
     )
     staged = tensor_size == 2 and far == 4 and near == 4
-    if far > 1:
-        packed = after(tuple(packed), x_items[near])
     received = [swap(packed[at], "dp", at * near) for at in reversed(range(1, far))][::-1]
     held = jnp.stack([packed[0], *received])
     x_core, g_core = {}, {}
@@ -467,9 +457,7 @@
     if staged:
         ffn_core, ffn_near = to_near(ffn_own, after(ffn_other, g_items[3 * near]))
         middle = after(tuple(middle), ffn_near)
-    part_shapes = [
-        shape((length,) + chunk_shape, BF16) for _ in range(chunks) for _, _, length in weight_parts
-    ]
+    part_shapes = [shape((length,) + packed_shape, BF16) for _, _, length in weight_parts]
     outs = call(
         functools.partial(
             behind,
@@ -478,8 +466,6 @@
             slot_count=slot_count,
             grad_scale=grad_scale,
             near=near,
-            chunks=chunks,
-            chunk_rows=chunk_rows,
             parts=parts,
         ),
         table,
@@ -491,19 +477,16 @@
         cost=40_000_000,
     )
     (input_own, input_other), tile_terms = outs[:2], outs[2:]
-    tile_terms = [
-        tile_terms[chunk * len(weight_parts) : (chunk + 1) * len(weight_parts)]
-        for chunk in range(chunks)
-    ]
 
     def halves(parts):
         return swap(parts[3], "dp", 1), swap(parts[4], "dp", 2)
 
     def folded(parts, got_1, got_2):
-        others = ((0, 0),) * 3
-        to_2 = add(parts[2], jnp.pad(got_1, ((0, far - half), *others)))
-        to_1 = add(parts[1], jnp.pad(got_2, ((half, 0), *others)))
-        return to_1, to_2
+        args = [parts[1], parts[2], got_1, got_2]
+        out_shapes = [shape(parts[1].shape, BF16)] * 2
+        return call(
+            fold, table, args, specs_of(args), specs_of(out_shapes), out_shapes, cost=40_000_000, vmem=16
+        )
 
     def summed(parts, to_1, to_2):
         from_1, from_2 = swap(to_1, "dp", 1), swap(to_2, "dp", 2)
@@ -515,13 +498,12 @@
     if staged:
         ffn_got = swap(ffn_near, "dp", near)
         tile_terms, input_other = after((tile_terms, input_other), ffn_got)
-        (tile_terms,) = tile_terms
         got = halves(tile_terms)
         ffn_last = to_far(ffn_own, ffn_core, ffn_got)
         ffn_far = swap(ffn_last, "dp", 2 * near)
         input_core, input_near = to_near(input_own, input_other)
-        input_got = swap(input_near, "dp", near)
-        to_1, to_2 = after(folded(tile_terms, *got), input_near, ffn_far)
+        input_got = swap(after(input_near, ffn_far), "dp", near)
+        to_1, to_2 = folded(after(tile_terms, ffn_last), *got)
         input_last = to_far(input_own, input_core, input_got)
         input_far = swap(input_last, "dp", 2 * near)
         sums = after(tuple(summed(tile_terms, to_1, to_2)), input_last)
@@ -529,19 +511,17 @@
         ffn_rows = add(ffn_own[0], ffn_core[0], ffn_got[0], ffn_far)
         input_rows = add(input_own[0], input_core[0], input_got[0], input_far)
     else:
-        back = []
-        for terms_of in tile_terms:
-            if split:
-                sums = summed(terms_of, *folded(terms_of, *halves(terms_of)))
-            else:
-                sums = scatter(dict(enumerate(terms_of)), "dp", near_strides)[0]
-            back += sent_back(sums)
+        if split:
+            sums = summed(tile_terms, *folded(tile_terms, *halves(tile_terms)))
+        else:
+            sums = scatter(dict(enumerate(tile_terms)), "dp", near_strides)[0]
+        back = sent_back(sums)
         ffn_rows = generic(ffn_own, ffn_other)
         input_rows = generic(input_own, input_other)
 
     grads = call(
         functools.partial(
-            unpack, chunks=chunks, chunk_rows=chunk_rows, blocks=blocks, slot_count=slot_count
+            unpack, blocks=blocks, slot_count=slot_count
         ),
         table,
         back,

time: 147 us -> 147 us (level)
  starting transfers between devices: 35.5 us -> 31.6 us
  waiting for transfers between devices: 78.9 us -> 82.5 us
    ppermute x31, starting transfers between devices: 35.5 us -> 31.6 us  [swap(): return lax.ppermute(value, axis, [(at, at ^ stride) for at in range(size)])]
    ppermute x31, waiting for transfers between devices: 78.9 us -> 82.5 us  [swap(): return lax.ppermute(value, axis, [(at, at ^ stride) for at in range(size)])]
    pallas_call x5 -> x6, Pallas kernels: 23.6 us -> 23.2 us  [call(): pl.pallas_call(kernel, grid_spec=pltpu.PrefetchScalarGridSpec(num_scalar_...]
  transfers between devices with their start and end apart: 31 -> 31, of which waited for: 17 -> 16; matrix products, arithmetic and copies ran while one was open for 5% -> 4% of each run, Pallas kernels for 14% -> 14%
where the time goes in v8:
time: 147 us; the launch traced here: 146 us
  waiting for transfers between devices  82.5 us (56%)
  starting transfers between devices  31.6 us (21%)
  Pallas kernels  23.2 us (16%)
  other arithmetic  4.88 us (3%)
  local copies, waits for them, and re-layouts  2.87 us (2%)
    ppermute x31, waiting for transfers between devices, swap(): return lax.ppermute(value, axis, [(at, at ^ stride) for at in range(size)])  82.5 us
    ppermute x31, starting transfers between devices, swap(): return lax.ppermute(value, axis, [(at, at ^ stride) for at in range(size)])  31.6 us
    pallas_call x6, Pallas kernels, call(): pl.pallas_call(kernel, grid_spec=pltpu.PrefetchScalarGridSpec(num_scalar_...  23.2 us
  transfers between devices with their start and end apart: 31, of which 16 were waited for; matrix products, arithmetic and copies ran while one was open for 4% of the time, Pallas kernels for 14%

profile of v8, /device:TPU:0, one launch (start us, length us, event | category | flops | bytes accessed | tf_op | source)
XLA Modules:
  0.0 145.9 jit_solution(6067052551482640188)
XLA Ops:
  0.6 3.1 %collective-permute-start = (bf16[32,4096]{1,0:T(8,128)(2,1)}, bf16[32,4096]{1,0:T(8,128)(2,1)S(1)}, u32[]{:S(2)}, u32[]{:S(2)}) collective-permute-start(bf16[32,4096]{1,0:T(8,128)(2,1)} %refs_0_.2), channel_id=1, source_target_pairs={{0,8},{2,10},{4,12},{6,14},{8,0},{10,2},{12,4},{14,6},{16,24},{18,... | collective-permute-start | bytes 786440 | tf_op jit(solution)/shard_map/ppermute | solution.py:22
  7.6 1.2 copy-done.1
  8.9 1.6 %shard_map.76 = (bf16[89,8,128]{2,1,0:T(8,128)(2,1)S(1)}, bf16[89,8,128]{2,1,0:T(8,128)(2,1)S(1)}, bf16[89,8,128]{2,1,0:T(8,128)(2,1)S(1)}, bf16[89,8,128]{2,1,0:T(8,128)(2,1)S(1)}) custom-call(s32[17,56]{1,0:T(8,128)S(1)} %pad_add_fusion.table, bf16[8,9,56,128]{3,2,1,0:T(8,128)(2,1)S(1)} %bitcast.36), custom_call_target="tpu_custom_call" | custom-call | bytes 1000000 | tf_op jit(solution)/shard_map/pallas_call | solution.py:261
  10.5 2.5 %collective-permute-start.3 = (bf16[89,8,128]{2,1,0:T(8,128)(2,1)S(1)}, bf16[89,8,128]{2,1,0:T(8,128)(2,1)S(1)}, u32[]{:S(2)}, u32[]{:S(2)}) collective-permute-start(bf16[89,8,128]{2,1,0:T(8,128)(2,1)S(1)} %get-tuple-element.53), channel_id=1, source_target_pairs={{0,24},{2,26},{4,28},{6,30},{8,16},{10,18},{12,20},{14,22},{16,8},... | collective-permute-start | bytes 546824 | tf_op jit(solution)/shard_map/ppermute | solution.py:22
  13.2 1.7 %collective-permute-start.1 = (bf16[89,8,128]{2,1,0:T(8,128)(2,1)S(1)}, bf16[89,8,128]{2,1,0:T(8,128)(2,1)S(1)}, u32[]{:S(2)}, u32[]{:S(2)}) collective-permute-start(bf16[89,8,128]{2,1,0:T(8,128)(2,1)S(1)} %get-tuple-element.51), channel_id=1, source_target_pairs={{0,8},{2,10},{4,12},{6,14},{8,0},{10,2},{12,4},{14,6},{16,24},{18,... | collective-permute-start | bytes 546824 | tf_op jit(solution)/shard_map/ppermute | solution.py:22
  14.9 5.0 %collective-permute-done.3 = bf16[89,8,128]{2,1,0:T(8,128)(2,1)S(1)} collective-permute-done((bf16[89,8,128]{2,1,0:T(8,128)(2,1)S(1)}, bf16[89,8,128]{2,1,0:T(8,128)(2,1)S(1)}, u32[]{:S(2)}, u32[]{:S(2)}) %collective-permute-start.3) | collective-permute-done | bytes 182304 | tf_op jit(solution)/shard_map/ppermute | solution.py:22
  20.5 8.7 %collective-permute-done.2 = bf16[89,8,128]{2,1,0:T(8,128)(2,1)S(1)} collective-permute-done((bf16[89,8,128]{2,1,0:T(8,128)(2,1)S(1)}, bf16[89,8,128]{2,1,0:T(8,128)(2,1)S(1)}, u32[]{:S(2)}, u32[]{:S(2)}) %collective-permute-start.2) | collective-permute-done | bytes 182304 | tf_op jit(solution)/shard_map/ppermute | solution.py:22
  29.3 1.6 %collective-permute-start.10 = (bf16[4,89,8,128]{3,2,1,0:T(8,128)(2,1)S(1)}, bf16[4,89,8,128]{3,2,1,0:T(8,128)(2,1)S(1)}, u32[]{:S(2)}, u32[]{:S(2)}) collective-permute-start(bf16[4,89,8,128]{3,2,1,0:T(8,128)(2,1)S(1)} %pad_maximum_fusion.1.refs_0_), channel_id=1, source_target_pairs={{0,2},{2,0},{4,6},{6,4},{8,10},{10,8},{12,14},{14,12},{16,18},{18,... | collective-permute-start | bytes 2187272 | tf_op jit(solution)/shard_map/ppermute | solution.py:22
  30.9 1.5 %collective-permute-start.12 = (bf16[4,89,8,128]{3,2,1,0:T(8,128)(2,1)S(1)}, bf16[4,89,8,128]{3,2,1,0:T(8,128)(2,1)S(1)}, u32[]{:S(2)}, u32[]{:S(2)}) collective-permute-start(bf16[4,89,8,128]{3,2,1,0:T(8,128)(2,1)S(1)} %pad_maximum_fusion.1.refs_0_), channel_id=1, source_target_pairs={{0,4},{2,6},{4,0},{6,2},{8,12},{10,14},{12,8},{14,10},{16,20},{18,... | collective-permute-start | bytes 2187272 | tf_op jit(solution)/shard_map/ppermute | solution.py:22
  33.0 2.6 %collective-permute-start.8 = (bf16[32,4096]{1,0:T(8,128)(2,1)S(1)}, bf16[32,4096]{1,0:T(8,128)(2,1)S(1)}, u32[]{:S(2)}, u32[]{:S(2)}) collective-permute-start(bf16[32,4096]{1,0:T(8,128)(2,1)S(1)} %copy-done.3), channel_id=1, source_target_pairs={{0,8},{2,10},{4,12},{6,14},{8,0},{10,2},{12,4},{14,6},{16,24},{18,... | collective-permute-start | bytes 786440 | tf_op jit(solution)/shard_map/ppermute | solution.py:22
  35.6 10.1 %collective-permute-done.7.refs_2_ = bf16[32,4096]{1,0:T(8,128)(2,1)S(1)} collective-permute-done((bf16[32,4096]{1,0:T(8,128)(2,1)S(1)}, bf16[32,4096]{1,0:T(8,128)(2,1)S(1)}, u32[]{:S(2)}, u32[]{:S(2)}) %collective-permute-start.7) | collective-permute-done | bytes 262176 | tf_op jit(solution)/shard_map/ppermute | solution.py:22
  46.5 2.3 %collective-permute-start.14 = (bf16[32,4096]{1,0:T(8,128)(2,1)S(1)}, bf16[32,4096]{1,0:T(8,128)(2,1)S(1)}, u32[]{:S(2)}, u32[]{:S(2)}) collective-permute-start(bf16[32,4096]{1,0:T(8,128)(2,1)S(1)} %copy-done.3), channel_id=1, source_target_pairs={{0,16},{2,18},{4,20},{6,22},{8,24},{10,26},{12,28},{14,30},{16,0},... | collective-permute-start | bytes 786440 | tf_op jit(solution)/shard_map/ppermute | solution.py:22
  50.0 9.1 %collective-permute-done.9.refs_3_ = bf16[32,4096]{1,0:T(8,128)(2,1)S(1)} collective-permute-done((bf16[32,4096]{1,0:T(8,128)(2,1)S(1)}, bf16[32,4096]{1,0:T(8,128)(2,1)S(1)}, u32[]{:S(2)}, u32[]{:S(2)}) %collective-permute-start.9) | collective-permute-done | bytes 262176 | tf_op jit(solution)/shard_map/ppermute | solution.py:22
  59.2 1.5 collective-permute-done.14.refs_2_
  61.1 1.8 %shard_map.77.refs_7_.refs_6_ = bf16[89,128,128]{2,1,0:T(8,128)(2,1)S(1)} custom-call(s32[17,56]{1,0:T(8,128)S(1)} %pad_add_fusion.table, bf16[4,89,8,128]{3,2,1,0:T(8,128)(2,1)S(1)} %pad_maximum_fusion.1.refs_0_, bf16[4,89,8,128]{3,2,1,0:T(8,128)(2,1)S(1)} %collective-permute-done.10.refs_1_, bf16[4,89,8,128]{3,2,1,0:T(8,128)(2,1)S(1)} %collective-permute-done.12.refs_2_, ...), custom_call_target="tpu_custom_call" | custom-call | bytes 10000000 | tf_op jit(solution)/shard_map/pallas_call | solution.py:261
  62.9 5.6 %shard_map.78 = (bf16[4096,256]{1,0:T(8,128)(2,1)S(1)}, f32[14,256,128]{2,1,0:T(8,128)S(1)}, f32[14,256,128]{2,1,0:T(8,128)S(1)}, bf16[14,128,256]{2,1,0:T(8,128...) custom-call(s32[17,56]{1,0:T(8,128)S(1)} %pad_add_fusion.table, ...), custom_call_target="tpu_custom_call" | custom-call | bytes 30000000 | tf_op jit(solution)/shard_map/pallas_call | solution.py:261
  70.0 2.0 %collective-permute-done.17 = bf16[4,32,4096]{2,1,0:T(8,128)(2,1)S(1)} collective-permute-done((bf16[4,32,4096]{2,1,0:T(8,128)(2,1)S(1)}, bf16[4,32,4096]{2,1,0:T(8,128)(2,1)S(1)}, u32[]{:S(2)}, u32[]{:S(2)}) %collective-permute-start.17) | collective-permute-done | bytes 1048608 | tf_op jit(solution)/shard_map/ppermute | solution.py:22
  72.2 1.0 collective-permute-start.18
  73.2 10.2 %shard_map.79 = (bf16[4,32,4096]{2,1,0:T(8,128)(2,1)S(1)}, bf16[4,32,4096]{2,1,0:T(8,128)(2,1)S(1)}, bf16[4,89,8,128]{3,2,1,0:T(8,128)(2,1)S(1)}, bf16[4,89,8,12...) custom-call(s32[17,56]{1,0:T(8,128)S(1)} %pad_add_fusion.table, ...), custom_call_target="tpu_custom_call" | custom-call | bytes 40000000 | tf_op jit(solution)/shard_map/pallas_call | solution.py:261
  83.4 2.8 %collective-permute-done.18 = bf16[2,32,4096]{2,1,0:T(8,128)(2,1)S(1)} collective-permute-done((bf16[2,32,4096]{2,1,0:T(8,128)(2,1)S(1)}, bf16[2,32,4096]{2,1,0:T(8,128)(2,1)S(1)}, u32[]{:S(2)}, u32[]{:S(2)}) %collective-permute-start.18) | collective-permute-done | bytes 524320 | tf_op jit(solution)/shard_map/ppermute | solution.py:22
  87.3 1.9 %collective-permute-start.19 = (bf16[32,4096]{1,0:T(8,128)(2,1)S(1)}, bf16[32,4096]{1,0:T(8,128)(2,1)S(1)}, u32[]{:S(2)}, u32[]{:S(2)}) collective-permute-start(bf16[32,4096]{1,0:T(8,128)(2,1)S(1)} %fusion.2), channel_id=1, source_target_pairs={{0,16},{2,18},{4,20},{6,22},{8,24},{10,26},{12,28},{14,30},{16,0},... | collective-permute-start | bytes 786440 | tf_op jit(solution)/shard_map/ppermute | solution.py:22
  89.2 7.9 %collective-permute-done.24.got_1 = bf16[2,89,8,128]{3,2,1,0:T(8,128)(2,1)S(1)} collective-permute-done((bf16[2,89,8,128]{3,2,1,0:T(8,128)(2,1)S(1)}, bf16[2,89,8,128]{3,2,1,0:T(8,128)(2,1)S(1)}, u32[]{:S(2)}, u32[]{:S(2)}) %collective-permute-start.24) | collective-permute-done | bytes 364576 | tf_op jit(solution)/shard_map/ppermute | solution.py:22
  98.9 1.5 %collective-permute-start.26 = (bf16[4,89,8,128]{3,2,1,0:T(8,128)(2,1)S(1)}, bf16[4,89,8,128]{3,2,1,0:T(8,128)(2,1)S(1)}, u32[]{:S(2)}, u32[]{:S(2)}) collective-permute-start(bf16[4,89,8,128]{3,2,1,0:T(8,128)(2,1)S(1)} %get-tuple-element.87), channel_id=1, source_target_pairs={{0,2},{2,0},{4,6},{6,4},{8,10},{10,8},{12,14},{14,12},{16,18},{18,... | collective-permute-start | bytes 2187272 | tf_op jit(solution)/shard_map/ppermute | solution.py:22
  100.5 1.6 %collective-permute-done.19 = bf16[32,4096]{1,0:T(8,128)(2,1)S(1)} collective-permute-done((bf16[32,4096]{1,0:T(8,128)(2,1)S(1)}, bf16[32,4096]{1,0:T(8,128)(2,1)S(1)}, u32[]{:S(2)}, u32[]{:S(2)}) %collective-permute-start.19) | collective-permute-done | bytes 262176 | tf_op jit(solution)/shard_map/ppermute | solution.py:22
  102.1 14.0 %collective-permute-done.27 = bf16[4,89,8,128]{3,2,1,0:T(8,128)(2,1)S(1)} collective-permute-done((bf16[4,89,8,128]{3,2,1,0:T(8,128)(2,1)S(1)}, bf16[4,89,8,128]{3,2,1,0:T(8,128)(2,1)S(1)}, u32[]{:S(2)}, u32[]{:S(2)}) %collective-permute-start.27) | collective-permute-done | bytes 729120 | tf_op jit(solution)/shard_map/ppermute | solution.py:22
  116.7 1.9 %collective-permute-start.23 = (bf16[32,4096]{1,0:T(8,128)(2,1)S(1)}, bf16[32,4096]{1,0:T(8,128)(2,1)S(1)}, u32[]{:S(2)}, u32[]{:S(2)}) collective-permute-start(bf16[32,4096]{1,0:T(8,128)(2,1)S(1)} %fusion.3), channel_id=1, source_target_pairs={{0,16},{2,18},{4,20},{6,22},{8,24},{10,26},{12,28},{14,30},{16,0},... | collective-permute-start | bytes 786440 | tf_op jit(solution)/shard_map/ppermute | solution.py:22
  118.6 1.1 collective-permute-start.28
  119.7 1.0 collective-permute-start.29
  120.7 2.3 %collective-permute-start.30 = (bf16[89,8,128]{2,1,0:T(8,128)(2,1)S(1)}, bf16[89,8,128]{2,1,0:T(8,128)(2,1)S(1)}, u32[]{:S(2)}, u32[]{:S(2)}) collective-permute-start(bf16[89,8,128]{2,1,0:T(8,128)(2,1)S(1)} %get-tuple-element.92), channel_id=1, source_target_pairs={{0,24},{2,26},{4,28},{6,30},{8,16},{10,18},{12,20},{14,22},{16,8},... | collective-permute-start | bytes 546824 | tf_op jit(solution)/shard_map/ppermute | solution.py:22
  123.8 5.4 %collective-permute-done.28.refs_1_ = bf16[89,8,128]{2,1,0:T(8,128)(2,1)S(1)} collective-permute-done((bf16[89,8,128]{2,1,0:T(8,128)(2,1)S(1)}, bf16[89,8,128]{2,1,0:T(8,128)(2,1)S(1)}, u32[]{:S(2)}, u32[]{:S(2)}) %collective-permute-start.28) | collective-permute-done | bytes 182304 | tf_op jit(solution)/shard_map/ppermute | solution.py:22
  129.3 12.8 %collective-permute-done.29.refs_2_ = bf16[89,8,128]{2,1,0:T(8,128)(2,1)S(1)} collective-permute-done((bf16[89,8,128]{2,1,0:T(8,128)(2,1)S(1)}, bf16[89,8,128]{2,1,0:T(8,128)(2,1)S(1)}, u32[]{:S(2)}, u32[]{:S(2)}) %collective-permute-start.29) | collective-permute-done | bytes 182304 | tf_op jit(solution)/shard_map/ppermute | solution.py:22
  142.1 3.0 %shard_map.81 = bf16[8,9,56,128]{3,2,1,0:T(8,128)(2,1)} custom-call(s32[17,56]{1,0:T(8,128)S(1)} %pad_add_fusion.table, bf16[89,8,128]{2,1,0:T(8,128)(2,1)S(1)} %get-tuple-element.93.refs_0_, bf16[89,8,128]{2,1,0:T(8,128)(2,1)S(1)} %collective-permute-done.28.refs_1_, bf16[89,8,128]{2,1,0:T(8,128)(2,1)S(1)} %collective-permute-done.29.refs_2_, ...), custom_call_target="tpu_custom_call" | custom-call | bytes 2000000 | tf_op jit(solution)/shard_map/pallas_call | solution.py:261
  (72 shorter events, 14.7 us)
Async XLA Ops:
  0.6 19.4 %collective-permute-start = (bf16[32,4096]{1,0:T(8,128)(2,1)}, bf16[32,4096]{1,0:T(8,128)(2,1)S(1)}, u32[]{:S(2)}, u32[]{:S(2)}) collective-permute-start(bf16[32,4096]{1,0:T(8,128)(2,1)} %refs_0_.2), channel_id=1, source_target_pairs={{0,8},{2,10},{4,12},{6,14},{8,0},{10,2},{12,4},{14,6},{16,24},{18,... | collective-permute-start | bytes 786440 | tf_op jit(solution)/shard_map/ppermute | solution.py:22
  8.9 24.2 %copy-start.3 = (bf16[32,4096]{1,0:T(8,128)(2,1)S(1)}, bf16[32,4096]{1,0:T(8,128)(2,1)}, u32[]{:S(2)}) copy-start(bf16[32,4096]{1,0:T(8,128)(2,1)} %refs_0_.3) | copy-start | bytes 786436
  10.5 9.5 %collective-permute-start.3 = (bf16[89,8,128]{2,1,0:T(8,128)(2,1)S(1)}, bf16[89,8,128]{2,1,0:T(8,128)(2,1)S(1)}, u32[]{:S(2)}, u32[]{:S(2)}) collective-permute-start(bf16[89,8,128]{2,1,0:T(8,128)(2,1)S(1)} %get-tuple-element.53), channel_id=1, source_target_pairs={{0,24},{2,26},{4,28},{6,30},{8,16},{10,18},{12,20},{14,22},{16,8},... | collective-permute-start | bytes 546824 | tf_op jit(solution)/shard_map/ppermute | solution.py:22
  13.0 16.1 %collective-permute-start.2 = (bf16[89,8,128]{2,1,0:T(8,128)(2,1)S(1)}, bf16[89,8,128]{2,1,0:T(8,128)(2,1)S(1)}, u32[]{:S(2)}, u32[]{:S(2)}) collective-permute-start(bf16[89,8,128]{2,1,0:T(8,128)(2,1)S(1)} %get-tuple-element.52), channel_id=1, source_target_pairs={{0,16},{2,18},{4,20},{6,22},{8,24},{10,26},{12,28},{14,30},{16,0},... | collective-permute-start | bytes 546824 | tf_op jit(solution)/shard_map/ppermute | solution.py:22
  13.2 16.0 %collective-permute-start.1 = (bf16[89,8,128]{2,1,0:T(8,128)(2,1)S(1)}, bf16[89,8,128]{2,1,0:T(8,128)(2,1)S(1)}, u32[]{:S(2)}, u32[]{:S(2)}) collective-permute-start(bf16[89,8,128]{2,1,0:T(8,128)(2,1)S(1)} %get-tuple-element.51), channel_id=1, source_target_pairs={{0,8},{2,10},{4,12},{6,14},{8,0},{10,2},{12,4},{14,6},{16,24},{18,... | collective-permute-start | bytes 546824 | tf_op jit(solution)/shard_map/ppermute | solution.py:22
  14.9 14.3 %collective-permute-start.4 = (bf16[32,4096]{1,0:T(8,128)(2,1)}, bf16[32,4096]{1,0:T(8,128)(2,1)S(1)}, u32[]{:S(2)}, u32[]{:S(2)}) collective-permute-start(bf16[32,4096]{1,0:T(8,128)(2,1)} %refs_0_.2), channel_id=1, source_target_pairs={{0,1},{1,0},{2,3},{3,2},{4,5},{5,4},{6,7},{7,6},{8,9},{9,8},{10,11... | collective-permute-start | bytes 786440 | tf_op jit(solution)/shard_map/ppermute | solution.py:22
  20.0 9.3 %collective-permute-start.6 = (bf16[32,4096]{1,0:T(8,128)(2,1)}, bf16[32,4096]{1,0:T(8,128)(2,1)S(1)}, u32[]{:S(2)}, u32[]{:S(2)}) collective-permute-start(bf16[32,4096]{1,0:T(8,128)(2,1)} %refs_0_.3), channel_id=1, source_target_pairs={{0,1},{1,0},{2,3},{3,2},{4,5},{5,4},{6,7},{7,6},{8,9},{9,8},{10,11... | collective-permute-start | bytes 786440 | tf_op jit(solution)/shard_map/ppermute | solution.py:22
  20.0 9.3 %collective-permute-start.5 = (bf16[32,4096]{1,0:T(8,128)(2,1)S(1)}, bf16[32,4096]{1,0:T(8,128)(2,1)S(1)}, u32[]{:S(2)}, u32[]{:S(2)}) collective-permute-start(bf16[32,4096]{1,0:T(8,128)(2,1)S(1)} %collective-permute-done.refs_1_), channel_id=1, source_target_pairs={{0,1},{1,0},{2,3},{3,2},{4,5},{5,4},{6,7},{7,6},{8,9},{9,8},{10,11... | collective-permute-start | bytes 786440 | tf_op jit(solution)/shard_map/ppermute | solution.py:22
  29.3 19.5 %collective-permute-start.10 = (bf16[4,89,8,128]{3,2,1,0:T(8,128)(2,1)S(1)}, bf16[4,89,8,128]{3,2,1,0:T(8,128)(2,1)S(1)}, u32[]{:S(2)}, u32[]{:S(2)}) collective-permute-start(bf16[4,89,8,128]{3,2,1,0:T(8,128)(2,1)S(1)} %pad_maximum_fusion.1.refs_0_), channel_id=1, source_target_pairs={{0,2},{2,0},{4,6},{6,4},{8,10},{10,8},{12,14},{14,12},{16,18},{18,... | collective-permute-start | bytes 2187272 | tf_op jit(solution)/shard_map/ppermute | solution.py:22
  30.9 18.5 %collective-permute-start.12 = (bf16[4,89,8,128]{3,2,1,0:T(8,128)(2,1)S(1)}, bf16[4,89,8,128]{3,2,1,0:T(8,128)(2,1)S(1)}, u32[]{:S(2)}, u32[]{:S(2)}) collective-permute-start(bf16[4,89,8,128]{3,2,1,0:T(8,128)(2,1)S(1)} %pad_maximum_fusion.1.refs_0_), channel_id=1, source_target_pairs={{0,4},{2,6},{4,0},{6,2},{8,12},{10,14},{12,8},{14,10},{16,20},{18,... | collective-permute-start | bytes 2187272 | tf_op jit(solution)/shard_map/ppermute | solution.py:22
  32.4 13.3 %collective-permute-start.7 = (bf16[32,4096]{1,0:T(8,128)(2,1)S(1)}, bf16[32,4096]{1,0:T(8,128)(2,1)S(1)}, u32[]{:S(2)}, u32[]{:S(2)}) collective-permute-start(bf16[32,4096]{1,0:T(8,128)(2,1)S(1)} %copy-done.2), channel_id=1, source_target_pairs={{0,16},{2,18},{4,20},{6,22},{8,24},{10,26},{12,28},{14,30},{16,0},... | collective-permute-start | bytes 786440 | tf_op jit(solution)/shard_map/ppermute | solution.py:22
  33.0 12.9 %collective-permute-start.8 = (bf16[32,4096]{1,0:T(8,128)(2,1)S(1)}, bf16[32,4096]{1,0:T(8,128)(2,1)S(1)}, u32[]{:S(2)}, u32[]{:S(2)}) collective-permute-start(bf16[32,4096]{1,0:T(8,128)(2,1)S(1)} %copy-done.3), channel_id=1, source_target_pairs={{0,8},{2,10},{4,12},{6,14},{8,0},{10,2},{12,4},{14,6},{16,24},{18,... | collective-permute-start | bytes 786440 | tf_op jit(solution)/shard_map/ppermute | solution.py:22
  45.9 13.2 %collective-permute-start.9 = (bf16[32,4096]{1,0:T(8,128)(2,1)S(1)}, bf16[32,4096]{1,0:T(8,128)(2,1)S(1)}, u32[]{:S(2)}, u32[]{:S(2)}) collective-permute-start(bf16[32,4096]{1,0:T(8,128)(2,1)S(1)} %collective-permute-done.7.refs_2_), channel_id=1, source_target_pairs={{0,8},{2,10},{4,12},{6,14},{8,0},{10,2},{12,4},{14,6},{16,24},{18,... | collective-permute-start | bytes 786440 | tf_op jit(solution)/shard_map/ppermute | solution.py:22
  46.5 14.2 %collective-permute-start.14 = (bf16[32,4096]{1,0:T(8,128)(2,1)S(1)}, bf16[32,4096]{1,0:T(8,128)(2,1)S(1)}, u32[]{:S(2)}, u32[]{:S(2)}) collective-permute-start(bf16[32,4096]{1,0:T(8,128)(2,1)S(1)} %copy-done.3), channel_id=1, source_target_pairs={{0,16},{2,18},{4,20},{6,22},{8,24},{10,26},{12,28},{14,30},{16,0},... | collective-permute-start | bytes 786440 | tf_op jit(solution)/shard_map/ppermute | solution.py:22
  48.8 11.8 %collective-permute-start.11 = (bf16[2,89,8,128]{3,2,1,0:T(8,128)(2,1)S(1)}, bf16[2,89,8,128]{3,2,1,0:T(8,128)(2,1)S(1)}, u32[]{:S(2)}, u32[]{:S(2)}) collective-permute-start(bf16[2,89,8,128]{3,2,1,0:T(8,128)(2,1)S(1)} %slice.135), channel_id=1, source_target_pairs={{0,4},{2,6},{4,0},{6,2},{8,12},{10,14},{12,8},{14,10},{16,20},{18,... | collective-permute-start | bytes 1093640 | tf_op jit(solution)/shard_map/ppermute | solution.py:22
  49.4 11.2 %collective-permute-start.13 = (bf16[2,89,8,128]{3,2,1,0:T(8,128)(2,1)S(1)}, bf16[2,89,8,128]{3,2,1,0:T(8,128)(2,1)S(1)}, u32[]{:S(2)}, u32[]{:S(2)}) collective-permute-start(bf16[2,89,8,128]{3,2,1,0:T(8,128)(2,1)S(1)} %slice.136), channel_id=1, source_target_pairs={{0,2},{2,0},{4,6},{6,4},{8,10},{10,8},{12,14},{14,12},{16,18},{18,... | collective-permute-start | bytes 1093640 | tf_op jit(solution)/shard_map/ppermute | solution.py:22
  60.7 2.2 %collective-permute-start.15 = (bf16[64,4096]{1,0:T(8,128)(2,1)S(1)}, bf16[64,4096]{1,0:T(8,128)(2,1)S(1)}, u32[]{:S(2)}, u32[]{:S(2)}) collective-permute-start(bf16[64,4096]{1,0:T(8,128)(2,1)S(1)} %pad_maximum_fusion.2), channel_id=1, source_target_pairs={{0,1},{1,0},{2,3},{3,2},{4,5},{5,4},{6,7},{7,6},{8,9},{9,8},{10,11... | collective-permute-start | bytes 1572872 | tf_op jit(solution)/shard_map/ppermute | solution.py:22
  60.7 8.7 %collective-permute-start.16 = (bf16[32,4096]{1,0:T(8,128)(2,1)S(1)}, bf16[32,4096]{1,0:T(8,128)(2,1)S(1)}, u32[]{:S(2)}, u32[]{:S(2)}) collective-permute-start(bf16[32,4096]{1,0:T(8,128)(2,1)S(1)} %collective-permute-done.14.refs_2_), channel_id=1, source_target_pairs={{0,8},{2,10},{4,12},{6,14},{8,0},{10,2},{12,4},{14,6},{16,24},{18,... | collective-permute-start | bytes 786440 | tf_op jit(solution)/shard_map/ppermute | solution.py:22
  69.4 2.7 %collective-permute-start.17 = (bf16[4,32,4096]{2,1,0:T(8,128)(2,1)S(1)}, bf16[4,32,4096]{2,1,0:T(8,128)(2,1)S(1)}, u32[]{:S(2)}, u32[]{:S(2)}) collective-permute-start(bf16[4,32,4096]{2,1,0:T(8,128)(2,1)S(1)} %get-tuple-element.62), channel_id=1, source_target_pairs={{0,1},{1,0},{2,3},{3,2},{4,5},{5,4},{6,7},{7,6},{8,9},{9,8},{10,11... | collective-permute-start | bytes 3145736 | tf_op jit(solution)/shard_map/ppermute | solution.py:22
  69.4 3.7 %collective-permute-start.20 = (bf16[96,4096]{1,0:T(8,128)(2,1)S(1)}, bf16[96,4096]{1,0:T(8,128)(2,1)S(1)}, u32[]{:S(2)}, u32[]{:S(2)}) collective-permute-start(bf16[96,4096]{1,0:T(8,128)(2,1)S(1)} %pad_maximum_fusion), channel_id=1, source_target_pairs={{0,1},{1,0},{2,3},{3,2},{4,5},{5,4},{6,7},{7,6},{8,9},{9,8},{10,11... | collective-permute-start | bytes 2359304 | tf_op jit(solution)/shard_map/ppermute | solution.py:22
  72.2 14.0 %collective-permute-start.18 = (bf16[2,32,4096]{2,1,0:T(8,128)(2,1)S(1)}, bf16[2,32,4096]{2,1,0:T(8,128)(2,1)S(1)}, u32[]{:S(2)}, u32[]{:S(2)}) collective-permute-start(bf16[2,32,4096]{2,1,0:T(8,128)(2,1)S(1)} %add_convert_fusion.1), channel_id=1, source_target_pairs={{0,8},{2,10},{4,12},{6,14},{8,0},{10,2},{12,4},{14,6},{16,24},{18,... | collective-permute-start | bytes 1572872 | tf_op jit(solution)/shard_map/ppermute | solution.py:22
  86.2 14.2 %collective-permute-start.21 = (bf16[4,32,4096]{2,1,0:T(8,128)(2,1)S(1)}, bf16[4,32,4096]{2,1,0:T(8,128)(2,1)S(1)}, u32[]{:S(2)}, u32[]{:S(2)}) collective-permute-start(bf16[4,32,4096]{2,1,0:T(8,128)(2,1)S(1)} %get-tuple-element.78), channel_id=1, source_target_pairs={{0,1},{1,0},{2,3},{3,2},{4,5},{5,4},{6,7},{7,6},{8,9},{9,8},{10,11... | collective-permute-start | bytes 3145736 | tf_op jit(solution)/shard_map/ppermute | solution.py:22
  86.2 10.9 %collective-permute-start.24 = (bf16[2,89,8,128]{3,2,1,0:T(8,128)(2,1)S(1)}, bf16[2,89,8,128]{3,2,1,0:T(8,128)(2,1)S(1)}, u32[]{:S(2)}, u32[]{:S(2)}) collective-permute-start(bf16[2,89,8,128]{3,2,1,0:T(8,128)(2,1)S(1)} %get-tuple-element.83), channel_id=1, source_target_pairs={{0,2},{2,0},{4,6},{6,4},{8,10},{10,8},{12,14},{14,12},{16,18},{18,... | collective-permute-start | bytes 1093640 | tf_op jit(solution)/shard_map/ppermute | solution.py:22
  86.7 10.6 %collective-permute-start.25 = (bf16[2,89,8,128]{3,2,1,0:T(8,128)(2,1)S(1)}, bf16[2,89,8,128]{3,2,1,0:T(8,128)(2,1)S(1)}, u32[]{:S(2)}, u32[]{:S(2)}) collective-permute-start(bf16[2,89,8,128]{3,2,1,0:T(8,128)(2,1)S(1)} %get-tuple-element.84), channel_id=1, source_target_pairs={{0,4},{2,6},{4,0},{6,2},{8,12},{10,14},{12,8},{14,10},{16,20},{18,... | collective-permute-start | bytes 1093640 | tf_op jit(solution)/shard_map/ppermute | solution.py:22
  87.3 14.7 %collective-permute-start.19 = (bf16[32,4096]{1,0:T(8,128)(2,1)S(1)}, bf16[32,4096]{1,0:T(8,128)(2,1)S(1)}, u32[]{:S(2)}, u32[]{:S(2)}) collective-permute-start(bf16[32,4096]{1,0:T(8,128)(2,1)S(1)} %fusion.2), channel_id=1, source_target_pairs={{0,16},{2,18},{4,20},{6,22},{8,24},{10,26},{12,28},{14,30},{16,0},... | collective-permute-start | bytes 786440 | tf_op jit(solution)/shard_map/ppermute | solution.py:22
  98.3 17.8 %collective-permute-start.27 = (bf16[4,89,8,128]{3,2,1,0:T(8,128)(2,1)S(1)}, bf16[4,89,8,128]{3,2,1,0:T(8,128)(2,1)S(1)}, u32[]{:S(2)}, u32[]{:S(2)}) collective-permute-start(bf16[4,89,8,128]{3,2,1,0:T(8,128)(2,1)S(1)} %get-tuple-element.88), channel_id=1, source_target_pairs={{0,4},{2,6},{4,0},{6,2},{8,12},{10,14},{12,8},{14,10},{16,20},{18,... | collective-permute-start | bytes 2187272 | tf_op jit(solution)/shard_map/ppermute | solution.py:22
  98.9 17.4 %collective-permute-start.26 = (bf16[4,89,8,128]{3,2,1,0:T(8,128)(2,1)S(1)}, bf16[4,89,8,128]{3,2,1,0:T(8,128)(2,1)S(1)}, u32[]{:S(2)}, u32[]{:S(2)}) collective-permute-start(bf16[4,89,8,128]{3,2,1,0:T(8,128)(2,1)S(1)} %get-tuple-element.87), channel_id=1, source_target_pairs={{0,2},{2,0},{4,6},{6,4},{8,10},{10,8},{12,14},{14,12},{16,18},{18,... | collective-permute-start | bytes 2187272 | tf_op jit(solution)/shard_map/ppermute | solution.py:22
  102.1 14.5 %collective-permute-start.22 = (bf16[2,32,4096]{2,1,0:T(8,128)(2,1)S(1)}, bf16[2,32,4096]{2,1,0:T(8,128)(2,1)S(1)}, u32[]{:S(2)}, u32[]{:S(2)}) collective-permute-start(bf16[2,32,4096]{2,1,0:T(8,128)(2,1)S(1)} %add_convert_fusion), channel_id=1, source_target_pairs={{0,8},{2,10},{4,12},{6,14},{8,0},{10,2},{12,4},{14,6},{16,24},{18,... | collective-permute-start | bytes 1572872 | tf_op jit(solution)/shard_map/ppermute | solution.py:22
  116.7 25.4 %collective-permute-start.23 = (bf16[32,4096]{1,0:T(8,128)(2,1)S(1)}, bf16[32,4096]{1,0:T(8,128)(2,1)S(1)}, u32[]{:S(2)}, u32[]{:S(2)}) collective-permute-start(bf16[32,4096]{1,0:T(8,128)(2,1)S(1)} %fusion.3), channel_id=1, source_target_pairs={{0,16},{2,18},{4,20},{6,22},{8,24},{10,26},{12,28},{14,30},{16,0},... | collective-permute-start | bytes 786440 | tf_op jit(solution)/shard_map/ppermute | solution.py:22
  118.6 10.7 %collective-permute-start.28 = (bf16[89,8,128]{2,1,0:T(8,128)(2,1)S(1)}, bf16[89,8,128]{2,1,0:T(8,128)(2,1)S(1)}, u32[]{:S(2)}, u32[]{:S(2)}) collective-permute-start(bf16[89,8,128]{2,1,0:T(8,128)(2,1)S(1)} %get-tuple-element.90), channel_id=1, source_target_pairs={{0,8},{2,10},{4,12},{6,14},{8,0},{10,2},{12,4},{14,6},{16,24},{18,... | collective-permute-start | bytes 546824 | tf_op jit(solution)/shard_map/ppermute | solution.py:22
  119.7 22.4 %collective-permute-start.29 = (bf16[89,8,128]{2,1,0:T(8,128)(2,1)S(1)}, bf16[89,8,128]{2,1,0:T(8,128)(2,1)S(1)}, u32[]{:S(2)}, u32[]{:S(2)}) collective-permute-start(bf16[89,8,128]{2,1,0:T(8,128)(2,1)S(1)} %get-tuple-element.91), channel_id=1, source_target_pairs={{0,16},{2,18},{4,20},{6,22},{8,24},{10,26},{12,28},{14,30},{16,0},... | collective-permute-start | bytes 546824 | tf_op jit(solution)/shard_map/ppermute | solution.py:22
  120.7 21.4 %collective-permute-start.30 = (bf16[89,8,128]{2,1,0:T(8,128)(2,1)S(1)}, bf16[89,8,128]{2,1,0:T(8,128)(2,1)S(1)}, u32[]{:S(2)}, u32[]{:S(2)}) collective-permute-start(bf16[89,8,128]{2,1,0:T(8,128)(2,1)S(1)} %get-tuple-element.92), channel_id=1, source_target_pairs={{0,24},{2,26},{4,28},{6,30},{8,16},{10,18},{12,20},{14,22},{16,8},... | collective-permute-start | bytes 546824 | tf_op jit(solution)/shard_map/ppermute | solution.py:22
  (3 other events, 30.4 us)

commit v9 on v8

--- a/solution.py
+++ b/solution.py
@@ -497,14 +497,14 @@
 
     if staged:
         ffn_got = swap(ffn_near, "dp", near)
-        tile_terms, input_other = after((tile_terms, input_other), ffn_got)
+        input_other = after(input_other, ffn_got)
         got = halves(tile_terms)
         ffn_last = to_far(ffn_own, ffn_core, ffn_got)
         ffn_far = swap(ffn_last, "dp", 2 * near)
         input_core, input_near = to_near(input_own, input_other)
-        input_got = swap(after(input_near, ffn_far), "dp", near)
-        to_1, to_2 = folded(after(tile_terms, ffn_last), *got)
-        input_last = to_far(input_own, input_core, input_got)
+        input_got = swap(input_near, "dp", near)
+        to_1, to_2 = folded(after(tile_terms, ffn_last, input_near), *got)
+        input_last = after(to_far(input_own, input_core, input_got), ffn_far)
         input_far = swap(input_last, "dp", 2 * near)
         sums = after(tuple(summed(tile_terms, to_1, to_2)), input_last)
         back = list(after(tuple(sent_back(sums)), input_far))

time: 147 us -> 139 us (0.946)
  waiting for transfers between devices: 82.5 us -> 74.5 us
    ppermute x31, waiting for transfers between devices: 82.5 us -> 74.5 us  [swap(): return lax.ppermute(value, axis, [(at, at ^ stride) for at in range(size)])]
  transfers between devices with their start and end apart: 31 -> 31, of which waited for: 16 -> 17; matrix products, arithmetic and copies ran while one was open for 4% -> 5% of each run, Pallas kernels for 14% -> 15%
where the time goes in v9:
time: 139 us
  waiting for transfers between devices  74.5 us (54%)
  starting transfers between devices  32.7 us (24%)
  Pallas kernels  23.1 us (17%)
  other arithmetic  4.88 us (4%)
  local copies, waits for them, and re-layouts  2.87 us (2%)
    ppermute x31, waiting for transfers between devices, swap(): return lax.ppermute(value, axis, [(at, at ^ stride) for at in range(size)])  74.5 us
    ppermute x31, starting transfers between devices, swap(): return lax.ppermute(value, axis, [(at, at ^ stride) for at in range(size)])  32.7 us
    pallas_call x6, Pallas kernels, call(): pl.pallas_call(kernel, grid_spec=pltpu.PrefetchScalarGridSpec(num_scalar_...  23.1 us
  transfers between devices with their start and end apart: 31, of which 17 were waited for; matrix products, arithmetic and copies ran while one was open for 5% of the time, Pallas kernels for 15%

profile of v9, /device:TPU:0, one launch (start us, length us, event | category | flops | bytes accessed | tf_op | source)
XLA Modules:
  0.0 138.9 jit_solution(17051047666973398394)
XLA Ops:
  0.6 3.1 %collective-permute-start = (bf16[32,4096]{1,0:T(8,128)(2,1)}, bf16[32,4096]{1,0:T(8,128)(2,1)S(1)}, u32[]{:S(2)}, u32[]{:S(2)}) collective-permute-start(bf16[32,4096]{1,0:T(8,128)(2,1)} %refs_0_.2), channel_id=1, source_target_pairs={{0,8},{2,10},{4,12},{6,14},{8,0},{10,2},{12,4},{14,6},{16,24},{18,... | collective-permute-start | bytes 786440 | tf_op jit(solution)/shard_map/ppermute | solution.py:22
  7.6 1.2 copy-done.1
  8.9 1.6 %shard_map.76 = (bf16[89,8,128]{2,1,0:T(8,128)(2,1)S(1)}, bf16[89,8,128]{2,1,0:T(8,128)(2,1)S(1)}, bf16[89,8,128]{2,1,0:T(8,128)(2,1)S(1)}, bf16[89,8,128]{2,1,0:T(8,128)(2,1)S(1)}) custom-call(s32[17,56]{1,0:T(8,128)S(1)} %pad_add_fusion.table, bf16[8,9,56,128]{3,2,1,0:T(8,128)(2,1)S(1)} %bitcast.36), custom_call_target="tpu_custom_call" | custom-call | bytes 1000000 | tf_op jit(solution)/shard_map/pallas_call | solution.py:261
  10.5 2.5 %collective-permute-start.3 = (bf16[89,8,128]{2,1,0:T(8,128)(2,1)S(1)}, bf16[89,8,128]{2,1,0:T(8,128)(2,1)S(1)}, u32[]{:S(2)}, u32[]{:S(2)}) collective-permute-start(bf16[89,8,128]{2,1,0:T(8,128)(2,1)S(1)} %get-tuple-element.48), channel_id=1, source_target_pairs={{0,24},{2,26},{4,28},{6,30},{8,16},{10,18},{12,20},{14,22},{16,8},... | collective-permute-start | bytes 546824 | tf_op jit(solution)/shard_map/ppermute | solution.py:22
  13.2 1.7 %collective-permute-start.1 = (bf16[89,8,128]{2,1,0:T(8,128)(2,1)S(1)}, bf16[89,8,128]{2,1,0:T(8,128)(2,1)S(1)}, u32[]{:S(2)}, u32[]{:S(2)}) collective-permute-start(bf16[89,8,128]{2,1,0:T(8,128)(2,1)S(1)} %get-tuple-element.46), channel_id=1, source_target_pairs={{0,8},{2,10},{4,12},{6,14},{8,0},{10,2},{12,4},{14,6},{16,24},{18,... | collective-permute-start | bytes 546824 | tf_op jit(solution)/shard_map/ppermute | solution.py:22
  14.9 5.0 %collective-permute-done.3 = bf16[89,8,128]{2,1,0:T(8,128)(2,1)S(1)} collective-permute-done((bf16[89,8,128]{2,1,0:T(8,128)(2,1)S(1)}, bf16[89,8,128]{2,1,0:T(8,128)(2,1)S(1)}, u32[]{:S(2)}, u32[]{:S(2)}) %collective-permute-start.3) | collective-permute-done | bytes 182304 | tf_op jit(solution)/shard_map/ppermute | solution.py:22
  20.5 8.7 %collective-permute-done.2 = bf16[89,8,128]{2,1,0:T(8,128)(2,1)S(1)} collective-permute-done((bf16[89,8,128]{2,1,0:T(8,128)(2,1)S(1)}, bf16[89,8,128]{2,1,0:T(8,128)(2,1)S(1)}, u32[]{:S(2)}, u32[]{:S(2)}) %collective-permute-start.2) | collective-permute-done | bytes 182304 | tf_op jit(solution)/shard_map/ppermute | solution.py:22
  29.3 1.6 %collective-permute-start.10 = (bf16[4,89,8,128]{3,2,1,0:T(8,128)(2,1)S(1)}, bf16[4,89,8,128]{3,2,1,0:T(8,128)(2,1)S(1)}, u32[]{:S(2)}, u32[]{:S(2)}) collective-permute-start(bf16[4,89,8,128]{3,2,1,0:T(8,128)(2,1)S(1)} %pad_maximum_fusion.1.refs_0_), channel_id=1, source_target_pairs={{0,2},{2,0},{4,6},{6,4},{8,10},{10,8},{12,14},{14,12},{16,18},{18,... | collective-permute-start | bytes 2187272 | tf_op jit(solution)/shard_map/ppermute | solution.py:22
  30.9 1.5 %collective-permute-start.12 = (bf16[4,89,8,128]{3,2,1,0:T(8,128)(2,1)S(1)}, bf16[4,89,8,128]{3,2,1,0:T(8,128)(2,1)S(1)}, u32[]{:S(2)}, u32[]{:S(2)}) collective-permute-start(bf16[4,89,8,128]{3,2,1,0:T(8,128)(2,1)S(1)} %pad_maximum_fusion.1.refs_0_), channel_id=1, source_target_pairs={{0,4},{2,6},{4,0},{6,2},{8,12},{10,14},{12,8},{14,10},{16,20},{18,... | collective-permute-start | bytes 2187272 | tf_op jit(solution)/shard_map/ppermute | solution.py:22
  33.0 2.6 %collective-permute-start.8 = (bf16[32,4096]{1,0:T(8,128)(2,1)S(1)}, bf16[32,4096]{1,0:T(8,128)(2,1)S(1)}, u32[]{:S(2)}, u32[]{:S(2)}) collective-permute-start(bf16[32,4096]{1,0:T(8,128)(2,1)S(1)} %copy-done.3), channel_id=1, source_target_pairs={{0,8},{2,10},{4,12},{6,14},{8,0},{10,2},{12,4},{14,6},{16,24},{18,... | collective-permute-start | bytes 786440 | tf_op jit(solution)/shard_map/ppermute | solution.py:22
  35.6 10.1 %collective-permute-done.7.refs_2_ = bf16[32,4096]{1,0:T(8,128)(2,1)S(1)} collective-permute-done((bf16[32,4096]{1,0:T(8,128)(2,1)S(1)}, bf16[32,4096]{1,0:T(8,128)(2,1)S(1)}, u32[]{:S(2)}, u32[]{:S(2)}) %collective-permute-start.7) | collective-permute-done | bytes 262176 | tf_op jit(solution)/shard_map/ppermute | solution.py:22
  46.5 2.3 %collective-permute-start.14 = (bf16[32,4096]{1,0:T(8,128)(2,1)S(1)}, bf16[32,4096]{1,0:T(8,128)(2,1)S(1)}, u32[]{:S(2)}, u32[]{:S(2)}) collective-permute-start(bf16[32,4096]{1,0:T(8,128)(2,1)S(1)} %copy-done.3), channel_id=1, source_target_pairs={{0,16},{2,18},{4,20},{6,22},{8,24},{10,26},{12,28},{14,30},{16,0},... | collective-permute-start | bytes 786440 | tf_op jit(solution)/shard_map/ppermute | solution.py:22
  50.0 9.1 %collective-permute-done.9.refs_3_ = bf16[32,4096]{1,0:T(8,128)(2,1)S(1)} collective-permute-done((bf16[32,4096]{1,0:T(8,128)(2,1)S(1)}, bf16[32,4096]{1,0:T(8,128)(2,1)S(1)}, u32[]{:S(2)}, u32[]{:S(2)}) %collective-permute-start.9) | collective-permute-done | bytes 262176 | tf_op jit(solution)/shard_map/ppermute | solution.py:22
  59.2 1.5 %collective-permute-done.14.refs_2_ = bf16[32,4096]{1,0:T(8,128)(2,1)S(1)} collective-permute-done((bf16[32,4096]{1,0:T(8,128)(2,1)S(1)}, bf16[32,4096]{1,0:T(8,128)(2,1)S(1)}, u32[]{:S(2)}, u32[]{:S(2)}) %collective-permute-start.14) | collective-permute-done | bytes 262176 | tf_op jit(solution)/shard_map/ppermute | solution.py:22
  61.1 1.8 %shard_map.77.refs_7_.refs_6_ = bf16[89,128,128]{2,1,0:T(8,128)(2,1)S(1)} custom-call(s32[17,56]{1,0:T(8,128)S(1)} %pad_add_fusion.table, bf16[4,89,8,128]{3,2,1,0:T(8,128)(2,1)S(1)} %pad_maximum_fusion.1.refs_0_, bf16[4,89,8,128]{3,2,1,0:T(8,128)(2,1)S(1)} %collective-permute-done.10.refs_1_, bf16[4,89,8,128]{3,2,1,0:T(8,128)(2,1)S(1)} %collective-permute-done.12.refs_2_, ...), custom_call_target="tpu_custom_call" | custom-call | bytes 10000000 | tf_op jit(solution)/shard_map/pallas_call | solution.py:261
  62.9 5.6 %shard_map.78 = (bf16[4096,256]{1,0:T(8,128)(2,1)S(1)}, f32[14,256,128]{2,1,0:T(8,128)S(1)}, f32[14,256,128]{2,1,0:T(8,128)S(1)}, bf16[14,128,256]{2,1,0:T(8,128...) custom-call(s32[17,56]{1,0:T(8,128)S(1)} %pad_add_fusion.table, ...), custom_call_target="tpu_custom_call" | custom-call | bytes 30000000 | tf_op jit(solution)/shard_map/pallas_call | solution.py:261
  70.0 2.0 %collective-permute-done.17 = bf16[4,32,4096]{2,1,0:T(8,128)(2,1)S(1)} collective-permute-done((bf16[4,32,4096]{2,1,0:T(8,128)(2,1)S(1)}, bf16[4,32,4096]{2,1,0:T(8,128)(2,1)S(1)}, u32[]{:S(2)}, u32[]{:S(2)}) %collective-permute-start.17) | collective-permute-done | bytes 1048608 | tf_op jit(solution)/shard_map/ppermute | solution.py:22
  73.2 10.2 %shard_map.79 = (bf16[4,32,4096]{2,1,0:T(8,128)(2,1)S(1)}, bf16[4,32,4096]{2,1,0:T(8,128)(2,1)S(1)}, bf16[4,89,8,128]{3,2,1,0:T(8,128)(2,1)S(1)}, bf16[4,89,8,12...) custom-call(s32[17,56]{1,0:T(8,128)S(1)} %pad_add_fusion.table, ...), custom_call_target="tpu_custom_call" | custom-call | bytes 40000000 | tf_op jit(solution)/shard_map/pallas_call | solution.py:261
  83.4 2.8 %collective-permute-done.18 = bf16[2,32,4096]{2,1,0:T(8,128)(2,1)S(1)} collective-permute-done((bf16[2,32,4096]{2,1,0:T(8,128)(2,1)S(1)}, bf16[2,32,4096]{2,1,0:T(8,128)(2,1)S(1)}, u32[]{:S(2)}, u32[]{:S(2)}) %collective-permute-start.18) | collective-permute-done | bytes 524320 | tf_op jit(solution)/shard_map/ppermute | solution.py:22
  87.2 1.6 %collective-permute-done.21 = bf16[4,32,4096]{2,1,0:T(8,128)(2,1)S(1)} collective-permute-done((bf16[4,32,4096]{2,1,0:T(8,128)(2,1)S(1)}, bf16[4,32,4096]{2,1,0:T(8,128)(2,1)S(1)}, u32[]{:S(2)}, u32[]{:S(2)}) %collective-permute-start.21) | collective-permute-done | bytes 1048608 | tf_op jit(solution)/shard_map/ppermute | solution.py:22
  89.0 1.0 collective-permute-start.22
  90.1 2.0 %collective-permute-start.19 = (bf16[32,4096]{1,0:T(8,128)(2,1)S(1)}, bf16[32,4096]{1,0:T(8,128)(2,1)S(1)}, u32[]{:S(2)}, u32[]{:S(2)}) collective-permute-start(bf16[32,4096]{1,0:T(8,128)(2,1)S(1)} %fusion.2), channel_id=1, source_target_pairs={{0,16},{2,18},{4,20},{6,22},{8,24},{10,26},{12,28},{14,30},{16,0},... | collective-permute-start | bytes 786440 | tf_op jit(solution)/shard_map/ppermute | solution.py:22
  92.1 5.0 %collective-permute-done.24.got_1 = bf16[2,89,8,128]{3,2,1,0:T(8,128)(2,1)S(1)} collective-permute-done((bf16[2,89,8,128]{3,2,1,0:T(8,128)(2,1)S(1)}, bf16[2,89,8,128]{3,2,1,0:T(8,128)(2,1)S(1)}, u32[]{:S(2)}, u32[]{:S(2)}) %collective-permute-start.24) | collective-permute-done | bytes 364576 | tf_op jit(solution)/shard_map/ppermute | solution.py:22
  98.9 1.5 %collective-permute-start.26 = (bf16[4,89,8,128]{3,2,1,0:T(8,128)(2,1)S(1)}, bf16[4,89,8,128]{3,2,1,0:T(8,128)(2,1)S(1)}, u32[]{:S(2)}, u32[]{:S(2)}) collective-permute-start(bf16[4,89,8,128]{3,2,1,0:T(8,128)(2,1)S(1)} %get-tuple-element.77), channel_id=1, source_target_pairs={{0,2},{2,0},{4,6},{6,4},{8,10},{10,8},{12,14},{14,12},{16,18},{18,... | collective-permute-start | bytes 2187272 | tf_op jit(solution)/shard_map/ppermute | solution.py:22
  100.4 8.3 %collective-permute-done.22 = bf16[2,32,4096]{2,1,0:T(8,128)(2,1)S(1)} collective-permute-done((bf16[2,32,4096]{2,1,0:T(8,128)(2,1)S(1)}, bf16[2,32,4096]{2,1,0:T(8,128)(2,1)S(1)}, u32[]{:S(2)}, u32[]{:S(2)}) %collective-permute-start.22) | collective-permute-done | bytes 524320 | tf_op jit(solution)/shard_map/ppermute | solution.py:22
  108.7 1.7 %collective-permute-start.23 = (bf16[32,4096]{1,0:T(8,128)(2,1)S(1)}, bf16[32,4096]{1,0:T(8,128)(2,1)S(1)}, u32[]{:S(2)}, u32[]{:S(2)}) collective-permute-start(bf16[32,4096]{1,0:T(8,128)(2,1)S(1)} %fusion.3), channel_id=1, source_target_pairs={{0,16},{2,18},{4,20},{6,22},{8,24},{10,26},{12,28},{14,30},{16,0},... | collective-permute-start | bytes 786440 | tf_op jit(solution)/shard_map/ppermute | solution.py:22
  111.3 4.7 %collective-permute-done.27 = bf16[4,89,8,128]{3,2,1,0:T(8,128)(2,1)S(1)} collective-permute-done((bf16[4,89,8,128]{3,2,1,0:T(8,128)(2,1)S(1)}, bf16[4,89,8,128]{3,2,1,0:T(8,128)(2,1)S(1)}, u32[]{:S(2)}, u32[]{:S(2)}) %collective-permute-start.27) | collective-permute-done | bytes 729120 | tf_op jit(solution)/shard_map/ppermute | solution.py:22
  117.6 2.0 %collective-permute-start.29 = (bf16[89,8,128]{2,1,0:T(8,128)(2,1)S(1)}, bf16[89,8,128]{2,1,0:T(8,128)(2,1)S(1)}, u32[]{:S(2)}, u32[]{:S(2)}) collective-permute-start(bf16[89,8,128]{2,1,0:T(8,128)(2,1)S(1)} %get-tuple-element.81), channel_id=1, source_target_pairs={{0,16},{2,18},{4,20},{6,22},{8,24},{10,26},{12,28},{14,30},{16,0},... | collective-permute-start | bytes 546824 | tf_op jit(solution)/shard_map/ppermute | solution.py:22
  119.6 1.5 %collective-permute-start.30 = (bf16[89,8,128]{2,1,0:T(8,128)(2,1)S(1)}, bf16[89,8,128]{2,1,0:T(8,128)(2,1)S(1)}, u32[]{:S(2)}, u32[]{:S(2)}) collective-permute-start(bf16[89,8,128]{2,1,0:T(8,128)(2,1)S(1)} %get-tuple-element.82), channel_id=1, source_target_pairs={{0,24},{2,26},{4,28},{6,30},{8,16},{10,18},{12,20},{14,22},{16,8},... | collective-permute-start | bytes 546824 | tf_op jit(solution)/shard_map/ppermute | solution.py:22
  121.1 11.0 %collective-permute-done.23 = bf16[32,4096]{1,0:T(8,128)(2,1)S(1)} collective-permute-done((bf16[32,4096]{1,0:T(8,128)(2,1)S(1)}, bf16[32,4096]{1,0:T(8,128)(2,1)S(1)}, u32[]{:S(2)}, u32[]{:S(2)}) %collective-permute-start.23) | collective-permute-done | bytes 262176 | tf_op jit(solution)/shard_map/ppermute | solution.py:22
  132.9 3.1 %collective-permute-done.29.refs_2_ = bf16[89,8,128]{2,1,0:T(8,128)(2,1)S(1)} collective-permute-done((bf16[89,8,128]{2,1,0:T(8,128)(2,1)S(1)}, bf16[89,8,128]{2,1,0:T(8,128)(2,1)S(1)}, u32[]{:S(2)}, u32[]{:S(2)}) %collective-permute-start.29) | collective-permute-done | bytes 182304 | tf_op jit(solution)/shard_map/ppermute | solution.py:22
  135.9 3.0 %shard_map.81 = bf16[8,9,56,128]{3,2,1,0:T(8,128)(2,1)} custom-call(s32[17,56]{1,0:T(8,128)S(1)} %pad_add_fusion.table, bf16[89,8,128]{2,1,0:T(8,128)(2,1)S(1)} %get-tuple-element.83.refs_0_, bf16[89,8,128]{2,1,0:T(8,128)(2,1)S(1)} %collective-permute-done.28.refs_1_, bf16[89,8,128]{2,1,0:T(8,128)(2,1)S(1)} %collective-permute-done.29.refs_2_, ...), custom_call_target="tpu_custom_call" | custom-call | bytes 2000000 | tf_op jit(solution)/shard_map/pallas_call | solution.py:261
  (72 shorter events, 16.7 us)
Async XLA Ops:
  0.6 19.4 %collective-permute-start = (bf16[32,4096]{1,0:T(8,128)(2,1)}, bf16[32,4096]{1,0:T(8,128)(2,1)S(1)}, u32[]{:S(2)}, u32[]{:S(2)}) collective-permute-start(bf16[32,4096]{1,0:T(8,128)(2,1)} %refs_0_.2), channel_id=1, source_target_pairs={{0,8},{2,10},{4,12},{6,14},{8,0},{10,2},{12,4},{14,6},{16,24},{18,... | collective-permute-start | bytes 786440 | tf_op jit(solution)/shard_map/ppermute | solution.py:22
  8.9 24.2 %copy-start.3 = (bf16[32,4096]{1,0:T(8,128)(2,1)S(1)}, bf16[32,4096]{1,0:T(8,128)(2,1)}, u32[]{:S(2)}) copy-start(bf16[32,4096]{1,0:T(8,128)(2,1)} %refs_0_.3) | copy-start | bytes 786436
  10.5 9.5 %collective-permute-start.3 = (bf16[89,8,128]{2,1,0:T(8,128)(2,1)S(1)}, bf16[89,8,128]{2,1,0:T(8,128)(2,1)S(1)}, u32[]{:S(2)}, u32[]{:S(2)}) collective-permute-start(bf16[89,8,128]{2,1,0:T(8,128)(2,1)S(1)} %get-tuple-element.48), channel_id=1, source_target_pairs={{0,24},{2,26},{4,28},{6,30},{8,16},{10,18},{12,20},{14,22},{16,8},... | collective-permute-start | bytes 546824 | tf_op jit(solution)/shard_map/ppermute | solution.py:22
  13.0 16.1 %collective-permute-start.2 = (bf16[89,8,128]{2,1,0:T(8,128)(2,1)S(1)}, bf16[89,8,128]{2,1,0:T(8,128)(2,1)S(1)}, u32[]{:S(2)}, u32[]{:S(2)}) collective-permute-start(bf16[89,8,128]{2,1,0:T(8,128)(2,1)S(1)} %get-tuple-element.47), channel_id=1, source_target_pairs={{0,16},{2,18},{4,20},{6,22},{8,24},{10,26},{12,28},{14,30},{16,0},... | collective-permute-start | bytes 546824 | tf_op jit(solution)/shard_map/ppermute | solution.py:22
  13.2 16.0 %collective-permute-start.1 = (bf16[89,8,128]{2,1,0:T(8,128)(2,1)S(1)}, bf16[89,8,128]{2,1,0:T(8,128)(2,1)S(1)}, u32[]{:S(2)}, u32[]{:S(2)}) collective-permute-start(bf16[89,8,128]{2,1,0:T(8,128)(2,1)S(1)} %get-tuple-element.46), channel_id=1, source_target_pairs={{0,8},{2,10},{4,12},{6,14},{8,0},{10,2},{12,4},{14,6},{16,24},{18,... | collective-permute-start | bytes 546824 | tf_op jit(solution)/shard_map/ppermute | solution.py:22
  14.9 14.3 %collective-permute-start.4 = (bf16[32,4096]{1,0:T(8,128)(2,1)}, bf16[32,4096]{1,0:T(8,128)(2,1)S(1)}, u32[]{:S(2)}, u32[]{:S(2)}) collective-permute-start(bf16[32,4096]{1,0:T(8,128)(2,1)} %refs_0_.2), channel_id=1, source_target_pairs={{0,1},{1,0},{2,3},{3,2},{4,5},{5,4},{6,7},{7,6},{8,9},{9,8},{10,11... | collective-permute-start | bytes 786440 | tf_op jit(solution)/shard_map/ppermute | solution.py:22
  20.0 9.3 %collective-permute-start.6 = (bf16[32,4096]{1,0:T(8,128)(2,1)}, bf16[32,4096]{1,0:T(8,128)(2,1)S(1)}, u32[]{:S(2)}, u32[]{:S(2)}) collective-permute-start(bf16[32,4096]{1,0:T(8,128)(2,1)} %refs_0_.3), channel_id=1, source_target_pairs={{0,1},{1,0},{2,3},{3,2},{4,5},{5,4},{6,7},{7,6},{8,9},{9,8},{10,11... | collective-permute-start | bytes 786440 | tf_op jit(solution)/shard_map/ppermute | solution.py:22
  20.0 9.3 %collective-permute-start.5 = (bf16[32,4096]{1,0:T(8,128)(2,1)S(1)}, bf16[32,4096]{1,0:T(8,128)(2,1)S(1)}, u32[]{:S(2)}, u32[]{:S(2)}) collective-permute-start(bf16[32,4096]{1,0:T(8,128)(2,1)S(1)} %collective-permute-done.refs_1_), channel_id=1, source_target_pairs={{0,1},{1,0},{2,3},{3,2},{4,5},{5,4},{6,7},{7,6},{8,9},{9,8},{10,11... | collective-permute-start | bytes 786440 | tf_op jit(solution)/shard_map/ppermute | solution.py:22
  29.3 19.5 %collective-permute-start.10 = (bf16[4,89,8,128]{3,2,1,0:T(8,128)(2,1)S(1)}, bf16[4,89,8,128]{3,2,1,0:T(8,128)(2,1)S(1)}, u32[]{:S(2)}, u32[]{:S(2)}) collective-permute-start(bf16[4,89,8,128]{3,2,1,0:T(8,128)(2,1)S(1)} %pad_maximum_fusion.1.refs_0_), channel_id=1, source_target_pairs={{0,2},{2,0},{4,6},{6,4},{8,10},{10,8},{12,14},{14,12},{16,18},{18,... | collective-permute-start | bytes 2187272 | tf_op jit(solution)/shard_map/ppermute | solution.py:22
  30.9 18.5 %collective-permute-start.12 = (bf16[4,89,8,128]{3,2,1,0:T(8,128)(2,1)S(1)}, bf16[4,89,8,128]{3,2,1,0:T(8,128)(2,1)S(1)}, u32[]{:S(2)}, u32[]{:S(2)}) collective-permute-start(bf16[4,89,8,128]{3,2,1,0:T(8,128)(2,1)S(1)} %pad_maximum_fusion.1.refs_0_), channel_id=1, source_target_pairs={{0,4},{2,6},{4,0},{6,2},{8,12},{10,14},{12,8},{14,10},{16,20},{18,... | collective-permute-start | bytes 2187272 | tf_op jit(solution)/shard_map/ppermute | solution.py:22
  32.4 13.3 %collective-permute-start.7 = (bf16[32,4096]{1,0:T(8,128)(2,1)S(1)}, bf16[32,4096]{1,0:T(8,128)(2,1)S(1)}, u32[]{:S(2)}, u32[]{:S(2)}) collective-permute-start(bf16[32,4096]{1,0:T(8,128)(2,1)S(1)} %copy-done.2), channel_id=1, source_target_pairs={{0,16},{2,18},{4,20},{6,22},{8,24},{10,26},{12,28},{14,30},{16,0},... | collective-permute-start | bytes 786440 | tf_op jit(solution)/shard_map/ppermute | solution.py:22
  33.0 12.9 %collective-permute-start.8 = (bf16[32,4096]{1,0:T(8,128)(2,1)S(1)}, bf16[32,4096]{1,0:T(8,128)(2,1)S(1)}, u32[]{:S(2)}, u32[]{:S(2)}) collective-permute-start(bf16[32,4096]{1,0:T(8,128)(2,1)S(1)} %copy-done.3), channel_id=1, source_target_pairs={{0,8},{2,10},{4,12},{6,14},{8,0},{10,2},{12,4},{14,6},{16,24},{18,... | collective-permute-start | bytes 786440 | tf_op jit(solution)/shard_map/ppermute | solution.py:22
  45.9 13.2 %collective-permute-start.9 = (bf16[32,4096]{1,0:T(8,128)(2,1)S(1)}, bf16[32,4096]{1,0:T(8,128)(2,1)S(1)}, u32[]{:S(2)}, u32[]{:S(2)}) collective-permute-start(bf16[32,4096]{1,0:T(8,128)(2,1)S(1)} %collective-permute-done.7.refs_2_), channel_id=1, source_target_pairs={{0,8},{2,10},{4,12},{6,14},{8,0},{10,2},{12,4},{14,6},{16,24},{18,... | collective-permute-start | bytes 786440 | tf_op jit(solution)/shard_map/ppermute | solution.py:22
  46.5 14.2 %collective-permute-start.14 = (bf16[32,4096]{1,0:T(8,128)(2,1)S(1)}, bf16[32,4096]{1,0:T(8,128)(2,1)S(1)}, u32[]{:S(2)}, u32[]{:S(2)}) collective-permute-start(bf16[32,4096]{1,0:T(8,128)(2,1)S(1)} %copy-done.3), channel_id=1, source_target_pairs={{0,16},{2,18},{4,20},{6,22},{8,24},{10,26},{12,28},{14,30},{16,0},... | collective-permute-start | bytes 786440 | tf_op jit(solution)/shard_map/ppermute | solution.py:22
  48.8 11.8 %collective-permute-start.11 = (bf16[2,89,8,128]{3,2,1,0:T(8,128)(2,1)S(1)}, bf16[2,89,8,128]{3,2,1,0:T(8,128)(2,1)S(1)}, u32[]{:S(2)}, u32[]{:S(2)}) collective-permute-start(bf16[2,89,8,128]{3,2,1,0:T(8,128)(2,1)S(1)} %slice.135), channel_id=1, source_target_pairs={{0,4},{2,6},{4,0},{6,2},{8,12},{10,14},{12,8},{14,10},{16,20},{18,... | collective-permute-start | bytes 1093640 | tf_op jit(solution)/shard_map/ppermute | solution.py:22
  49.4 11.2 %collective-permute-start.13 = (bf16[2,89,8,128]{3,2,1,0:T(8,128)(2,1)S(1)}, bf16[2,89,8,128]{3,2,1,0:T(8,128)(2,1)S(1)}, u32[]{:S(2)}, u32[]{:S(2)}) collective-permute-start(bf16[2,89,8,128]{3,2,1,0:T(8,128)(2,1)S(1)} %slice.136), channel_id=1, source_target_pairs={{0,2},{2,0},{4,6},{6,4},{8,10},{10,8},{12,14},{14,12},{16,18},{18,... | collective-permute-start | bytes 1093640 | tf_op jit(solution)/shard_map/ppermute | solution.py:22
  60.7 2.2 %collective-permute-start.15 = (bf16[64,4096]{1,0:T(8,128)(2,1)S(1)}, bf16[64,4096]{1,0:T(8,128)(2,1)S(1)}, u32[]{:S(2)}, u32[]{:S(2)}) collective-permute-start(bf16[64,4096]{1,0:T(8,128)(2,1)S(1)} %pad_maximum_fusion.2), channel_id=1, source_target_pairs={{0,1},{1,0},{2,3},{3,2},{4,5},{5,4},{6,7},{7,6},{8,9},{9,8},{10,11... | collective-permute-start | bytes 1572872 | tf_op jit(solution)/shard_map/ppermute | solution.py:22
  60.7 8.7 %collective-permute-start.16 = (bf16[32,4096]{1,0:T(8,128)(2,1)S(1)}, bf16[32,4096]{1,0:T(8,128)(2,1)S(1)}, u32[]{:S(2)}, u32[]{:S(2)}) collective-permute-start(bf16[32,4096]{1,0:T(8,128)(2,1)S(1)} %collective-permute-done.14.refs_2_), channel_id=1, source_target_pairs={{0,8},{2,10},{4,12},{6,14},{8,0},{10,2},{12,4},{14,6},{16,24},{18,... | collective-permute-start | bytes 786440 | tf_op jit(solution)/shard_map/ppermute | solution.py:22
  69.4 2.7 %collective-permute-start.17 = (bf16[4,32,4096]{2,1,0:T(8,128)(2,1)S(1)}, bf16[4,32,4096]{2,1,0:T(8,128)(2,1)S(1)}, u32[]{:S(2)}, u32[]{:S(2)}) collective-permute-start(bf16[4,32,4096]{2,1,0:T(8,128)(2,1)S(1)} %get-tuple-element.57), channel_id=1, source_target_pairs={{0,1},{1,0},{2,3},{3,2},{4,5},{5,4},{6,7},{7,6},{8,9},{9,8},{10,11... | collective-permute-start | bytes 3145736 | tf_op jit(solution)/shard_map/ppermute | solution.py:22
  69.4 3.7 %collective-permute-start.20 = (bf16[96,4096]{1,0:T(8,128)(2,1)S(1)}, bf16[96,4096]{1,0:T(8,128)(2,1)S(1)}, u32[]{:S(2)}, u32[]{:S(2)}) collective-permute-start(bf16[96,4096]{1,0:T(8,128)(2,1)S(1)} %pad_maximum_fusion), channel_id=1, source_target_pairs={{0,1},{1,0},{2,3},{3,2},{4,5},{5,4},{6,7},{7,6},{8,9},{9,8},{10,11... | collective-permute-start | bytes 2359304 | tf_op jit(solution)/shard_map/ppermute | solution.py:22
  72.2 14.0 %collective-permute-start.18 = (bf16[2,32,4096]{2,1,0:T(8,128)(2,1)S(1)}, bf16[2,32,4096]{2,1,0:T(8,128)(2,1)S(1)}, u32[]{:S(2)}, u32[]{:S(2)}) collective-permute-start(bf16[2,32,4096]{2,1,0:T(8,128)(2,1)S(1)} %add_convert_fusion.1), channel_id=1, source_target_pairs={{0,8},{2,10},{4,12},{6,14},{8,0},{10,2},{12,4},{14,6},{16,24},{18,... | collective-permute-start | bytes 1572872 | tf_op jit(solution)/shard_map/ppermute | solution.py:22
  86.2 2.7 %collective-permute-start.21 = (bf16[4,32,4096]{2,1,0:T(8,128)(2,1)S(1)}, bf16[4,32,4096]{2,1,0:T(8,128)(2,1)S(1)}, u32[]{:S(2)}, u32[]{:S(2)}) collective-permute-start(bf16[4,32,4096]{2,1,0:T(8,128)(2,1)S(1)} %get-tuple-element.68), channel_id=1, source_target_pairs={{0,1},{1,0},{2,3},{3,2},{4,5},{5,4},{6,7},{7,6},{8,9},{9,8},{10,11... | collective-permute-start | bytes 3145736 | tf_op jit(solution)/shard_map/ppermute | solution.py:22
  86.2 10.9 %collective-permute-start.24 = (bf16[2,89,8,128]{3,2,1,0:T(8,128)(2,1)S(1)}, bf16[2,89,8,128]{3,2,1,0:T(8,128)(2,1)S(1)}, u32[]{:S(2)}, u32[]{:S(2)}) collective-permute-start(bf16[2,89,8,128]{3,2,1,0:T(8,128)(2,1)S(1)} %get-tuple-element.73), channel_id=1, source_target_pairs={{0,2},{2,0},{4,6},{6,4},{8,10},{10,8},{12,14},{14,12},{16,18},{18,... | collective-permute-start | bytes 1093640 | tf_op jit(solution)/shard_map/ppermute | solution.py:22
  86.7 10.6 %collective-permute-start.25 = (bf16[2,89,8,128]{3,2,1,0:T(8,128)(2,1)S(1)}, bf16[2,89,8,128]{3,2,1,0:T(8,128)(2,1)S(1)}, u32[]{:S(2)}, u32[]{:S(2)}) collective-permute-start(bf16[2,89,8,128]{3,2,1,0:T(8,128)(2,1)S(1)} %get-tuple-element.74), channel_id=1, source_target_pairs={{0,4},{2,6},{4,0},{6,2},{8,12},{10,14},{12,8},{14,10},{16,20},{18,... | collective-permute-start | bytes 1093640 | tf_op jit(solution)/shard_map/ppermute | solution.py:22
  89.0 19.6 %collective-permute-start.22 = (bf16[2,32,4096]{2,1,0:T(8,128)(2,1)S(1)}, bf16[2,32,4096]{2,1,0:T(8,128)(2,1)S(1)}, u32[]{:S(2)}, u32[]{:S(2)}) collective-permute-start(bf16[2,32,4096]{2,1,0:T(8,128)(2,1)S(1)} %add_convert_fusion), channel_id=1, source_target_pairs={{0,8},{2,10},{4,12},{6,14},{8,0},{10,2},{12,4},{14,6},{16,24},{18,... | collective-permute-start | bytes 1572872 | tf_op jit(solution)/shard_map/ppermute | solution.py:22
  90.1 18.6 %collective-permute-start.19 = (bf16[32,4096]{1,0:T(8,128)(2,1)S(1)}, bf16[32,4096]{1,0:T(8,128)(2,1)S(1)}, u32[]{:S(2)}, u32[]{:S(2)}) collective-permute-start(bf16[32,4096]{1,0:T(8,128)(2,1)S(1)} %fusion.2), channel_id=1, source_target_pairs={{0,16},{2,18},{4,20},{6,22},{8,24},{10,26},{12,28},{14,30},{16,0},... | collective-permute-start | bytes 786440 | tf_op jit(solution)/shard_map/ppermute | solution.py:22
  98.3 17.8 %collective-permute-start.27 = (bf16[4,89,8,128]{3,2,1,0:T(8,128)(2,1)S(1)}, bf16[4,89,8,128]{3,2,1,0:T(8,128)(2,1)S(1)}, u32[]{:S(2)}, u32[]{:S(2)}) collective-permute-start(bf16[4,89,8,128]{3,2,1,0:T(8,128)(2,1)S(1)} %get-tuple-element.78), channel_id=1, source_target_pairs={{0,4},{2,6},{4,0},{6,2},{8,12},{10,14},{12,8},{14,10},{16,20},{18,... | collective-permute-start | bytes 2187272 | tf_op jit(solution)/shard_map/ppermute | solution.py:22
  98.9 17.4 %collective-permute-start.26 = (bf16[4,89,8,128]{3,2,1,0:T(8,128)(2,1)S(1)}, bf16[4,89,8,128]{3,2,1,0:T(8,128)(2,1)S(1)}, u32[]{:S(2)}, u32[]{:S(2)}) collective-permute-start(bf16[4,89,8,128]{3,2,1,0:T(8,128)(2,1)S(1)} %get-tuple-element.77), channel_id=1, source_target_pairs={{0,2},{2,0},{4,6},{6,4},{8,10},{10,8},{12,14},{14,12},{16,18},{18,... | collective-permute-start | bytes 2187272 | tf_op jit(solution)/shard_map/ppermute | solution.py:22
  108.7 23.3 %collective-permute-start.23 = (bf16[32,4096]{1,0:T(8,128)(2,1)S(1)}, bf16[32,4096]{1,0:T(8,128)(2,1)S(1)}, u32[]{:S(2)}, u32[]{:S(2)}) collective-permute-start(bf16[32,4096]{1,0:T(8,128)(2,1)S(1)} %fusion.3), channel_id=1, source_target_pairs={{0,16},{2,18},{4,20},{6,22},{8,24},{10,26},{12,28},{14,30},{16,0},... | collective-permute-start | bytes 786440 | tf_op jit(solution)/shard_map/ppermute | solution.py:22
  116.6 16.3 %collective-permute-start.28 = (bf16[89,8,128]{2,1,0:T(8,128)(2,1)S(1)}, bf16[89,8,128]{2,1,0:T(8,128)(2,1)S(1)}, u32[]{:S(2)}, u32[]{:S(2)}) collective-permute-start(bf16[89,8,128]{2,1,0:T(8,128)(2,1)S(1)} %get-tuple-element.80), channel_id=1, source_target_pairs={{0,8},{2,10},{4,12},{6,14},{8,0},{10,2},{12,4},{14,6},{16,24},{18,... | collective-permute-start | bytes 546824 | tf_op jit(solution)/shard_map/ppermute | solution.py:22
  117.6 18.3 %collective-permute-start.29 = (bf16[89,8,128]{2,1,0:T(8,128)(2,1)S(1)}, bf16[89,8,128]{2,1,0:T(8,128)(2,1)S(1)}, u32[]{:S(2)}, u32[]{:S(2)}) collective-permute-start(bf16[89,8,128]{2,1,0:T(8,128)(2,1)S(1)} %get-tuple-element.81), channel_id=1, source_target_pairs={{0,16},{2,18},{4,20},{6,22},{8,24},{10,26},{12,28},{14,30},{16,0},... | collective-permute-start | bytes 546824 | tf_op jit(solution)/shard_map/ppermute | solution.py:22
  119.6 16.4 %collective-permute-start.30 = (bf16[89,8,128]{2,1,0:T(8,128)(2,1)S(1)}, bf16[89,8,128]{2,1,0:T(8,128)(2,1)S(1)}, u32[]{:S(2)}, u32[]{:S(2)}) collective-permute-start(bf16[89,8,128]{2,1,0:T(8,128)(2,1)S(1)} %get-tuple-element.82), channel_id=1, source_target_pairs={{0,24},{2,26},{4,28},{6,30},{8,16},{10,18},{12,20},{14,22},{16,8},... | collective-permute-start | bytes 546824 | tf_op jit(solution)/shard_map/ppermute | solution.py:22
  (3 other events, 30.4 us)

commit v10 on v9

--- a/solution.py
+++ b/solution.py
@@ -288,9 +288,12 @@
     tensor_strides = strides_of(tensor_size)
     shape = jax.ShapeDtypeStruct
 
+    staged = tensor_size == 2 and far == 4 and near == 4
     x_items, g_items = {0: tokens}, {0: out_grad}
-    if far > 1:
+    if staged:
+        x_items[2 * near] = swap(tokens, "dp", 2 * near)
         x_items[near] = swap(tokens, "dp", near)
+        g_items[near] = swap(out_grad, "dp", near)
 
     capacity = (terms * blocks_dev - 3 * blocks_dev + 3 * (slot_count - 1) * (far - 1)) // far
     slots = capacity + 1
@@ -335,52 +338,48 @@
         [whole(packed_shape)] * far,
         [shape(packed_shape, BF16)] * far,
         scratch=[pltpu.VMEM((row_share * terms * blocks_dev, tile), F32)],
-        cost=1_000_000,
+        cost=30_000_000,
         vmem=24,
     )
-    staged = tensor_size == 2 and far == 4 and near == 4
-    received = [swap(packed[at], "dp", at * near) for at in reversed(range(1, far))][::-1]
-    held = jnp.stack([packed[0], *received])
-    x_core, g_core = {}, {}
     if staged:
-        x_core = {at: swap(x_items[at], "tensor", 1) for at in (0, near)}
-        g_core = {0: swap(out_grad, "tensor", 1)}
-        held = after(held, *x_core.values(), *g_core.values())
-
+        packed = after(tuple(packed), x_items[2 * near])
+    received = {at: swap(packed[at], "dp", at * near) for at in range(1, far)}
     half = far // 2
     split = near == 4 and far % 2 == 0
-    if split:
-        from_1, from_2 = swap(held, "dp", 1), swap(held, "dp", 2)
-        pass_1, pass_2 = from_1[:half], from_2[half:]
-        weight_list = [held, from_1, from_2, swap(pass_1, "dp", 2), swap(pass_2, "dp", 1)]
-        weight_parts = [(0, 0, far), (1, 0, far), (2, 0, far), (3, 0, half), (3, half, half)]
+    if staged:
+        held_a = jnp.stack([packed[0], received[1]])
+        a_1, a_2 = swap(held_a, "dp", 1), swap(held_a, "dp", 2)
+        held_b = jnp.stack([received[2], received[3]])
+        held_b, x_source, g_source = after(
+            (held_b, x_items[2 * near], out_grad), a_1, a_2, x_items[near], g_items[near]
+        )
+        b_1, b_2 = swap(held_b, "dp", 1), swap(held_b, "dp", 2)
+        g_items[2 * near] = swap(g_source, "dp", 2 * near)
+        x_items[3 * near] = swap(x_source, "dp", near)
+        a_far, b_far = after((a_1, b_2), b_1, g_items[2 * near], x_items[3 * near])
+        a_3, b_3 = swap(a_far, "dp", 2), swap(b_far, "dp", 1)
+        x_own = jnp.concatenate(after([x_items[at * near] for at in range(far)], b_1, b_2, g_items[2 * near]))
+        x_core = swap(x_own, "tensor", 1)
+        g_items[3 * near] = swap(g_items[2 * near], "dp", near)
+        g_own = jnp.concatenate([g_items[at * near] for at in range(far)])
+        g_core = swap(g_own, "tensor", 1)
+        weight_list = [held_a, a_1, a_2, a_3, held_b, b_1, b_2, after(b_3, g_items[3 * near])]
+        held_parts = [(at, first, half) for first in (0, half) for at in range(near)]
     else:
+        held = jnp.stack([packed[0], *received.values()])
         items = gather({0: held}, "dp", near_strides)
-        pass_1 = pass_2 = held
         weight_list = [items[at] for at in range(near)]
-        weight_parts = [(at, 0, far) for at in range(near)]
-
-    if staged:
-        x_source, g_source = after((tokens, out_grad), held)
-        x_items[2 * near] = swap(x_source, "dp", 2 * near)
-        g_items[near] = swap(g_source, "dp", near)
-        x_source, g_source = after((x_items[2 * near], out_grad), x_items[2 * near], g_items[near])
-        x_items[3 * near] = swap(x_source, "dp", near)
-        g_items[2 * near] = swap(g_source, "dp", 2 * near)
-        g_items[3 * near] = swap(g_items[2 * near], "dp", near)
-        x_late = jnp.concatenate([x_items[2 * near], x_items[3 * near]])
-        x_late = swap(after(x_late, *weight_list[3:], g_items[2 * near]), "tensor", 1)
-        g_late = jnp.concatenate([g_items[at * near] for at in range(1, far)])
-        g_late = swap(g_late, "tensor", 1)
-    else:
+        held_parts = [(at, 0, far) for at in range(near)]
         for items, value in ((x_items, tokens), (g_items, out_grad)):
             items.update(gather({0: value}, "dp", far_strides))
+    weight_parts = [(at, 0, far) for at in range(near)]
+    if split:
+        weight_parts[3:] = [(3, 0, half), (3, half, half)]
 
     far_order = [at * near for at in range(0, far, 2)] + [at * near for at in range(1, far, 2)]
     if staged:
         order = [at * near for at in range(far)]
-        x_list = [x_items[at] for at in order] + [x_core[at] for at in order[:2]] + [x_late]
-        g_list = [g_items[at] for at in order] + [g_core[0], g_late]
+        x_list, g_list = [x_own, x_core], [g_own, g_core]
         parts = [(other, far_order.index(at)) for other in (False, True) for at in order]
         other_parts = [(at, 1) for at in far_order]
     else:
@@ -401,12 +400,12 @@
     steps = 2 if slots % 2 == 0 else 1
     tiles_shape = (slots, tile, tile)
     tiles = call(
-        functools.partial(assemble, weight_parts=weight_parts, near=near),
+        functools.partial(assemble, weight_parts=held_parts, near=near),
         table,
         weight_list,
         [
             pl.BlockSpec((length, slots // steps, row_share, tile), lambda step, *_: (0, step, 0, 0))
-            for _, _, length in weight_parts
+            for _, _, length in held_parts
         ],
         pl.BlockSpec((slots // steps, tile, tile), lambda step, *_: (step, 0, 0)),
         shape(tiles_shape, BF16),

time: 139 us -> 149 us (1.072)
  starting transfers between devices: 32.7 us -> 42.5 us
    ppermute x31 -> x30, starting transfers between devices: 32.7 us -> 42.5 us  [swap(): return lax.ppermute(value, axis, [(at, at ^ stride) for at in range(size)])]
    ppermute x31 -> x30, waiting for transfers between devices: 74.5 us -> 74.4 us  [swap(): return lax.ppermute(value, axis, [(at, at ^ stride) for at in range(size)])]
  transfers between devices with their start and end apart: 31 -> 30, of which waited for: 17 -> 19; matrix products, arithmetic and copies ran while one was open for 5% -> 4% of each run, Pallas kernels for 15% -> 10%
where the time goes in v10:
time: 149 us
  waiting for transfers between devices  74.4 us (50%)
  starting transfers between devices  42.5 us (29%)
  Pallas kernels  23.1 us (16%)
  other arithmetic  4.76 us (3%)
  local copies, waits for them, and re-layouts  2.98 us (2%)
    ppermute x30, waiting for transfers between devices, swap(): return lax.ppermute(value, axis, [(at, at ^ stride) for at in range(size)])  74.4 us
    ppermute x30, starting transfers between devices, swap(): return lax.ppermute(value, axis, [(at, at ^ stride) for at in range(size)])  42.5 us
    pallas_call x6, Pallas kernels, call(): pl.pallas_call(kernel, grid_spec=pltpu.PrefetchScalarGridSpec(num_scalar_...  23.1 us
  transfers between devices with their start and end apart: 30, of which 19 were waited for; matrix products, arithmetic and copies ran while one was open for 4% of the time, Pallas kernels for 10%

profile of v10, /device:TPU:0, one launch (start us, length us, event | category | flops | bytes accessed | tf_op | source)
XLA Modules:
  0.0 148.7 jit_solution(206040296621992367)
XLA Ops:
  0.6 4.1 %collective-permute-start.1 = (bf16[32,4096]{1,0:T(8,128)(2,1)}, bf16[32,4096]{1,0:T(8,128)(2,1)S(1)}, u32[]{:S(2)}, u32[]{:S(2)}) collective-permute-start(bf16[32,4096]{1,0:T(8,128)(2,1)} %param.5), channel_id=1, source_target_pairs={{0,16},{2,18},{4,20},{6,22},{8,24},{10,26},{12,28},{14,30},{16,0},... | collective-permute-start | bytes 786440 | tf_op jit(solution)/shard_map/ppermute | solution.py:22
  9.9 1.6 %shard_map.76 = (bf16[89,8,128]{2,1,0:T(8,128)(2,1)S(1)}, bf16[89,8,128]{2,1,0:T(8,128)(2,1)S(1)}, bf16[89,8,128]{2,1,0:T(8,128)(2,1)S(1)}, bf16[89,8,128]{2,1,0:T(8,128)(2,1)S(1)}) custom-call(s32[17,56]{1,0:T(8,128)S(1)} %pad_add_fusion.table, bf16[8,9,56,128]{3,2,1,0:T(8,128)(2,1)S(1)} %bitcast.36), custom_call_target="tpu_custom_call" | custom-call | bytes 30000000 | tf_op jit(solution)/shard_map/pallas_call | solution.py:261
  11.5 5.4 %collective-permute-done.1 = bf16[32,4096]{1,0:T(8,128)(2,1)S(1)} collective-permute-done((bf16[32,4096]{1,0:T(8,128)(2,1)}, bf16[32,4096]{1,0:T(8,128)(2,1)S(1)}, u32[]{:S(2)}, u32[]{:S(2)}) %collective-permute-start.1) | collective-permute-done | bytes 262176 | tf_op jit(solution)/shard_map/ppermute | solution.py:22
  17.7 2.7 %collective-permute-start.3 = (bf16[89,8,128]{2,1,0:T(8,128)(2,1)S(1)}, bf16[89,8,128]{2,1,0:T(8,128)(2,1)S(1)}, u32[]{:S(2)}, u32[]{:S(2)}) collective-permute-start(bf16[89,8,128]{2,1,0:T(8,128)(2,1)S(1)} %get-tuple-element.58), channel_id=1, source_target_pairs={{0,24},{2,26},{4,28},{6,30},{8,16},{10,18},{12,20},{14,22},{16,8},... | collective-permute-start | bytes 546824 | tf_op jit(solution)/shard_map/ppermute | solution.py:22
  20.4 2.3 %collective-permute-done.4 = bf16[89,8,128]{2,1,0:T(8,128)(2,1)S(1)} collective-permute-done((bf16[89,8,128]{2,1,0:T(8,128)(2,1)S(1)}, bf16[89,8,128]{2,1,0:T(8,128)(2,1)S(1)}, u32[]{:S(2)}, u32[]{:S(2)}) %collective-permute-start.4) | collective-permute-done | bytes 182304 | tf_op jit(solution)/shard_map/ppermute | solution.py:22
  25.8 6.6 %collective-permute-start.2 = (bf16[89,8,128]{2,1,0:T(8,128)(2,1)S(1)}, bf16[89,8,128]{2,1,0:T(8,128)(2,1)S(1)}, u32[]{:S(2)}, u32[]{:S(2)}) collective-permute-start(bf16[89,8,128]{2,1,0:T(8,128)(2,1)S(1)} %get-tuple-element.57), channel_id=1, source_target_pairs={{0,16},{2,18},{4,20},{6,22},{8,24},{10,26},{12,28},{14,30},{16,0},... | collective-permute-start | bytes 546824 | tf_op jit(solution)/shard_map/ppermute | solution.py:22
  32.4 2.5 %collective-permute-start = (bf16[32,4096]{1,0:T(8,128)(2,1)}, bf16[32,4096]{1,0:T(8,128)(2,1)S(1)}, u32[]{:S(2)}, u32[]{:S(2)}) collective-permute-start(bf16[32,4096]{1,0:T(8,128)(2,1)} %param.5), channel_id=1, source_target_pairs={{0,8},{2,10},{4,12},{6,14},{8,0},{10,2},{12,4},{14,6},{16,24},{18,... | collective-permute-start | bytes 786440 | tf_op jit(solution)/shard_map/ppermute | solution.py:22
  34.9 2.5 %collective-permute-done.2 = bf16[89,8,128]{2,1,0:T(8,128)(2,1)S(1)} collective-permute-done((bf16[89,8,128]{2,1,0:T(8,128)(2,1)S(1)}, bf16[89,8,128]{2,1,0:T(8,128)(2,1)S(1)}, u32[]{:S(2)}, u32[]{:S(2)}) %collective-permute-start.2) | collective-permute-done | bytes 182304 | tf_op jit(solution)/shard_map/ppermute | solution.py:22
  37.5 4.6 %collective-permute-done = bf16[32,4096]{1,0:T(8,128)(2,1)S(1)} collective-permute-done((bf16[32,4096]{1,0:T(8,128)(2,1)}, bf16[32,4096]{1,0:T(8,128)(2,1)S(1)}, u32[]{:S(2)}, u32[]{:S(2)}) %collective-permute-start) | collective-permute-done | bytes 262176 | tf_op jit(solution)/shard_map/ppermute | solution.py:22
  42.1 2.8 %collective-permute-done.7 = bf16[32,4096]{1,0:T(8,128)(2,1)S(1)} collective-permute-done((bf16[32,4096]{1,0:T(8,128)(2,1)}, bf16[32,4096]{1,0:T(8,128)(2,1)S(1)}, u32[]{:S(2)}, u32[]{:S(2)}) %collective-permute-start.7) | collective-permute-done | bytes 262176 | tf_op jit(solution)/shard_map/ppermute | solution.py:22
  47.5 2.1 %collective-permute-start.11 = (bf16[32,4096]{1,0:T(8,128)(2,1)S(1)}, bf16[32,4096]{1,0:T(8,128)(2,1)S(1)}, u32[]{:S(2)}, u32[]{:S(2)}) collective-permute-start(bf16[32,4096]{1,0:T(8,128)(2,1)S(1)} %copy-done.3), channel_id=1, source_target_pairs={{0,16},{2,18},{4,20},{6,22},{8,24},{10,26},{12,28},{14,30},{16,0},... | collective-permute-start | bytes 786440 | tf_op jit(solution)/shard_map/ppermute | solution.py:22
  49.7 7.3 %collective-permute-done.8 = bf16[32,4096]{1,0:T(8,128)(2,1)S(1)} collective-permute-done((bf16[32,4096]{1,0:T(8,128)(2,1)S(1)}, bf16[32,4096]{1,0:T(8,128)(2,1)S(1)}, u32[]{:S(2)}, u32[]{:S(2)}) %collective-permute-start.8) | collective-permute-done | bytes 262176 | tf_op jit(solution)/shard_map/ppermute | solution.py:22
  56.9 2.6 %collective-permute-done.11 = bf16[32,4096]{1,0:T(8,128)(2,1)S(1)} collective-permute-done((bf16[32,4096]{1,0:T(8,128)(2,1)S(1)}, bf16[32,4096]{1,0:T(8,128)(2,1)S(1)}, u32[]{:S(2)}, u32[]{:S(2)}) %collective-permute-start.11) | collective-permute-done | bytes 262176 | tf_op jit(solution)/shard_map/ppermute | solution.py:22
  61.7 6.8 %collective-permute-done.15 = bf16[32,4096]{1,0:T(8,128)(2,1)S(1)} collective-permute-done((bf16[32,4096]{1,0:T(8,128)(2,1)S(1)}, bf16[32,4096]{1,0:T(8,128)(2,1)S(1)}, u32[]{:S(2)}, u32[]{:S(2)}) %collective-permute-start.15) | collective-permute-done | bytes 262176 | tf_op jit(solution)/shard_map/ppermute | solution.py:22
  68.4 3.3 %collective-permute-done.14.refs_7_ = bf16[2,89,8,128]{3,2,1,0:T(8,128)(2,1)S(1)} collective-permute-done((bf16[2,89,8,128]{3,2,1,0:T(8,128)(2,1)S(1)}, bf16[2,89,8,128]{3,2,1,0:T(8,128)(2,1)S(1)}, u32[]{:S(2)}, u32[]{:S(2)}) %collective-permute-start.14) | collective-permute-done | bytes 364576 | tf_op jit(solution)/shard_map/ppermute | solution.py:22
  71.7 1.8 %shard_map.77.refs_2_ = bf16[89,128,128]{2,1,0:T(8,128)(2,1)S(1)} custom-call(s32[17,56]{1,0:T(8,128)S(1)} %pad_add_fusion.table, bf16[2,89,8,128]{3,2,1,0:T(8,128)(2,1)S(1)} %pad_maximum_fusion.1.refs_0_, bf16[2,89,8,128]{3,2,1,0:T(8,128)(2,1)S(1)} %collective-permute-done.5.refs_1_, bf16[2,89,8,128]{3,2,1,0:T(8,128)(2,1)S(1)} %collective-permute-done.6.refs_2_, ...), custom_call_target="tpu_custom_call" | custom-call | bytes 10000000 | tf_op jit(solution)/shard_map/pallas_call | solution.py:261
  73.6 5.6 %shard_map.78 = (bf16[4096,256]{1,0:T(8,128)(2,1)S(1)}, f32[14,256,128]{2,1,0:T(8,128)S(1)}, f32[14,256,128]{2,1,0:T(8,128)S(1)}, bf16[14,128,256]{2,1,0:T(8,128...) custom-call(s32[17,56]{1,0:T(8,128)S(1)} %pad_add_fusion.table, ...), custom_call_target="tpu_custom_call" | custom-call | bytes 30000000 | tf_op jit(solution)/shard_map/pallas_call | solution.py:261
  79.9 2.0 %collective-permute-done.16 = bf16[4,32,4096]{2,1,0:T(8,128)(2,1)S(1)} collective-permute-done((bf16[4,32,4096]{2,1,0:T(8,128)(2,1)S(1)}, bf16[4,32,4096]{2,1,0:T(8,128)(2,1)S(1)}, u32[]{:S(2)}, u32[]{:S(2)}) %collective-permute-start.16) | collective-permute-done | bytes 1048608 | tf_op jit(solution)/shard_map/ppermute | solution.py:22
  82.0 1.8 %collective-permute-start.17 = (bf16[2,32,4096]{2,1,0:T(8,128)(2,1)S(1)}, bf16[2,32,4096]{2,1,0:T(8,128)(2,1)S(1)}, u32[]{:S(2)}, u32[]{:S(2)}) collective-permute-start(bf16[2,32,4096]{2,1,0:T(8,128)(2,1)S(1)} %add_convert_fusion.1), channel_id=1, source_target_pairs={{0,8},{2,10},{4,12},{6,14},{8,0},{10,2},{12,4},{14,6},{16,24},{18,... | collective-permute-start | bytes 1572872 | tf_op jit(solution)/shard_map/ppermute | solution.py:22
  83.8 10.2 %shard_map.79 = (bf16[4,32,4096]{2,1,0:T(8,128)(2,1)S(1)}, bf16[4,32,4096]{2,1,0:T(8,128)(2,1)S(1)}, bf16[4,89,8,128]{3,2,1,0:T(8,128)(2,1)S(1)}, bf16[4,89,8,12...) custom-call(s32[17,56]{1,0:T(8,128)S(1)} %pad_add_fusion.table, ...), custom_call_target="tpu_custom_call" | custom-call | bytes 40000000 | tf_op jit(solution)/shard_map/pallas_call | solution.py:261
  94.1 2.0 %collective-permute-done.17 = bf16[2,32,4096]{2,1,0:T(8,128)(2,1)S(1)} collective-permute-done((bf16[2,32,4096]{2,1,0:T(8,128)(2,1)S(1)}, bf16[2,32,4096]{2,1,0:T(8,128)(2,1)S(1)}, u32[]{:S(2)}, u32[]{:S(2)}) %collective-permute-start.17) | collective-permute-done | bytes 524320 | tf_op jit(solution)/shard_map/ppermute | solution.py:22
  98.9 1.8 %collective-permute-start.21 = (bf16[2,32,4096]{2,1,0:T(8,128)(2,1)S(1)}, bf16[2,32,4096]{2,1,0:T(8,128)(2,1)S(1)}, u32[]{:S(2)}, u32[]{:S(2)}) collective-permute-start(bf16[2,32,4096]{2,1,0:T(8,128)(2,1)S(1)} %add_convert_fusion), channel_id=1, source_target_pairs={{0,8},{2,10},{4,12},{6,14},{8,0},{10,2},{12,4},{14,6},{16,24},{18,... | collective-permute-start | bytes 1572872 | tf_op jit(solution)/shard_map/ppermute | solution.py:22
  101.1 5.8 %collective-permute-done.23.got_1 = bf16[2,89,8,128]{3,2,1,0:T(8,128)(2,1)S(1)} collective-permute-done((bf16[2,89,8,128]{3,2,1,0:T(8,128)(2,1)S(1)}, bf16[2,89,8,128]{3,2,1,0:T(8,128)(2,1)S(1)}, u32[]{:S(2)}, u32[]{:S(2)}) %collective-permute-start.23) | collective-permute-done | bytes 364576 | tf_op jit(solution)/shard_map/ppermute | solution.py:22
  108.0 1.7 %collective-permute-start.26 = (bf16[4,89,8,128]{3,2,1,0:T(8,128)(2,1)S(1)}, bf16[4,89,8,128]{3,2,1,0:T(8,128)(2,1)S(1)}, u32[]{:S(2)}, u32[]{:S(2)}) collective-permute-start(bf16[4,89,8,128]{3,2,1,0:T(8,128)(2,1)S(1)} %get-tuple-element.94), channel_id=1, source_target_pairs={{0,4},{2,6},{4,0},{6,2},{8,12},{10,14},{12,8},{14,10},{16,20},{18,... | collective-permute-start | bytes 2187272 | tf_op jit(solution)/shard_map/ppermute | solution.py:22
  110.4 8.1 %collective-permute-done.21 = bf16[2,32,4096]{2,1,0:T(8,128)(2,1)S(1)} collective-permute-done((bf16[2,32,4096]{2,1,0:T(8,128)(2,1)S(1)}, bf16[2,32,4096]{2,1,0:T(8,128)(2,1)S(1)}, u32[]{:S(2)}, u32[]{:S(2)}) %collective-permute-start.21) | collective-permute-done | bytes 524320 | tf_op jit(solution)/shard_map/ppermute | solution.py:22
  118.6 2.5 %collective-permute-start.22 = (bf16[32,4096]{1,0:T(8,128)(2,1)S(1)}, bf16[32,4096]{1,0:T(8,128)(2,1)S(1)}, u32[]{:S(2)}, u32[]{:S(2)}) collective-permute-start(bf16[32,4096]{1,0:T(8,128)(2,1)S(1)} %fusion.3), channel_id=1, source_target_pairs={{0,16},{2,18},{4,20},{6,22},{8,24},{10,26},{12,28},{14,30},{16,0},... | collective-permute-start | bytes 786440 | tf_op jit(solution)/shard_map/ppermute | solution.py:22
  122.0 3.9 %collective-permute-done.26 = bf16[4,89,8,128]{3,2,1,0:T(8,128)(2,1)S(1)} collective-permute-done((bf16[4,89,8,128]{3,2,1,0:T(8,128)(2,1)S(1)}, bf16[4,89,8,128]{3,2,1,0:T(8,128)(2,1)S(1)}, u32[]{:S(2)}, u32[]{:S(2)}) %collective-permute-start.26) | collective-permute-done | bytes 729120 | tf_op jit(solution)/shard_map/ppermute | solution.py:22
  127.3 1.8 %collective-permute-start.27 = (bf16[89,8,128]{2,1,0:T(8,128)(2,1)S(1)}, bf16[89,8,128]{2,1,0:T(8,128)(2,1)S(1)}, u32[]{:S(2)}, u32[]{:S(2)}) collective-permute-start(bf16[89,8,128]{2,1,0:T(8,128)(2,1)S(1)} %get-tuple-element.96), channel_id=1, source_target_pairs={{0,8},{2,10},{4,12},{6,14},{8,0},{10,2},{12,4},{14,6},{16,24},{18,... | collective-permute-start | bytes 546824 | tf_op jit(solution)/shard_map/ppermute | solution.py:22
  129.4 2.3 %collective-permute-start.29 = (bf16[89,8,128]{2,1,0:T(8,128)(2,1)S(1)}, bf16[89,8,128]{2,1,0:T(8,128)(2,1)S(1)}, u32[]{:S(2)}, u32[]{:S(2)}) collective-permute-start(bf16[89,8,128]{2,1,0:T(8,128)(2,1)S(1)} %get-tuple-element.98), channel_id=1, source_target_pairs={{0,24},{2,26},{4,28},{6,30},{8,16},{10,18},{12,20},{14,22},{16,8},... | collective-permute-start | bytes 546824 | tf_op jit(solution)/shard_map/ppermute | solution.py:22
  131.8 10.0 %collective-permute-done.22 = bf16[32,4096]{1,0:T(8,128)(2,1)S(1)} collective-permute-done((bf16[32,4096]{1,0:T(8,128)(2,1)S(1)}, bf16[32,4096]{1,0:T(8,128)(2,1)S(1)}, u32[]{:S(2)}, u32[]{:S(2)}) %collective-permute-start.22) | collective-permute-done | bytes 262176 | tf_op jit(solution)/shard_map/ppermute | solution.py:22
  142.6 3.1 %collective-permute-done.28.refs_2_ = bf16[89,8,128]{2,1,0:T(8,128)(2,1)S(1)} collective-permute-done((bf16[89,8,128]{2,1,0:T(8,128)(2,1)S(1)}, bf16[89,8,128]{2,1,0:T(8,128)(2,1)S(1)}, u32[]{:S(2)}, u32[]{:S(2)}) %collective-permute-start.28) | collective-permute-done | bytes 182304 | tf_op jit(solution)/shard_map/ppermute | solution.py:22
  145.7 3.0 %shard_map.81 = bf16[8,9,56,128]{3,2,1,0:T(8,128)(2,1)} custom-call(s32[17,56]{1,0:T(8,128)S(1)} %pad_add_fusion.table, bf16[89,8,128]{2,1,0:T(8,128)(2,1)S(1)} %get-tuple-element.99.refs_0_, bf16[89,8,128]{2,1,0:T(8,128)(2,1)S(1)} %collective-permute-done.27.refs_1_, bf16[89,8,128]{2,1,0:T(8,128)(2,1)S(1)} %collective-permute-done.28.refs_2_, ...), custom_call_target="tpu_custom_call" | custom-call | bytes 2000000 | tf_op jit(solution)/shard_map/pallas_call | solution.py:261
  (75 shorter events, 23.1 us)
Async XLA Ops:
  0.6 16.2 %collective-permute-start.1 = (bf16[32,4096]{1,0:T(8,128)(2,1)}, bf16[32,4096]{1,0:T(8,128)(2,1)S(1)}, u32[]{:S(2)}, u32[]{:S(2)}) collective-permute-start(bf16[32,4096]{1,0:T(8,128)(2,1)} %param.5), channel_id=1, source_target_pairs={{0,16},{2,18},{4,20},{6,22},{8,24},{10,26},{12,28},{14,30},{16,0},... | collective-permute-start | bytes 786440 | tf_op jit(solution)/shard_map/ppermute | solution.py:22
  9.9 37.7 %copy-start.3 = (bf16[32,4096]{1,0:T(8,128)(2,1)S(1)}, bf16[32,4096]{1,0:T(8,128)(2,1)}, u32[]{:S(2)}) copy-start(bf16[32,4096]{1,0:T(8,128)(2,1)} %param.6) | copy-start | bytes 786436
  9.9 49.6 %copy-start.2 = (bf16[32,4096]{1,0:T(8,128)(2,1)S(1)}, bf16[32,4096]{1,0:T(8,128)(2,1)}, u32[]{:S(2)}) copy-start(bf16[32,4096]{1,0:T(8,128)(2,1)} %param.5) | copy-start | bytes 786436
  16.9 5.8 %collective-permute-start.4 = (bf16[89,8,128]{2,1,0:T(8,128)(2,1)S(1)}, bf16[89,8,128]{2,1,0:T(8,128)(2,1)S(1)}, u32[]{:S(2)}, u32[]{:S(2)}) collective-permute-start(bf16[89,8,128]{2,1,0:T(8,128)(2,1)S(1)} %get-tuple-element.60), channel_id=1, source_target_pairs={{0,8},{2,10},{4,12},{6,14},{8,0},{10,2},{12,4},{14,6},{16,24},{18,... | collective-permute-start | bytes 546824 | tf_op jit(solution)/shard_map/ppermute | solution.py:22
  17.7 17.2 %collective-permute-start.3 = (bf16[89,8,128]{2,1,0:T(8,128)(2,1)S(1)}, bf16[89,8,128]{2,1,0:T(8,128)(2,1)S(1)}, u32[]{:S(2)}, u32[]{:S(2)}) collective-permute-start(bf16[89,8,128]{2,1,0:T(8,128)(2,1)S(1)} %get-tuple-element.58), channel_id=1, source_target_pairs={{0,24},{2,26},{4,28},{6,30},{8,16},{10,18},{12,20},{14,22},{16,8},... | collective-permute-start | bytes 546824 | tf_op jit(solution)/shard_map/ppermute | solution.py:22
  22.7 22.2 %collective-permute-start.5 = (bf16[2,89,8,128]{3,2,1,0:T(8,128)(2,1)S(1)}, bf16[2,89,8,128]{3,2,1,0:T(8,128)(2,1)S(1)}, u32[]{:S(2)}, u32[]{:S(2)}) collective-permute-start(bf16[2,89,8,128]{3,2,1,0:T(8,128)(2,1)S(1)} %pad_maximum_fusion.1.refs_0_), channel_id=1, source_target_pairs={{0,2},{2,0},{4,6},{6,4},{8,10},{10,8},{12,14},{14,12},{16,18},{18,... | collective-permute-start | bytes 1093640 | tf_op jit(solution)/shard_map/ppermute | solution.py:22
  24.3 20.6 %collective-permute-start.6 = (bf16[2,89,8,128]{3,2,1,0:T(8,128)(2,1)S(1)}, bf16[2,89,8,128]{3,2,1,0:T(8,128)(2,1)S(1)}, u32[]{:S(2)}, u32[]{:S(2)}) collective-permute-start(bf16[2,89,8,128]{3,2,1,0:T(8,128)(2,1)S(1)} %pad_maximum_fusion.1.refs_0_), channel_id=1, source_target_pairs={{0,4},{2,6},{4,0},{6,2},{8,12},{10,14},{12,8},{14,10},{16,20},{18,... | collective-permute-start | bytes 1093640 | tf_op jit(solution)/shard_map/ppermute | solution.py:22
  25.8 11.7 %collective-permute-start.2 = (bf16[89,8,128]{2,1,0:T(8,128)(2,1)S(1)}, bf16[89,8,128]{2,1,0:T(8,128)(2,1)S(1)}, u32[]{:S(2)}, u32[]{:S(2)}) collective-permute-start(bf16[89,8,128]{2,1,0:T(8,128)(2,1)S(1)} %get-tuple-element.57), channel_id=1, source_target_pairs={{0,16},{2,18},{4,20},{6,22},{8,24},{10,26},{12,28},{14,30},{16,0},... | collective-permute-start | bytes 546824 | tf_op jit(solution)/shard_map/ppermute | solution.py:22
  32.4 9.7 %collective-permute-start = (bf16[32,4096]{1,0:T(8,128)(2,1)}, bf16[32,4096]{1,0:T(8,128)(2,1)S(1)}, u32[]{:S(2)}, u32[]{:S(2)}) collective-permute-start(bf16[32,4096]{1,0:T(8,128)(2,1)} %param.5), channel_id=1, source_target_pairs={{0,8},{2,10},{4,12},{6,14},{8,0},{10,2},{12,4},{14,6},{16,24},{18,... | collective-permute-start | bytes 786440 | tf_op jit(solution)/shard_map/ppermute | solution.py:22
  34.9 10.0 %collective-permute-start.7 = (bf16[32,4096]{1,0:T(8,128)(2,1)}, bf16[32,4096]{1,0:T(8,128)(2,1)S(1)}, u32[]{:S(2)}, u32[]{:S(2)}) collective-permute-start(bf16[32,4096]{1,0:T(8,128)(2,1)} %param.6), channel_id=1, source_target_pairs={{0,8},{2,10},{4,12},{6,14},{8,0},{10,2},{12,4},{14,6},{16,24},{18,... | collective-permute-start | bytes 786440 | tf_op jit(solution)/shard_map/ppermute | solution.py:22
  44.9 14.6 %collective-permute-start.9 = (bf16[2,89,8,128]{3,2,1,0:T(8,128)(2,1)S(1)}, bf16[2,89,8,128]{3,2,1,0:T(8,128)(2,1)S(1)}, u32[]{:S(2)}, u32[]{:S(2)}) collective-permute-start(bf16[2,89,8,128]{3,2,1,0:T(8,128)(2,1)S(1)} %pad_maximum_fusion.refs_4_), channel_id=1, source_target_pairs={{0,2},{2,0},{4,6},{6,4},{8,10},{10,8},{12,14},{14,12},{16,18},{18,... | collective-permute-start | bytes 1093640 | tf_op jit(solution)/shard_map/ppermute | solution.py:22
  46.5 13.0 %collective-permute-start.10 = (bf16[2,89,8,128]{3,2,1,0:T(8,128)(2,1)S(1)}, bf16[2,89,8,128]{3,2,1,0:T(8,128)(2,1)S(1)}, u32[]{:S(2)}, u32[]{:S(2)}) collective-permute-start(bf16[2,89,8,128]{3,2,1,0:T(8,128)(2,1)S(1)} %pad_maximum_fusion.refs_4_), channel_id=1, source_target_pairs={{0,4},{2,6},{4,0},{6,2},{8,12},{10,14},{12,8},{14,10},{16,20},{18,... | collective-permute-start | bytes 1093640 | tf_op jit(solution)/shard_map/ppermute | solution.py:22
  47.5 9.4 %collective-permute-start.8 = (bf16[32,4096]{1,0:T(8,128)(2,1)S(1)}, bf16[32,4096]{1,0:T(8,128)(2,1)S(1)}, u32[]{:S(2)}, u32[]{:S(2)}) collective-permute-start(bf16[32,4096]{1,0:T(8,128)(2,1)S(1)} %collective-permute-done.1), channel_id=1, source_target_pairs={{0,8},{2,10},{4,12},{6,14},{8,0},{10,2},{12,4},{14,6},{16,24},{18,... | collective-permute-start | bytes 786440 | tf_op jit(solution)/shard_map/ppermute | solution.py:22
  47.5 12.0 %collective-permute-start.11 = (bf16[32,4096]{1,0:T(8,128)(2,1)S(1)}, bf16[32,4096]{1,0:T(8,128)(2,1)S(1)}, u32[]{:S(2)}, u32[]{:S(2)}) collective-permute-start(bf16[32,4096]{1,0:T(8,128)(2,1)S(1)} %copy-done.3), channel_id=1, source_target_pairs={{0,16},{2,18},{4,20},{6,22},{8,24},{10,26},{12,28},{14,30},{16,0},... | collective-permute-start | bytes 786440 | tf_op jit(solution)/shard_map/ppermute | solution.py:22
  59.6 13.9 %collective-permute-start.12 = (bf16[128,4096]{1,0:T(8,128)(2,1)S(1)}, bf16[128,4096]{1,0:T(8,128)(2,1)S(1)}, u32[]{:S(2)}, u32[]{:S(2)}) collective-permute-start(bf16[128,4096]{1,0:T(8,128)(2,1)S(1)} %constant_dynamic-update-slice_fusion.refs_0_), channel_id=1, source_target_pairs={{0,1},{1,0},{2,3},{3,2},{4,5},{5,4},{6,7},{7,6},{8,9},{9,8},{10,11... | collective-permute-start | bytes 3145736 | tf_op jit(solution)/shard_map/ppermute | solution.py:22
  59.7 8.7 %collective-permute-start.15 = (bf16[32,4096]{1,0:T(8,128)(2,1)S(1)}, bf16[32,4096]{1,0:T(8,128)(2,1)S(1)}, u32[]{:S(2)}, u32[]{:S(2)}) collective-permute-start(bf16[32,4096]{1,0:T(8,128)(2,1)S(1)} %collective-permute-done.11), channel_id=1, source_target_pairs={{0,8},{2,10},{4,12},{6,14},{8,0},{10,2},{12,4},{14,6},{16,24},{18,... | collective-permute-start | bytes 786440 | tf_op jit(solution)/shard_map/ppermute | solution.py:22
  59.8 11.9 %collective-permute-start.13 = (bf16[2,89,8,128]{3,2,1,0:T(8,128)(2,1)S(1)}, bf16[2,89,8,128]{3,2,1,0:T(8,128)(2,1)S(1)}, u32[]{:S(2)}, u32[]{:S(2)}) collective-permute-start(bf16[2,89,8,128]{3,2,1,0:T(8,128)(2,1)S(1)} %collective-permute-done.5.refs_1_), channel_id=1, source_target_pairs={{0,4},{2,6},{4,0},{6,2},{8,12},{10,14},{12,8},{14,10},{16,20},{18,... | collective-permute-start | bytes 1093640 | tf_op jit(solution)/shard_map/ppermute | solution.py:22
  61.2 10.5 %collective-permute-start.14 = (bf16[2,89,8,128]{3,2,1,0:T(8,128)(2,1)S(1)}, bf16[2,89,8,128]{3,2,1,0:T(8,128)(2,1)S(1)}, u32[]{:S(2)}, u32[]{:S(2)}) collective-permute-start(bf16[2,89,8,128]{3,2,1,0:T(8,128)(2,1)S(1)} %collective-permute-done.10.refs_6_), channel_id=1, source_target_pairs={{0,2},{2,0},{4,6},{6,4},{8,10},{10,8},{12,14},{14,12},{16,18},{18,... | collective-permute-start | bytes 1093640 | tf_op jit(solution)/shard_map/ppermute | solution.py:22
  79.2 2.7 %collective-permute-start.16 = (bf16[4,32,4096]{2,1,0:T(8,128)(2,1)S(1)}, bf16[4,32,4096]{2,1,0:T(8,128)(2,1)S(1)}, u32[]{:S(2)}, u32[]{:S(2)}) collective-permute-start(bf16[4,32,4096]{2,1,0:T(8,128)(2,1)S(1)} %get-tuple-element.73), channel_id=1, source_target_pairs={{0,1},{1,0},{2,3},{3,2},{4,5},{5,4},{6,7},{7,6},{8,9},{9,8},{10,11... | collective-permute-start | bytes 3145736 | tf_op jit(solution)/shard_map/ppermute | solution.py:22
  79.3 4.5 %collective-permute-start.19 = (bf16[128,4096]{1,0:T(8,128)(2,1)S(1)}, bf16[128,4096]{1,0:T(8,128)(2,1)S(1)}, u32[]{:S(2)}, u32[]{:S(2)}) collective-permute-start(bf16[128,4096]{1,0:T(8,128)(2,1)S(1)} %constant_dynamic-update-slice_fusion.4.refs_0_), channel_id=1, source_target_pairs={{0,1},{1,0},{2,3},{3,2},{4,5},{5,4},{6,7},{7,6},{8,9},{9,8},{10,11... | collective-permute-start | bytes 3145736 | tf_op jit(solution)/shard_map/ppermute | solution.py:22
  82.0 14.0 %collective-permute-start.17 = (bf16[2,32,4096]{2,1,0:T(8,128)(2,1)S(1)}, bf16[2,32,4096]{2,1,0:T(8,128)(2,1)S(1)}, u32[]{:S(2)}, u32[]{:S(2)}) collective-permute-start(bf16[2,32,4096]{2,1,0:T(8,128)(2,1)S(1)} %add_convert_fusion.1), channel_id=1, source_target_pairs={{0,8},{2,10},{4,12},{6,14},{8,0},{10,2},{12,4},{14,6},{16,24},{18,... | collective-permute-start | bytes 1572872 | tf_op jit(solution)/shard_map/ppermute | solution.py:22
  96.1 2.7 %collective-permute-start.20 = (bf16[4,32,4096]{2,1,0:T(8,128)(2,1)S(1)}, bf16[4,32,4096]{2,1,0:T(8,128)(2,1)S(1)}, u32[]{:S(2)}, u32[]{:S(2)}) collective-permute-start(bf16[4,32,4096]{2,1,0:T(8,128)(2,1)S(1)} %get-tuple-element.84), channel_id=1, source_target_pairs={{0,1},{1,0},{2,3},{3,2},{4,5},{5,4},{6,7},{7,6},{8,9},{9,8},{10,11... | collective-permute-start | bytes 3145736 | tf_op jit(solution)/shard_map/ppermute | solution.py:22
  96.1 10.9 %collective-permute-start.23 = (bf16[2,89,8,128]{3,2,1,0:T(8,128)(2,1)S(1)}, bf16[2,89,8,128]{3,2,1,0:T(8,128)(2,1)S(1)}, u32[]{:S(2)}, u32[]{:S(2)}) collective-permute-start(bf16[2,89,8,128]{3,2,1,0:T(8,128)(2,1)S(1)} %get-tuple-element.89), channel_id=1, source_target_pairs={{0,2},{2,0},{4,6},{6,4},{8,10},{10,8},{12,14},{14,12},{16,18},{18,... | collective-permute-start | bytes 1093640 | tf_op jit(solution)/shard_map/ppermute | solution.py:22
  96.5 10.6 %collective-permute-start.24 = (bf16[2,89,8,128]{3,2,1,0:T(8,128)(2,1)S(1)}, bf16[2,89,8,128]{3,2,1,0:T(8,128)(2,1)S(1)}, u32[]{:S(2)}, u32[]{:S(2)}) collective-permute-start(bf16[2,89,8,128]{3,2,1,0:T(8,128)(2,1)S(1)} %get-tuple-element.90), channel_id=1, source_target_pairs={{0,4},{2,6},{4,0},{6,2},{8,12},{10,14},{12,8},{14,10},{16,20},{18,... | collective-permute-start | bytes 1093640 | tf_op jit(solution)/shard_map/ppermute | solution.py:22
  98.9 19.6 %collective-permute-start.21 = (bf16[2,32,4096]{2,1,0:T(8,128)(2,1)S(1)}, bf16[2,32,4096]{2,1,0:T(8,128)(2,1)S(1)}, u32[]{:S(2)}, u32[]{:S(2)}) collective-permute-start(bf16[2,32,4096]{2,1,0:T(8,128)(2,1)S(1)} %add_convert_fusion), channel_id=1, source_target_pairs={{0,8},{2,10},{4,12},{6,14},{8,0},{10,2},{12,4},{14,6},{16,24},{18,... | collective-permute-start | bytes 1572872 | tf_op jit(solution)/shard_map/ppermute | solution.py:22
  100.8 17.8 %collective-permute-start.18 = (bf16[32,4096]{1,0:T(8,128)(2,1)S(1)}, bf16[32,4096]{1,0:T(8,128)(2,1)S(1)}, u32[]{:S(2)}, u32[]{:S(2)}) collective-permute-start(bf16[32,4096]{1,0:T(8,128)(2,1)S(1)} %fusion.2), channel_id=1, source_target_pairs={{0,16},{2,18},{4,20},{6,22},{8,24},{10,26},{12,28},{14,30},{16,0},... | collective-permute-start | bytes 786440 | tf_op jit(solution)/shard_map/ppermute | solution.py:22
  108.0 17.9 %collective-permute-start.26 = (bf16[4,89,8,128]{3,2,1,0:T(8,128)(2,1)S(1)}, bf16[4,89,8,128]{3,2,1,0:T(8,128)(2,1)S(1)}, u32[]{:S(2)}, u32[]{:S(2)}) collective-permute-start(bf16[4,89,8,128]{3,2,1,0:T(8,128)(2,1)S(1)} %get-tuple-element.94), channel_id=1, source_target_pairs={{0,4},{2,6},{4,0},{6,2},{8,12},{10,14},{12,8},{14,10},{16,20},{18,... | collective-permute-start | bytes 2187272 | tf_op jit(solution)/shard_map/ppermute | solution.py:22
  109.7 17.3 %collective-permute-start.25 = (bf16[4,89,8,128]{3,2,1,0:T(8,128)(2,1)S(1)}, bf16[4,89,8,128]{3,2,1,0:T(8,128)(2,1)S(1)}, u32[]{:S(2)}, u32[]{:S(2)}) collective-permute-start(bf16[4,89,8,128]{3,2,1,0:T(8,128)(2,1)S(1)} %get-tuple-element.93), channel_id=1, source_target_pairs={{0,2},{2,0},{4,6},{6,4},{8,10},{10,8},{12,14},{14,12},{16,18},{18,... | collective-permute-start | bytes 2187272 | tf_op jit(solution)/shard_map/ppermute | solution.py:22
  118.6 23.2 %collective-permute-start.22 = (bf16[32,4096]{1,0:T(8,128)(2,1)S(1)}, bf16[32,4096]{1,0:T(8,128)(2,1)S(1)}, u32[]{:S(2)}, u32[]{:S(2)}) collective-permute-start(bf16[32,4096]{1,0:T(8,128)(2,1)S(1)} %fusion.3), channel_id=1, source_target_pairs={{0,16},{2,18},{4,20},{6,22},{8,24},{10,26},{12,28},{14,30},{16,0},... | collective-permute-start | bytes 786440 | tf_op jit(solution)/shard_map/ppermute | solution.py:22
  127.3 15.3 %collective-permute-start.27 = (bf16[89,8,128]{2,1,0:T(8,128)(2,1)S(1)}, bf16[89,8,128]{2,1,0:T(8,128)(2,1)S(1)}, u32[]{:S(2)}, u32[]{:S(2)}) collective-permute-start(bf16[89,8,128]{2,1,0:T(8,128)(2,1)S(1)} %get-tuple-element.96), channel_id=1, source_target_pairs={{0,8},{2,10},{4,12},{6,14},{8,0},{10,2},{12,4},{14,6},{16,24},{18,... | collective-permute-start | bytes 546824 | tf_op jit(solution)/shard_map/ppermute | solution.py:22
  129.1 16.6 %collective-permute-start.28 = (bf16[89,8,128]{2,1,0:T(8,128)(2,1)S(1)}, bf16[89,8,128]{2,1,0:T(8,128)(2,1)S(1)}, u32[]{:S(2)}, u32[]{:S(2)}) collective-permute-start(bf16[89,8,128]{2,1,0:T(8,128)(2,1)S(1)} %get-tuple-element.97), channel_id=1, source_target_pairs={{0,16},{2,18},{4,20},{6,22},{8,24},{10,26},{12,28},{14,30},{16,0},... | collective-permute-start | bytes 546824 | tf_op jit(solution)/shard_map/ppermute | solution.py:22
  129.4 16.3 %collective-permute-start.29 = (bf16[89,8,128]{2,1,0:T(8,128)(2,1)S(1)}, bf16[89,8,128]{2,1,0:T(8,128)(2,1)S(1)}, u32[]{:S(2)}, u32[]{:S(2)}) collective-permute-start(bf16[89,8,128]{2,1,0:T(8,128)(2,1)S(1)} %get-tuple-element.98), channel_id=1, source_target_pairs={{0,24},{2,26},{4,28},{6,30},{8,16},{10,18},{12,20},{14,22},{16,8},... | collective-permute-start | bytes 546824 | tf_op jit(solution)/shard_map/ppermute | solution.py:22
  (2 other events, 6.9 us)

commit v11 on v9

--- a/solution.py
+++ b/solution.py
@@ -289,9 +289,6 @@
     shape = jax.ShapeDtypeStruct
 
     x_items, g_items = {0: tokens}, {0: out_grad}
-    if far > 1:
-        x_items[near] = swap(tokens, "dp", near)
-
     capacity = (terms * blocks_dev - 3 * blocks_dev + 3 * (slot_count - 1) * (far - 1)) // far
     slots = capacity + 1
     block_ids = jnp.arange(blocks_dev, dtype=jnp.int32)
@@ -339,6 +336,8 @@
         vmem=24,
     )
     staged = tensor_size == 2 and far == 4 and near == 4
+    if far > 1:
+        x_items[near] = swap(after(tokens, *packed), "dp", near)
     received = [swap(packed[at], "dp", at * near) for at in reversed(range(1, far))][::-1]
     held = jnp.stack([packed[0], *received])
     x_core, g_core = {}, {}
@@ -365,6 +364,7 @@
         x_items[2 * near] = swap(x_source, "dp", 2 * near)
         g_items[near] = swap(g_source, "dp", near)
         x_source, g_source = after((x_items[2 * near], out_grad), x_items[2 * near], g_items[near])
+        g_source = after(g_source, pass_1, pass_2)
         x_items[3 * near] = swap(x_source, "dp", near)
         g_items[2 * near] = swap(g_source, "dp", 2 * near)
         g_items[3 * near] = swap(g_items[2 * near], "dp", near)

time: 139 us -> 141 us (1.014)
  starting transfers between devices: 32.7 us -> 35.6 us
  waiting for transfers between devices: 74.5 us -> 72.1 us
    ppermute x31, starting transfers between devices: 32.7 us -> 35.6 us  [swap(): return lax.ppermute(value, axis, [(at, at ^ stride) for at in range(size)])]
    ppermute x31, waiting for transfers between devices: 74.5 us -> 72.1 us  [swap(): return lax.ppermute(value, axis, [(at, at ^ stride) for at in range(size)])]
  transfers between devices with their start and end apart: 31 -> 31, of which waited for: 17 -> 17; matrix products, arithmetic and copies ran while one was open for 5% -> 2% of each run, Pallas kernels for 15% -> 13%
where the time goes in v11:
time: 141 us; the launch traced here: 140 us
  waiting for transfers between devices  72.1 us (51%)
  starting transfers between devices  35.6 us (25%)
  Pallas kernels  23.2 us (16%)
  other arithmetic  4.88 us (3%)
  local copies, waits for them, and re-layouts  2.87 us (2%)
    ppermute x31, waiting for transfers between devices, swap(): return lax.ppermute(value, axis, [(at, at ^ stride) for at in range(size)])  72.1 us
    ppermute x31, starting transfers between devices, swap(): return lax.ppermute(value, axis, [(at, at ^ stride) for at in range(size)])  35.6 us
    pallas_call x6, Pallas kernels, call(): pl.pallas_call(kernel, grid_spec=pltpu.PrefetchScalarGridSpec(num_scalar_...  23.2 us
  transfers between devices with their start and end apart: 31, of which 17 were waited for; matrix products, arithmetic and copies ran while one was open for 2% of the time, Pallas kernels for 13%

profile of v11, /device:TPU:0, one launch (start us, length us, event | category | flops | bytes accessed | tf_op | source)
XLA Modules:
  0.0 139.5 jit_solution(967714090859412695)
XLA Ops:
  4.6 1.2 copy-done.1
  5.8 1.6 %shard_map.76 = (bf16[89,8,128]{2,1,0:T(8,128)(2,1)S(1)}, bf16[89,8,128]{2,1,0:T(8,128)(2,1)S(1)}, bf16[89,8,128]{2,1,0:T(8,128)(2,1)S(1)}, bf16[89,8,128]{2,1,0:T(8,128)(2,1)S(1)}) custom-call(s32[17,56]{1,0:T(8,128)S(1)} %pad_add_fusion.table, bf16[8,9,56,128]{3,2,1,0:T(8,128)(2,1)S(1)} %bitcast.36), custom_call_target="tpu_custom_call" | custom-call | bytes 1000000 | tf_op jit(solution)/shard_map/pallas_call | solution.py:261
  7.5 3.1 %collective-permute-start = (bf16[32,4096]{1,0:T(8,128)(2,1)}, bf16[32,4096]{1,0:T(8,128)(2,1)S(1)}, u32[]{:S(2)}, u32[]{:S(2)}) collective-permute-start(bf16[32,4096]{1,0:T(8,128)(2,1)} %refs_0_.2), channel_id=1, source_target_pairs={{0,8},{2,10},{4,12},{6,14},{8,0},{10,2},{12,4},{14,6},{16,24},{18,... | collective-permute-start | bytes 786440 | tf_op jit(solution)/shard_map/ppermute | solution.py:22
  10.6 2.5 %collective-permute-start.3 = (bf16[89,8,128]{2,1,0:T(8,128)(2,1)S(1)}, bf16[89,8,128]{2,1,0:T(8,128)(2,1)S(1)}, u32[]{:S(2)}, u32[]{:S(2)}) collective-permute-start(bf16[89,8,128]{2,1,0:T(8,128)(2,1)S(1)} %get-tuple-element.50), channel_id=1, source_target_pairs={{0,24},{2,26},{4,28},{6,30},{8,16},{10,18},{12,20},{14,22},{16,8},... | collective-permute-start | bytes 546824 | tf_op jit(solution)/shard_map/ppermute | solution.py:22
  13.1 1.8 %collective-permute-start.1 = (bf16[89,8,128]{2,1,0:T(8,128)(2,1)S(1)}, bf16[89,8,128]{2,1,0:T(8,128)(2,1)S(1)}, u32[]{:S(2)}, u32[]{:S(2)}) collective-permute-start(bf16[89,8,128]{2,1,0:T(8,128)(2,1)S(1)} %get-tuple-element.48), channel_id=1, source_target_pairs={{0,8},{2,10},{4,12},{6,14},{8,0},{10,2},{12,4},{14,6},{16,24},{18,... | collective-permute-start | bytes 546824 | tf_op jit(solution)/shard_map/ppermute | solution.py:22
  14.9 9.5 %collective-permute-done.3 = bf16[89,8,128]{2,1,0:T(8,128)(2,1)S(1)} collective-permute-done((bf16[89,8,128]{2,1,0:T(8,128)(2,1)S(1)}, bf16[89,8,128]{2,1,0:T(8,128)(2,1)S(1)}, u32[]{:S(2)}, u32[]{:S(2)}) %collective-permute-start.3) | collective-permute-done | bytes 182304 | tf_op jit(solution)/shard_map/ppermute | solution.py:22
  24.9 4.2 %collective-permute-done.2 = bf16[89,8,128]{2,1,0:T(8,128)(2,1)S(1)} collective-permute-done((bf16[89,8,128]{2,1,0:T(8,128)(2,1)S(1)}, bf16[89,8,128]{2,1,0:T(8,128)(2,1)S(1)}, u32[]{:S(2)}, u32[]{:S(2)}) %collective-permute-start.2) | collective-permute-done | bytes 182304 | tf_op jit(solution)/shard_map/ppermute | solution.py:22
  29.3 1.6 %collective-permute-start.10 = (bf16[4,89,8,128]{3,2,1,0:T(8,128)(2,1)S(1)}, bf16[4,89,8,128]{3,2,1,0:T(8,128)(2,1)S(1)}, u32[]{:S(2)}, u32[]{:S(2)}) collective-permute-start(bf16[4,89,8,128]{3,2,1,0:T(8,128)(2,1)S(1)} %pad_maximum_fusion.1.refs_0_), channel_id=1, source_target_pairs={{0,2},{2,0},{4,6},{6,4},{8,10},{10,8},{12,14},{14,12},{16,18},{18,... | collective-permute-start | bytes 2187272 | tf_op jit(solution)/shard_map/ppermute | solution.py:22
  30.9 1.5 %collective-permute-start.12 = (bf16[4,89,8,128]{3,2,1,0:T(8,128)(2,1)S(1)}, bf16[4,89,8,128]{3,2,1,0:T(8,128)(2,1)S(1)}, u32[]{:S(2)}, u32[]{:S(2)}) collective-permute-start(bf16[4,89,8,128]{3,2,1,0:T(8,128)(2,1)S(1)} %pad_maximum_fusion.1.refs_0_), channel_id=1, source_target_pairs={{0,4},{2,6},{4,0},{6,2},{8,12},{10,14},{12,8},{14,10},{16,20},{18,... | collective-permute-start | bytes 2187272 | tf_op jit(solution)/shard_map/ppermute | solution.py:22
  32.4 2.4 %collective-permute-start.7 = (bf16[32,4096]{1,0:T(8,128)(2,1)S(1)}, bf16[32,4096]{1,0:T(8,128)(2,1)S(1)}, u32[]{:S(2)}, u32[]{:S(2)}) collective-permute-start(bf16[32,4096]{1,0:T(8,128)(2,1)S(1)} %copy-done.2), channel_id=1, source_target_pairs={{0,16},{2,18},{4,20},{6,22},{8,24},{10,26},{12,28},{14,30},{16,0},... | collective-permute-start | bytes 786440 | tf_op jit(solution)/shard_map/ppermute | solution.py:22
  34.8 1.5 %collective-permute-start.8 = (bf16[32,4096]{1,0:T(8,128)(2,1)S(1)}, bf16[32,4096]{1,0:T(8,128)(2,1)S(1)}, u32[]{:S(2)}, u32[]{:S(2)}) collective-permute-start(bf16[32,4096]{1,0:T(8,128)(2,1)S(1)} %copy-done.3), channel_id=1, source_target_pairs={{0,8},{2,10},{4,12},{6,14},{8,0},{10,2},{12,4},{14,6},{16,24},{18,... | collective-permute-start | bytes 786440 | tf_op jit(solution)/shard_map/ppermute | solution.py:22
  36.3 9.1 %collective-permute-done.7.refs_2_ = bf16[32,4096]{1,0:T(8,128)(2,1)S(1)} collective-permute-done((bf16[32,4096]{1,0:T(8,128)(2,1)S(1)}, bf16[32,4096]{1,0:T(8,128)(2,1)S(1)}, u32[]{:S(2)}, u32[]{:S(2)}) %collective-permute-start.7) | collective-permute-done | bytes 262176 | tf_op jit(solution)/shard_map/ppermute | solution.py:22
  45.6 1.5 %collective-permute-start.9 = (bf16[32,4096]{1,0:T(8,128)(2,1)S(1)}, bf16[32,4096]{1,0:T(8,128)(2,1)S(1)}, u32[]{:S(2)}, u32[]{:S(2)}) collective-permute-start(bf16[32,4096]{1,0:T(8,128)(2,1)S(1)} %collective-permute-done.7.refs_2_), channel_id=1, source_target_pairs={{0,8},{2,10},{4,12},{6,14},{8,0},{10,2},{12,4},{14,6},{16,24},{18,... | collective-permute-start | bytes 786440 | tf_op jit(solution)/shard_map/ppermute | solution.py:22
  48.0 1.5 %collective-permute-start.13 = (bf16[2,89,8,128]{3,2,1,0:T(8,128)(2,1)S(1)}, bf16[2,89,8,128]{3,2,1,0:T(8,128)(2,1)S(1)}, u32[]{:S(2)}, u32[]{:S(2)}) collective-permute-start(bf16[2,89,8,128]{3,2,1,0:T(8,128)(2,1)S(1)} %slice.136), channel_id=1, source_target_pairs={{0,2},{2,0},{4,6},{6,4},{8,10},{10,8},{12,14},{14,12},{16,18},{18,... | collective-permute-start | bytes 1093640 | tf_op jit(solution)/shard_map/ppermute | solution.py:22
  49.5 2.7 %collective-permute-start.14 = (bf16[32,4096]{1,0:T(8,128)(2,1)S(1)}, bf16[32,4096]{1,0:T(8,128)(2,1)S(1)}, u32[]{:S(2)}, u32[]{:S(2)}) collective-permute-start(bf16[32,4096]{1,0:T(8,128)(2,1)S(1)} %copy-done.3), channel_id=1, source_target_pairs={{0,16},{2,18},{4,20},{6,22},{8,24},{10,26},{12,28},{14,30},{16,0},... | collective-permute-start | bytes 786440 | tf_op jit(solution)/shard_map/ppermute | solution.py:22
  52.2 3.1 %collective-permute-done.9.refs_3_ = bf16[32,4096]{1,0:T(8,128)(2,1)S(1)} collective-permute-done((bf16[32,4096]{1,0:T(8,128)(2,1)S(1)}, bf16[32,4096]{1,0:T(8,128)(2,1)S(1)}, u32[]{:S(2)}, u32[]{:S(2)}) %collective-permute-start.9) | collective-permute-done | bytes 262176 | tf_op jit(solution)/shard_map/ppermute | solution.py:22
  55.3 6.5 %collective-permute-done.14.refs_2_ = bf16[32,4096]{1,0:T(8,128)(2,1)S(1)} collective-permute-done((bf16[32,4096]{1,0:T(8,128)(2,1)S(1)}, bf16[32,4096]{1,0:T(8,128)(2,1)S(1)}, u32[]{:S(2)}, u32[]{:S(2)}) %collective-permute-start.14) | collective-permute-done | bytes 262176 | tf_op jit(solution)/shard_map/ppermute | solution.py:22
  61.9 1.8 %shard_map.77.refs_7_.refs_6_ = bf16[89,128,128]{2,1,0:T(8,128)(2,1)S(1)} custom-call(s32[17,56]{1,0:T(8,128)S(1)} %pad_add_fusion.table, bf16[4,89,8,128]{3,2,1,0:T(8,128)(2,1)S(1)} %pad_maximum_fusion.1.refs_0_, bf16[4,89,8,128]{3,2,1,0:T(8,128)(2,1)S(1)} %collective-permute-done.10.refs_1_, bf16[4,89,8,128]{3,2,1,0:T(8,128)(2,1)S(1)} %collective-permute-done.12.refs_2_, ...), custom_call_target="tpu_custom_call" | custom-call | bytes 10000000 | tf_op jit(solution)/shard_map/pallas_call | solution.py:261
  63.7 5.6 %shard_map.78 = (bf16[4096,256]{1,0:T(8,128)(2,1)S(1)}, f32[14,256,128]{2,1,0:T(8,128)S(1)}, f32[14,256,128]{2,1,0:T(8,128)S(1)}, bf16[14,128,256]{2,1,0:T(8,128...) custom-call(s32[17,56]{1,0:T(8,128)S(1)} %pad_add_fusion.table, ...), custom_call_target="tpu_custom_call" | custom-call | bytes 30000000 | tf_op jit(solution)/shard_map/pallas_call | solution.py:261
  71.1 2.0 %collective-permute-done.17 = bf16[4,32,4096]{2,1,0:T(8,128)(2,1)S(1)} collective-permute-done((bf16[4,32,4096]{2,1,0:T(8,128)(2,1)S(1)}, bf16[4,32,4096]{2,1,0:T(8,128)(2,1)S(1)}, u32[]{:S(2)}, u32[]{:S(2)}) %collective-permute-start.17) | collective-permute-done | bytes 1048608 | tf_op jit(solution)/shard_map/ppermute | solution.py:22
  74.3 10.2 %shard_map.79 = (bf16[4,32,4096]{2,1,0:T(8,128)(2,1)S(1)}, bf16[4,32,4096]{2,1,0:T(8,128)(2,1)S(1)}, bf16[4,89,8,128]{3,2,1,0:T(8,128)(2,1)S(1)}, bf16[4,89,8,12...) custom-call(s32[17,56]{1,0:T(8,128)S(1)} %pad_add_fusion.table, ...), custom_call_target="tpu_custom_call" | custom-call | bytes 40000000 | tf_op jit(solution)/shard_map/pallas_call | solution.py:261
  84.5 2.8 %collective-permute-done.18 = bf16[2,32,4096]{2,1,0:T(8,128)(2,1)S(1)} collective-permute-done((bf16[2,32,4096]{2,1,0:T(8,128)(2,1)S(1)}, bf16[2,32,4096]{2,1,0:T(8,128)(2,1)S(1)}, u32[]{:S(2)}, u32[]{:S(2)}) %collective-permute-start.18) | collective-permute-done | bytes 524320 | tf_op jit(solution)/shard_map/ppermute | solution.py:22
  91.2 1.6 %collective-permute-start.19 = (bf16[32,4096]{1,0:T(8,128)(2,1)S(1)}, bf16[32,4096]{1,0:T(8,128)(2,1)S(1)}, u32[]{:S(2)}, u32[]{:S(2)}) collective-permute-start(bf16[32,4096]{1,0:T(8,128)(2,1)S(1)} %fusion.2), channel_id=1, source_target_pairs={{0,16},{2,18},{4,20},{6,22},{8,24},{10,26},{12,28},{14,30},{16,0},... | collective-permute-start | bytes 786440 | tf_op jit(solution)/shard_map/ppermute | solution.py:22
  92.8 5.4 %collective-permute-done.24.got_1 = bf16[2,89,8,128]{3,2,1,0:T(8,128)(2,1)S(1)} collective-permute-done((bf16[2,89,8,128]{3,2,1,0:T(8,128)(2,1)S(1)}, bf16[2,89,8,128]{3,2,1,0:T(8,128)(2,1)S(1)}, u32[]{:S(2)}, u32[]{:S(2)}) %collective-permute-start.24) | collective-permute-done | bytes 364576 | tf_op jit(solution)/shard_map/ppermute | solution.py:22
  101.5 8.3 %collective-permute-done.22 = bf16[2,32,4096]{2,1,0:T(8,128)(2,1)S(1)} collective-permute-done((bf16[2,32,4096]{2,1,0:T(8,128)(2,1)S(1)}, bf16[2,32,4096]{2,1,0:T(8,128)(2,1)S(1)}, u32[]{:S(2)}, u32[]{:S(2)}) %collective-permute-start.22) | collective-permute-done | bytes 524320 | tf_op jit(solution)/shard_map/ppermute | solution.py:22
  109.9 1.7 %collective-permute-start.23 = (bf16[32,4096]{1,0:T(8,128)(2,1)S(1)}, bf16[32,4096]{1,0:T(8,128)(2,1)S(1)}, u32[]{:S(2)}, u32[]{:S(2)}) collective-permute-start(bf16[32,4096]{1,0:T(8,128)(2,1)S(1)} %fusion.3), channel_id=1, source_target_pairs={{0,16},{2,18},{4,20},{6,22},{8,24},{10,26},{12,28},{14,30},{16,0},... | collective-permute-start | bytes 786440 | tf_op jit(solution)/shard_map/ppermute | solution.py:22
  112.4 4.7 %collective-permute-done.27 = bf16[4,89,8,128]{3,2,1,0:T(8,128)(2,1)S(1)} collective-permute-done((bf16[4,89,8,128]{3,2,1,0:T(8,128)(2,1)S(1)}, bf16[4,89,8,128]{3,2,1,0:T(8,128)(2,1)S(1)}, u32[]{:S(2)}, u32[]{:S(2)}) %collective-permute-start.27) | collective-permute-done | bytes 729120 | tf_op jit(solution)/shard_map/ppermute | solution.py:22
  119.3 1.5 %collective-permute-start.29 = (bf16[89,8,128]{2,1,0:T(8,128)(2,1)S(1)}, bf16[89,8,128]{2,1,0:T(8,128)(2,1)S(1)}, u32[]{:S(2)}, u32[]{:S(2)}) collective-permute-start(bf16[89,8,128]{2,1,0:T(8,128)(2,1)S(1)} %get-tuple-element.85), channel_id=1, source_target_pairs={{0,16},{2,18},{4,20},{6,22},{8,24},{10,26},{12,28},{14,30},{16,0},... | collective-permute-start | bytes 546824 | tf_op jit(solution)/shard_map/ppermute | solution.py:22
  120.8 2.0 %collective-permute-start.30 = (bf16[89,8,128]{2,1,0:T(8,128)(2,1)S(1)}, bf16[89,8,128]{2,1,0:T(8,128)(2,1)S(1)}, u32[]{:S(2)}, u32[]{:S(2)}) collective-permute-start(bf16[89,8,128]{2,1,0:T(8,128)(2,1)S(1)} %get-tuple-element.86), channel_id=1, source_target_pairs={{0,24},{2,26},{4,28},{6,30},{8,16},{10,18},{12,20},{14,22},{16,8},... | collective-permute-start | bytes 546824 | tf_op jit(solution)/shard_map/ppermute | solution.py:22
  122.7 9.9 %collective-permute-done.23 = bf16[32,4096]{1,0:T(8,128)(2,1)S(1)} collective-permute-done((bf16[32,4096]{1,0:T(8,128)(2,1)S(1)}, bf16[32,4096]{1,0:T(8,128)(2,1)S(1)}, u32[]{:S(2)}, u32[]{:S(2)}) %collective-permute-start.23) | collective-permute-done | bytes 262176 | tf_op jit(solution)/shard_map/ppermute | solution.py:22
  133.5 3.1 %collective-permute-done.29.refs_2_ = bf16[89,8,128]{2,1,0:T(8,128)(2,1)S(1)} collective-permute-done((bf16[89,8,128]{2,1,0:T(8,128)(2,1)S(1)}, bf16[89,8,128]{2,1,0:T(8,128)(2,1)S(1)}, u32[]{:S(2)}, u32[]{:S(2)}) %collective-permute-start.29) | collective-permute-done | bytes 182304 | tf_op jit(solution)/shard_map/ppermute | solution.py:22
  136.6 3.0 %shard_map.81 = bf16[8,9,56,128]{3,2,1,0:T(8,128)(2,1)} custom-call(s32[17,56]{1,0:T(8,128)S(1)} %pad_add_fusion.table, bf16[89,8,128]{2,1,0:T(8,128)(2,1)S(1)} %get-tuple-element.87.refs_0_, bf16[89,8,128]{2,1,0:T(8,128)(2,1)S(1)} %collective-permute-done.28.refs_1_, bf16[89,8,128]{2,1,0:T(8,128)(2,1)S(1)} %collective-permute-done.29.refs_2_, ...), custom_call_target="tpu_custom_call" | custom-call | bytes 2000000 | tf_op jit(solution)/shard_map/pallas_call | solution.py:261
  (72 shorter events, 19.8 us)
Async XLA Ops:
  5.8 29.0 %copy-start.3 = (bf16[32,4096]{1,0:T(8,128)(2,1)S(1)}, bf16[32,4096]{1,0:T(8,128)(2,1)}, u32[]{:S(2)}) copy-start(bf16[32,4096]{1,0:T(8,128)(2,1)} %refs_0_.3) | copy-start | bytes 786436
  7.5 17.0 %collective-permute-start = (bf16[32,4096]{1,0:T(8,128)(2,1)}, bf16[32,4096]{1,0:T(8,128)(2,1)S(1)}, u32[]{:S(2)}, u32[]{:S(2)}) collective-permute-start(bf16[32,4096]{1,0:T(8,128)(2,1)} %refs_0_.2), channel_id=1, source_target_pairs={{0,8},{2,10},{4,12},{6,14},{8,0},{10,2},{12,4},{14,6},{16,24},{18,... | collective-permute-start | bytes 786440 | tf_op jit(solution)/shard_map/ppermute | solution.py:22
  10.6 13.9 %collective-permute-start.3 = (bf16[89,8,128]{2,1,0:T(8,128)(2,1)S(1)}, bf16[89,8,128]{2,1,0:T(8,128)(2,1)S(1)}, u32[]{:S(2)}, u32[]{:S(2)}) collective-permute-start(bf16[89,8,128]{2,1,0:T(8,128)(2,1)S(1)} %get-tuple-element.50), channel_id=1, source_target_pairs={{0,24},{2,26},{4,28},{6,30},{8,16},{10,18},{12,20},{14,22},{16,8},... | collective-permute-start | bytes 546824 | tf_op jit(solution)/shard_map/ppermute | solution.py:22
  13.0 16.1 %collective-permute-start.2 = (bf16[89,8,128]{2,1,0:T(8,128)(2,1)S(1)}, bf16[89,8,128]{2,1,0:T(8,128)(2,1)S(1)}, u32[]{:S(2)}, u32[]{:S(2)}) collective-permute-start(bf16[89,8,128]{2,1,0:T(8,128)(2,1)S(1)} %get-tuple-element.49), channel_id=1, source_target_pairs={{0,16},{2,18},{4,20},{6,22},{8,24},{10,26},{12,28},{14,30},{16,0},... | collective-permute-start | bytes 546824 | tf_op jit(solution)/shard_map/ppermute | solution.py:22
  13.1 16.0 %collective-permute-start.1 = (bf16[89,8,128]{2,1,0:T(8,128)(2,1)S(1)}, bf16[89,8,128]{2,1,0:T(8,128)(2,1)S(1)}, u32[]{:S(2)}, u32[]{:S(2)}) collective-permute-start(bf16[89,8,128]{2,1,0:T(8,128)(2,1)S(1)} %get-tuple-element.48), channel_id=1, source_target_pairs={{0,8},{2,10},{4,12},{6,14},{8,0},{10,2},{12,4},{14,6},{16,24},{18,... | collective-permute-start | bytes 546824 | tf_op jit(solution)/shard_map/ppermute | solution.py:22
  14.9 14.3 %collective-permute-start.4 = (bf16[32,4096]{1,0:T(8,128)(2,1)}, bf16[32,4096]{1,0:T(8,128)(2,1)S(1)}, u32[]{:S(2)}, u32[]{:S(2)}) collective-permute-start(bf16[32,4096]{1,0:T(8,128)(2,1)} %refs_0_.2), channel_id=1, source_target_pairs={{0,1},{1,0},{2,3},{3,2},{4,5},{5,4},{6,7},{7,6},{8,9},{9,8},{10,11... | collective-permute-start | bytes 786440 | tf_op jit(solution)/shard_map/ppermute | solution.py:22
  24.4 4.9 %collective-permute-start.6 = (bf16[32,4096]{1,0:T(8,128)(2,1)}, bf16[32,4096]{1,0:T(8,128)(2,1)S(1)}, u32[]{:S(2)}, u32[]{:S(2)}) collective-permute-start(bf16[32,4096]{1,0:T(8,128)(2,1)} %refs_0_.3), channel_id=1, source_target_pairs={{0,1},{1,0},{2,3},{3,2},{4,5},{5,4},{6,7},{7,6},{8,9},{9,8},{10,11... | collective-permute-start | bytes 786440 | tf_op jit(solution)/shard_map/ppermute | solution.py:22
  24.4 4.9 %collective-permute-start.5 = (bf16[32,4096]{1,0:T(8,128)(2,1)S(1)}, bf16[32,4096]{1,0:T(8,128)(2,1)S(1)}, u32[]{:S(2)}, u32[]{:S(2)}) collective-permute-start(bf16[32,4096]{1,0:T(8,128)(2,1)S(1)} %collective-permute-done.refs_1_), channel_id=1, source_target_pairs={{0,1},{1,0},{2,3},{3,2},{4,5},{5,4},{6,7},{7,6},{8,9},{9,8},{10,11... | collective-permute-start | bytes 786440 | tf_op jit(solution)/shard_map/ppermute | solution.py:22
  29.3 17.8 %collective-permute-start.10 = (bf16[4,89,8,128]{3,2,1,0:T(8,128)(2,1)S(1)}, bf16[4,89,8,128]{3,2,1,0:T(8,128)(2,1)S(1)}, u32[]{:S(2)}, u32[]{:S(2)}) collective-permute-start(bf16[4,89,8,128]{3,2,1,0:T(8,128)(2,1)S(1)} %pad_maximum_fusion.1.refs_0_), channel_id=1, source_target_pairs={{0,2},{2,0},{4,6},{6,4},{8,10},{10,8},{12,14},{14,12},{16,18},{18,... | collective-permute-start | bytes 2187272 | tf_op jit(solution)/shard_map/ppermute | solution.py:22
  30.9 17.1 %collective-permute-start.12 = (bf16[4,89,8,128]{3,2,1,0:T(8,128)(2,1)S(1)}, bf16[4,89,8,128]{3,2,1,0:T(8,128)(2,1)S(1)}, u32[]{:S(2)}, u32[]{:S(2)}) collective-permute-start(bf16[4,89,8,128]{3,2,1,0:T(8,128)(2,1)S(1)} %pad_maximum_fusion.1.refs_0_), channel_id=1, source_target_pairs={{0,4},{2,6},{4,0},{6,2},{8,12},{10,14},{12,8},{14,10},{16,20},{18,... | collective-permute-start | bytes 2187272 | tf_op jit(solution)/shard_map/ppermute | solution.py:22
  32.4 13.0 %collective-permute-start.7 = (bf16[32,4096]{1,0:T(8,128)(2,1)S(1)}, bf16[32,4096]{1,0:T(8,128)(2,1)S(1)}, u32[]{:S(2)}, u32[]{:S(2)}) collective-permute-start(bf16[32,4096]{1,0:T(8,128)(2,1)S(1)} %copy-done.2), channel_id=1, source_target_pairs={{0,16},{2,18},{4,20},{6,22},{8,24},{10,26},{12,28},{14,30},{16,0},... | collective-permute-start | bytes 786440 | tf_op jit(solution)/shard_map/ppermute | solution.py:22
  34.8 10.8 %collective-permute-start.8 = (bf16[32,4096]{1,0:T(8,128)(2,1)S(1)}, bf16[32,4096]{1,0:T(8,128)(2,1)S(1)}, u32[]{:S(2)}, u32[]{:S(2)}) collective-permute-start(bf16[32,4096]{1,0:T(8,128)(2,1)S(1)} %copy-done.3), channel_id=1, source_target_pairs={{0,8},{2,10},{4,12},{6,14},{8,0},{10,2},{12,4},{14,6},{16,24},{18,... | collective-permute-start | bytes 786440 | tf_op jit(solution)/shard_map/ppermute | solution.py:22
  45.6 9.6 %collective-permute-start.9 = (bf16[32,4096]{1,0:T(8,128)(2,1)S(1)}, bf16[32,4096]{1,0:T(8,128)(2,1)S(1)}, u32[]{:S(2)}, u32[]{:S(2)}) collective-permute-start(bf16[32,4096]{1,0:T(8,128)(2,1)S(1)} %collective-permute-done.7.refs_2_), channel_id=1, source_target_pairs={{0,8},{2,10},{4,12},{6,14},{8,0},{10,2},{12,4},{14,6},{16,24},{18,... | collective-permute-start | bytes 786440 | tf_op jit(solution)/shard_map/ppermute | solution.py:22
  47.1 14.7 %collective-permute-start.11 = (bf16[2,89,8,128]{3,2,1,0:T(8,128)(2,1)S(1)}, bf16[2,89,8,128]{3,2,1,0:T(8,128)(2,1)S(1)}, u32[]{:S(2)}, u32[]{:S(2)}) collective-permute-start(bf16[2,89,8,128]{3,2,1,0:T(8,128)(2,1)S(1)} %slice.135), channel_id=1, source_target_pairs={{0,4},{2,6},{4,0},{6,2},{8,12},{10,14},{12,8},{14,10},{16,20},{18,... | collective-permute-start | bytes 1093640 | tf_op jit(solution)/shard_map/ppermute | solution.py:22
  48.0 13.8 %collective-permute-start.13 = (bf16[2,89,8,128]{3,2,1,0:T(8,128)(2,1)S(1)}, bf16[2,89,8,128]{3,2,1,0:T(8,128)(2,1)S(1)}, u32[]{:S(2)}, u32[]{:S(2)}) collective-permute-start(bf16[2,89,8,128]{3,2,1,0:T(8,128)(2,1)S(1)} %slice.136), channel_id=1, source_target_pairs={{0,2},{2,0},{4,6},{6,4},{8,10},{10,8},{12,14},{14,12},{16,18},{18,... | collective-permute-start | bytes 1093640 | tf_op jit(solution)/shard_map/ppermute | solution.py:22
  49.5 12.3 %collective-permute-start.14 = (bf16[32,4096]{1,0:T(8,128)(2,1)S(1)}, bf16[32,4096]{1,0:T(8,128)(2,1)S(1)}, u32[]{:S(2)}, u32[]{:S(2)}) collective-permute-start(bf16[32,4096]{1,0:T(8,128)(2,1)S(1)} %copy-done.3), channel_id=1, source_target_pairs={{0,16},{2,18},{4,20},{6,22},{8,24},{10,26},{12,28},{14,30},{16,0},... | collective-permute-start | bytes 786440 | tf_op jit(solution)/shard_map/ppermute | solution.py:22
  61.8 1.9 %collective-permute-start.15 = (bf16[64,4096]{1,0:T(8,128)(2,1)S(1)}, bf16[64,4096]{1,0:T(8,128)(2,1)S(1)}, u32[]{:S(2)}, u32[]{:S(2)}) collective-permute-start(bf16[64,4096]{1,0:T(8,128)(2,1)S(1)} %pad_maximum_fusion.2), channel_id=1, source_target_pairs={{0,1},{1,0},{2,3},{3,2},{4,5},{5,4},{6,7},{7,6},{8,9},{9,8},{10,11... | collective-permute-start | bytes 1572872 | tf_op jit(solution)/shard_map/ppermute | solution.py:22
  61.8 8.7 %collective-permute-start.16 = (bf16[32,4096]{1,0:T(8,128)(2,1)S(1)}, bf16[32,4096]{1,0:T(8,128)(2,1)S(1)}, u32[]{:S(2)}, u32[]{:S(2)}) collective-permute-start(bf16[32,4096]{1,0:T(8,128)(2,1)S(1)} %collective-permute-done.14.refs_2_), channel_id=1, source_target_pairs={{0,8},{2,10},{4,12},{6,14},{8,0},{10,2},{12,4},{14,6},{16,24},{18,... | collective-permute-start | bytes 786440 | tf_op jit(solution)/shard_map/ppermute | solution.py:22
  70.5 2.7 %collective-permute-start.17 = (bf16[4,32,4096]{2,1,0:T(8,128)(2,1)S(1)}, bf16[4,32,4096]{2,1,0:T(8,128)(2,1)S(1)}, u32[]{:S(2)}, u32[]{:S(2)}) collective-permute-start(bf16[4,32,4096]{2,1,0:T(8,128)(2,1)S(1)} %get-tuple-element.61), channel_id=1, source_target_pairs={{0,1},{1,0},{2,3},{3,2},{4,5},{5,4},{6,7},{7,6},{8,9},{9,8},{10,11... | collective-permute-start | bytes 3145736 | tf_op jit(solution)/shard_map/ppermute | solution.py:22
  70.6 3.7 %collective-permute-start.20 = (bf16[96,4096]{1,0:T(8,128)(2,1)S(1)}, bf16[96,4096]{1,0:T(8,128)(2,1)S(1)}, u32[]{:S(2)}, u32[]{:S(2)}) collective-permute-start(bf16[96,4096]{1,0:T(8,128)(2,1)S(1)} %pad_maximum_fusion), channel_id=1, source_target_pairs={{0,1},{1,0},{2,3},{3,2},{4,5},{5,4},{6,7},{7,6},{8,9},{9,8},{10,11... | collective-permute-start | bytes 2359304 | tf_op jit(solution)/shard_map/ppermute | solution.py:22
  73.3 14.0 %collective-permute-start.18 = (bf16[2,32,4096]{2,1,0:T(8,128)(2,1)S(1)}, bf16[2,32,4096]{2,1,0:T(8,128)(2,1)S(1)}, u32[]{:S(2)}, u32[]{:S(2)}) collective-permute-start(bf16[2,32,4096]{2,1,0:T(8,128)(2,1)S(1)} %add_convert_fusion.1), channel_id=1, source_target_pairs={{0,8},{2,10},{4,12},{6,14},{8,0},{10,2},{12,4},{14,6},{16,24},{18,... | collective-permute-start | bytes 1572872 | tf_op jit(solution)/shard_map/ppermute | solution.py:22
  87.3 2.7 %collective-permute-start.21 = (bf16[4,32,4096]{2,1,0:T(8,128)(2,1)S(1)}, bf16[4,32,4096]{2,1,0:T(8,128)(2,1)S(1)}, u32[]{:S(2)}, u32[]{:S(2)}) collective-permute-start(bf16[4,32,4096]{2,1,0:T(8,128)(2,1)S(1)} %get-tuple-element.72), channel_id=1, source_target_pairs={{0,1},{1,0},{2,3},{3,2},{4,5},{5,4},{6,7},{7,6},{8,9},{9,8},{10,11... | collective-permute-start | bytes 3145736 | tf_op jit(solution)/shard_map/ppermute | solution.py:22
  87.3 10.9 %collective-permute-start.24 = (bf16[2,89,8,128]{3,2,1,0:T(8,128)(2,1)S(1)}, bf16[2,89,8,128]{3,2,1,0:T(8,128)(2,1)S(1)}, u32[]{:S(2)}, u32[]{:S(2)}) collective-permute-start(bf16[2,89,8,128]{3,2,1,0:T(8,128)(2,1)S(1)} %get-tuple-element.77), channel_id=1, source_target_pairs={{0,2},{2,0},{4,6},{6,4},{8,10},{10,8},{12,14},{14,12},{16,18},{18,... | collective-permute-start | bytes 1093640 | tf_op jit(solution)/shard_map/ppermute | solution.py:22
  87.9 10.6 %collective-permute-start.25 = (bf16[2,89,8,128]{3,2,1,0:T(8,128)(2,1)S(1)}, bf16[2,89,8,128]{3,2,1,0:T(8,128)(2,1)S(1)}, u32[]{:S(2)}, u32[]{:S(2)}) collective-permute-start(bf16[2,89,8,128]{3,2,1,0:T(8,128)(2,1)S(1)} %get-tuple-element.78), channel_id=1, source_target_pairs={{0,4},{2,6},{4,0},{6,2},{8,12},{10,14},{12,8},{14,10},{16,20},{18,... | collective-permute-start | bytes 1093640 | tf_op jit(solution)/shard_map/ppermute | solution.py:22
  90.1 19.6 %collective-permute-start.22 = (bf16[2,32,4096]{2,1,0:T(8,128)(2,1)S(1)}, bf16[2,32,4096]{2,1,0:T(8,128)(2,1)S(1)}, u32[]{:S(2)}, u32[]{:S(2)}) collective-permute-start(bf16[2,32,4096]{2,1,0:T(8,128)(2,1)S(1)} %add_convert_fusion), channel_id=1, source_target_pairs={{0,8},{2,10},{4,12},{6,14},{8,0},{10,2},{12,4},{14,6},{16,24},{18,... | collective-permute-start | bytes 1572872 | tf_op jit(solution)/shard_map/ppermute | solution.py:22
  91.2 18.6 %collective-permute-start.19 = (bf16[32,4096]{1,0:T(8,128)(2,1)S(1)}, bf16[32,4096]{1,0:T(8,128)(2,1)S(1)}, u32[]{:S(2)}, u32[]{:S(2)}) collective-permute-start(bf16[32,4096]{1,0:T(8,128)(2,1)S(1)} %fusion.2), channel_id=1, source_target_pairs={{0,16},{2,18},{4,20},{6,22},{8,24},{10,26},{12,28},{14,30},{16,0},... | collective-permute-start | bytes 786440 | tf_op jit(solution)/shard_map/ppermute | solution.py:22
  99.4 17.8 %collective-permute-start.27 = (bf16[4,89,8,128]{3,2,1,0:T(8,128)(2,1)S(1)}, bf16[4,89,8,128]{3,2,1,0:T(8,128)(2,1)S(1)}, u32[]{:S(2)}, u32[]{:S(2)}) collective-permute-start(bf16[4,89,8,128]{3,2,1,0:T(8,128)(2,1)S(1)} %get-tuple-element.82), channel_id=1, source_target_pairs={{0,4},{2,6},{4,0},{6,2},{8,12},{10,14},{12,8},{14,10},{16,20},{18,... | collective-permute-start | bytes 2187272 | tf_op jit(solution)/shard_map/ppermute | solution.py:22
  100.6 17.3 %collective-permute-start.26 = (bf16[4,89,8,128]{3,2,1,0:T(8,128)(2,1)S(1)}, bf16[4,89,8,128]{3,2,1,0:T(8,128)(2,1)S(1)}, u32[]{:S(2)}, u32[]{:S(2)}) collective-permute-start(bf16[4,89,8,128]{3,2,1,0:T(8,128)(2,1)S(1)} %get-tuple-element.81), channel_id=1, source_target_pairs={{0,2},{2,0},{4,6},{6,4},{8,10},{10,8},{12,14},{14,12},{16,18},{18,... | collective-permute-start | bytes 2187272 | tf_op jit(solution)/shard_map/ppermute | solution.py:22
  109.9 22.8 %collective-permute-start.23 = (bf16[32,4096]{1,0:T(8,128)(2,1)S(1)}, bf16[32,4096]{1,0:T(8,128)(2,1)S(1)}, u32[]{:S(2)}, u32[]{:S(2)}) collective-permute-start(bf16[32,4096]{1,0:T(8,128)(2,1)S(1)} %fusion.3), channel_id=1, source_target_pairs={{0,16},{2,18},{4,20},{6,22},{8,24},{10,26},{12,28},{14,30},{16,0},... | collective-permute-start | bytes 786440 | tf_op jit(solution)/shard_map/ppermute | solution.py:22
  118.3 15.2 %collective-permute-start.28 = (bf16[89,8,128]{2,1,0:T(8,128)(2,1)S(1)}, bf16[89,8,128]{2,1,0:T(8,128)(2,1)S(1)}, u32[]{:S(2)}, u32[]{:S(2)}) collective-permute-start(bf16[89,8,128]{2,1,0:T(8,128)(2,1)S(1)} %get-tuple-element.84), channel_id=1, source_target_pairs={{0,8},{2,10},{4,12},{6,14},{8,0},{10,2},{12,4},{14,6},{16,24},{18,... | collective-permute-start | bytes 546824 | tf_op jit(solution)/shard_map/ppermute | solution.py:22
  119.3 17.3 %collective-permute-start.29 = (bf16[89,8,128]{2,1,0:T(8,128)(2,1)S(1)}, bf16[89,8,128]{2,1,0:T(8,128)(2,1)S(1)}, u32[]{:S(2)}, u32[]{:S(2)}) collective-permute-start(bf16[89,8,128]{2,1,0:T(8,128)(2,1)S(1)} %get-tuple-element.85), channel_id=1, source_target_pairs={{0,16},{2,18},{4,20},{6,22},{8,24},{10,26},{12,28},{14,30},{16,0},... | collective-permute-start | bytes 546824 | tf_op jit(solution)/shard_map/ppermute | solution.py:22
  120.8 15.8 %collective-permute-start.30 = (bf16[89,8,128]{2,1,0:T(8,128)(2,1)S(1)}, bf16[89,8,128]{2,1,0:T(8,128)(2,1)S(1)}, u32[]{:S(2)}, u32[]{:S(2)}) collective-permute-start(bf16[89,8,128]{2,1,0:T(8,128)(2,1)S(1)} %get-tuple-element.86), channel_id=1, source_target_pairs={{0,24},{2,26},{4,28},{6,30},{8,16},{10,18},{12,20},{14,22},{16,8},... | collective-permute-start | bytes 546824 | tf_op jit(solution)/shard_map/ppermute | solution.py:22
  (3 other events, 33.4 us)

commit v12 on v9

--- a/solution.py
+++ b/solution.py
@@ -289,9 +289,6 @@
     shape = jax.ShapeDtypeStruct
 
     x_items, g_items = {0: tokens}, {0: out_grad}
-    if far > 1:
-        x_items[near] = swap(tokens, "dp", near)
-
     capacity = (terms * blocks_dev - 3 * blocks_dev + 3 * (slot_count - 1) * (far - 1)) // far
     slots = capacity + 1
     block_ids = jnp.arange(blocks_dev, dtype=jnp.int32)
@@ -341,11 +338,10 @@
     staged = tensor_size == 2 and far == 4 and near == 4
     received = [swap(packed[at], "dp", at * near) for at in reversed(range(1, far))][::-1]
     held = jnp.stack([packed[0], *received])
-    x_core, g_core = {}, {}
     if staged:
-        x_core = {at: swap(x_items[at], "tensor", 1) for at in (0, near)}
-        g_core = {0: swap(out_grad, "tensor", 1)}
-        held = after(held, *x_core.values(), *g_core.values())
+        x_items[near] = swap(after(tokens, received[0]), "dp", near)
+        x_core, g_core = swap(tokens, "tensor", 1), swap(out_grad, "tensor", 1)
+        held = after(held, x_core, g_core, x_items[near])
 
     half = far // 2
     split = near == 4 and far % 2 == 0
@@ -364,11 +360,13 @@
         x_source, g_source = after((tokens, out_grad), held)
         x_items[2 * near] = swap(x_source, "dp", 2 * near)
         g_items[near] = swap(g_source, "dp", near)
-        x_source, g_source = after((x_items[2 * near], out_grad), x_items[2 * near], g_items[near])
+        x_source, g_source = after(
+            (x_items[2 * near], out_grad), x_items[2 * near], x_items[near], g_items[near]
+        )
         x_items[3 * near] = swap(x_source, "dp", near)
         g_items[2 * near] = swap(g_source, "dp", 2 * near)
         g_items[3 * near] = swap(g_items[2 * near], "dp", near)
-        x_late = jnp.concatenate([x_items[2 * near], x_items[3 * near]])
+        x_late = jnp.concatenate([x_items[at * near] for at in range(1, far)])
         x_late = swap(after(x_late, *weight_list[3:], g_items[2 * near]), "tensor", 1)
         g_late = jnp.concatenate([g_items[at * near] for at in range(1, far)])
         g_late = swap(g_late, "tensor", 1)
@@ -379,8 +377,8 @@
     far_order = [at * near for at in range(0, far, 2)] + [at * near for at in range(1, far, 2)]
     if staged:
         order = [at * near for at in range(far)]
-        x_list = [x_items[at] for at in order] + [x_core[at] for at in order[:2]] + [x_late]
-        g_list = [g_items[at] for at in order] + [g_core[0], g_late]
+        x_list = [x_items[at] for at in order] + [x_core, x_late]
+        g_list = [g_items[at] for at in order] + [g_core, g_late]
         parts = [(other, far_order.index(at)) for other in (False, True) for at in order]
         other_parts = [(at, 1) for at in far_order]
     else:

time: 139 us -> 140 us (level); the launches traced: 139 us -> 138 us
    ppermute x31 -> x30, waiting for transfers between devices: 74.5 us -> 74 us  [swap(): return lax.ppermute(value, axis, [(at, at ^ stride) for at in range(size)])]
    ppermute x31 -> x30, starting transfers between devices: 32.7 us -> 32.2 us  [swap(): return lax.ppermute(value, axis, [(at, at ^ stride) for at in range(size)])]
  transfers between devices with their start and end apart: 31 -> 30, of which waited for: 17 -> 20; matrix products, arithmetic and copies ran while one was open for 5% -> 2% of each run, Pallas kernels for 15% -> 13%
where the time goes in v12:
time: 140 us; the launch traced here: 138 us
  waiting for transfers between devices  74 us (53%)
  starting transfers between devices  32.2 us (23%)
  Pallas kernels  23.1 us (16%)
  other arithmetic  4.88 us (3%)
  local copies, waits for them, and re-layouts  2.87 us (2%)
    ppermute x30, waiting for transfers between devices, swap(): return lax.ppermute(value, axis, [(at, at ^ stride) for at in range(size)])  74 us
    ppermute x30, starting transfers between devices, swap(): return lax.ppermute(value, axis, [(at, at ^ stride) for at in range(size)])  32.2 us
    pallas_call x6, Pallas kernels, call(): pl.pallas_call(kernel, grid_spec=pltpu.PrefetchScalarGridSpec(num_scalar_...  23.1 us
  transfers between devices with their start and end apart: 30, of which 20 were waited for; matrix products, arithmetic and copies ran while one was open for 2% of the time, Pallas kernels for 13%

profile of v12, /device:TPU:0, one launch (start us, length us, event | category | flops | bytes accessed | tf_op | source)
XLA Modules:
  0.0 138.1 jit_solution(8173242222811143951)
XLA Ops:
  4.6 1.2 copy-done.1
  5.8 1.6 %shard_map.76 = (bf16[89,8,128]{2,1,0:T(8,128)(2,1)S(1)}, bf16[89,8,128]{2,1,0:T(8,128)(2,1)S(1)}, bf16[89,8,128]{2,1,0:T(8,128)(2,1)S(1)}, bf16[89,8,128]{2,1,0:T(8,128)(2,1)S(1)}) custom-call(s32[17,56]{1,0:T(8,128)S(1)} %pad_add_fusion.table, bf16[8,9,56,128]{3,2,1,0:T(8,128)(2,1)S(1)} %bitcast.36), custom_call_target="tpu_custom_call" | custom-call | bytes 1000000 | tf_op jit(solution)/shard_map/pallas_call | solution.py:261
  7.5 3.1 %collective-permute-start = (bf16[89,8,128]{2,1,0:T(8,128)(2,1)S(1)}, bf16[89,8,128]{2,1,0:T(8,128)(2,1)S(1)}, u32[]{:S(2)}, u32[]{:S(2)}) collective-permute-start(bf16[89,8,128]{2,1,0:T(8,128)(2,1)S(1)} %get-tuple-element.46), channel_id=1, source_target_pairs={{0,8},{2,10},{4,12},{6,14},{8,0},{10,2},{12,4},{14,6},{16,24},{18,... | collective-permute-start | bytes 546824 | tf_op jit(solution)/shard_map/ppermute | solution.py:22
  10.6 2.5 %collective-permute-start.3 = (bf16[89,8,128]{2,1,0:T(8,128)(2,1)S(1)}, bf16[89,8,128]{2,1,0:T(8,128)(2,1)S(1)}, u32[]{:S(2)}, u32[]{:S(2)}) collective-permute-start(bf16[89,8,128]{2,1,0:T(8,128)(2,1)S(1)} %get-tuple-element.50), channel_id=1, source_target_pairs={{0,24},{2,26},{4,28},{6,30},{8,16},{10,18},{12,20},{14,22},{16,8},... | collective-permute-start | bytes 546824 | tf_op jit(solution)/shard_map/ppermute | solution.py:22
  13.7 1.9 %collective-permute-done = bf16[89,8,128]{2,1,0:T(8,128)(2,1)S(1)} collective-permute-done((bf16[89,8,128]{2,1,0:T(8,128)(2,1)S(1)}, bf16[89,8,128]{2,1,0:T(8,128)(2,1)S(1)}, u32[]{:S(2)}, u32[]{:S(2)}) %collective-permute-start) | collective-permute-done | bytes 182304 | tf_op jit(solution)/shard_map/ppermute | solution.py:22
  15.6 2.5 %collective-permute-start.1 = (bf16[32,4096]{1,0:T(8,128)(2,1)}, bf16[32,4096]{1,0:T(8,128)(2,1)S(1)}, u32[]{:S(2)}, u32[]{:S(2)}) collective-permute-start(bf16[32,4096]{1,0:T(8,128)(2,1)} %refs_0_.2), channel_id=1, source_target_pairs={{0,8},{2,10},{4,12},{6,14},{8,0},{10,2},{12,4},{14,6},{16,24},{18,... | collective-permute-start | bytes 786440 | tf_op jit(solution)/shard_map/ppermute | solution.py:22
  18.0 4.5 %collective-permute-done.3 = bf16[89,8,128]{2,1,0:T(8,128)(2,1)S(1)} collective-permute-done((bf16[89,8,128]{2,1,0:T(8,128)(2,1)S(1)}, bf16[89,8,128]{2,1,0:T(8,128)(2,1)S(1)}, u32[]{:S(2)}, u32[]{:S(2)}) %collective-permute-start.3) | collective-permute-done | bytes 182304 | tf_op jit(solution)/shard_map/ppermute | solution.py:22
  22.5 6.8 %collective-permute-done.2 = bf16[89,8,128]{2,1,0:T(8,128)(2,1)S(1)} collective-permute-done((bf16[89,8,128]{2,1,0:T(8,128)(2,1)S(1)}, bf16[89,8,128]{2,1,0:T(8,128)(2,1)S(1)}, u32[]{:S(2)}, u32[]{:S(2)}) %collective-permute-start.2) | collective-permute-done | bytes 182304 | tf_op jit(solution)/shard_map/ppermute | solution.py:22
  29.9 1.5 %collective-permute-start.9 = (bf16[4,89,8,128]{3,2,1,0:T(8,128)(2,1)S(1)}, bf16[4,89,8,128]{3,2,1,0:T(8,128)(2,1)S(1)}, u32[]{:S(2)}, u32[]{:S(2)}) collective-permute-start(bf16[4,89,8,128]{3,2,1,0:T(8,128)(2,1)S(1)} %pad_maximum_fusion.2.refs_0_), channel_id=1, source_target_pairs={{0,2},{2,0},{4,6},{6,4},{8,10},{10,8},{12,14},{14,12},{16,18},{18,... | collective-permute-start | bytes 2187272 | tf_op jit(solution)/shard_map/ppermute | solution.py:22
  31.4 1.5 %collective-permute-start.11 = (bf16[4,89,8,128]{3,2,1,0:T(8,128)(2,1)S(1)}, bf16[4,89,8,128]{3,2,1,0:T(8,128)(2,1)S(1)}, u32[]{:S(2)}, u32[]{:S(2)}) collective-permute-start(bf16[4,89,8,128]{3,2,1,0:T(8,128)(2,1)S(1)} %pad_maximum_fusion.2.refs_0_), channel_id=1, source_target_pairs={{0,4},{2,6},{4,0},{6,2},{8,12},{10,14},{12,8},{14,10},{16,20},{18,... | collective-permute-start | bytes 2187272 | tf_op jit(solution)/shard_map/ppermute | solution.py:22
  32.9 1.5 %collective-permute-start.6 = (bf16[32,4096]{1,0:T(8,128)(2,1)S(1)}, bf16[32,4096]{1,0:T(8,128)(2,1)S(1)}, u32[]{:S(2)}, u32[]{:S(2)}) collective-permute-start(bf16[32,4096]{1,0:T(8,128)(2,1)S(1)} %copy-done.2), channel_id=1, source_target_pairs={{0,16},{2,18},{4,20},{6,22},{8,24},{10,26},{12,28},{14,30},{16,0},... | collective-permute-start | bytes 786440 | tf_op jit(solution)/shard_map/ppermute | solution.py:22
  34.4 1.6 %collective-permute-start.7 = (bf16[32,4096]{1,0:T(8,128)(2,1)S(1)}, bf16[32,4096]{1,0:T(8,128)(2,1)S(1)}, u32[]{:S(2)}, u32[]{:S(2)}) collective-permute-start(bf16[32,4096]{1,0:T(8,128)(2,1)S(1)} %copy-done.3), channel_id=1, source_target_pairs={{0,8},{2,10},{4,12},{6,14},{8,0},{10,2},{12,4},{14,6},{16,24},{18,... | collective-permute-start | bytes 786440 | tf_op jit(solution)/shard_map/ppermute | solution.py:22
  36.0 10.1 %collective-permute-done.6.refs_2_ = bf16[32,4096]{1,0:T(8,128)(2,1)S(1)} collective-permute-done((bf16[32,4096]{1,0:T(8,128)(2,1)S(1)}, bf16[32,4096]{1,0:T(8,128)(2,1)S(1)}, u32[]{:S(2)}, u32[]{:S(2)}) %collective-permute-start.6) | collective-permute-done | bytes 262176 | tf_op jit(solution)/shard_map/ppermute | solution.py:22
  46.7 1.8 %collective-permute-start.13 = (bf16[32,4096]{1,0:T(8,128)(2,1)S(1)}, bf16[32,4096]{1,0:T(8,128)(2,1)S(1)}, u32[]{:S(2)}, u32[]{:S(2)}) collective-permute-start(bf16[32,4096]{1,0:T(8,128)(2,1)S(1)} %copy-done.3), channel_id=1, source_target_pairs={{0,16},{2,18},{4,20},{6,22},{8,24},{10,26},{12,28},{14,30},{16,0},... | collective-permute-start | bytes 786440 | tf_op jit(solution)/shard_map/ppermute | solution.py:22
  49.4 1.6 %collective-permute-start.12 = (bf16[2,89,8,128]{3,2,1,0:T(8,128)(2,1)S(1)}, bf16[2,89,8,128]{3,2,1,0:T(8,128)(2,1)S(1)}, u32[]{:S(2)}, u32[]{:S(2)}) collective-permute-start(bf16[2,89,8,128]{3,2,1,0:T(8,128)(2,1)S(1)} %slice.136), channel_id=1, source_target_pairs={{0,2},{2,0},{4,6},{6,4},{8,10},{10,8},{12,14},{14,12},{16,18},{18,... | collective-permute-start | bytes 1093640 | tf_op jit(solution)/shard_map/ppermute | solution.py:22
  50.9 7.7 %collective-permute-done.8.refs_3_ = bf16[32,4096]{1,0:T(8,128)(2,1)S(1)} collective-permute-done((bf16[32,4096]{1,0:T(8,128)(2,1)S(1)}, bf16[32,4096]{1,0:T(8,128)(2,1)S(1)}, u32[]{:S(2)}, u32[]{:S(2)}) %collective-permute-start.8) | collective-permute-done | bytes 262176 | tf_op jit(solution)/shard_map/ppermute | solution.py:22
  58.7 2.1 %collective-permute-done.13.refs_2_ = bf16[32,4096]{1,0:T(8,128)(2,1)S(1)} collective-permute-done((bf16[32,4096]{1,0:T(8,128)(2,1)S(1)}, bf16[32,4096]{1,0:T(8,128)(2,1)S(1)}, u32[]{:S(2)}, u32[]{:S(2)}) %collective-permute-start.13) | collective-permute-done | bytes 262176 | tf_op jit(solution)/shard_map/ppermute | solution.py:22
  60.9 1.8 %shard_map.77.refs_6_ = bf16[89,128,128]{2,1,0:T(8,128)(2,1)S(1)} custom-call(s32[17,56]{1,0:T(8,128)S(1)} %pad_add_fusion.table, bf16[4,89,8,128]{3,2,1,0:T(8,128)(2,1)S(1)} %pad_maximum_fusion.2.refs_0_, bf16[4,89,8,128]{3,2,1,0:T(8,128)(2,1)S(1)} %collective-permute-done.9.refs_1_, bf16[4,89,8,128]{3,2,1,0:T(8,128)(2,1)S(1)} %collective-permute-done.11.refs_2_, ...), custom_call_target="tpu_custom_call" | custom-call | bytes 10000000 | tf_op jit(solution)/shard_map/pallas_call | solution.py:261
  63.1 5.6 %shard_map.78 = (bf16[4096,256]{1,0:T(8,128)(2,1)S(1)}, f32[14,256,128]{2,1,0:T(8,128)S(1)}, f32[14,256,128]{2,1,0:T(8,128)S(1)}, bf16[14,128,256]{2,1,0:T(8,128...) custom-call(s32[17,56]{1,0:T(8,128)S(1)} %pad_add_fusion.table, ...), custom_call_target="tpu_custom_call" | custom-call | bytes 30000000 | tf_op jit(solution)/shard_map/pallas_call | solution.py:261
  70.2 2.0 %collective-permute-done.16 = bf16[4,32,4096]{2,1,0:T(8,128)(2,1)S(1)} collective-permute-done((bf16[4,32,4096]{2,1,0:T(8,128)(2,1)S(1)}, bf16[4,32,4096]{2,1,0:T(8,128)(2,1)S(1)}, u32[]{:S(2)}, u32[]{:S(2)}) %collective-permute-start.16) | collective-permute-done | bytes 1048608 | tf_op jit(solution)/shard_map/ppermute | solution.py:22
  73.3 10.2 %shard_map.79 = (bf16[4,32,4096]{2,1,0:T(8,128)(2,1)S(1)}, bf16[4,32,4096]{2,1,0:T(8,128)(2,1)S(1)}, bf16[4,89,8,128]{3,2,1,0:T(8,128)(2,1)S(1)}, bf16[4,89,8,12...) custom-call(s32[17,56]{1,0:T(8,128)S(1)} %pad_add_fusion.table, ...), custom_call_target="tpu_custom_call" | custom-call | bytes 40000000 | tf_op jit(solution)/shard_map/pallas_call | solution.py:261
  83.5 2.8 %collective-permute-done.17 = bf16[2,32,4096]{2,1,0:T(8,128)(2,1)S(1)} collective-permute-done((bf16[2,32,4096]{2,1,0:T(8,128)(2,1)S(1)}, bf16[2,32,4096]{2,1,0:T(8,128)(2,1)S(1)}, u32[]{:S(2)}, u32[]{:S(2)}) %collective-permute-start.17) | collective-permute-done | bytes 524320 | tf_op jit(solution)/shard_map/ppermute | solution.py:22
  87.4 1.6 %collective-permute-done.20 = bf16[4,32,4096]{2,1,0:T(8,128)(2,1)S(1)} collective-permute-done((bf16[4,32,4096]{2,1,0:T(8,128)(2,1)S(1)}, bf16[4,32,4096]{2,1,0:T(8,128)(2,1)S(1)}, u32[]{:S(2)}, u32[]{:S(2)}) %collective-permute-start.20) | collective-permute-done | bytes 1048608 | tf_op jit(solution)/shard_map/ppermute | solution.py:22
  91.4 5.9 %collective-permute-done.23.got_1 = bf16[2,89,8,128]{3,2,1,0:T(8,128)(2,1)S(1)} collective-permute-done((bf16[2,89,8,128]{3,2,1,0:T(8,128)(2,1)S(1)}, bf16[2,89,8,128]{3,2,1,0:T(8,128)(2,1)S(1)}, u32[]{:S(2)}, u32[]{:S(2)}) %collective-permute-start.23) | collective-permute-done | bytes 364576 | tf_op jit(solution)/shard_map/ppermute | solution.py:22
  99.0 1.5 %collective-permute-start.25 = (bf16[4,89,8,128]{3,2,1,0:T(8,128)(2,1)S(1)}, bf16[4,89,8,128]{3,2,1,0:T(8,128)(2,1)S(1)}, u32[]{:S(2)}, u32[]{:S(2)}) collective-permute-start(bf16[4,89,8,128]{3,2,1,0:T(8,128)(2,1)S(1)} %get-tuple-element.79), channel_id=1, source_target_pairs={{0,2},{2,0},{4,6},{6,4},{8,10},{10,8},{12,14},{14,12},{16,18},{18,... | collective-permute-start | bytes 2187272 | tf_op jit(solution)/shard_map/ppermute | solution.py:22
  100.5 8.3 %collective-permute-done.21 = bf16[2,32,4096]{2,1,0:T(8,128)(2,1)S(1)} collective-permute-done((bf16[2,32,4096]{2,1,0:T(8,128)(2,1)S(1)}, bf16[2,32,4096]{2,1,0:T(8,128)(2,1)S(1)}, u32[]{:S(2)}, u32[]{:S(2)}) %collective-permute-start.21) | collective-permute-done | bytes 524320 | tf_op jit(solution)/shard_map/ppermute | solution.py:22
  108.9 1.7 %collective-permute-start.22 = (bf16[32,4096]{1,0:T(8,128)(2,1)S(1)}, bf16[32,4096]{1,0:T(8,128)(2,1)S(1)}, u32[]{:S(2)}, u32[]{:S(2)}) collective-permute-start(bf16[32,4096]{1,0:T(8,128)(2,1)S(1)} %fusion.3), channel_id=1, source_target_pairs={{0,16},{2,18},{4,20},{6,22},{8,24},{10,26},{12,28},{14,30},{16,0},... | collective-permute-start | bytes 786440 | tf_op jit(solution)/shard_map/ppermute | solution.py:22
  111.4 4.8 %collective-permute-done.26 = bf16[4,89,8,128]{3,2,1,0:T(8,128)(2,1)S(1)} collective-permute-done((bf16[4,89,8,128]{3,2,1,0:T(8,128)(2,1)S(1)}, bf16[4,89,8,128]{3,2,1,0:T(8,128)(2,1)S(1)}, u32[]{:S(2)}, u32[]{:S(2)}) %collective-permute-start.26) | collective-permute-done | bytes 729120 | tf_op jit(solution)/shard_map/ppermute | solution.py:22
  118.8 2.4 %collective-permute-start.29 = (bf16[89,8,128]{2,1,0:T(8,128)(2,1)S(1)}, bf16[89,8,128]{2,1,0:T(8,128)(2,1)S(1)}, u32[]{:S(2)}, u32[]{:S(2)}) collective-permute-start(bf16[89,8,128]{2,1,0:T(8,128)(2,1)S(1)} %get-tuple-element.84), channel_id=1, source_target_pairs={{0,24},{2,26},{4,28},{6,30},{8,16},{10,18},{12,20},{14,22},{16,8},... | collective-permute-start | bytes 546824 | tf_op jit(solution)/shard_map/ppermute | solution.py:22
  121.2 10.0 %collective-permute-done.22 = bf16[32,4096]{1,0:T(8,128)(2,1)S(1)} collective-permute-done((bf16[32,4096]{1,0:T(8,128)(2,1)S(1)}, bf16[32,4096]{1,0:T(8,128)(2,1)S(1)}, u32[]{:S(2)}, u32[]{:S(2)}) %collective-permute-start.22) | collective-permute-done | bytes 262176 | tf_op jit(solution)/shard_map/ppermute | solution.py:22
  132.0 3.1 %collective-permute-done.28.refs_2_ = bf16[89,8,128]{2,1,0:T(8,128)(2,1)S(1)} collective-permute-done((bf16[89,8,128]{2,1,0:T(8,128)(2,1)S(1)}, bf16[89,8,128]{2,1,0:T(8,128)(2,1)S(1)}, u32[]{:S(2)}, u32[]{:S(2)}) %collective-permute-start.28) | collective-permute-done | bytes 182304 | tf_op jit(solution)/shard_map/ppermute | solution.py:22
  135.1 3.0 %shard_map.81 = bf16[8,9,56,128]{3,2,1,0:T(8,128)(2,1)} custom-call(s32[17,56]{1,0:T(8,128)S(1)} %pad_add_fusion.table, bf16[89,8,128]{2,1,0:T(8,128)(2,1)S(1)} %get-tuple-element.85.refs_0_, bf16[89,8,128]{2,1,0:T(8,128)(2,1)S(1)} %collective-permute-done.27.refs_1_, bf16[89,8,128]{2,1,0:T(8,128)(2,1)S(1)} %collective-permute-done.28.refs_2_, ...), custom_call_target="tpu_custom_call" | custom-call | bytes 2000000 | tf_op jit(solution)/shard_map/pallas_call | solution.py:261
  (70 shorter events, 19.3 us)
Async XLA Ops:
  5.8 27.1 %copy-start.2 = (bf16[32,4096]{1,0:T(8,128)(2,1)S(1)}, bf16[32,4096]{1,0:T(8,128)(2,1)}, u32[]{:S(2)}) copy-start(bf16[32,4096]{1,0:T(8,128)(2,1)} %refs_0_.2) | copy-start | bytes 786436
  5.8 28.6 %copy-start.3 = (bf16[32,4096]{1,0:T(8,128)(2,1)S(1)}, bf16[32,4096]{1,0:T(8,128)(2,1)}, u32[]{:S(2)}) copy-start(bf16[32,4096]{1,0:T(8,128)(2,1)} %refs_0_.3) | copy-start | bytes 786436
  7.5 8.1 %collective-permute-start = (bf16[89,8,128]{2,1,0:T(8,128)(2,1)S(1)}, bf16[89,8,128]{2,1,0:T(8,128)(2,1)S(1)}, u32[]{:S(2)}, u32[]{:S(2)}) collective-permute-start(bf16[89,8,128]{2,1,0:T(8,128)(2,1)S(1)} %get-tuple-element.46), channel_id=1, source_target_pairs={{0,8},{2,10},{4,12},{6,14},{8,0},{10,2},{12,4},{14,6},{16,24},{18,... | collective-permute-start | bytes 546824 | tf_op jit(solution)/shard_map/ppermute | solution.py:22
  10.6 11.9 %collective-permute-start.3 = (bf16[89,8,128]{2,1,0:T(8,128)(2,1)S(1)}, bf16[89,8,128]{2,1,0:T(8,128)(2,1)S(1)}, u32[]{:S(2)}, u32[]{:S(2)}) collective-permute-start(bf16[89,8,128]{2,1,0:T(8,128)(2,1)S(1)} %get-tuple-element.50), channel_id=1, source_target_pairs={{0,24},{2,26},{4,28},{6,30},{8,16},{10,18},{12,20},{14,22},{16,8},... | collective-permute-start | bytes 546824 | tf_op jit(solution)/shard_map/ppermute | solution.py:22
  13.0 16.3 %collective-permute-start.2 = (bf16[89,8,128]{2,1,0:T(8,128)(2,1)S(1)}, bf16[89,8,128]{2,1,0:T(8,128)(2,1)S(1)}, u32[]{:S(2)}, u32[]{:S(2)}) collective-permute-start(bf16[89,8,128]{2,1,0:T(8,128)(2,1)S(1)} %get-tuple-element.49), channel_id=1, source_target_pairs={{0,16},{2,18},{4,20},{6,22},{8,24},{10,26},{12,28},{14,30},{16,0},... | collective-permute-start | bytes 546824 | tf_op jit(solution)/shard_map/ppermute | solution.py:22
  13.1 16.2 %collective-permute-start.4 = (bf16[32,4096]{1,0:T(8,128)(2,1)}, bf16[32,4096]{1,0:T(8,128)(2,1)S(1)}, u32[]{:S(2)}, u32[]{:S(2)}) collective-permute-start(bf16[32,4096]{1,0:T(8,128)(2,1)} %refs_0_.2), channel_id=1, source_target_pairs={{0,1},{1,0},{2,3},{3,2},{4,5},{5,4},{6,7},{7,6},{8,9},{9,8},{10,11... | collective-permute-start | bytes 786440 | tf_op jit(solution)/shard_map/ppermute | solution.py:22
  13.1 16.2 %collective-permute-start.5 = (bf16[32,4096]{1,0:T(8,128)(2,1)}, bf16[32,4096]{1,0:T(8,128)(2,1)S(1)}, u32[]{:S(2)}, u32[]{:S(2)}) collective-permute-start(bf16[32,4096]{1,0:T(8,128)(2,1)} %refs_0_.3), channel_id=1, source_target_pairs={{0,1},{1,0},{2,3},{3,2},{4,5},{5,4},{6,7},{7,6},{8,9},{9,8},{10,11... | collective-permute-start | bytes 786440 | tf_op jit(solution)/shard_map/ppermute | solution.py:22
  15.6 14.4 %collective-permute-start.1 = (bf16[32,4096]{1,0:T(8,128)(2,1)}, bf16[32,4096]{1,0:T(8,128)(2,1)S(1)}, u32[]{:S(2)}, u32[]{:S(2)}) collective-permute-start(bf16[32,4096]{1,0:T(8,128)(2,1)} %refs_0_.2), channel_id=1, source_target_pairs={{0,8},{2,10},{4,12},{6,14},{8,0},{10,2},{12,4},{14,6},{16,24},{18,... | collective-permute-start | bytes 786440 | tf_op jit(solution)/shard_map/ppermute | solution.py:22
  29.9 18.5 %collective-permute-start.9 = (bf16[4,89,8,128]{3,2,1,0:T(8,128)(2,1)S(1)}, bf16[4,89,8,128]{3,2,1,0:T(8,128)(2,1)S(1)}, u32[]{:S(2)}, u32[]{:S(2)}) collective-permute-start(bf16[4,89,8,128]{3,2,1,0:T(8,128)(2,1)S(1)} %pad_maximum_fusion.2.refs_0_), channel_id=1, source_target_pairs={{0,2},{2,0},{4,6},{6,4},{8,10},{10,8},{12,14},{14,12},{16,18},{18,... | collective-permute-start | bytes 2187272 | tf_op jit(solution)/shard_map/ppermute | solution.py:22
  31.4 17.9 %collective-permute-start.11 = (bf16[4,89,8,128]{3,2,1,0:T(8,128)(2,1)S(1)}, bf16[4,89,8,128]{3,2,1,0:T(8,128)(2,1)S(1)}, u32[]{:S(2)}, u32[]{:S(2)}) collective-permute-start(bf16[4,89,8,128]{3,2,1,0:T(8,128)(2,1)S(1)} %pad_maximum_fusion.2.refs_0_), channel_id=1, source_target_pairs={{0,4},{2,6},{4,0},{6,2},{8,12},{10,14},{12,8},{14,10},{16,20},{18,... | collective-permute-start | bytes 2187272 | tf_op jit(solution)/shard_map/ppermute | solution.py:22
  32.9 13.1 %collective-permute-start.6 = (bf16[32,4096]{1,0:T(8,128)(2,1)S(1)}, bf16[32,4096]{1,0:T(8,128)(2,1)S(1)}, u32[]{:S(2)}, u32[]{:S(2)}) collective-permute-start(bf16[32,4096]{1,0:T(8,128)(2,1)S(1)} %copy-done.2), channel_id=1, source_target_pairs={{0,16},{2,18},{4,20},{6,22},{8,24},{10,26},{12,28},{14,30},{16,0},... | collective-permute-start | bytes 786440 | tf_op jit(solution)/shard_map/ppermute | solution.py:22
  34.4 12.0 %collective-permute-start.7 = (bf16[32,4096]{1,0:T(8,128)(2,1)S(1)}, bf16[32,4096]{1,0:T(8,128)(2,1)S(1)}, u32[]{:S(2)}, u32[]{:S(2)}) collective-permute-start(bf16[32,4096]{1,0:T(8,128)(2,1)S(1)} %copy-done.3), channel_id=1, source_target_pairs={{0,8},{2,10},{4,12},{6,14},{8,0},{10,2},{12,4},{14,6},{16,24},{18,... | collective-permute-start | bytes 786440 | tf_op jit(solution)/shard_map/ppermute | solution.py:22
  46.3 12.3 %collective-permute-start.8 = (bf16[32,4096]{1,0:T(8,128)(2,1)S(1)}, bf16[32,4096]{1,0:T(8,128)(2,1)S(1)}, u32[]{:S(2)}, u32[]{:S(2)}) collective-permute-start(bf16[32,4096]{1,0:T(8,128)(2,1)S(1)} %collective-permute-done.6.refs_2_), channel_id=1, source_target_pairs={{0,8},{2,10},{4,12},{6,14},{8,0},{10,2},{12,4},{14,6},{16,24},{18,... | collective-permute-start | bytes 786440 | tf_op jit(solution)/shard_map/ppermute | solution.py:22
  46.7 14.1 %collective-permute-start.13 = (bf16[32,4096]{1,0:T(8,128)(2,1)S(1)}, bf16[32,4096]{1,0:T(8,128)(2,1)S(1)}, u32[]{:S(2)}, u32[]{:S(2)}) collective-permute-start(bf16[32,4096]{1,0:T(8,128)(2,1)S(1)} %copy-done.3), channel_id=1, source_target_pairs={{0,16},{2,18},{4,20},{6,22},{8,24},{10,26},{12,28},{14,30},{16,0},... | collective-permute-start | bytes 786440 | tf_op jit(solution)/shard_map/ppermute | solution.py:22
  48.5 12.3 %collective-permute-start.10 = (bf16[2,89,8,128]{3,2,1,0:T(8,128)(2,1)S(1)}, bf16[2,89,8,128]{3,2,1,0:T(8,128)(2,1)S(1)}, u32[]{:S(2)}, u32[]{:S(2)}) collective-permute-start(bf16[2,89,8,128]{3,2,1,0:T(8,128)(2,1)S(1)} %slice.135), channel_id=1, source_target_pairs={{0,4},{2,6},{4,0},{6,2},{8,12},{10,14},{12,8},{14,10},{16,20},{18,... | collective-permute-start | bytes 1093640 | tf_op jit(solution)/shard_map/ppermute | solution.py:22
  49.4 11.4 %collective-permute-start.12 = (bf16[2,89,8,128]{3,2,1,0:T(8,128)(2,1)S(1)}, bf16[2,89,8,128]{3,2,1,0:T(8,128)(2,1)S(1)}, u32[]{:S(2)}, u32[]{:S(2)}) collective-permute-start(bf16[2,89,8,128]{3,2,1,0:T(8,128)(2,1)S(1)} %slice.136), channel_id=1, source_target_pairs={{0,2},{2,0},{4,6},{6,4},{8,10},{10,8},{12,14},{14,12},{16,18},{18,... | collective-permute-start | bytes 1093640 | tf_op jit(solution)/shard_map/ppermute | solution.py:22
  60.8 2.3 %collective-permute-start.14 = (bf16[96,4096]{1,0:T(8,128)(2,1)S(1)}, bf16[96,4096]{1,0:T(8,128)(2,1)S(1)}, u32[]{:S(2)}, u32[]{:S(2)}) collective-permute-start(bf16[96,4096]{1,0:T(8,128)(2,1)S(1)} %pad_maximum_fusion), channel_id=1, source_target_pairs={{0,1},{1,0},{2,3},{3,2},{4,5},{5,4},{6,7},{7,6},{8,9},{9,8},{10,11... | collective-permute-start | bytes 2359304 | tf_op jit(solution)/shard_map/ppermute | solution.py:22
  60.8 8.7 %collective-permute-start.15 = (bf16[32,4096]{1,0:T(8,128)(2,1)S(1)}, bf16[32,4096]{1,0:T(8,128)(2,1)S(1)}, u32[]{:S(2)}, u32[]{:S(2)}) collective-permute-start(bf16[32,4096]{1,0:T(8,128)(2,1)S(1)} %collective-permute-done.13.refs_2_), channel_id=1, source_target_pairs={{0,8},{2,10},{4,12},{6,14},{8,0},{10,2},{12,4},{14,6},{16,24},{18,... | collective-permute-start | bytes 786440 | tf_op jit(solution)/shard_map/ppermute | solution.py:22
  69.5 2.7 %collective-permute-start.16 = (bf16[4,32,4096]{2,1,0:T(8,128)(2,1)S(1)}, bf16[4,32,4096]{2,1,0:T(8,128)(2,1)S(1)}, u32[]{:S(2)}, u32[]{:S(2)}) collective-permute-start(bf16[4,32,4096]{2,1,0:T(8,128)(2,1)S(1)} %get-tuple-element.59), channel_id=1, source_target_pairs={{0,1},{1,0},{2,3},{3,2},{4,5},{5,4},{6,7},{7,6},{8,9},{9,8},{10,11... | collective-permute-start | bytes 3145736 | tf_op jit(solution)/shard_map/ppermute | solution.py:22
  69.6 3.7 %collective-permute-start.19 = (bf16[96,4096]{1,0:T(8,128)(2,1)S(1)}, bf16[96,4096]{1,0:T(8,128)(2,1)S(1)}, u32[]{:S(2)}, u32[]{:S(2)}) collective-permute-start(bf16[96,4096]{1,0:T(8,128)(2,1)S(1)} %pad_maximum_fusion.1), channel_id=1, source_target_pairs={{0,1},{1,0},{2,3},{3,2},{4,5},{5,4},{6,7},{7,6},{8,9},{9,8},{10,11... | collective-permute-start | bytes 2359304 | tf_op jit(solution)/shard_map/ppermute | solution.py:22
  72.3 14.0 %collective-permute-start.17 = (bf16[2,32,4096]{2,1,0:T(8,128)(2,1)S(1)}, bf16[2,32,4096]{2,1,0:T(8,128)(2,1)S(1)}, u32[]{:S(2)}, u32[]{:S(2)}) collective-permute-start(bf16[2,32,4096]{2,1,0:T(8,128)(2,1)S(1)} %add_convert_fusion.1), channel_id=1, source_target_pairs={{0,8},{2,10},{4,12},{6,14},{8,0},{10,2},{12,4},{14,6},{16,24},{18,... | collective-permute-start | bytes 1572872 | tf_op jit(solution)/shard_map/ppermute | solution.py:22
  86.3 2.7 %collective-permute-start.20 = (bf16[4,32,4096]{2,1,0:T(8,128)(2,1)S(1)}, bf16[4,32,4096]{2,1,0:T(8,128)(2,1)S(1)}, u32[]{:S(2)}, u32[]{:S(2)}) collective-permute-start(bf16[4,32,4096]{2,1,0:T(8,128)(2,1)S(1)} %get-tuple-element.70), channel_id=1, source_target_pairs={{0,1},{1,0},{2,3},{3,2},{4,5},{5,4},{6,7},{7,6},{8,9},{9,8},{10,11... | collective-permute-start | bytes 3145736 | tf_op jit(solution)/shard_map/ppermute | solution.py:22
  86.3 10.9 %collective-permute-start.23 = (bf16[2,89,8,128]{3,2,1,0:T(8,128)(2,1)S(1)}, bf16[2,89,8,128]{3,2,1,0:T(8,128)(2,1)S(1)}, u32[]{:S(2)}, u32[]{:S(2)}) collective-permute-start(bf16[2,89,8,128]{3,2,1,0:T(8,128)(2,1)S(1)} %get-tuple-element.75), channel_id=1, source_target_pairs={{0,2},{2,0},{4,6},{6,4},{8,10},{10,8},{12,14},{14,12},{16,18},{18,... | collective-permute-start | bytes 1093640 | tf_op jit(solution)/shard_map/ppermute | solution.py:22
  86.9 10.6 %collective-permute-start.24 = (bf16[2,89,8,128]{3,2,1,0:T(8,128)(2,1)S(1)}, bf16[2,89,8,128]{3,2,1,0:T(8,128)(2,1)S(1)}, u32[]{:S(2)}, u32[]{:S(2)}) collective-permute-start(bf16[2,89,8,128]{3,2,1,0:T(8,128)(2,1)S(1)} %get-tuple-element.76), channel_id=1, source_target_pairs={{0,4},{2,6},{4,0},{6,2},{8,12},{10,14},{12,8},{14,10},{16,20},{18,... | collective-permute-start | bytes 1093640 | tf_op jit(solution)/shard_map/ppermute | solution.py:22
  89.1 19.6 %collective-permute-start.21 = (bf16[2,32,4096]{2,1,0:T(8,128)(2,1)S(1)}, bf16[2,32,4096]{2,1,0:T(8,128)(2,1)S(1)}, u32[]{:S(2)}, u32[]{:S(2)}) collective-permute-start(bf16[2,32,4096]{2,1,0:T(8,128)(2,1)S(1)} %add_convert_fusion), channel_id=1, source_target_pairs={{0,8},{2,10},{4,12},{6,14},{8,0},{10,2},{12,4},{14,6},{16,24},{18,... | collective-permute-start | bytes 1572872 | tf_op jit(solution)/shard_map/ppermute | solution.py:22
  90.2 18.7 %collective-permute-start.18 = (bf16[32,4096]{1,0:T(8,128)(2,1)S(1)}, bf16[32,4096]{1,0:T(8,128)(2,1)S(1)}, u32[]{:S(2)}, u32[]{:S(2)}) collective-permute-start(bf16[32,4096]{1,0:T(8,128)(2,1)S(1)} %fusion.2), channel_id=1, source_target_pairs={{0,16},{2,18},{4,20},{6,22},{8,24},{10,26},{12,28},{14,30},{16,0},... | collective-permute-start | bytes 786440 | tf_op jit(solution)/shard_map/ppermute | solution.py:22
  98.4 17.8 %collective-permute-start.26 = (bf16[4,89,8,128]{3,2,1,0:T(8,128)(2,1)S(1)}, bf16[4,89,8,128]{3,2,1,0:T(8,128)(2,1)S(1)}, u32[]{:S(2)}, u32[]{:S(2)}) collective-permute-start(bf16[4,89,8,128]{3,2,1,0:T(8,128)(2,1)S(1)} %get-tuple-element.80), channel_id=1, source_target_pairs={{0,4},{2,6},{4,0},{6,2},{8,12},{10,14},{12,8},{14,10},{16,20},{18,... | collective-permute-start | bytes 2187272 | tf_op jit(solution)/shard_map/ppermute | solution.py:22
  99.0 17.4 %collective-permute-start.25 = (bf16[4,89,8,128]{3,2,1,0:T(8,128)(2,1)S(1)}, bf16[4,89,8,128]{3,2,1,0:T(8,128)(2,1)S(1)}, u32[]{:S(2)}, u32[]{:S(2)}) collective-permute-start(bf16[4,89,8,128]{3,2,1,0:T(8,128)(2,1)S(1)} %get-tuple-element.79), channel_id=1, source_target_pairs={{0,2},{2,0},{4,6},{6,4},{8,10},{10,8},{12,14},{14,12},{16,18},{18,... | collective-permute-start | bytes 2187272 | tf_op jit(solution)/shard_map/ppermute | solution.py:22
  108.9 22.3 %collective-permute-start.22 = (bf16[32,4096]{1,0:T(8,128)(2,1)S(1)}, bf16[32,4096]{1,0:T(8,128)(2,1)S(1)}, u32[]{:S(2)}, u32[]{:S(2)}) collective-permute-start(bf16[32,4096]{1,0:T(8,128)(2,1)S(1)} %fusion.3), channel_id=1, source_target_pairs={{0,16},{2,18},{4,20},{6,22},{8,24},{10,26},{12,28},{14,30},{16,0},... | collective-permute-start | bytes 786440 | tf_op jit(solution)/shard_map/ppermute | solution.py:22
  116.7 15.3 %collective-permute-start.27 = (bf16[89,8,128]{2,1,0:T(8,128)(2,1)S(1)}, bf16[89,8,128]{2,1,0:T(8,128)(2,1)S(1)}, u32[]{:S(2)}, u32[]{:S(2)}) collective-permute-start(bf16[89,8,128]{2,1,0:T(8,128)(2,1)S(1)} %get-tuple-element.82), channel_id=1, source_target_pairs={{0,8},{2,10},{4,12},{6,14},{8,0},{10,2},{12,4},{14,6},{16,24},{18,... | collective-permute-start | bytes 546824 | tf_op jit(solution)/shard_map/ppermute | solution.py:22
  117.7 17.4 %collective-permute-start.28 = (bf16[89,8,128]{2,1,0:T(8,128)(2,1)S(1)}, bf16[89,8,128]{2,1,0:T(8,128)(2,1)S(1)}, u32[]{:S(2)}, u32[]{:S(2)}) collective-permute-start(bf16[89,8,128]{2,1,0:T(8,128)(2,1)S(1)} %get-tuple-element.83), channel_id=1, source_target_pairs={{0,16},{2,18},{4,20},{6,22},{8,24},{10,26},{12,28},{14,30},{16,0},... | collective-permute-start | bytes 546824 | tf_op jit(solution)/shard_map/ppermute | solution.py:22
  118.8 16.3 %collective-permute-start.29 = (bf16[89,8,128]{2,1,0:T(8,128)(2,1)S(1)}, bf16[89,8,128]{2,1,0:T(8,128)(2,1)S(1)}, u32[]{:S(2)}, u32[]{:S(2)}) collective-permute-start(bf16[89,8,128]{2,1,0:T(8,128)(2,1)S(1)} %get-tuple-element.84), channel_id=1, source_target_pairs={{0,24},{2,26},{4,28},{6,30},{8,16},{10,18},{12,20},{14,22},{16,8},... | collective-permute-start | bytes 546824 | tf_op jit(solution)/shard_map/ppermute | solution.py:22
  (2 other events, 7.2 us)

commit v13 on v12

--- a/solution.py
+++ b/solution.py
@@ -13,7 +13,7 @@
 PLAIN = (((1,), (0,)), ((), ()))
 TURNED = (((1,), (1,)), ((), ()))
 MIB = 1024 * 1024
-UNROLL = 7
+UNROLL = 14
 dot = functools.partial(lax.dot_general, preferred_element_type=F32)
 
 
@@ -339,7 +339,7 @@
     received = [swap(packed[at], "dp", at * near) for at in reversed(range(1, far))][::-1]
     held = jnp.stack([packed[0], *received])
     if staged:
-        x_items[near] = swap(after(tokens, received[0]), "dp", near)
+        x_items[near] = swap(after(tokens, received[-1]), "dp", near)
         x_core, g_core = swap(tokens, "tensor", 1), swap(out_grad, "tensor", 1)
         held = after(held, x_core, g_core, x_items[near])
 

time: 140 us -> 143 us (1.021)
  starting transfers between devices: 32.2 us -> 37 us
    ppermute x30, starting transfers between devices: 32.2 us -> 37 us  [swap(): return lax.ppermute(value, axis, [(at, at ^ stride) for at in range(size)])]
  transfers between devices with their start and end apart: 30 -> 30, of which waited for: 20 -> 20; matrix products, arithmetic and copies ran while one was open for 2% -> 2% of each run, Pallas kernels for 13% -> 12%
where the time goes in v13:
time: 143 us; the launch traced here: 142 us
  waiting for transfers between devices  74.3 us (52%)
  starting transfers between devices  37 us (26%)
  Pallas kernels  22 us (15%)
  other arithmetic  4.88 us (3%)
  local copies, waits for them, and re-layouts  2.87 us (2%)
    ppermute x30, waiting for transfers between devices, swap(): return lax.ppermute(value, axis, [(at, at ^ stride) for at in range(size)])  74.3 us
    ppermute x30, starting transfers between devices, swap(): return lax.ppermute(value, axis, [(at, at ^ stride) for at in range(size)])  37 us
    pallas_call x6, Pallas kernels, call(): pl.pallas_call(kernel, grid_spec=pltpu.PrefetchScalarGridSpec(num_scalar_...  22 us
  transfers between devices with their start and end apart: 30, of which 20 were waited for; matrix products, arithmetic and copies ran while one was open for 2% of the time, Pallas kernels for 12%

profile of v13, /device:TPU:0, one launch (start us, length us, event | category | flops | bytes accessed | tf_op | source)
XLA Modules:
  0.0 142.0 jit_solution(9874685165966844880)
XLA Ops:
  4.6 1.2 copy-done.1
  5.8 1.6 %shard_map.76 = (bf16[89,8,128]{2,1,0:T(8,128)(2,1)S(1)}, bf16[89,8,128]{2,1,0:T(8,128)(2,1)S(1)}, bf16[89,8,128]{2,1,0:T(8,128)(2,1)S(1)}, bf16[89,8,128]{2,1,0:T(8,128)(2,1)S(1)}) custom-call(s32[17,56]{1,0:T(8,128)S(1)} %pad_add_fusion.table, bf16[8,9,56,128]{3,2,1,0:T(8,128)(2,1)S(1)} %bitcast.36), custom_call_target="tpu_custom_call" | custom-call | bytes 1000000 | tf_op jit(solution)/shard_map/pallas_call | solution.py:261
  7.5 5.1 %collective-permute-start = (bf16[89,8,128]{2,1,0:T(8,128)(2,1)S(1)}, bf16[89,8,128]{2,1,0:T(8,128)(2,1)S(1)}, u32[]{:S(2)}, u32[]{:S(2)}) collective-permute-start(bf16[89,8,128]{2,1,0:T(8,128)(2,1)S(1)} %get-tuple-element.46), channel_id=1, source_target_pairs={{0,24},{2,26},{4,28},{6,30},{8,16},{10,18},{12,20},{14,22},{16,8},... | collective-permute-start | bytes 546824 | tf_op jit(solution)/shard_map/ppermute | solution.py:22
  13.7 4.4 %collective-permute-done = bf16[89,8,128]{2,1,0:T(8,128)(2,1)S(1)} collective-permute-done((bf16[89,8,128]{2,1,0:T(8,128)(2,1)S(1)}, bf16[89,8,128]{2,1,0:T(8,128)(2,1)S(1)}, u32[]{:S(2)}, u32[]{:S(2)}) %collective-permute-start) | collective-permute-done | bytes 182304 | tf_op jit(solution)/shard_map/ppermute | solution.py:22
  18.1 7.5 %collective-permute-start.1 = (bf16[32,4096]{1,0:T(8,128)(2,1)}, bf16[32,4096]{1,0:T(8,128)(2,1)S(1)}, u32[]{:S(2)}, u32[]{:S(2)}) collective-permute-start(bf16[32,4096]{1,0:T(8,128)(2,1)} %refs_0_.2), channel_id=1, source_target_pairs={{0,8},{2,10},{4,12},{6,14},{8,0},{10,2},{12,4},{14,6},{16,24},{18,... | collective-permute-start | bytes 786440 | tf_op jit(solution)/shard_map/ppermute | solution.py:22
  25.7 2.5 %collective-permute-done.3 = bf16[89,8,128]{2,1,0:T(8,128)(2,1)S(1)} collective-permute-done((bf16[89,8,128]{2,1,0:T(8,128)(2,1)S(1)}, bf16[89,8,128]{2,1,0:T(8,128)(2,1)S(1)}, u32[]{:S(2)}, u32[]{:S(2)}) %collective-permute-start.3) | collective-permute-done | bytes 182304 | tf_op jit(solution)/shard_map/ppermute | solution.py:22
  28.3 5.3 %collective-permute-done.1.refs_1_ = bf16[32,4096]{1,0:T(8,128)(2,1)S(1)} collective-permute-done((bf16[32,4096]{1,0:T(8,128)(2,1)}, bf16[32,4096]{1,0:T(8,128)(2,1)S(1)}, u32[]{:S(2)}, u32[]{:S(2)}) %collective-permute-start.1) | collective-permute-done | bytes 262176 | tf_op jit(solution)/shard_map/ppermute | solution.py:22
  33.6 1.5 %collective-permute-start.9 = (bf16[4,89,8,128]{3,2,1,0:T(8,128)(2,1)S(1)}, bf16[4,89,8,128]{3,2,1,0:T(8,128)(2,1)S(1)}, u32[]{:S(2)}, u32[]{:S(2)}) collective-permute-start(bf16[4,89,8,128]{3,2,1,0:T(8,128)(2,1)S(1)} %pad_maximum_fusion.2.refs_0_), channel_id=1, source_target_pairs={{0,2},{2,0},{4,6},{6,4},{8,10},{10,8},{12,14},{14,12},{16,18},{18,... | collective-permute-start | bytes 2187272 | tf_op jit(solution)/shard_map/ppermute | solution.py:22
  35.1 1.5 %collective-permute-start.11 = (bf16[4,89,8,128]{3,2,1,0:T(8,128)(2,1)S(1)}, bf16[4,89,8,128]{3,2,1,0:T(8,128)(2,1)S(1)}, u32[]{:S(2)}, u32[]{:S(2)}) collective-permute-start(bf16[4,89,8,128]{3,2,1,0:T(8,128)(2,1)S(1)} %pad_maximum_fusion.2.refs_0_), channel_id=1, source_target_pairs={{0,4},{2,6},{4,0},{6,2},{8,12},{10,14},{12,8},{14,10},{16,20},{18,... | collective-permute-start | bytes 2187272 | tf_op jit(solution)/shard_map/ppermute | solution.py:22
  36.9 2.4 %collective-permute-start.7 = (bf16[32,4096]{1,0:T(8,128)(2,1)S(1)}, bf16[32,4096]{1,0:T(8,128)(2,1)S(1)}, u32[]{:S(2)}, u32[]{:S(2)}) collective-permute-start(bf16[32,4096]{1,0:T(8,128)(2,1)S(1)} %copy-done.3), channel_id=1, source_target_pairs={{0,8},{2,10},{4,12},{6,14},{8,0},{10,2},{12,4},{14,6},{16,24},{18,... | collective-permute-start | bytes 786440 | tf_op jit(solution)/shard_map/ppermute | solution.py:22
  39.3 10.6 %collective-permute-done.6.refs_2_ = bf16[32,4096]{1,0:T(8,128)(2,1)S(1)} collective-permute-done((bf16[32,4096]{1,0:T(8,128)(2,1)S(1)}, bf16[32,4096]{1,0:T(8,128)(2,1)S(1)}, u32[]{:S(2)}, u32[]{:S(2)}) %collective-permute-start.6) | collective-permute-done | bytes 262176 | tf_op jit(solution)/shard_map/ppermute | solution.py:22
  50.1 2.6 %collective-permute-start.13 = (bf16[32,4096]{1,0:T(8,128)(2,1)S(1)}, bf16[32,4096]{1,0:T(8,128)(2,1)S(1)}, u32[]{:S(2)}, u32[]{:S(2)}) collective-permute-start(bf16[32,4096]{1,0:T(8,128)(2,1)S(1)} %copy-done.3), channel_id=1, source_target_pairs={{0,16},{2,18},{4,20},{6,22},{8,24},{10,26},{12,28},{14,30},{16,0},... | collective-permute-start | bytes 786440 | tf_op jit(solution)/shard_map/ppermute | solution.py:22
  53.4 1.6 %collective-permute-start.12 = (bf16[2,89,8,128]{3,2,1,0:T(8,128)(2,1)S(1)}, bf16[2,89,8,128]{3,2,1,0:T(8,128)(2,1)S(1)}, u32[]{:S(2)}, u32[]{:S(2)}) collective-permute-start(bf16[2,89,8,128]{3,2,1,0:T(8,128)(2,1)S(1)} %slice.136), channel_id=1, source_target_pairs={{0,2},{2,0},{4,6},{6,4},{8,10},{10,8},{12,14},{14,12},{16,18},{18,... | collective-permute-start | bytes 1093640 | tf_op jit(solution)/shard_map/ppermute | solution.py:22
  54.9 8.2 %collective-permute-done.8.refs_3_ = bf16[32,4096]{1,0:T(8,128)(2,1)S(1)} collective-permute-done((bf16[32,4096]{1,0:T(8,128)(2,1)S(1)}, bf16[32,4096]{1,0:T(8,128)(2,1)S(1)}, u32[]{:S(2)}, u32[]{:S(2)}) %collective-permute-start.8) | collective-permute-done | bytes 262176 | tf_op jit(solution)/shard_map/ppermute | solution.py:22
  63.2 1.4 collective-permute-done.13.refs_2_
  64.7 1.8 %shard_map.77.refs_6_ = bf16[89,128,128]{2,1,0:T(8,128)(2,1)S(1)} custom-call(s32[17,56]{1,0:T(8,128)S(1)} %pad_add_fusion.table, bf16[4,89,8,128]{3,2,1,0:T(8,128)(2,1)S(1)} %pad_maximum_fusion.2.refs_0_, bf16[4,89,8,128]{3,2,1,0:T(8,128)(2,1)S(1)} %collective-permute-done.9.refs_1_, bf16[4,89,8,128]{3,2,1,0:T(8,128)(2,1)S(1)} %collective-permute-done.11.refs_2_, ...), custom_call_target="tpu_custom_call" | custom-call | bytes 10000000 | tf_op jit(solution)/shard_map/pallas_call | solution.py:261
  66.9 5.0 %shard_map.78 = (bf16[4096,256]{1,0:T(8,128)(2,1)S(1)}, f32[14,256,128]{2,1,0:T(8,128)S(1)}, f32[14,256,128]{2,1,0:T(8,128)S(1)}, bf16[14,128,256]{2,1,0:T(8,128...) custom-call(s32[17,56]{1,0:T(8,128)S(1)} %pad_add_fusion.table, ...), custom_call_target="tpu_custom_call" | custom-call | bytes 30000000 | tf_op jit(solution)/shard_map/pallas_call | solution.py:261
  71.9 1.4 %collective-permute-done.15.refs_3_ = bf16[32,4096]{1,0:T(8,128)(2,1)S(1)} collective-permute-done((bf16[32,4096]{1,0:T(8,128)(2,1)S(1)}, bf16[32,4096]{1,0:T(8,128)(2,1)S(1)}, u32[]{:S(2)}, u32[]{:S(2)}) %collective-permute-start.15) | collective-permute-done | bytes 262176 | tf_op jit(solution)/shard_map/ppermute | solution.py:22
  74.0 2.0 %collective-permute-done.16 = bf16[4,32,4096]{2,1,0:T(8,128)(2,1)S(1)} collective-permute-done((bf16[4,32,4096]{2,1,0:T(8,128)(2,1)S(1)}, bf16[4,32,4096]{2,1,0:T(8,128)(2,1)S(1)}, u32[]{:S(2)}, u32[]{:S(2)}) %collective-permute-start.16) | collective-permute-done | bytes 1048608 | tf_op jit(solution)/shard_map/ppermute | solution.py:22
  77.1 9.7 %shard_map.79 = (bf16[4,32,4096]{2,1,0:T(8,128)(2,1)S(1)}, bf16[4,32,4096]{2,1,0:T(8,128)(2,1)S(1)}, bf16[4,89,8,128]{3,2,1,0:T(8,128)(2,1)S(1)}, bf16[4,89,8,12...) custom-call(s32[17,56]{1,0:T(8,128)S(1)} %pad_add_fusion.table, ...), custom_call_target="tpu_custom_call" | custom-call | bytes 40000000 | tf_op jit(solution)/shard_map/pallas_call | solution.py:261
  86.8 3.3 %collective-permute-done.17 = bf16[2,32,4096]{2,1,0:T(8,128)(2,1)S(1)} collective-permute-done((bf16[2,32,4096]{2,1,0:T(8,128)(2,1)S(1)}, bf16[2,32,4096]{2,1,0:T(8,128)(2,1)S(1)}, u32[]{:S(2)}, u32[]{:S(2)}) %collective-permute-start.17) | collective-permute-done | bytes 524320 | tf_op jit(solution)/shard_map/ppermute | solution.py:22
  91.2 1.6 %collective-permute-done.20 = bf16[4,32,4096]{2,1,0:T(8,128)(2,1)S(1)} collective-permute-done((bf16[4,32,4096]{2,1,0:T(8,128)(2,1)S(1)}, bf16[4,32,4096]{2,1,0:T(8,128)(2,1)S(1)}, u32[]{:S(2)}, u32[]{:S(2)}) %collective-permute-start.20) | collective-permute-done | bytes 1048608 | tf_op jit(solution)/shard_map/ppermute | solution.py:22
  93.5 2.3 %collective-permute-start.18 = (bf16[32,4096]{1,0:T(8,128)(2,1)S(1)}, bf16[32,4096]{1,0:T(8,128)(2,1)S(1)}, u32[]{:S(2)}, u32[]{:S(2)}) collective-permute-start(bf16[32,4096]{1,0:T(8,128)(2,1)S(1)} %fusion.2), channel_id=1, source_target_pairs={{0,16},{2,18},{4,20},{6,22},{8,24},{10,26},{12,28},{14,30},{16,0},... | collective-permute-start | bytes 786440 | tf_op jit(solution)/shard_map/ppermute | solution.py:22
  95.8 5.2 %collective-permute-done.23.got_1 = bf16[2,89,8,128]{3,2,1,0:T(8,128)(2,1)S(1)} collective-permute-done((bf16[2,89,8,128]{3,2,1,0:T(8,128)(2,1)S(1)}, bf16[2,89,8,128]{3,2,1,0:T(8,128)(2,1)S(1)}, u32[]{:S(2)}, u32[]{:S(2)}) %collective-permute-start.23) | collective-permute-done | bytes 364576 | tf_op jit(solution)/shard_map/ppermute | solution.py:22
  102.8 1.5 %collective-permute-start.25 = (bf16[4,89,8,128]{3,2,1,0:T(8,128)(2,1)S(1)}, bf16[4,89,8,128]{3,2,1,0:T(8,128)(2,1)S(1)}, u32[]{:S(2)}, u32[]{:S(2)}) collective-permute-start(bf16[4,89,8,128]{3,2,1,0:T(8,128)(2,1)S(1)} %get-tuple-element.79), channel_id=1, source_target_pairs={{0,2},{2,0},{4,6},{6,4},{8,10},{10,8},{12,14},{14,12},{16,18},{18,... | collective-permute-start | bytes 2187272 | tf_op jit(solution)/shard_map/ppermute | solution.py:22
  104.3 8.3 %collective-permute-done.21 = bf16[2,32,4096]{2,1,0:T(8,128)(2,1)S(1)} collective-permute-done((bf16[2,32,4096]{2,1,0:T(8,128)(2,1)S(1)}, bf16[2,32,4096]{2,1,0:T(8,128)(2,1)S(1)}, u32[]{:S(2)}, u32[]{:S(2)}) %collective-permute-start.21) | collective-permute-done | bytes 524320 | tf_op jit(solution)/shard_map/ppermute | solution.py:22
  114.7 5.3 %collective-permute-done.26 = bf16[4,89,8,128]{3,2,1,0:T(8,128)(2,1)S(1)} collective-permute-done((bf16[4,89,8,128]{3,2,1,0:T(8,128)(2,1)S(1)}, bf16[4,89,8,128]{3,2,1,0:T(8,128)(2,1)S(1)}, u32[]{:S(2)}, u32[]{:S(2)}) %collective-permute-start.26) | collective-permute-done | bytes 729120 | tf_op jit(solution)/shard_map/ppermute | solution.py:22
  121.0 2.3 %collective-permute-start.28 = (bf16[89,8,128]{2,1,0:T(8,128)(2,1)S(1)}, bf16[89,8,128]{2,1,0:T(8,128)(2,1)S(1)}, u32[]{:S(2)}, u32[]{:S(2)}) collective-permute-start(bf16[89,8,128]{2,1,0:T(8,128)(2,1)S(1)} %get-tuple-element.83), channel_id=1, source_target_pairs={{0,16},{2,18},{4,20},{6,22},{8,24},{10,26},{12,28},{14,30},{16,0},... | collective-permute-start | bytes 546824 | tf_op jit(solution)/shard_map/ppermute | solution.py:22
  123.3 1.7 %collective-permute-start.29 = (bf16[89,8,128]{2,1,0:T(8,128)(2,1)S(1)}, bf16[89,8,128]{2,1,0:T(8,128)(2,1)S(1)}, u32[]{:S(2)}, u32[]{:S(2)}) collective-permute-start(bf16[89,8,128]{2,1,0:T(8,128)(2,1)S(1)} %get-tuple-element.84), channel_id=1, source_target_pairs={{0,24},{2,26},{4,28},{6,30},{8,16},{10,18},{12,20},{14,22},{16,8},... | collective-permute-start | bytes 546824 | tf_op jit(solution)/shard_map/ppermute | solution.py:22
  125.0 10.2 %collective-permute-done.22 = bf16[32,4096]{1,0:T(8,128)(2,1)S(1)} collective-permute-done((bf16[32,4096]{1,0:T(8,128)(2,1)S(1)}, bf16[32,4096]{1,0:T(8,128)(2,1)S(1)}, u32[]{:S(2)}, u32[]{:S(2)}) %collective-permute-start.22) | collective-permute-done | bytes 262176 | tf_op jit(solution)/shard_map/ppermute | solution.py:22
  136.0 3.1 %collective-permute-done.28.refs_2_ = bf16[89,8,128]{2,1,0:T(8,128)(2,1)S(1)} collective-permute-done((bf16[89,8,128]{2,1,0:T(8,128)(2,1)S(1)}, bf16[89,8,128]{2,1,0:T(8,128)(2,1)S(1)}, u32[]{:S(2)}, u32[]{:S(2)}) %collective-permute-start.28) | collective-permute-done | bytes 182304 | tf_op jit(solution)/shard_map/ppermute | solution.py:22
  139.0 3.0 %shard_map.81 = bf16[8,9,56,128]{3,2,1,0:T(8,128)(2,1)} custom-call(s32[17,56]{1,0:T(8,128)S(1)} %pad_add_fusion.table, bf16[89,8,128]{2,1,0:T(8,128)(2,1)S(1)} %get-tuple-element.85.refs_0_, bf16[89,8,128]{2,1,0:T(8,128)(2,1)S(1)} %collective-permute-done.27.refs_1_, bf16[89,8,128]{2,1,0:T(8,128)(2,1)S(1)} %collective-permute-done.28.refs_2_, ...), custom_call_target="tpu_custom_call" | custom-call | bytes 2000000 | tf_op jit(solution)/shard_map/pallas_call | solution.py:261
  (70 shorter events, 16.0 us)
Async XLA Ops:
  5.8 30.8 %copy-start.2 = (bf16[32,4096]{1,0:T(8,128)(2,1)S(1)}, bf16[32,4096]{1,0:T(8,128)(2,1)}, u32[]{:S(2)}) copy-start(bf16[32,4096]{1,0:T(8,128)(2,1)} %refs_0_.2) | copy-start | bytes 786436
  5.8 31.0 %copy-start.3 = (bf16[32,4096]{1,0:T(8,128)(2,1)S(1)}, bf16[32,4096]{1,0:T(8,128)(2,1)}, u32[]{:S(2)}) copy-start(bf16[32,4096]{1,0:T(8,128)(2,1)} %refs_0_.3) | copy-start | bytes 786436
  7.5 10.7 %collective-permute-start = (bf16[89,8,128]{2,1,0:T(8,128)(2,1)S(1)}, bf16[89,8,128]{2,1,0:T(8,128)(2,1)S(1)}, u32[]{:S(2)}, u32[]{:S(2)}) collective-permute-start(bf16[89,8,128]{2,1,0:T(8,128)(2,1)S(1)} %get-tuple-element.46), channel_id=1, source_target_pairs={{0,24},{2,26},{4,28},{6,30},{8,16},{10,18},{12,20},{14,22},{16,8},... | collective-permute-start | bytes 546824 | tf_op jit(solution)/shard_map/ppermute | solution.py:22
  12.6 15.6 %collective-permute-start.3 = (bf16[89,8,128]{2,1,0:T(8,128)(2,1)S(1)}, bf16[89,8,128]{2,1,0:T(8,128)(2,1)S(1)}, u32[]{:S(2)}, u32[]{:S(2)}) collective-permute-start(bf16[89,8,128]{2,1,0:T(8,128)(2,1)S(1)} %get-tuple-element.50), channel_id=1, source_target_pairs={{0,16},{2,18},{4,20},{6,22},{8,24},{10,26},{12,28},{14,30},{16,0},... | collective-permute-start | bytes 546824 | tf_op jit(solution)/shard_map/ppermute | solution.py:22
  12.6 15.6 %collective-permute-start.2 = (bf16[89,8,128]{2,1,0:T(8,128)(2,1)S(1)}, bf16[89,8,128]{2,1,0:T(8,128)(2,1)S(1)}, u32[]{:S(2)}, u32[]{:S(2)}) collective-permute-start(bf16[89,8,128]{2,1,0:T(8,128)(2,1)S(1)} %get-tuple-element.49), channel_id=1, source_target_pairs={{0,8},{2,10},{4,12},{6,14},{8,0},{10,2},{12,4},{14,6},{16,24},{18,... | collective-permute-start | bytes 546824 | tf_op jit(solution)/shard_map/ppermute | solution.py:22
  13.2 15.0 %collective-permute-start.4 = (bf16[32,4096]{1,0:T(8,128)(2,1)}, bf16[32,4096]{1,0:T(8,128)(2,1)S(1)}, u32[]{:S(2)}, u32[]{:S(2)}) collective-permute-start(bf16[32,4096]{1,0:T(8,128)(2,1)} %refs_0_.2), channel_id=1, source_target_pairs={{0,1},{1,0},{2,3},{3,2},{4,5},{5,4},{6,7},{7,6},{8,9},{9,8},{10,11... | collective-permute-start | bytes 786440 | tf_op jit(solution)/shard_map/ppermute | solution.py:22
  13.2 15.0 %collective-permute-start.5 = (bf16[32,4096]{1,0:T(8,128)(2,1)}, bf16[32,4096]{1,0:T(8,128)(2,1)S(1)}, u32[]{:S(2)}, u32[]{:S(2)}) collective-permute-start(bf16[32,4096]{1,0:T(8,128)(2,1)} %refs_0_.3), channel_id=1, source_target_pairs={{0,1},{1,0},{2,3},{3,2},{4,5},{5,4},{6,7},{7,6},{8,9},{9,8},{10,11... | collective-permute-start | bytes 786440 | tf_op jit(solution)/shard_map/ppermute | solution.py:22
  18.1 15.4 %collective-permute-start.1 = (bf16[32,4096]{1,0:T(8,128)(2,1)}, bf16[32,4096]{1,0:T(8,128)(2,1)S(1)}, u32[]{:S(2)}, u32[]{:S(2)}) collective-permute-start(bf16[32,4096]{1,0:T(8,128)(2,1)} %refs_0_.2), channel_id=1, source_target_pairs={{0,8},{2,10},{4,12},{6,14},{8,0},{10,2},{12,4},{14,6},{16,24},{18,... | collective-permute-start | bytes 786440 | tf_op jit(solution)/shard_map/ppermute | solution.py:22
  33.6 19.1 %collective-permute-start.9 = (bf16[4,89,8,128]{3,2,1,0:T(8,128)(2,1)S(1)}, bf16[4,89,8,128]{3,2,1,0:T(8,128)(2,1)S(1)}, u32[]{:S(2)}, u32[]{:S(2)}) collective-permute-start(bf16[4,89,8,128]{3,2,1,0:T(8,128)(2,1)S(1)} %pad_maximum_fusion.2.refs_0_), channel_id=1, source_target_pairs={{0,2},{2,0},{4,6},{6,4},{8,10},{10,8},{12,14},{14,12},{16,18},{18,... | collective-permute-start | bytes 2187272 | tf_op jit(solution)/shard_map/ppermute | solution.py:22
  35.1 18.3 %collective-permute-start.11 = (bf16[4,89,8,128]{3,2,1,0:T(8,128)(2,1)S(1)}, bf16[4,89,8,128]{3,2,1,0:T(8,128)(2,1)S(1)}, u32[]{:S(2)}, u32[]{:S(2)}) collective-permute-start(bf16[4,89,8,128]{3,2,1,0:T(8,128)(2,1)S(1)} %pad_maximum_fusion.2.refs_0_), channel_id=1, source_target_pairs={{0,4},{2,6},{4,0},{6,2},{8,12},{10,14},{12,8},{14,10},{16,20},{18,... | collective-permute-start | bytes 2187272 | tf_op jit(solution)/shard_map/ppermute | solution.py:22
  36.6 13.3 %collective-permute-start.6 = (bf16[32,4096]{1,0:T(8,128)(2,1)S(1)}, bf16[32,4096]{1,0:T(8,128)(2,1)S(1)}, u32[]{:S(2)}, u32[]{:S(2)}) collective-permute-start(bf16[32,4096]{1,0:T(8,128)(2,1)S(1)} %copy-done.2), channel_id=1, source_target_pairs={{0,16},{2,18},{4,20},{6,22},{8,24},{10,26},{12,28},{14,30},{16,0},... | collective-permute-start | bytes 786440 | tf_op jit(solution)/shard_map/ppermute | solution.py:22
  36.9 13.1 %collective-permute-start.7 = (bf16[32,4096]{1,0:T(8,128)(2,1)S(1)}, bf16[32,4096]{1,0:T(8,128)(2,1)S(1)}, u32[]{:S(2)}, u32[]{:S(2)}) collective-permute-start(bf16[32,4096]{1,0:T(8,128)(2,1)S(1)} %copy-done.3), channel_id=1, source_target_pairs={{0,8},{2,10},{4,12},{6,14},{8,0},{10,2},{12,4},{14,6},{16,24},{18,... | collective-permute-start | bytes 786440 | tf_op jit(solution)/shard_map/ppermute | solution.py:22
  50.0 13.2 %collective-permute-start.8 = (bf16[32,4096]{1,0:T(8,128)(2,1)S(1)}, bf16[32,4096]{1,0:T(8,128)(2,1)S(1)}, u32[]{:S(2)}, u32[]{:S(2)}) collective-permute-start(bf16[32,4096]{1,0:T(8,128)(2,1)S(1)} %collective-permute-done.6.refs_2_), channel_id=1, source_target_pairs={{0,8},{2,10},{4,12},{6,14},{8,0},{10,2},{12,4},{14,6},{16,24},{18,... | collective-permute-start | bytes 786440 | tf_op jit(solution)/shard_map/ppermute | solution.py:22
  50.1 14.5 %collective-permute-start.13 = (bf16[32,4096]{1,0:T(8,128)(2,1)S(1)}, bf16[32,4096]{1,0:T(8,128)(2,1)S(1)}, u32[]{:S(2)}, u32[]{:S(2)}) collective-permute-start(bf16[32,4096]{1,0:T(8,128)(2,1)S(1)} %copy-done.3), channel_id=1, source_target_pairs={{0,16},{2,18},{4,20},{6,22},{8,24},{10,26},{12,28},{14,30},{16,0},... | collective-permute-start | bytes 786440 | tf_op jit(solution)/shard_map/ppermute | solution.py:22
  52.7 11.9 %collective-permute-start.10 = (bf16[2,89,8,128]{3,2,1,0:T(8,128)(2,1)S(1)}, bf16[2,89,8,128]{3,2,1,0:T(8,128)(2,1)S(1)}, u32[]{:S(2)}, u32[]{:S(2)}) collective-permute-start(bf16[2,89,8,128]{3,2,1,0:T(8,128)(2,1)S(1)} %slice.135), channel_id=1, source_target_pairs={{0,4},{2,6},{4,0},{6,2},{8,12},{10,14},{12,8},{14,10},{16,20},{18,... | collective-permute-start | bytes 1093640 | tf_op jit(solution)/shard_map/ppermute | solution.py:22
  53.4 11.3 %collective-permute-start.12 = (bf16[2,89,8,128]{3,2,1,0:T(8,128)(2,1)S(1)}, bf16[2,89,8,128]{3,2,1,0:T(8,128)(2,1)S(1)}, u32[]{:S(2)}, u32[]{:S(2)}) collective-permute-start(bf16[2,89,8,128]{3,2,1,0:T(8,128)(2,1)S(1)} %slice.136), channel_id=1, source_target_pairs={{0,2},{2,0},{4,6},{6,4},{8,10},{10,8},{12,14},{14,12},{16,18},{18,... | collective-permute-start | bytes 1093640 | tf_op jit(solution)/shard_map/ppermute | solution.py:22
  64.6 2.3 %collective-permute-start.14 = (bf16[96,4096]{1,0:T(8,128)(2,1)S(1)}, bf16[96,4096]{1,0:T(8,128)(2,1)S(1)}, u32[]{:S(2)}, u32[]{:S(2)}) collective-permute-start(bf16[96,4096]{1,0:T(8,128)(2,1)S(1)} %pad_maximum_fusion), channel_id=1, source_target_pairs={{0,1},{1,0},{2,3},{3,2},{4,5},{5,4},{6,7},{7,6},{8,9},{9,8},{10,11... | collective-permute-start | bytes 2359304 | tf_op jit(solution)/shard_map/ppermute | solution.py:22
  64.6 8.7 %collective-permute-start.15 = (bf16[32,4096]{1,0:T(8,128)(2,1)S(1)}, bf16[32,4096]{1,0:T(8,128)(2,1)S(1)}, u32[]{:S(2)}, u32[]{:S(2)}) collective-permute-start(bf16[32,4096]{1,0:T(8,128)(2,1)S(1)} %collective-permute-done.13.refs_2_), channel_id=1, source_target_pairs={{0,8},{2,10},{4,12},{6,14},{8,0},{10,2},{12,4},{14,6},{16,24},{18,... | collective-permute-start | bytes 786440 | tf_op jit(solution)/shard_map/ppermute | solution.py:22
  73.3 2.7 %collective-permute-start.16 = (bf16[4,32,4096]{2,1,0:T(8,128)(2,1)S(1)}, bf16[4,32,4096]{2,1,0:T(8,128)(2,1)S(1)}, u32[]{:S(2)}, u32[]{:S(2)}) collective-permute-start(bf16[4,32,4096]{2,1,0:T(8,128)(2,1)S(1)} %get-tuple-element.59), channel_id=1, source_target_pairs={{0,1},{1,0},{2,3},{3,2},{4,5},{5,4},{6,7},{7,6},{8,9},{9,8},{10,11... | collective-permute-start | bytes 3145736 | tf_op jit(solution)/shard_map/ppermute | solution.py:22
  73.4 3.7 %collective-permute-start.19 = (bf16[96,4096]{1,0:T(8,128)(2,1)S(1)}, bf16[96,4096]{1,0:T(8,128)(2,1)S(1)}, u32[]{:S(2)}, u32[]{:S(2)}) collective-permute-start(bf16[96,4096]{1,0:T(8,128)(2,1)S(1)} %pad_maximum_fusion.1), channel_id=1, source_target_pairs={{0,1},{1,0},{2,3},{3,2},{4,5},{5,4},{6,7},{7,6},{8,9},{9,8},{10,11... | collective-permute-start | bytes 2359304 | tf_op jit(solution)/shard_map/ppermute | solution.py:22
  76.1 14.0 %collective-permute-start.17 = (bf16[2,32,4096]{2,1,0:T(8,128)(2,1)S(1)}, bf16[2,32,4096]{2,1,0:T(8,128)(2,1)S(1)}, u32[]{:S(2)}, u32[]{:S(2)}) collective-permute-start(bf16[2,32,4096]{2,1,0:T(8,128)(2,1)S(1)} %add_convert_fusion.1), channel_id=1, source_target_pairs={{0,8},{2,10},{4,12},{6,14},{8,0},{10,2},{12,4},{14,6},{16,24},{18,... | collective-permute-start | bytes 1572872 | tf_op jit(solution)/shard_map/ppermute | solution.py:22
  90.2 2.7 %collective-permute-start.20 = (bf16[4,32,4096]{2,1,0:T(8,128)(2,1)S(1)}, bf16[4,32,4096]{2,1,0:T(8,128)(2,1)S(1)}, u32[]{:S(2)}, u32[]{:S(2)}) collective-permute-start(bf16[4,32,4096]{2,1,0:T(8,128)(2,1)S(1)} %get-tuple-element.70), channel_id=1, source_target_pairs={{0,1},{1,0},{2,3},{3,2},{4,5},{5,4},{6,7},{7,6},{8,9},{9,8},{10,11... | collective-permute-start | bytes 3145736 | tf_op jit(solution)/shard_map/ppermute | solution.py:22
  90.2 10.9 %collective-permute-start.23 = (bf16[2,89,8,128]{3,2,1,0:T(8,128)(2,1)S(1)}, bf16[2,89,8,128]{3,2,1,0:T(8,128)(2,1)S(1)}, u32[]{:S(2)}, u32[]{:S(2)}) collective-permute-start(bf16[2,89,8,128]{3,2,1,0:T(8,128)(2,1)S(1)} %get-tuple-element.75), channel_id=1, source_target_pairs={{0,2},{2,0},{4,6},{6,4},{8,10},{10,8},{12,14},{14,12},{16,18},{18,... | collective-permute-start | bytes 1093640 | tf_op jit(solution)/shard_map/ppermute | solution.py:22
  90.7 10.6 %collective-permute-start.24 = (bf16[2,89,8,128]{3,2,1,0:T(8,128)(2,1)S(1)}, bf16[2,89,8,128]{3,2,1,0:T(8,128)(2,1)S(1)}, u32[]{:S(2)}, u32[]{:S(2)}) collective-permute-start(bf16[2,89,8,128]{3,2,1,0:T(8,128)(2,1)S(1)} %get-tuple-element.76), channel_id=1, source_target_pairs={{0,4},{2,6},{4,0},{6,2},{8,12},{10,14},{12,8},{14,10},{16,20},{18,... | collective-permute-start | bytes 1093640 | tf_op jit(solution)/shard_map/ppermute | solution.py:22
  92.9 19.6 %collective-permute-start.21 = (bf16[2,32,4096]{2,1,0:T(8,128)(2,1)S(1)}, bf16[2,32,4096]{2,1,0:T(8,128)(2,1)S(1)}, u32[]{:S(2)}, u32[]{:S(2)}) collective-permute-start(bf16[2,32,4096]{2,1,0:T(8,128)(2,1)S(1)} %add_convert_fusion), channel_id=1, source_target_pairs={{0,8},{2,10},{4,12},{6,14},{8,0},{10,2},{12,4},{14,6},{16,24},{18,... | collective-permute-start | bytes 1572872 | tf_op jit(solution)/shard_map/ppermute | solution.py:22
  93.5 19.2 %collective-permute-start.18 = (bf16[32,4096]{1,0:T(8,128)(2,1)S(1)}, bf16[32,4096]{1,0:T(8,128)(2,1)S(1)}, u32[]{:S(2)}, u32[]{:S(2)}) collective-permute-start(bf16[32,4096]{1,0:T(8,128)(2,1)S(1)} %fusion.2), channel_id=1, source_target_pairs={{0,16},{2,18},{4,20},{6,22},{8,24},{10,26},{12,28},{14,30},{16,0},... | collective-permute-start | bytes 786440 | tf_op jit(solution)/shard_map/ppermute | solution.py:22
  102.3 17.8 %collective-permute-start.26 = (bf16[4,89,8,128]{3,2,1,0:T(8,128)(2,1)S(1)}, bf16[4,89,8,128]{3,2,1,0:T(8,128)(2,1)S(1)}, u32[]{:S(2)}, u32[]{:S(2)}) collective-permute-start(bf16[4,89,8,128]{3,2,1,0:T(8,128)(2,1)S(1)} %get-tuple-element.80), channel_id=1, source_target_pairs={{0,4},{2,6},{4,0},{6,2},{8,12},{10,14},{12,8},{14,10},{16,20},{18,... | collective-permute-start | bytes 2187272 | tf_op jit(solution)/shard_map/ppermute | solution.py:22
  102.8 17.4 %collective-permute-start.25 = (bf16[4,89,8,128]{3,2,1,0:T(8,128)(2,1)S(1)}, bf16[4,89,8,128]{3,2,1,0:T(8,128)(2,1)S(1)}, u32[]{:S(2)}, u32[]{:S(2)}) collective-permute-start(bf16[4,89,8,128]{3,2,1,0:T(8,128)(2,1)S(1)} %get-tuple-element.79), channel_id=1, source_target_pairs={{0,2},{2,0},{4,6},{6,4},{8,10},{10,8},{12,14},{14,12},{16,18},{18,... | collective-permute-start | bytes 2187272 | tf_op jit(solution)/shard_map/ppermute | solution.py:22
  112.7 22.4 %collective-permute-start.22 = (bf16[32,4096]{1,0:T(8,128)(2,1)S(1)}, bf16[32,4096]{1,0:T(8,128)(2,1)S(1)}, u32[]{:S(2)}, u32[]{:S(2)}) collective-permute-start(bf16[32,4096]{1,0:T(8,128)(2,1)S(1)} %fusion.3), channel_id=1, source_target_pairs={{0,16},{2,18},{4,20},{6,22},{8,24},{10,26},{12,28},{14,30},{16,0},... | collective-permute-start | bytes 786440 | tf_op jit(solution)/shard_map/ppermute | solution.py:22
  120.5 15.4 %collective-permute-start.27 = (bf16[89,8,128]{2,1,0:T(8,128)(2,1)S(1)}, bf16[89,8,128]{2,1,0:T(8,128)(2,1)S(1)}, u32[]{:S(2)}, u32[]{:S(2)}) collective-permute-start(bf16[89,8,128]{2,1,0:T(8,128)(2,1)S(1)} %get-tuple-element.82), channel_id=1, source_target_pairs={{0,8},{2,10},{4,12},{6,14},{8,0},{10,2},{12,4},{14,6},{16,24},{18,... | collective-permute-start | bytes 546824 | tf_op jit(solution)/shard_map/ppermute | solution.py:22
  121.0 18.1 %collective-permute-start.28 = (bf16[89,8,128]{2,1,0:T(8,128)(2,1)S(1)}, bf16[89,8,128]{2,1,0:T(8,128)(2,1)S(1)}, u32[]{:S(2)}, u32[]{:S(2)}) collective-permute-start(bf16[89,8,128]{2,1,0:T(8,128)(2,1)S(1)} %get-tuple-element.83), channel_id=1, source_target_pairs={{0,16},{2,18},{4,20},{6,22},{8,24},{10,26},{12,28},{14,30},{16,0},... | collective-permute-start | bytes 546824 | tf_op jit(solution)/shard_map/ppermute | solution.py:22
  123.3 15.8 %collective-permute-start.29 = (bf16[89,8,128]{2,1,0:T(8,128)(2,1)S(1)}, bf16[89,8,128]{2,1,0:T(8,128)(2,1)S(1)}, u32[]{:S(2)}, u32[]{:S(2)}) collective-permute-start(bf16[89,8,128]{2,1,0:T(8,128)(2,1)S(1)} %get-tuple-element.84), channel_id=1, source_target_pairs={{0,24},{2,26},{4,28},{6,30},{8,16},{10,18},{12,20},{14,22},{16,8},... | collective-permute-start | bytes 546824 | tf_op jit(solution)/shard_map/ppermute | solution.py:22
  (2 other events, 6.6 us)

commit v14 on v9

--- a/solution.py
+++ b/solution.py
@@ -13,7 +13,7 @@
 PLAIN = (((1,), (0,)), ((), ()))
 TURNED = (((1,), (1,)), ((), ()))
 MIB = 1024 * 1024
-UNROLL = 7
+UNROLL = 14
 dot = functools.partial(lax.dot_general, preferred_element_type=F32)
 
 

time: 139 us -> 139 us (level)
  waiting for transfers between devices: 74.5 us -> 76.1 us
    ppermute x31, waiting for transfers between devices: 74.5 us -> 76.1 us  [swap(): return lax.ppermute(value, axis, [(at, at ^ stride) for at in range(size)])]
  transfers between devices with their start and end apart: 31 -> 31, of which waited for: 17 -> 18; matrix products, arithmetic and copies ran while one was open for 5% -> 5% of each run, Pallas kernels for 15% -> 14%
where the time goes in v14:
time: 139 us; the launch traced here: 138 us
  waiting for transfers between devices  76.1 us (55%)
  starting transfers between devices  31.5 us (23%)
  Pallas kernels  22 us (16%)
  other arithmetic  4.88 us (4%)
  local copies, waits for them, and re-layouts  2.87 us (2%)
    ppermute x31, waiting for transfers between devices, swap(): return lax.ppermute(value, axis, [(at, at ^ stride) for at in range(size)])  76.1 us
    ppermute x31, starting transfers between devices, swap(): return lax.ppermute(value, axis, [(at, at ^ stride) for at in range(size)])  31.5 us
    pallas_call x6, Pallas kernels, call(): pl.pallas_call(kernel, grid_spec=pltpu.PrefetchScalarGridSpec(num_scalar_...  22 us
  transfers between devices with their start and end apart: 31, of which 18 were waited for; matrix products, arithmetic and copies ran while one was open for 5% of the time, Pallas kernels for 14%

profile of v14, /device:TPU:0, one launch (start us, length us, event | category | flops | bytes accessed | tf_op | source)
XLA Modules:
  0.0 138.3 jit_solution(6377562705089507192)
XLA Ops:
  0.6 3.1 %collective-permute-start = (bf16[32,4096]{1,0:T(8,128)(2,1)}, bf16[32,4096]{1,0:T(8,128)(2,1)S(1)}, u32[]{:S(2)}, u32[]{:S(2)}) collective-permute-start(bf16[32,4096]{1,0:T(8,128)(2,1)} %refs_0_.2), channel_id=1, source_target_pairs={{0,8},{2,10},{4,12},{6,14},{8,0},{10,2},{12,4},{14,6},{16,24},{18,... | collective-permute-start | bytes 786440 | tf_op jit(solution)/shard_map/ppermute | solution.py:22
  7.6 1.2 copy-done.1
  8.9 1.6 %shard_map.76 = (bf16[89,8,128]{2,1,0:T(8,128)(2,1)S(1)}, bf16[89,8,128]{2,1,0:T(8,128)(2,1)S(1)}, bf16[89,8,128]{2,1,0:T(8,128)(2,1)S(1)}, bf16[89,8,128]{2,1,0:T(8,128)(2,1)S(1)}) custom-call(s32[17,56]{1,0:T(8,128)S(1)} %pad_add_fusion.table, bf16[8,9,56,128]{3,2,1,0:T(8,128)(2,1)S(1)} %bitcast.36), custom_call_target="tpu_custom_call" | custom-call | bytes 1000000 | tf_op jit(solution)/shard_map/pallas_call | solution.py:261
  10.5 2.5 %collective-permute-start.3 = (bf16[89,8,128]{2,1,0:T(8,128)(2,1)S(1)}, bf16[89,8,128]{2,1,0:T(8,128)(2,1)S(1)}, u32[]{:S(2)}, u32[]{:S(2)}) collective-permute-start(bf16[89,8,128]{2,1,0:T(8,128)(2,1)S(1)} %get-tuple-element.48), channel_id=1, source_target_pairs={{0,24},{2,26},{4,28},{6,30},{8,16},{10,18},{12,20},{14,22},{16,8},... | collective-permute-start | bytes 546824 | tf_op jit(solution)/shard_map/ppermute | solution.py:22
  13.2 1.7 %collective-permute-start.1 = (bf16[89,8,128]{2,1,0:T(8,128)(2,1)S(1)}, bf16[89,8,128]{2,1,0:T(8,128)(2,1)S(1)}, u32[]{:S(2)}, u32[]{:S(2)}) collective-permute-start(bf16[89,8,128]{2,1,0:T(8,128)(2,1)S(1)} %get-tuple-element.46), channel_id=1, source_target_pairs={{0,8},{2,10},{4,12},{6,14},{8,0},{10,2},{12,4},{14,6},{16,24},{18,... | collective-permute-start | bytes 546824 | tf_op jit(solution)/shard_map/ppermute | solution.py:22
  14.9 5.0 %collective-permute-done.3 = bf16[89,8,128]{2,1,0:T(8,128)(2,1)S(1)} collective-permute-done((bf16[89,8,128]{2,1,0:T(8,128)(2,1)S(1)}, bf16[89,8,128]{2,1,0:T(8,128)(2,1)S(1)}, u32[]{:S(2)}, u32[]{:S(2)}) %collective-permute-start.3) | collective-permute-done | bytes 182304 | tf_op jit(solution)/shard_map/ppermute | solution.py:22
  20.5 8.7 %collective-permute-done.2 = bf16[89,8,128]{2,1,0:T(8,128)(2,1)S(1)} collective-permute-done((bf16[89,8,128]{2,1,0:T(8,128)(2,1)S(1)}, bf16[89,8,128]{2,1,0:T(8,128)(2,1)S(1)}, u32[]{:S(2)}, u32[]{:S(2)}) %collective-permute-start.2) | collective-permute-done | bytes 182304 | tf_op jit(solution)/shard_map/ppermute | solution.py:22
  29.3 1.6 %collective-permute-start.10 = (bf16[4,89,8,128]{3,2,1,0:T(8,128)(2,1)S(1)}, bf16[4,89,8,128]{3,2,1,0:T(8,128)(2,1)S(1)}, u32[]{:S(2)}, u32[]{:S(2)}) collective-permute-start(bf16[4,89,8,128]{3,2,1,0:T(8,128)(2,1)S(1)} %pad_maximum_fusion.1.refs_0_), channel_id=1, source_target_pairs={{0,2},{2,0},{4,6},{6,4},{8,10},{10,8},{12,14},{14,12},{16,18},{18,... | collective-permute-start | bytes 2187272 | tf_op jit(solution)/shard_map/ppermute | solution.py:22
  30.9 1.5 %collective-permute-start.12 = (bf16[4,89,8,128]{3,2,1,0:T(8,128)(2,1)S(1)}, bf16[4,89,8,128]{3,2,1,0:T(8,128)(2,1)S(1)}, u32[]{:S(2)}, u32[]{:S(2)}) collective-permute-start(bf16[4,89,8,128]{3,2,1,0:T(8,128)(2,1)S(1)} %pad_maximum_fusion.1.refs_0_), channel_id=1, source_target_pairs={{0,4},{2,6},{4,0},{6,2},{8,12},{10,14},{12,8},{14,10},{16,20},{18,... | collective-permute-start | bytes 2187272 | tf_op jit(solution)/shard_map/ppermute | solution.py:22
  33.0 2.6 %collective-permute-start.8 = (bf16[32,4096]{1,0:T(8,128)(2,1)S(1)}, bf16[32,4096]{1,0:T(8,128)(2,1)S(1)}, u32[]{:S(2)}, u32[]{:S(2)}) collective-permute-start(bf16[32,4096]{1,0:T(8,128)(2,1)S(1)} %copy-done.3), channel_id=1, source_target_pairs={{0,8},{2,10},{4,12},{6,14},{8,0},{10,2},{12,4},{14,6},{16,24},{18,... | collective-permute-start | bytes 786440 | tf_op jit(solution)/shard_map/ppermute | solution.py:22
  35.6 10.1 %collective-permute-done.7.refs_2_ = bf16[32,4096]{1,0:T(8,128)(2,1)S(1)} collective-permute-done((bf16[32,4096]{1,0:T(8,128)(2,1)S(1)}, bf16[32,4096]{1,0:T(8,128)(2,1)S(1)}, u32[]{:S(2)}, u32[]{:S(2)}) %collective-permute-start.7) | collective-permute-done | bytes 262176 | tf_op jit(solution)/shard_map/ppermute | solution.py:22
  46.5 2.3 %collective-permute-start.14 = (bf16[32,4096]{1,0:T(8,128)(2,1)S(1)}, bf16[32,4096]{1,0:T(8,128)(2,1)S(1)}, u32[]{:S(2)}, u32[]{:S(2)}) collective-permute-start(bf16[32,4096]{1,0:T(8,128)(2,1)S(1)} %copy-done.3), channel_id=1, source_target_pairs={{0,16},{2,18},{4,20},{6,22},{8,24},{10,26},{12,28},{14,30},{16,0},... | collective-permute-start | bytes 786440 | tf_op jit(solution)/shard_map/ppermute | solution.py:22
  50.0 9.1 %collective-permute-done.9.refs_3_ = bf16[32,4096]{1,0:T(8,128)(2,1)S(1)} collective-permute-done((bf16[32,4096]{1,0:T(8,128)(2,1)S(1)}, bf16[32,4096]{1,0:T(8,128)(2,1)S(1)}, u32[]{:S(2)}, u32[]{:S(2)}) %collective-permute-start.9) | collective-permute-done | bytes 262176 | tf_op jit(solution)/shard_map/ppermute | solution.py:22
  59.2 1.5 %collective-permute-done.14.refs_2_ = bf16[32,4096]{1,0:T(8,128)(2,1)S(1)} collective-permute-done((bf16[32,4096]{1,0:T(8,128)(2,1)S(1)}, bf16[32,4096]{1,0:T(8,128)(2,1)S(1)}, u32[]{:S(2)}, u32[]{:S(2)}) %collective-permute-start.14) | collective-permute-done | bytes 262176 | tf_op jit(solution)/shard_map/ppermute | solution.py:22
  61.1 1.8 %shard_map.77.refs_7_.refs_6_ = bf16[89,128,128]{2,1,0:T(8,128)(2,1)S(1)} custom-call(s32[17,56]{1,0:T(8,128)S(1)} %pad_add_fusion.table, bf16[4,89,8,128]{3,2,1,0:T(8,128)(2,1)S(1)} %pad_maximum_fusion.1.refs_0_, bf16[4,89,8,128]{3,2,1,0:T(8,128)(2,1)S(1)} %collective-permute-done.10.refs_1_, bf16[4,89,8,128]{3,2,1,0:T(8,128)(2,1)S(1)} %collective-permute-done.12.refs_2_, ...), custom_call_target="tpu_custom_call" | custom-call | bytes 10000000 | tf_op jit(solution)/shard_map/pallas_call | solution.py:261
  62.9 5.0 %shard_map.78 = (bf16[4096,256]{1,0:T(8,128)(2,1)S(1)}, f32[14,256,128]{2,1,0:T(8,128)S(1)}, f32[14,256,128]{2,1,0:T(8,128)S(1)}, bf16[14,128,256]{2,1,0:T(8,128...) custom-call(s32[17,56]{1,0:T(8,128)S(1)} %pad_add_fusion.table, ...), custom_call_target="tpu_custom_call" | custom-call | bytes 30000000 | tf_op jit(solution)/shard_map/pallas_call | solution.py:261
  67.9 1.5 %collective-permute-done.16.refs_3_ = bf16[32,4096]{1,0:T(8,128)(2,1)S(1)} collective-permute-done((bf16[32,4096]{1,0:T(8,128)(2,1)S(1)}, bf16[32,4096]{1,0:T(8,128)(2,1)S(1)}, u32[]{:S(2)}, u32[]{:S(2)}) %collective-permute-start.16) | collective-permute-done | bytes 262176 | tf_op jit(solution)/shard_map/ppermute | solution.py:22
  70.0 2.0 %collective-permute-done.17 = bf16[4,32,4096]{2,1,0:T(8,128)(2,1)S(1)} collective-permute-done((bf16[4,32,4096]{2,1,0:T(8,128)(2,1)S(1)}, bf16[4,32,4096]{2,1,0:T(8,128)(2,1)S(1)}, u32[]{:S(2)}, u32[]{:S(2)}) %collective-permute-start.17) | collective-permute-done | bytes 1048608 | tf_op jit(solution)/shard_map/ppermute | solution.py:22
  73.2 9.7 %shard_map.79 = (bf16[4,32,4096]{2,1,0:T(8,128)(2,1)S(1)}, bf16[4,32,4096]{2,1,0:T(8,128)(2,1)S(1)}, bf16[4,89,8,128]{3,2,1,0:T(8,128)(2,1)S(1)}, bf16[4,89,8,12...) custom-call(s32[17,56]{1,0:T(8,128)S(1)} %pad_add_fusion.table, ...), custom_call_target="tpu_custom_call" | custom-call | bytes 40000000 | tf_op jit(solution)/shard_map/pallas_call | solution.py:261
  82.9 3.3 %collective-permute-done.18 = bf16[2,32,4096]{2,1,0:T(8,128)(2,1)S(1)} collective-permute-done((bf16[2,32,4096]{2,1,0:T(8,128)(2,1)S(1)}, bf16[2,32,4096]{2,1,0:T(8,128)(2,1)S(1)}, u32[]{:S(2)}, u32[]{:S(2)}) %collective-permute-start.18) | collective-permute-done | bytes 524320 | tf_op jit(solution)/shard_map/ppermute | solution.py:22
  87.2 1.6 %collective-permute-done.21 = bf16[4,32,4096]{2,1,0:T(8,128)(2,1)S(1)} collective-permute-done((bf16[4,32,4096]{2,1,0:T(8,128)(2,1)S(1)}, bf16[4,32,4096]{2,1,0:T(8,128)(2,1)S(1)}, u32[]{:S(2)}, u32[]{:S(2)}) %collective-permute-start.21) | collective-permute-done | bytes 1048608 | tf_op jit(solution)/shard_map/ppermute | solution.py:22
  89.5 2.6 %collective-permute-start.19 = (bf16[32,4096]{1,0:T(8,128)(2,1)S(1)}, bf16[32,4096]{1,0:T(8,128)(2,1)S(1)}, u32[]{:S(2)}, u32[]{:S(2)}) collective-permute-start(bf16[32,4096]{1,0:T(8,128)(2,1)S(1)} %fusion.2), channel_id=1, source_target_pairs={{0,16},{2,18},{4,20},{6,22},{8,24},{10,26},{12,28},{14,30},{16,0},... | collective-permute-start | bytes 786440 | tf_op jit(solution)/shard_map/ppermute | solution.py:22
  92.1 5.0 %collective-permute-done.24.got_1 = bf16[2,89,8,128]{3,2,1,0:T(8,128)(2,1)S(1)} collective-permute-done((bf16[2,89,8,128]{3,2,1,0:T(8,128)(2,1)S(1)}, bf16[2,89,8,128]{3,2,1,0:T(8,128)(2,1)S(1)}, u32[]{:S(2)}, u32[]{:S(2)}) %collective-permute-start.24) | collective-permute-done | bytes 364576 | tf_op jit(solution)/shard_map/ppermute | solution.py:22
  98.9 1.5 %collective-permute-start.26 = (bf16[4,89,8,128]{3,2,1,0:T(8,128)(2,1)S(1)}, bf16[4,89,8,128]{3,2,1,0:T(8,128)(2,1)S(1)}, u32[]{:S(2)}, u32[]{:S(2)}) collective-permute-start(bf16[4,89,8,128]{3,2,1,0:T(8,128)(2,1)S(1)} %get-tuple-element.77), channel_id=1, source_target_pairs={{0,2},{2,0},{4,6},{6,4},{8,10},{10,8},{12,14},{14,12},{16,18},{18,... | collective-permute-start | bytes 2187272 | tf_op jit(solution)/shard_map/ppermute | solution.py:22
  100.4 8.3 %collective-permute-done.22 = bf16[2,32,4096]{2,1,0:T(8,128)(2,1)S(1)} collective-permute-done((bf16[2,32,4096]{2,1,0:T(8,128)(2,1)S(1)}, bf16[2,32,4096]{2,1,0:T(8,128)(2,1)S(1)}, u32[]{:S(2)}, u32[]{:S(2)}) %collective-permute-start.22) | collective-permute-done | bytes 524320 | tf_op jit(solution)/shard_map/ppermute | solution.py:22
  108.7 1.2 collective-permute-start.23
  110.7 5.3 %collective-permute-done.27 = bf16[4,89,8,128]{3,2,1,0:T(8,128)(2,1)S(1)} collective-permute-done((bf16[4,89,8,128]{3,2,1,0:T(8,128)(2,1)S(1)}, bf16[4,89,8,128]{3,2,1,0:T(8,128)(2,1)S(1)}, u32[]{:S(2)}, u32[]{:S(2)}) %collective-permute-start.27) | collective-permute-done | bytes 729120 | tf_op jit(solution)/shard_map/ppermute | solution.py:22
  117.0 2.6 %collective-permute-start.29 = (bf16[89,8,128]{2,1,0:T(8,128)(2,1)S(1)}, bf16[89,8,128]{2,1,0:T(8,128)(2,1)S(1)}, u32[]{:S(2)}, u32[]{:S(2)}) collective-permute-start(bf16[89,8,128]{2,1,0:T(8,128)(2,1)S(1)} %get-tuple-element.81), channel_id=1, source_target_pairs={{0,16},{2,18},{4,20},{6,22},{8,24},{10,26},{12,28},{14,30},{16,0},... | collective-permute-start | bytes 546824 | tf_op jit(solution)/shard_map/ppermute | solution.py:22
  119.6 1.5 %collective-permute-start.30 = (bf16[89,8,128]{2,1,0:T(8,128)(2,1)S(1)}, bf16[89,8,128]{2,1,0:T(8,128)(2,1)S(1)}, u32[]{:S(2)}, u32[]{:S(2)}) collective-permute-start(bf16[89,8,128]{2,1,0:T(8,128)(2,1)S(1)} %get-tuple-element.82), channel_id=1, source_target_pairs={{0,24},{2,26},{4,28},{6,30},{8,16},{10,18},{12,20},{14,22},{16,8},... | collective-permute-start | bytes 546824 | tf_op jit(solution)/shard_map/ppermute | solution.py:22
  121.1 10.3 %collective-permute-done.23 = bf16[32,4096]{1,0:T(8,128)(2,1)S(1)} collective-permute-done((bf16[32,4096]{1,0:T(8,128)(2,1)S(1)}, bf16[32,4096]{1,0:T(8,128)(2,1)S(1)}, u32[]{:S(2)}, u32[]{:S(2)}) %collective-permute-start.23) | collective-permute-done | bytes 262176 | tf_op jit(solution)/shard_map/ppermute | solution.py:22
  132.2 3.1 %collective-permute-done.29.refs_2_ = bf16[89,8,128]{2,1,0:T(8,128)(2,1)S(1)} collective-permute-done((bf16[89,8,128]{2,1,0:T(8,128)(2,1)S(1)}, bf16[89,8,128]{2,1,0:T(8,128)(2,1)S(1)}, u32[]{:S(2)}, u32[]{:S(2)}) %collective-permute-start.29) | collective-permute-done | bytes 182304 | tf_op jit(solution)/shard_map/ppermute | solution.py:22
  135.3 3.0 %shard_map.81 = bf16[8,9,56,128]{3,2,1,0:T(8,128)(2,1)} custom-call(s32[17,56]{1,0:T(8,128)S(1)} %pad_add_fusion.table, bf16[89,8,128]{2,1,0:T(8,128)(2,1)S(1)} %get-tuple-element.83.refs_0_, bf16[89,8,128]{2,1,0:T(8,128)(2,1)S(1)} %collective-permute-done.28.refs_1_, bf16[89,8,128]{2,1,0:T(8,128)(2,1)S(1)} %collective-permute-done.29.refs_2_, ...), custom_call_target="tpu_custom_call" | custom-call | bytes 2000000 | tf_op jit(solution)/shard_map/pallas_call | solution.py:261
  (72 shorter events, 15.7 us)
Async XLA Ops:
  0.6 19.4 %collective-permute-start = (bf16[32,4096]{1,0:T(8,128)(2,1)}, bf16[32,4096]{1,0:T(8,128)(2,1)S(1)}, u32[]{:S(2)}, u32[]{:S(2)}) collective-permute-start(bf16[32,4096]{1,0:T(8,128)(2,1)} %refs_0_.2), channel_id=1, source_target_pairs={{0,8},{2,10},{4,12},{6,14},{8,0},{10,2},{12,4},{14,6},{16,24},{18,... | collective-permute-start | bytes 786440 | tf_op jit(solution)/shard_map/ppermute | solution.py:22
  8.9 24.2 %copy-start.3 = (bf16[32,4096]{1,0:T(8,128)(2,1)S(1)}, bf16[32,4096]{1,0:T(8,128)(2,1)}, u32[]{:S(2)}) copy-start(bf16[32,4096]{1,0:T(8,128)(2,1)} %refs_0_.3) | copy-start | bytes 786436
  10.5 9.5 %collective-permute-start.3 = (bf16[89,8,128]{2,1,0:T(8,128)(2,1)S(1)}, bf16[89,8,128]{2,1,0:T(8,128)(2,1)S(1)}, u32[]{:S(2)}, u32[]{:S(2)}) collective-permute-start(bf16[89,8,128]{2,1,0:T(8,128)(2,1)S(1)} %get-tuple-element.48), channel_id=1, source_target_pairs={{0,24},{2,26},{4,28},{6,30},{8,16},{10,18},{12,20},{14,22},{16,8},... | collective-permute-start | bytes 546824 | tf_op jit(solution)/shard_map/ppermute | solution.py:22
  13.0 16.1 %collective-permute-start.2 = (bf16[89,8,128]{2,1,0:T(8,128)(2,1)S(1)}, bf16[89,8,128]{2,1,0:T(8,128)(2,1)S(1)}, u32[]{:S(2)}, u32[]{:S(2)}) collective-permute-start(bf16[89,8,128]{2,1,0:T(8,128)(2,1)S(1)} %get-tuple-element.47), channel_id=1, source_target_pairs={{0,16},{2,18},{4,20},{6,22},{8,24},{10,26},{12,28},{14,30},{16,0},... | collective-permute-start | bytes 546824 | tf_op jit(solution)/shard_map/ppermute | solution.py:22
  13.2 16.0 %collective-permute-start.1 = (bf16[89,8,128]{2,1,0:T(8,128)(2,1)S(1)}, bf16[89,8,128]{2,1,0:T(8,128)(2,1)S(1)}, u32[]{:S(2)}, u32[]{:S(2)}) collective-permute-start(bf16[89,8,128]{2,1,0:T(8,128)(2,1)S(1)} %get-tuple-element.46), channel_id=1, source_target_pairs={{0,8},{2,10},{4,12},{6,14},{8,0},{10,2},{12,4},{14,6},{16,24},{18,... | collective-permute-start | bytes 546824 | tf_op jit(solution)/shard_map/ppermute | solution.py:22
  14.9 14.3 %collective-permute-start.4 = (bf16[32,4096]{1,0:T(8,128)(2,1)}, bf16[32,4096]{1,0:T(8,128)(2,1)S(1)}, u32[]{:S(2)}, u32[]{:S(2)}) collective-permute-start(bf16[32,4096]{1,0:T(8,128)(2,1)} %refs_0_.2), channel_id=1, source_target_pairs={{0,1},{1,0},{2,3},{3,2},{4,5},{5,4},{6,7},{7,6},{8,9},{9,8},{10,11... | collective-permute-start | bytes 786440 | tf_op jit(solution)/shard_map/ppermute | solution.py:22
  20.0 9.3 %collective-permute-start.6 = (bf16[32,4096]{1,0:T(8,128)(2,1)}, bf16[32,4096]{1,0:T(8,128)(2,1)S(1)}, u32[]{:S(2)}, u32[]{:S(2)}) collective-permute-start(bf16[32,4096]{1,0:T(8,128)(2,1)} %refs_0_.3), channel_id=1, source_target_pairs={{0,1},{1,0},{2,3},{3,2},{4,5},{5,4},{6,7},{7,6},{8,9},{9,8},{10,11... | collective-permute-start | bytes 786440 | tf_op jit(solution)/shard_map/ppermute | solution.py:22
  20.0 9.3 %collective-permute-start.5 = (bf16[32,4096]{1,0:T(8,128)(2,1)S(1)}, bf16[32,4096]{1,0:T(8,128)(2,1)S(1)}, u32[]{:S(2)}, u32[]{:S(2)}) collective-permute-start(bf16[32,4096]{1,0:T(8,128)(2,1)S(1)} %collective-permute-done.refs_1_), channel_id=1, source_target_pairs={{0,1},{1,0},{2,3},{3,2},{4,5},{5,4},{6,7},{7,6},{8,9},{9,8},{10,11... | collective-permute-start | bytes 786440 | tf_op jit(solution)/shard_map/ppermute | solution.py:22
  29.3 19.5 %collective-permute-start.10 = (bf16[4,89,8,128]{3,2,1,0:T(8,128)(2,1)S(1)}, bf16[4,89,8,128]{3,2,1,0:T(8,128)(2,1)S(1)}, u32[]{:S(2)}, u32[]{:S(2)}) collective-permute-start(bf16[4,89,8,128]{3,2,1,0:T(8,128)(2,1)S(1)} %pad_maximum_fusion.1.refs_0_), channel_id=1, source_target_pairs={{0,2},{2,0},{4,6},{6,4},{8,10},{10,8},{12,14},{14,12},{16,18},{18,... | collective-permute-start | bytes 2187272 | tf_op jit(solution)/shard_map/ppermute | solution.py:22
  30.9 18.5 %collective-permute-start.12 = (bf16[4,89,8,128]{3,2,1,0:T(8,128)(2,1)S(1)}, bf16[4,89,8,128]{3,2,1,0:T(8,128)(2,1)S(1)}, u32[]{:S(2)}, u32[]{:S(2)}) collective-permute-start(bf16[4,89,8,128]{3,2,1,0:T(8,128)(2,1)S(1)} %pad_maximum_fusion.1.refs_0_), channel_id=1, source_target_pairs={{0,4},{2,6},{4,0},{6,2},{8,12},{10,14},{12,8},{14,10},{16,20},{18,... | collective-permute-start | bytes 2187272 | tf_op jit(solution)/shard_map/ppermute | solution.py:22
  32.4 13.3 %collective-permute-start.7 = (bf16[32,4096]{1,0:T(8,128)(2,1)S(1)}, bf16[32,4096]{1,0:T(8,128)(2,1)S(1)}, u32[]{:S(2)}, u32[]{:S(2)}) collective-permute-start(bf16[32,4096]{1,0:T(8,128)(2,1)S(1)} %copy-done.2), channel_id=1, source_target_pairs={{0,16},{2,18},{4,20},{6,22},{8,24},{10,26},{12,28},{14,30},{16,0},... | collective-permute-start | bytes 786440 | tf_op jit(solution)/shard_map/ppermute | solution.py:22
  33.0 12.9 %collective-permute-start.8 = (bf16[32,4096]{1,0:T(8,128)(2,1)S(1)}, bf16[32,4096]{1,0:T(8,128)(2,1)S(1)}, u32[]{:S(2)}, u32[]{:S(2)}) collective-permute-start(bf16[32,4096]{1,0:T(8,128)(2,1)S(1)} %copy-done.3), channel_id=1, source_target_pairs={{0,8},{2,10},{4,12},{6,14},{8,0},{10,2},{12,4},{14,6},{16,24},{18,... | collective-permute-start | bytes 786440 | tf_op jit(solution)/shard_map/ppermute | solution.py:22
  45.9 13.2 %collective-permute-start.9 = (bf16[32,4096]{1,0:T(8,128)(2,1)S(1)}, bf16[32,4096]{1,0:T(8,128)(2,1)S(1)}, u32[]{:S(2)}, u32[]{:S(2)}) collective-permute-start(bf16[32,4096]{1,0:T(8,128)(2,1)S(1)} %collective-permute-done.7.refs_2_), channel_id=1, source_target_pairs={{0,8},{2,10},{4,12},{6,14},{8,0},{10,2},{12,4},{14,6},{16,24},{18,... | collective-permute-start | bytes 786440 | tf_op jit(solution)/shard_map/ppermute | solution.py:22
  46.5 14.2 %collective-permute-start.14 = (bf16[32,4096]{1,0:T(8,128)(2,1)S(1)}, bf16[32,4096]{1,0:T(8,128)(2,1)S(1)}, u32[]{:S(2)}, u32[]{:S(2)}) collective-permute-start(bf16[32,4096]{1,0:T(8,128)(2,1)S(1)} %copy-done.3), channel_id=1, source_target_pairs={{0,16},{2,18},{4,20},{6,22},{8,24},{10,26},{12,28},{14,30},{16,0},... | collective-permute-start | bytes 786440 | tf_op jit(solution)/shard_map/ppermute | solution.py:22
  48.8 11.8 %collective-permute-start.11 = (bf16[2,89,8,128]{3,2,1,0:T(8,128)(2,1)S(1)}, bf16[2,89,8,128]{3,2,1,0:T(8,128)(2,1)S(1)}, u32[]{:S(2)}, u32[]{:S(2)}) collective-permute-start(bf16[2,89,8,128]{3,2,1,0:T(8,128)(2,1)S(1)} %slice.135), channel_id=1, source_target_pairs={{0,4},{2,6},{4,0},{6,2},{8,12},{10,14},{12,8},{14,10},{16,20},{18,... | collective-permute-start | bytes 1093640 | tf_op jit(solution)/shard_map/ppermute | solution.py:22
  49.4 11.2 %collective-permute-start.13 = (bf16[2,89,8,128]{3,2,1,0:T(8,128)(2,1)S(1)}, bf16[2,89,8,128]{3,2,1,0:T(8,128)(2,1)S(1)}, u32[]{:S(2)}, u32[]{:S(2)}) collective-permute-start(bf16[2,89,8,128]{3,2,1,0:T(8,128)(2,1)S(1)} %slice.136), channel_id=1, source_target_pairs={{0,2},{2,0},{4,6},{6,4},{8,10},{10,8},{12,14},{14,12},{16,18},{18,... | collective-permute-start | bytes 1093640 | tf_op jit(solution)/shard_map/ppermute | solution.py:22
  60.7 2.2 %collective-permute-start.15 = (bf16[64,4096]{1,0:T(8,128)(2,1)S(1)}, bf16[64,4096]{1,0:T(8,128)(2,1)S(1)}, u32[]{:S(2)}, u32[]{:S(2)}) collective-permute-start(bf16[64,4096]{1,0:T(8,128)(2,1)S(1)} %pad_maximum_fusion.2), channel_id=1, source_target_pairs={{0,1},{1,0},{2,3},{3,2},{4,5},{5,4},{6,7},{7,6},{8,9},{9,8},{10,11... | collective-permute-start | bytes 1572872 | tf_op jit(solution)/shard_map/ppermute | solution.py:22
  60.7 8.7 %collective-permute-start.16 = (bf16[32,4096]{1,0:T(8,128)(2,1)S(1)}, bf16[32,4096]{1,0:T(8,128)(2,1)S(1)}, u32[]{:S(2)}, u32[]{:S(2)}) collective-permute-start(bf16[32,4096]{1,0:T(8,128)(2,1)S(1)} %collective-permute-done.14.refs_2_), channel_id=1, source_target_pairs={{0,8},{2,10},{4,12},{6,14},{8,0},{10,2},{12,4},{14,6},{16,24},{18,... | collective-permute-start | bytes 786440 | tf_op jit(solution)/shard_map/ppermute | solution.py:22
  69.4 2.7 %collective-permute-start.17 = (bf16[4,32,4096]{2,1,0:T(8,128)(2,1)S(1)}, bf16[4,32,4096]{2,1,0:T(8,128)(2,1)S(1)}, u32[]{:S(2)}, u32[]{:S(2)}) collective-permute-start(bf16[4,32,4096]{2,1,0:T(8,128)(2,1)S(1)} %get-tuple-element.57), channel_id=1, source_target_pairs={{0,1},{1,0},{2,3},{3,2},{4,5},{5,4},{6,7},{7,6},{8,9},{9,8},{10,11... | collective-permute-start | bytes 3145736 | tf_op jit(solution)/shard_map/ppermute | solution.py:22
  69.4 3.7 %collective-permute-start.20 = (bf16[96,4096]{1,0:T(8,128)(2,1)S(1)}, bf16[96,4096]{1,0:T(8,128)(2,1)S(1)}, u32[]{:S(2)}, u32[]{:S(2)}) collective-permute-start(bf16[96,4096]{1,0:T(8,128)(2,1)S(1)} %pad_maximum_fusion), channel_id=1, source_target_pairs={{0,1},{1,0},{2,3},{3,2},{4,5},{5,4},{6,7},{7,6},{8,9},{9,8},{10,11... | collective-permute-start | bytes 2359304 | tf_op jit(solution)/shard_map/ppermute | solution.py:22
  72.2 14.0 %collective-permute-start.18 = (bf16[2,32,4096]{2,1,0:T(8,128)(2,1)S(1)}, bf16[2,32,4096]{2,1,0:T(8,128)(2,1)S(1)}, u32[]{:S(2)}, u32[]{:S(2)}) collective-permute-start(bf16[2,32,4096]{2,1,0:T(8,128)(2,1)S(1)} %add_convert_fusion.1), channel_id=1, source_target_pairs={{0,8},{2,10},{4,12},{6,14},{8,0},{10,2},{12,4},{14,6},{16,24},{18,... | collective-permute-start | bytes 1572872 | tf_op jit(solution)/shard_map/ppermute | solution.py:22
  86.2 2.7 %collective-permute-start.21 = (bf16[4,32,4096]{2,1,0:T(8,128)(2,1)S(1)}, bf16[4,32,4096]{2,1,0:T(8,128)(2,1)S(1)}, u32[]{:S(2)}, u32[]{:S(2)}) collective-permute-start(bf16[4,32,4096]{2,1,0:T(8,128)(2,1)S(1)} %get-tuple-element.68), channel_id=1, source_target_pairs={{0,1},{1,0},{2,3},{3,2},{4,5},{5,4},{6,7},{7,6},{8,9},{9,8},{10,11... | collective-permute-start | bytes 3145736 | tf_op jit(solution)/shard_map/ppermute | solution.py:22
  86.2 10.9 %collective-permute-start.24 = (bf16[2,89,8,128]{3,2,1,0:T(8,128)(2,1)S(1)}, bf16[2,89,8,128]{3,2,1,0:T(8,128)(2,1)S(1)}, u32[]{:S(2)}, u32[]{:S(2)}) collective-permute-start(bf16[2,89,8,128]{3,2,1,0:T(8,128)(2,1)S(1)} %get-tuple-element.73), channel_id=1, source_target_pairs={{0,2},{2,0},{4,6},{6,4},{8,10},{10,8},{12,14},{14,12},{16,18},{18,... | collective-permute-start | bytes 1093640 | tf_op jit(solution)/shard_map/ppermute | solution.py:22
  86.7 10.6 %collective-permute-start.25 = (bf16[2,89,8,128]{3,2,1,0:T(8,128)(2,1)S(1)}, bf16[2,89,8,128]{3,2,1,0:T(8,128)(2,1)S(1)}, u32[]{:S(2)}, u32[]{:S(2)}) collective-permute-start(bf16[2,89,8,128]{3,2,1,0:T(8,128)(2,1)S(1)} %get-tuple-element.74), channel_id=1, source_target_pairs={{0,4},{2,6},{4,0},{6,2},{8,12},{10,14},{12,8},{14,10},{16,20},{18,... | collective-permute-start | bytes 1093640 | tf_op jit(solution)/shard_map/ppermute | solution.py:22
  89.0 19.6 %collective-permute-start.22 = (bf16[2,32,4096]{2,1,0:T(8,128)(2,1)S(1)}, bf16[2,32,4096]{2,1,0:T(8,128)(2,1)S(1)}, u32[]{:S(2)}, u32[]{:S(2)}) collective-permute-start(bf16[2,32,4096]{2,1,0:T(8,128)(2,1)S(1)} %add_convert_fusion), channel_id=1, source_target_pairs={{0,8},{2,10},{4,12},{6,14},{8,0},{10,2},{12,4},{14,6},{16,24},{18,... | collective-permute-start | bytes 1572872 | tf_op jit(solution)/shard_map/ppermute | solution.py:22
  89.5 19.2 %collective-permute-start.19 = (bf16[32,4096]{1,0:T(8,128)(2,1)S(1)}, bf16[32,4096]{1,0:T(8,128)(2,1)S(1)}, u32[]{:S(2)}, u32[]{:S(2)}) collective-permute-start(bf16[32,4096]{1,0:T(8,128)(2,1)S(1)} %fusion.2), channel_id=1, source_target_pairs={{0,16},{2,18},{4,20},{6,22},{8,24},{10,26},{12,28},{14,30},{16,0},... | collective-permute-start | bytes 786440 | tf_op jit(solution)/shard_map/ppermute | solution.py:22
  98.3 17.8 %collective-permute-start.27 = (bf16[4,89,8,128]{3,2,1,0:T(8,128)(2,1)S(1)}, bf16[4,89,8,128]{3,2,1,0:T(8,128)(2,1)S(1)}, u32[]{:S(2)}, u32[]{:S(2)}) collective-permute-start(bf16[4,89,8,128]{3,2,1,0:T(8,128)(2,1)S(1)} %get-tuple-element.78), channel_id=1, source_target_pairs={{0,4},{2,6},{4,0},{6,2},{8,12},{10,14},{12,8},{14,10},{16,20},{18,... | collective-permute-start | bytes 2187272 | tf_op jit(solution)/shard_map/ppermute | solution.py:22
  98.9 17.4 %collective-permute-start.26 = (bf16[4,89,8,128]{3,2,1,0:T(8,128)(2,1)S(1)}, bf16[4,89,8,128]{3,2,1,0:T(8,128)(2,1)S(1)}, u32[]{:S(2)}, u32[]{:S(2)}) collective-permute-start(bf16[4,89,8,128]{3,2,1,0:T(8,128)(2,1)S(1)} %get-tuple-element.77), channel_id=1, source_target_pairs={{0,2},{2,0},{4,6},{6,4},{8,10},{10,8},{12,14},{14,12},{16,18},{18,... | collective-permute-start | bytes 2187272 | tf_op jit(solution)/shard_map/ppermute | solution.py:22
  108.7 22.7 %collective-permute-start.23 = (bf16[32,4096]{1,0:T(8,128)(2,1)S(1)}, bf16[32,4096]{1,0:T(8,128)(2,1)S(1)}, u32[]{:S(2)}, u32[]{:S(2)}) collective-permute-start(bf16[32,4096]{1,0:T(8,128)(2,1)S(1)} %fusion.3), channel_id=1, source_target_pairs={{0,16},{2,18},{4,20},{6,22},{8,24},{10,26},{12,28},{14,30},{16,0},... | collective-permute-start | bytes 786440 | tf_op jit(solution)/shard_map/ppermute | solution.py:22
  116.6 15.6 %collective-permute-start.28 = (bf16[89,8,128]{2,1,0:T(8,128)(2,1)S(1)}, bf16[89,8,128]{2,1,0:T(8,128)(2,1)S(1)}, u32[]{:S(2)}, u32[]{:S(2)}) collective-permute-start(bf16[89,8,128]{2,1,0:T(8,128)(2,1)S(1)} %get-tuple-element.80), channel_id=1, source_target_pairs={{0,8},{2,10},{4,12},{6,14},{8,0},{10,2},{12,4},{14,6},{16,24},{18,... | collective-permute-start | bytes 546824 | tf_op jit(solution)/shard_map/ppermute | solution.py:22
  117.0 18.3 %collective-permute-start.29 = (bf16[89,8,128]{2,1,0:T(8,128)(2,1)S(1)}, bf16[89,8,128]{2,1,0:T(8,128)(2,1)S(1)}, u32[]{:S(2)}, u32[]{:S(2)}) collective-permute-start(bf16[89,8,128]{2,1,0:T(8,128)(2,1)S(1)} %get-tuple-element.81), channel_id=1, source_target_pairs={{0,16},{2,18},{4,20},{6,22},{8,24},{10,26},{12,28},{14,30},{16,0},... | collective-permute-start | bytes 546824 | tf_op jit(solution)/shard_map/ppermute | solution.py:22
  119.6 15.7 %collective-permute-start.30 = (bf16[89,8,128]{2,1,0:T(8,128)(2,1)S(1)}, bf16[89,8,128]{2,1,0:T(8,128)(2,1)S(1)}, u32[]{:S(2)}, u32[]{:S(2)}) collective-permute-start(bf16[89,8,128]{2,1,0:T(8,128)(2,1)S(1)} %get-tuple-element.82), channel_id=1, source_target_pairs={{0,24},{2,26},{4,28},{6,30},{8,16},{10,18},{12,20},{14,22},{16,8},... | collective-permute-start | bytes 546824 | tf_op jit(solution)/shard_map/ppermute | solution.py:22
  (3 other events, 29.8 us)
